TPU v7x, 32 devices: a whole 2x2x4 slice. The times are simulated.
32 devices in a mesh: group: 2 (over x), gx: 16 (over z, y, core).
Axes of the slice: x: 2, y: 2, z: 4, core: 2. Of those that a mesh axis runs over, the one named last changes fastest.
Arguments:
- hidden: bfloat16 [2, 64, 16384], P(None, ('group', 'gx')), parts along dimension 1, may hold values from -6 to 6
- norm_gain: bfloat16 [16384], replicated, may hold values from 0.5 to 1.5
- w_query: bfloat16 [16384, 8192], P(None, 'gx'), may hold values from -0.046875 to 0.046875
- w_keyval: bfloat16 [2, 16384, 512], P(None, 'gx'), may hold values from -0.046875 to 0.046875
- w_out: bfloat16 [8192, 16384], P(None, 'gx'), may hold values from -0.5 to 0.5
- kv_cache: bfloat16 [2, 64, 1024, 512], P(None, ('group', 'gx')), parts along dimension 1, may hold values from -1700 to 1700
- lengths: int32 [64], P(('group', 'gx')), parts along dimension 0, may hold values from 1 to 1024, as said below
Outputs:
- attended: bfloat16 [2, 64, 16384], P(None, ('group', 'gx')), parts along dimension 1
There are 2 independent parts, one for each index of `group`. A program takes and returns all parts, laid end to end along the dimension named above; an argument that names none is the same for every part. Nothing has to cross between parts.
Inputs may be any that keep to these rules, and one draw needn't show every extreme that they name: `lengths`: some row has exactly 1024 valid entries in every draw.
All inputs are finite; a program needn't handle non-finite values.
Results may differ from a plain program's by a relative error of at most 0.0055.
The roundings to bfloat16 on the way count: a program that leaves them out, or rounds other values in their place, can miss the bound.
Values may be sent and summed in bfloat16 or wider, within the bound.
No kernel may reach another device: no remote copies, remote signals or barrier semaphores. Data moves between devices by JAX's collectives and lax.ppermute only.
A program may use at most 192 MiB of HBM per device.

v0:
```python
import functools
import math

import jax
import jax.numpy as jnp
import numpy as np
from jax import lax
from jax.experimental import pallas as pl
from jax.experimental.pallas import tpu as pltpu
from jax.sharding import PartitionSpec as P

HD = 128
ROPE_BASE = 500000.0
EPSILON = 1e-05
TAG = 128
VMEM_LIMIT = 8 * 1024 * 1024
OUT_VMEM_LIMIT = 18 * 1024 * 1024
VMEM = pl.BlockSpec(memory_space=pltpu.VMEM)
SMEM = pl.BlockSpec(memory_space=pltpu.SMEM)
HBM = pl.BlockSpec(memory_space=pltpu.HBM)


def permute(block, target):
    return lax.ppermute(block, "gx", [(int(i), int(t)) for i, t in enumerate(target)])


def moved(source, target):
    result = np.empty_like(source)
    result[target] = source
    return result


class Group:
    def __init__(self, blocks, sources, crossed=False):
        self.blocks, self.sources, self.crossed = blocks, sources, crossed

    def send(self, target, crossed=False):
        return Group(permute(self.blocks, target), [moved(source, target) for source in self.sources], crossed)


def join(groups):
    if len(groups) == 1:
        return groups[0]
    return Group(jnp.concatenate([g.blocks for g in groups], 0), [source for g in groups for source in g.sources])


def ring_order(size):
    if size > 4:
        return list(range(size))
    return list(range(0, size, 2)) + list(range(1, size, 2))[::-1]


def axes_of(devices):
    chips, inner = devices // 2, 1
    while inner * inner * 4 <= chips and chips % (inner * 2) == 0:
        inner *= 2
    sizes = (chips // inner, inner, 2)
    place = np.arange(devices).reshape(sizes)
    result = []
    for axis, size in enumerate(sizes):
        order = ring_order(size)
        after = np.empty(size, int)
        for here, there in zip(order, order[1:] + order[:1]):
            after[here] = there
        before = np.argsort(after)
        result.append((size, np.take(place, after, axis).ravel(), np.take(place, before, axis).ravel()))
    return result


def ring(group, axis):
    size, following, preceding = axis
    groups = []
    forward = backward = group
    for step in range(1, size // 2 + 1):
        forward = forward.send(following)
        groups.append(forward)
        if 2 * step < size:
            backward = backward.send(preceding)
            groups.append(backward)
    return groups


def gather(block, devices, meanwhile=()):
    (size, following, preceding), inner, core = axes_of(devices)
    own = Group(block[None], [np.arange(devices)])
    near = ring(own, inner)
    groups = [own] + near + [join([own] + near).send(core[1], crossed=True)]
    forward = backward = own
    for step in range(1, size // 2 + 1):
        before = forward.blocks
        arrived = [forward.send(following)] + ([backward.send(preceding)] if 2 * step < size else [])
        forward, backward = arrived[0], arrived[-1]
        if step <= len(meanwhile):
            onward = (step < size // 2) + (2 * step + 2 < size)
            chips, *alone = hold(arrived, onward, meanwhile[step - 1](before))
            forward, backward = (alone + [forward])[0], (alone + [backward])[-1]
        else:
            chips = join(arrived)
        reached = [chips] + ring(chips, inner)
        groups += reached + [group.send(core[1], crossed=True) for group in reached]
    return groups


def hold_kernel(count, *refs):
    stacked, *alone = refs[count + 1 :]
    for at in range(count):
        stacked[at] = refs[at][0]
    for at in range(len(alone)):
        alone[at][...] = refs[at][...]


def hold(groups, onward, after):
    blocks = [group.blocks for group in groups]
    stacked, *alone = pl.pallas_call(
        functools.partial(hold_kernel, len(blocks)),
        out_shape=[jax.ShapeDtypeStruct((len(blocks), *blocks[0].shape[1:]), blocks[0].dtype)]
        + [jax.ShapeDtypeStruct(block.shape, block.dtype) for block in blocks[:onward]],
        in_specs=[VMEM] * len(blocks) + [pl.BlockSpec(memory_space=pl.ANY)],
        out_specs=[VMEM] * (onward + 1),
        compiler_params=pltpu.CompilerParams(vmem_limit_bytes=VMEM_LIMIT),
    )(*blocks, after)
    sources = [group.sources for group in groups]
    return [Group(stacked, sum(sources, []))] + [Group(block, source) for block, source in zip(alone, sources)]


def swap_cores(block, devices):
    return permute(block, np.arange(devices) ^ 1)


def exchange(pieces, devices):
    same_core = [list(range(core, devices, 2)) for core in range(2)]
    return lax.all_to_all(pieces, "gx", 0, 0, axis_index_groups=same_core, tiled=True)


def places(groups, devices):
    here = np.arange(devices)
    chips = [source // 2 for group in groups for source in group.sources]
    columns = [chip * 2 + (here % 2 ^ other) for chip in range(devices // 2) for other in range(2)]
    return np.stack(chips + columns + [here], 1).astype(np.int32)


def norm_kernel(lengths_far, hidden_far, gain_far, out, lengths, hidden, gain, arrived):
    copies = [
        pltpu.make_async_copy(far, near, arrived.at[at])
        for at, (far, near) in enumerate(((hidden_far, hidden), (gain_far, gain), (lengths_far, lengths)))
    ]
    for copy in copies:
        copy.start()
    copies[0].wait()
    states = hidden[...].astype(jnp.float32)
    scale = lax.rsqrt(jnp.mean(states * states, -1, keepdims=True) + EPSILON)
    copies[1].wait()
    normed = states * scale * gain[...].astype(jnp.float32).reshape(1, 1, gain.shape[0])
    steps, rows, width = normed.shape
    lines = [normed[step, row : row + 1] for row in range(rows) for step in range(steps)]
    out[:, :width] = jnp.concatenate(lines, 0).astype(out.dtype)
    line = lax.broadcasted_iota(jnp.int32, (steps * rows, TAG), 0)
    lane = lax.broadcasted_iota(jnp.int32, (steps * rows, TAG), 1)
    position = line % steps
    copies[2].wait()
    for row in range(rows):
        position = jnp.where(line // steps == row, position + lengths[row], position)
    tag = jnp.where(lane == 0, position // 32, position % 32)
    out[:, width:] = tag.astype(jnp.float32).astype(out.dtype)


def norm(hidden, gain, lengths):
    steps, rows, width = hidden.shape
    return pl.pallas_call(
        norm_kernel,
        out_shape=jax.ShapeDtypeStruct((steps * rows, width + TAG), jnp.bfloat16),
        in_specs=[HBM] * 3,
        out_specs=VMEM,
        scratch_shapes=[
            pltpu.SMEM(lengths.shape, lengths.dtype),
            pltpu.VMEM(hidden.shape, hidden.dtype),
            pltpu.VMEM(gain.shape, gain.dtype),
            pltpu.SemaphoreType.DMA((3,)),
        ],
        compiler_params=pltpu.CompilerParams(vmem_limit_bytes=VMEM_LIMIT),
        cost_estimate=pl.CostEstimate(flops=6 * steps * rows * width, bytes_accessed=4 * steps * rows * width, transcendentals=0),
    )(*[pltpu.with_memory_space_constraint(array, pltpu.HBM) for array in (lengths, hidden, gain)])


def fetch_kernel(firsts, chunks, *refs):
    copies, count, arrived = [], len(firsts), refs[-1]
    refs[-2][...] = jnp.zeros_like(refs[-2])
    for first, far, near in zip(firsts, refs[:count], refs[count + 1 : 2 * count + 1]):
        size = near.shape[0] // min(chunks, near.shape[0])
        for at in range(0, near.shape[0], size):
            source = far.at[pl.ds(first + at, size)]
            copies.append(pltpu.make_async_copy(source, near.at[pl.ds(at, size)], arrived.at[len(copies)]))
            copies[-1].start()
    for copy in copies:
        copy.wait()


def fetch(ranges, after):
    chunks = 8
    arrays = [array for array, _, _ in ranges]
    shapes = [(count, *array.shape[1:]) for array, _, count in ranges]
    return pl.pallas_call(
        functools.partial(fetch_kernel, [first for _, first, _ in ranges], chunks),
        out_shape=[pltpu.VMEM(shape, array.dtype) for shape, array in zip(shapes, arrays)]
        + [jax.ShapeDtypeStruct((8, HD), jnp.float32)],
        in_specs=[HBM] * len(arrays) + [pl.BlockSpec(memory_space=pl.ANY)],
        out_specs=[VMEM] * (len(arrays) + 1),
        scratch_shapes=[pltpu.SemaphoreType.DMA((chunks * len(arrays),))],
        compiler_params=pltpu.CompilerParams(vmem_limit_bytes=VMEM_LIMIT),
        cost_estimate=pl.CostEstimate(
            flops=0, bytes_accessed=sum(2 * math.prod(shape) for shape in shapes), transcendentals=0
        ),
    )(*[pltpu.with_memory_space_constraint(array, pltpu.HBM) for array in arrays], after)


def slots_of(refs, counts):
    return [(ref, at) for ref, count in zip(refs, counts) for at in range(count)]


def assemble(slots, first, width):
    lanes = slice(first, first + width)
    return jnp.concatenate([ref[at, :, lanes].astype(jnp.float32) for ref, at in slots], 0).astype(jnp.bfloat16)


def multiply(slots, weights, depth, total, kept):
    total[...] = jnp.zeros_like(total)
    chunk = 0
    for part, copies in weights:
        for at in range(part.shape[0] // depth):
            kept[chunk] = assemble(slots, chunk * depth, depth)
            if copies:
                copies[at].wait()
            total[...] += jnp.dot(kept[chunk], part[at * depth : (at + 1) * depth, :], preferred_element_type=jnp.float32)
            chunk += 1


def turns(positions):
    shape = (positions.shape[0], HD)
    lane = lax.broadcasted_iota(jnp.int32, shape, 1)
    pair = (lane // 2).astype(jnp.float32)
    angles = positions * jnp.exp(pair * (-2.0 * math.log(ROPE_BASE) / HD))
    return jnp.cos(angles), jnp.where(lane % 2 == 0, -1.0, 1.0) * jnp.sin(angles)


def turn(values, cosine, sine):
    lanes = values.shape[-1]
    even = lax.broadcasted_iota(jnp.int32, values.shape, 1) % 2 == 0
    swapped = jnp.where(even, pltpu.roll(values, lanes - 1, 1), pltpu.roll(values, 1, 1))
    return values * cosine + swapped * sine


def project_kernel(counts, crossed, width, place, *refs):
    slots = slots_of(refs, counts)
    weights, keyval, *outs = refs[len(counts) : len(counts) + 6]
    kept, total, packed = refs[len(counts) + 6 :]
    queries, fresh = outs[:2], outs[2:]
    depth = keyval.shape[1]
    tags = jnp.concatenate([ref[at, :, width:].astype(jnp.float32) for ref, at in slots], 0)
    cosine, sine = turns(tags[:, 0:1] * 32.0 + tags[:, 1:2])
    multiply(slots, [(weights, None)], depth, total, kept)
    own = kept[place[2 * len(slots)]]
    blocks = keyval.shape[2] // HD
    for which in range(2):
        term = jnp.dot(own, keyval[which], preferred_element_type=jnp.float32)
        for slot in range(len(slots)):
            for at in range(blocks):
                row = (which * blocks + at) * 4
                fresh[crossed[slot]][place[slot], row : row + 4, :] = term[
                    slot * 4 : slot * 4 + 4, at * HD : (at + 1) * HD
                ]
    heads = total.shape[1] // HD
    for head in range(heads):
        turned = turn(total[:, head * HD : (head + 1) * HD], cosine, sine)
        for slot in range(len(slots)):
            for row in range(2):
                line, at = row * 2 * heads + head * 2, slot * 4 + row * 2
                packed[slot, line : line + 2, :] = turned[at : at + 2, :]
    for slot in range(len(slots)):
        queries[crossed[slot]][place[slot]] = packed[slot].astype(jnp.bfloat16)


def group_shape(groups):
    counts = [len(group.sources) for group in groups]
    return counts, [int(group.crossed) for group, count in zip(groups, counts) for _ in range(count)]


def project(groups, w_query, w_keyval, place, devices):
    counts, crossed = group_shape(groups)
    width, columns = w_query.shape
    depth, kv_width = w_keyval.shape[1:]
    own = groups[0].blocks.shape[1]
    rows, tile = devices * own, own * (columns // HD)
    query = jax.ShapeDtypeStruct((devices // 2, tile, HD), jnp.bfloat16)
    fresh = jax.ShapeDtypeStruct((devices // 2, own * 2 * kv_width // HD, HD), jnp.float32)
    return pl.pallas_call(
        functools.partial(project_kernel, counts, crossed, width),
        out_shape=[query, query, fresh, fresh],
        in_specs=[SMEM] + [VMEM] * (len(groups) + 2),
        out_specs=[VMEM] * 4,
        scratch_shapes=[
            pltpu.VMEM((devices, rows, depth), jnp.bfloat16),
            pltpu.VMEM((rows, columns), jnp.float32),
            pltpu.VMEM((devices, tile, HD), jnp.float32),
        ],
        compiler_params=pltpu.CompilerParams(vmem_limit_bytes=VMEM_LIMIT),
        cost_estimate=pl.CostEstimate(
            flops=2 * rows * columns * width, bytes_accessed=2 * columns * width, transcendentals=2 * rows * HD
        ),
    )(place, *[group.blocks for group in groups], w_query, w_keyval)


def pack_kernel(near, far, near_sum, far_sum, out):
    tile, lines = near.shape[1], near_sum.shape[1]
    out[:, :tile, :] = near[...]
    out[:, tile : 2 * tile, :] = far[...]
    total = near_sum[...] + far_sum[...]
    high = total.astype(jnp.bfloat16)
    out[:, 2 * tile : 2 * tile + lines, :] = high
    out[:, 2 * tile + lines :, :] = (total - high.astype(jnp.float32)).astype(jnp.bfloat16)


def pack(near, far, near_sum, far_sum):
    chips, tile, _ = near.shape
    return pl.pallas_call(
        pack_kernel,
        out_shape=jax.ShapeDtypeStruct((chips, 2 * tile + 2 * near_sum.shape[1], HD), jnp.bfloat16),
        in_specs=[VMEM] * 4,
        out_specs=VMEM,
        compiler_params=pltpu.CompilerParams(vmem_limit_bytes=VMEM_LIMIT),
    )(near, far, near_sum, far_sum)


def out_kernel(counts, crossed, place, *refs):
    slots = slots_of(refs, counts)
    upper, weights, near, far, lower, kept, total, arrived = refs[len(counts) :]
    depth, first = kept.shape[2], upper.shape[0]
    copies = []
    for at in range(lower.shape[0] // depth):
        source = weights.at[pl.ds(first + at * depth, depth)]
        copies.append(pltpu.make_async_copy(source, lower.at[pl.ds(at * depth, depth)], arrived.at[at]))
        copies[-1].start()
    multiply(slots, [(upper, None), (lower, copies)], depth, total, kept)
    own = near.shape[1]
    for slot in range(len(slots)):
        (near, far)[crossed[slot]][place[slot]] = total[slot * own : (slot + 1) * own].astype(near.dtype)


def project_out(groups, w_upper, w_out, place, devices):
    counts, crossed = group_shape(groups)
    columns = w_out.shape[1]
    own, width = groups[0].blocks.shape[1:]
    chunks = devices // 2
    piece = jax.ShapeDtypeStruct((devices // 2, own, columns), jnp.bfloat16)
    return pl.pallas_call(
        functools.partial(out_kernel, counts, crossed),
        out_shape=[piece, piece],
        in_specs=[SMEM] + [VMEM] * (len(groups) + 1) + [HBM],
        out_specs=[VMEM, VMEM],
        scratch_shapes=[
            pltpu.VMEM((width - w_upper.shape[0], columns), w_out.dtype),
            pltpu.VMEM((chunks, devices * own, width // chunks), jnp.bfloat16),
            pltpu.VMEM((devices * own, columns), jnp.float32),
            pltpu.SemaphoreType.DMA((chunks // 2,)),
        ],
        compiler_params=pltpu.CompilerParams(vmem_limit_bytes=OUT_VMEM_LIMIT),
        cost_estimate=pl.CostEstimate(
            flops=2 * devices * own * columns * width, bytes_accessed=2 * columns * width, transcendentals=0
        ),
    )(place, *[group.blocks for group in groups], w_upper, pltpu.with_memory_space_constraint(w_out, pltpu.HBM))


def attend_kernel(devices, kv_heads, tile, lengths, place, pieces, cache, out, fresh, queries, mixed):
    length, width = cache.shape[2:]
    extra = fresh.shape[2]
    half = tile // 2
    per_head = devices // kv_heads * half
    scale = 1.0 / math.sqrt(HD)
    for chip in range(devices // 2):
        for other in range(2):
            piece = pieces[chip, other * tile : (other + 1) * tile, :]
            queries[place[devices + 2 * chip + other]] = piece.astype(jnp.float32)
    line = lax.broadcasted_iota(jnp.int32, (8, 1), 0)
    first = jnp.where(line % 4 < 2, lengths[0], lengths[1])
    cosine, sine = turns((first + line % 2).astype(jnp.float32))
    terms = pieces[:, 2 * tile :, :].astype(jnp.float32)
    total = jnp.sum(terms, 0)
    total = total[: total.shape[0] // 2] + total[total.shape[0] // 2 :]
    twice = [jnp.concatenate([total[4 * at : 4 * at + 4]] * 2, 0) for at in range(2 * kv_heads)]
    new_keys = jnp.concatenate([turn(part, cosine, sine) for part in twice[:kv_heads]], 1)
    new_values = jnp.concatenate(twice[kv_heads:], 1)
    spot = lax.broadcasted_iota(jnp.int32, (extra, width), 0)
    for row in range(2):
        for which, new in enumerate((new_keys, new_values)):
            spread = jnp.where(spot == 0, new[2 * row : 2 * row + 1, :], 0.0)
            spread = jnp.where(spot == 1, new[2 * row + 1 : 2 * row + 2, :], spread)
            fresh[which, row] = spread.astype(fresh.dtype)
    every = queries[...]
    lines = kv_heads * per_head
    column = lax.broadcasted_iota(jnp.int32, (lines, length), 1)
    new_column = lax.broadcasted_iota(jnp.int32, (lines, extra), 1)
    step = lax.broadcasted_iota(jnp.int32, (lines, extra), 0) % 2
    across = (((1,), (1,)), ((), ()))
    for row in range(2):
        mine = every[:, row * half : row * half + half, :].reshape(lines, HD)
        spread = jnp.concatenate([mine] * kv_heads, 1)
        own_row = lax.broadcasted_iota(jnp.int32, spread.shape, 0) // per_head
        own_lane = lax.broadcasted_iota(jnp.int32, spread.shape, 1) // HD
        spread = jnp.where(own_row == own_lane, spread, 0.0).astype(jnp.bfloat16)
        scores = lax.dot_general(spread, cache[0, row], across, preferred_element_type=jnp.float32) * scale
        scores = jnp.where(column < lengths[row], scores, -jnp.inf)
        new_scores = lax.dot_general(spread, fresh[0, row], across, preferred_element_type=jnp.float32) * scale
        new_scores = jnp.where(new_column <= step, new_scores, -jnp.inf)
        peak = jnp.maximum(jnp.max(scores, 1, keepdims=True), jnp.max(new_scores, 1, keepdims=True))
        weight = jnp.exp(scores - peak)
        new_weight = jnp.exp(new_scores - peak)
        denominator = jnp.sum(weight, 1, keepdims=True) + jnp.sum(new_weight, 1, keepdims=True)
        result = jnp.dot(weight.astype(jnp.bfloat16), cache[1, row], preferred_element_type=jnp.float32)
        result += jnp.dot(new_weight.astype(jnp.bfloat16), fresh[1, row], preferred_element_type=jnp.float32)
        for head in range(kv_heads):
            rows = slice(head * per_head, (head + 1) * per_head)
            part = result[rows, head * HD : (head + 1) * HD] / denominator[rows]
            for query in range(per_head // 2):
                lanes = slice((head * per_head // 2 + query) * HD, (head * per_head // 2 + query + 1) * HD)
                for at in range(2):
                    mixed[at * 2 + row : at * 2 + row + 1, lanes] = part[2 * query + at : 2 * query + at + 1]
    out[...] = mixed[...].astype(out.dtype)


def attend(pieces, tile, cache, lengths, place, devices):
    length, width = cache.shape[2], cache.shape[3]
    columns = devices * tile // 4 * HD
    return pl.pallas_call(
        functools.partial(attend_kernel, devices, width // HD, tile),
        out_shape=jax.ShapeDtypeStruct((4, columns), jnp.bfloat16),
        in_specs=[SMEM, SMEM, VMEM, VMEM],
        out_specs=VMEM,
        scratch_shapes=[
            pltpu.VMEM((2, 2, HD, width), cache.dtype),
            pltpu.VMEM((devices, tile, HD), jnp.float32),
            pltpu.VMEM((4, columns), jnp.float32),
        ],
        compiler_params=pltpu.CompilerParams(vmem_limit_bytes=VMEM_LIMIT),
        cost_estimate=pl.CostEstimate(
            flops=8 * 128 * length * width, bytes_accessed=8 * length * width, transcendentals=256 * length
        ),
    )(lengths, place, pieces, cache)


def finish_kernel(devices, place, pieces, out):
    columns = pieces.shape[3]
    steps, rows = out.shape[:2]
    for chip in range(devices // 2):
        for other in range(2):
            source = place[devices + 2 * chip + other]
            lanes = pl.ds(pl.multiple_of(source * columns, columns), columns)
            piece = pieces[chip, other].astype(jnp.float32)
            for step in range(steps):
                out[step, :, lanes] = piece[step * rows : (step + 1) * rows].astype(out.dtype)


def finish(pieces, place, steps, devices):
    own, columns = pieces.shape[2:]
    return pl.pallas_call(
        functools.partial(finish_kernel, devices),
        out_shape=jax.ShapeDtypeStruct((steps, own // steps, devices * columns), jnp.bfloat16),
        in_specs=[SMEM, VMEM],
        out_specs=VMEM,
        compiler_params=pltpu.CompilerParams(vmem_limit_bytes=VMEM_LIMIT),
    )(place, pieces)


def body(hidden, norm_gain, w_query, w_keyval, w_out, kv_cache, lengths):
    steps = hidden.shape[0]
    devices = lax.axis_size("gx")

    normed = norm(hidden, norm_gain, lengths)
    half = w_out.shape[0] // 2
    fetched = []

    def bring(ranges, after):
        *arrays, done = fetch(ranges, after)
        fetched.append(arrays)
        return done

    groups = gather(
        normed,
        devices,
        [
            functools.partial(bring, [(w_query, 0, w_query.shape[0]), (w_keyval, 0, 2)]),
            functools.partial(bring, [(kv_cache, 0, 2), (w_out, 0, half)]),
        ],
    )
    (w_query, w_keyval), (kv_cache, w_upper) = fetched
    table = jnp.asarray(places(groups, devices))
    place = lax.dynamic_index_in_dim(table, lax.axis_index("gx"), 0, keepdims=False)
    near, far, near_sum, far_sum = project(groups, w_query, w_keyval, place, devices)
    pieces = pack(near, swap_cores(far, devices), near_sum, swap_cores(far_sum, devices))

    mixed = attend(exchange(pieces, devices), near.shape[1], kv_cache, lengths, place, devices)
    near, far = project_out(gather(mixed, devices), w_upper, w_out, place, devices)
    pieces = jnp.stack([near, swap_cores(far, devices)], 1)
    return finish(exchange(pieces, devices), place, steps, devices)


def rotate(values, positions):
    row_total, head_count, head_width = values.shape
    half_width = head_width // 2
    frequency = ROPE_BASE ** (-2.0 * jnp.arange(half_width, dtype=jnp.float32) / head_width)
    angles = positions[:, None, None] * frequency[None, None, :]
    cosine = jnp.cos(angles)
    sine_part = jnp.sin(angles)
    paired = values.reshape(row_total, head_count, half_width, 2)
    first_half = paired[..., 0]
    second_half = paired[..., 1]
    turned = jnp.stack(
        [
            first_half * cosine - second_half * sine_part,
            first_half * sine_part + second_half * cosine,
        ],
        -1,
    )
    return turned.reshape(row_total, head_count, head_width)


def attend_split_heads(queries, cache_keys, cache_values, lengths, fresh_keys, fresh_values):
    score_scale = 1.0 / math.sqrt(HD)
    fresh_scores = (
        jnp.einsum("rkgd,rskd->rkgs", queries, fresh_keys, preferred_element_type=jnp.float32)
        * score_scale
    )
    cached = (
        jnp.einsum("rkgd,rlkd->rkgl", queries, cache_keys, preferred_element_type=jnp.float32)
        * score_scale
    )
    in_range = jnp.arange(cache_keys.shape[1])[None, :] < lengths[:, None]
    cached = jnp.where(in_range[:, None, None, :], cached, -jnp.inf)
    row_peak = jnp.maximum(cached.max(-1), fresh_scores.max(-1))
    cached_exp = jnp.exp(cached - row_peak[..., None])
    fresh_exp = jnp.exp(fresh_scores - row_peak[..., None])
    denominator = cached_exp.sum(-1) + fresh_exp.sum(-1)
    mixed = jnp.einsum(
        "rkgl,rlkd->rkgd",
        cached_exp.astype(jnp.bfloat16),
        cache_values,
        preferred_element_type=jnp.float32,
    )
    mixed = mixed + jnp.einsum(
        "rkgs,rskd->rkgd",
        fresh_exp.astype(jnp.bfloat16),
        fresh_values,
        preferred_element_type=jnp.float32,
    )
    return (mixed / denominator[..., None]).astype(jnp.bfloat16)


def body_split_heads(hidden, norm_gain, w_query, w_keyval, w_out, kv_cache, lengths):
    step_count, rows_dev, model_width = hidden.shape
    devices = lax.axis_size("gx")
    device_index = lax.axis_index("gx")
    row_slab = w_keyval.shape[1]
    kv_width = w_keyval.shape[2]
    query_cols = w_query.shape[1]
    heads_width = query_cols * devices
    head_count = heads_width // HD
    kv_heads = kv_width // HD
    kv_both = jnp.concatenate([w_keyval[0], w_keyval[1]], 1)
    cache_keys = kv_cache[0].reshape(rows_dev, kv_cache.shape[2], kv_heads, HD)
    cache_values = kv_cache[1].reshape(rows_dev, kv_cache.shape[2], kv_heads, HD)
    states = hidden.astype(jnp.float32)
    scaled = states * lax.rsqrt(jnp.mean(states * states, -1, keepdims=True) + EPSILON)
    normed = (scaled * norm_gain.astype(jnp.float32)).astype(jnp.bfloat16)
    new_keys = []
    new_values = []
    outputs = []
    for step_index in range(step_count):
        shard_piece = lax.all_gather(normed[step_index], "gx", axis=0, tiled=True)
        queries = jnp.dot(shard_piece, w_query, preferred_element_type=jnp.float32)
        own_slab = lax.dynamic_slice_in_dim(shard_piece, device_index * row_slab, row_slab, 1)
        partial_kv = jnp.dot(own_slab, kv_both, preferred_element_type=jnp.float32)
        joined = jnp.concatenate([queries, partial_kv], 1)
        project_query_rows = lax.all_to_all(
            joined[:, :query_cols], "gx", split_axis=0, concat_axis=1, tiled=True
        )
        project_keyval = lax.psum_scatter(
            joined[:, query_cols:], "gx", scatter_dimension=0, tiled=True
        )
        positions = (lengths + step_index).astype(jnp.float32)
        prepare_queries = rotate(
            project_query_rows.reshape(rows_dev, head_count, HD), positions
        ).astype(jnp.bfloat16)
        prepare_queries = prepare_queries.reshape(rows_dev, kv_heads, head_count // kv_heads, HD)
        key_new = rotate(
            project_keyval[:, :kv_width].reshape(rows_dev, kv_heads, HD), positions
        ).astype(jnp.bfloat16)
        value_new = (
            project_keyval[:, kv_width:].reshape(rows_dev, kv_heads, HD).astype(jnp.bfloat16)
        )
        queries, key_new, value_new = (prepare_queries, key_new, value_new)
        new_keys.append(key_new)
        new_values.append(value_new)
        mixed = attend_split_heads(
            queries,
            cache_keys,
            cache_values,
            lengths,
            jnp.stack(new_keys, 1),
            jnp.stack(new_values, 1),
        )
        out_cols = jnp.dot(
            lax.all_gather(mixed.reshape(rows_dev, heads_width), "gx", axis=0, tiled=True),
            w_out,
            preferred_element_type=jnp.float32,
        ).astype(jnp.bfloat16)
        outputs.append(lax.all_to_all(out_cols, "gx", split_axis=0, concat_axis=1, tiled=True))
    return jnp.stack(outputs)


def solution(mesh):
    devices = mesh.shape["gx"]

    def run(*arrays):
        whole_heads = arrays[2].shape[1] % HD == 0 and devices % 2 == 0
        return (body if whole_heads else body_split_heads)(*arrays)

    in_specs = (
        P(None, ("group", "gx"), None),
        P(),
        P(None, "gx"),
        P(None, "gx", None),
        P(None, "gx"),
        P(None, ("group", "gx"), None, None),
        P(("group", "gx")),
    )
    out_specs = P(None, ("group", "gx"), None)
    return jax.shard_map(run, mesh=mesh, in_specs=in_specs, out_specs=out_specs, check_vma=False)
```

profile of v0, /device:TPU:0, one launch (start us, length us, event | category | flops | bytes accessed | tf_op | source)
XLA Modules:
  0.0 102.7 jit_solution(16397995359898150114)
XLA Ops:
  0.0 1.4 %shard_map.82 = bf16[4,16512]{1,0:T(4,128)(2,1)S(1)} custom-call(s32[2]{0:T(128)} %lengths.1, bf16[2,2,16384]{2,1,0:T(2,128)(2,1)} %hidden_far.1, bf16[16384]{0:T(1024)(128)(2,1)} %gain_far.1), custom_call_target="tpu_custom_call" | custom-call | flops 393216 | bytes 262144 | tf_op jit(solution)/shard_map/pallas_call | solution.py:169
  1.5 3.1 %collective-permute-start.3 = (bf16[1,4,16512]{2,1,0:T(4,128)(2,1)S(1)}, bf16[1,4,16512]{2,1,0:T(4,128)(2,1)S(1)}, u32[]{:S(2)}, u32[]{:S(2)}) collective-permute-start(bf16[1,4,16512]{2,1,0:T(4,128)(2,1)S(1)} %bitcast.6), channel_id=1, source_target_pairs={{0,4},{1,5},{2,6},{3,7},{4,12},{5,13},{6,14},{7,15},{8,0},{9,1},{1... | collective-permute-start | bytes 396296 | tf_op jit(solution)/shard_map/ppermute | solution.py:24
  5.6 1.8 %collective-permute-start = (bf16[1,4,16512]{2,1,0:T(4,128)(2,1)S(1)}, bf16[1,4,16512]{2,1,0:T(4,128)(2,1)S(1)}, u32[]{:S(2)}, u32[]{:S(2)}) collective-permute-start(bf16[1,4,16512]{2,1,0:T(4,128)(2,1)S(1)} %bitcast.8), channel_id=1, source_target_pairs={{0,2},{1,3},{2,0},{3,1},{4,6},{5,7},{6,4},{7,5},{8,10},{9,11},{10,... | collective-permute-start | bytes 396296 | tf_op jit(solution)/shard_map/ppermute | solution.py:24
  7.4 6.5 %shard_map.83 = (bf16[16384,512]{1,0:T(8,128)(2,1)S(1)}, bf16[2,1024,512]{2,1,0:T(8,128)(2,1)S(1)}, f32[8,128]{1,0:T(8,128)S(1)}) custom-call(bf16[16384,512]{1,0:T(8,128)(2,1)} %refs_0_.2, bf16[2,1024,512]{2,1,0:T(8,128)(2,1)} %refs_1_.2, bf16[1,4,16512]{2,1,0:T(4,128)(2,1)S(1)} %bitcast.9), custom_call_target="tpu_custom_call" | custom-call | bytes 18874368 | tf_op jit(solution)/shard_map/pallas_call | solution.py:202
  13.9 5.8 %copy-done = bf16[16384,512]{1,0:T(8,128)(2,1)} copy-done((bf16[16384,512]{1,0:T(8,128)(2,1)}, bf16[16384,512]{1,0:T(8,128)(2,1)S(1)}, u32[]{:S(2)}) %copy-start) | copy-done | bytes 16777240
  20.1 2.0 %collective-permute-start.7 = (bf16[1,4,16512]{2,1,0:T(4,128)(2,1)S(1)}, bf16[1,4,16512]{2,1,0:T(4,128)(2,1)S(1)}, u32[]{:S(2)}, u32[]{:S(2)}) collective-permute-start(bf16[1,4,16512]{2,1,0:T(4,128)(2,1)S(1)} %get-tuple-element.21.refs_2_), channel_id=1, source_target_pairs={{0,8},{1,9},{2,10},{3,11},{4,0},{5,1},{6,2},{7,3},{8,12},{9,13},{1... | collective-permute-start | bytes 396296 | tf_op jit(solution)/shard_map/ppermute | solution.py:24
  23.0 4.7 %shard_map.85 = (bf16[2,2,1024,512]{3,2,1,0:T(8,128)(2,1)S(1)}, bf16[4096,1024]{1,0:T(8,128)(2,1)S(1)}, f32[8,128]{1,0:T(8,128)S(1)}) custom-call(bf16[2,2,1024,512]{3,2,1,0:T(8,128)(2,1)} %refs_0_.3, bf16[8192,1024]{1,0:T(8,128)(2,1)} %refs_12_.1, bf16[1,4,16512]{2,1,0:T(4,128)(2,1)S(1)} %get-tuple-element.21.refs_2_), custom_call_target="tpu_custom_call" | custom-call | bytes 12582912 | tf_op jit(solution)/shard_map/pallas_call | solution.py:202
  27.7 3.3 %copy-done.2 = bf16[4096,1024]{1,0:T(8,128)(2,1)} copy-done((bf16[4096,1024]{1,0:T(8,128)(2,1)}, bf16[4096,1024]{1,0:T(8,128)(2,1)S(1)}, u32[]{:S(2)}) %copy-start.2) | copy-done | bytes 8388632
  31.0 2.0 %copy-done.4 = bf16[2,2,1024,512]{3,2,1,0:T(8,128)(2,1)} copy-done((bf16[2,2,1024,512]{3,2,1,0:T(8,128)(2,1)}, bf16[2,2,1024,512]{3,2,1,0:T(8,128)(2,1)S(1)}, u32[]{:S(2)}) %copy-start.4) | copy-done | bytes 4194328
  33.0 1.6 %collective-permute-start.8 = (bf16[1,4,16512]{2,1,0:T(4,128)(2,1)S(1)}, bf16[1,4,16512]{2,1,0:T(4,128)(2,1)S(1)}, u32[]{:S(2)}, u32[]{:S(2)}) collective-permute-start(bf16[1,4,16512]{2,1,0:T(4,128)(2,1)S(1)} %shard_map.86.refs_7_), channel_id=1, source_target_pairs={{0,2},{1,3},{2,0},{3,1},{4,6},{5,7},{6,4},{7,5},{8,10},{9,11},{10,... | collective-permute-start | bytes 396296 | tf_op jit(solution)/shard_map/ppermute | solution.py:24
  35.1 3.9 %collective-permute-done.8.refs_8_ = bf16[1,4,16512]{2,1,0:T(4,128)(2,1)S(1)} collective-permute-done((bf16[1,4,16512]{2,1,0:T(4,128)(2,1)S(1)}, bf16[1,4,16512]{2,1,0:T(4,128)(2,1)S(1)}, u32[]{:S(2)}, u32[]{:S(2)}) %collective-permute-start.8) | collective-permute-done | bytes 132128 | tf_op jit(solution)/shard_map/ppermute | solution.py:24
  40.5 5.8 %copy-done.1 = bf16[16384,512]{1,0:T(8,128)(2,1)S(1)} copy-done((bf16[16384,512]{1,0:T(8,128)(2,1)S(1)}, bf16[16384,512]{1,0:T(8,128)(2,1)}, u32[]{:S(2)}) %copy-start.1) | copy-done | bytes 16777240
  46.3 4.7 %shard_map.87 = (bf16[8,16,128]{2,1,0:T(8,128)(2,1)S(1)}, bf16[8,16,128]{2,1,0:T(8,128)(2,1)S(1)}, f32[8,32,128]{2,1,0:T(8,128)S(1)}, f32[8,32,128]{2,1,0:T(8,128)S(1)}) custom-call(s32[33]{0:T(128)S(1)} %dynamic-slice_bitcast_fusion.place, bf16[1,4,16512]{2,1,0:T(4,128)(2,1)S(1)} %bitcast.11, bf16[1,4,16512]{2,1,0:T(4,128)(2,1)S(1)} %collective-permute-done.refs_1_, ...), custom_call_target="tpu_custom_call" | custom-call | flops 1073741824 | bytes 16777216 | tf_op jit(solution)/shard_map/pallas_call | solution.py:295
  52.4 12.9 %all_to_all.10.pieces = bf16[8,96,128]{2,1,0:T(8,128)(2,1)S(1)} all-to-all(bf16[8,96,128]{2,1,0:T(8,128)(2,1)S(1)} %shard_map.88), channel_id=1, replica_groups={{0,2,4,6,8,10,12,14},{1,3,5,7,9,11,13,15},{16,18,20,22,24,26,28,30},{17..., dimensions={0} | all-to-all | bytes 393216 | tf_op jit(solution)/shard_map/all_to_all | solution.py:132
  65.4 2.5 %shard_map.89 = bf16[4,8192]{1,0:T(4,128)(2,1)S(1)} custom-call(s32[2]{0:T(128)S(1)} %copy-done.6, s32[33]{0:T(128)S(1)} %dynamic-slice_bitcast_fusion.place, bf16[8,96,128]{2,1,0:T(8,128)(2,1)S(1)} %all_to_all.10.pieces, bf16[2,2,1024,512]{3,2,1,0:T(8,128)(2,1)S(1)} %copy-done.5), custom_call_target="tpu_custom_call" | custom-call | flops 536870912 | bytes 4194304 | tf_op jit(solution)/shard_map/pallas_call | solution.py:432
  68.6 1.3 %collective-permute-start.16 = (bf16[1,4,8192]{2,1,0:T(4,128)(2,1)S(1)}, bf16[1,4,8192]{2,1,0:T(4,128)(2,1)S(1)}, u32[]{:S(2)}, u32[]{:S(2)}) collective-permute-start(bf16[1,4,8192]{2,1,0:T(4,128)(2,1)S(1)} %bitcast.13), channel_id=1, source_target_pairs={{0,4},{1,5},{2,6},{3,7},{4,12},{5,13},{6,14},{7,15},{8,0},{9,1},{1... | collective-permute-start | bytes 196616 | tf_op jit(solution)/shard_map/ppermute | solution.py:24
  70.9 1.9 %collective-permute-done.15 = bf16[1,4,8192]{2,1,0:T(4,128)(2,1)S(1)} collective-permute-done((bf16[1,4,8192]{2,1,0:T(4,128)(2,1)S(1)}, bf16[1,4,8192]{2,1,0:T(4,128)(2,1)S(1)}, u32[]{:S(2)}, u32[]{:S(2)}) %collective-permute-start.15) | collective-permute-done | bytes 65568 | tf_op jit(solution)/shard_map/ppermute | solution.py:24
  75.6 3.5 %collective-permute-done.20.refs_7_ = bf16[1,4,8192]{2,1,0:T(4,128)(2,1)S(1)} collective-permute-done((bf16[1,4,8192]{2,1,0:T(4,128)(2,1)S(1)}, bf16[1,4,8192]{2,1,0:T(4,128)(2,1)S(1)}, u32[]{:S(2)}, u32[]{:S(2)}) %collective-permute-start.20) | collective-permute-done | bytes 65568 | tf_op jit(solution)/shard_map/ppermute | solution.py:24
  79.1 1.2 %collective-permute-start.21 = (bf16[1,4,8192]{2,1,0:T(4,128)(2,1)S(1)}, bf16[1,4,8192]{2,1,0:T(4,128)(2,1)S(1)}, u32[]{:S(2)}, u32[]{:S(2)}) collective-permute-start(bf16[1,4,8192]{2,1,0:T(4,128)(2,1)S(1)} %collective-permute-done.20.refs_7_), channel_id=1, source_target_pairs={{0,2},{1,3},{2,0},{3,1},{4,6},{5,7},{6,4},{7,5},{8,10},{9,11},{10,... | collective-permute-start | bytes 196616 | tf_op jit(solution)/shard_map/ppermute | solution.py:24
  80.8 2.5 %collective-permute-done.21.refs_8_ = bf16[1,4,8192]{2,1,0:T(4,128)(2,1)S(1)} collective-permute-done((bf16[1,4,8192]{2,1,0:T(4,128)(2,1)S(1)}, bf16[1,4,8192]{2,1,0:T(4,128)(2,1)S(1)}, u32[]{:S(2)}, u32[]{:S(2)}) %collective-permute-start.21) | collective-permute-done | bytes 65568 | tf_op jit(solution)/shard_map/ppermute | solution.py:24
  83.4 1.2 %collective-permute-done.23.refs_10_ = bf16[1,4,8192]{2,1,0:T(4,128)(2,1)S(1)} collective-permute-done((bf16[1,4,8192]{2,1,0:T(4,128)(2,1)S(1)}, bf16[1,4,8192]{2,1,0:T(4,128)(2,1)S(1)}, u32[]{:S(2)}, u32[]{:S(2)}) %collective-permute-start.23) | collective-permute-done | bytes 65568 | tf_op jit(solution)/shard_map/ppermute | solution.py:24
  84.6 4.5 %shard_map.90 = (bf16[8,4,1024]{2,1,0:T(4,128)(2,1)S(1)}, bf16[8,4,1024]{2,1,0:T(4,128)(2,1)S(1)}) custom-call(s32[33]{0:T(128)S(1)} %dynamic-slice_bitcast_fusion.place, bf16[1,4,8192]{2,1,0:T(4,128)(2,1)S(1)} %bitcast.16, bf16[1,4,8192]{2,1,0:T(4,128)(2,1)S(1)} %collective-permute-done.13.refs_1_, bf16[2,4,8192]{2,1,0:T(4,128)(2,1)S(1)} %collective-permute-done.14.refs_2_, ...), custom_call_target="tpu_custom_call" | custom-call | flops 1073741824 | bytes 16777216 | tf_op jit(solution)/shard_map/pallas_call | solution.py:354
  90.6 10.9 %all_to_all.11.pieces = bf16[8,2,4,1024]{3,2,1,0:T(4,128)(2,1)S(1)} all-to-all(bf16[8,2,4,1024]{3,2,1,0:T(4,128)(2,1)S(1)} %pad_maximum_fusion.2), channel_id=1, replica_groups={{0,2,4,6,8,10,12,14},{1,3,5,7,9,11,13,15},{16,18,20,22,24,26,28,30},{17..., dimensions={0} | all-to-all | bytes 262144 | tf_op jit(solution)/shard_map/all_to_all | solution.py:132
  101.5 1.3 %shard_map.91 = bf16[2,2,16384]{2,1,0:T(2,128)(2,1)} custom-call(s32[33]{0:T(128)S(1)} %dynamic-slice_bitcast_fusion.place, bf16[8,2,4,1024]{3,2,1,0:T(4,128)(2,1)S(1)} %all_to_all.11.pieces), custom_call_target="tpu_custom_call" | custom-call | tf_op jit(solution)/shard_map/pallas_call | solution.py:463
  (58 shorter events, 12.3 us)
Async XLA Ops:
  1.5 18.2 %collective-permute-start.3 = (bf16[1,4,16512]{2,1,0:T(4,128)(2,1)S(1)}, bf16[1,4,16512]{2,1,0:T(4,128)(2,1)S(1)}, u32[]{:S(2)}, u32[]{:S(2)}) collective-permute-start(bf16[1,4,16512]{2,1,0:T(4,128)(2,1)S(1)} %bitcast.6), channel_id=1, source_target_pairs={{0,4},{1,5},{2,6},{3,7},{4,12},{5,13},{6,14},{7,15},{8,0},{9,1},{1... | collective-permute-start | bytes 396296 | tf_op jit(solution)/shard_map/ppermute | solution.py:24
  4.5 15.2 %collective-permute-start.2 = (bf16[1,4,16512]{2,1,0:T(4,128)(2,1)S(1)}, bf16[1,4,16512]{2,1,0:T(4,128)(2,1)S(1)}, u32[]{:S(2)}, u32[]{:S(2)}) collective-permute-start(bf16[1,4,16512]{2,1,0:T(4,128)(2,1)S(1)} %bitcast.7), channel_id=1, source_target_pairs={{0,8},{1,9},{2,10},{3,11},{4,0},{5,1},{6,2},{7,3},{8,12},{9,13},{1... | collective-permute-start | bytes 396296 | tf_op jit(solution)/shard_map/ppermute | solution.py:24
  5.6 16.5 %collective-permute-start = (bf16[1,4,16512]{2,1,0:T(4,128)(2,1)S(1)}, bf16[1,4,16512]{2,1,0:T(4,128)(2,1)S(1)}, u32[]{:S(2)}, u32[]{:S(2)}) collective-permute-start(bf16[1,4,16512]{2,1,0:T(4,128)(2,1)S(1)} %bitcast.8), channel_id=1, source_target_pairs={{0,2},{1,3},{2,0},{3,1},{4,6},{5,7},{6,4},{7,5},{8,10},{9,11},{10,... | collective-permute-start | bytes 396296 | tf_op jit(solution)/shard_map/ppermute | solution.py:24
  19.7 20.0 %collective-permute-start.5 = (bf16[2,4,16512]{2,1,0:T(4,128)(2,1)S(1)}, bf16[2,4,16512]{2,1,0:T(4,128)(2,1)S(1)}, u32[]{:S(2)}, u32[]{:S(2)}) collective-permute-start(bf16[2,4,16512]{2,1,0:T(4,128)(2,1)S(1)} %get-tuple-element.20.refs_3_), channel_id=1, source_target_pairs={{0,1},{1,0},{2,3},{3,2},{4,5},{5,4},{6,7},{7,6},{8,9},{9,8},{10,11... | collective-permute-start | bytes 792584 | tf_op jit(solution)/shard_map/ppermute | solution.py:24
  19.8 14.8 %collective-permute-start.4 = (bf16[2,4,16512]{2,1,0:T(4,128)(2,1)S(1)}, bf16[2,4,16512]{2,1,0:T(4,128)(2,1)S(1)}, u32[]{:S(2)}, u32[]{:S(2)}) collective-permute-start(bf16[2,4,16512]{2,1,0:T(4,128)(2,1)S(1)} %get-tuple-element.20.refs_3_), channel_id=1, source_target_pairs={{0,2},{1,3},{2,0},{3,1},{4,6},{5,7},{6,4},{7,5},{8,10},{9,11},{10,... | collective-permute-start | bytes 792584 | tf_op jit(solution)/shard_map/ppermute | solution.py:24
  20.1 12.9 %collective-permute-start.7 = (bf16[1,4,16512]{2,1,0:T(4,128)(2,1)S(1)}, bf16[1,4,16512]{2,1,0:T(4,128)(2,1)S(1)}, u32[]{:S(2)}, u32[]{:S(2)}) collective-permute-start(bf16[1,4,16512]{2,1,0:T(4,128)(2,1)S(1)} %get-tuple-element.21.refs_2_), channel_id=1, source_target_pairs={{0,8},{1,9},{2,10},{3,11},{4,0},{5,1},{6,2},{7,3},{8,12},{9,13},{1... | collective-permute-start | bytes 396296 | tf_op jit(solution)/shard_map/ppermute | solution.py:24
  23.0 16.7 %collective-permute-start.1 = (bf16[2,4,16512]{2,1,0:T(4,128)(2,1)}, bf16[2,4,16512]{2,1,0:T(4,128)(2,1)}, u32[]{:S(2)}, u32[]{:S(2)}) collective-permute-start(bf16[2,4,16512]{2,1,0:T(4,128)(2,1)} %pad_maximum_fusion), channel_id=1, source_target_pairs={{0,1},{1,0},{2,3},{3,2},{4,5},{5,4},{6,7},{7,6},{8,9},{9,8},{10,11... | collective-permute-start | bytes 792584 | tf_op jit(solution)/shard_map/ppermute | solution.py:24
  33.0 6.0 %collective-permute-start.8 = (bf16[1,4,16512]{2,1,0:T(4,128)(2,1)S(1)}, bf16[1,4,16512]{2,1,0:T(4,128)(2,1)S(1)}, u32[]{:S(2)}, u32[]{:S(2)}) collective-permute-start(bf16[1,4,16512]{2,1,0:T(4,128)(2,1)S(1)} %shard_map.86.refs_7_), channel_id=1, source_target_pairs={{0,2},{1,3},{2,0},{3,1},{4,6},{5,7},{6,4},{7,5},{8,10},{9,11},{10,... | collective-permute-start | bytes 396296 | tf_op jit(solution)/shard_map/ppermute | solution.py:24
  34.6 5.9 %collective-permute-start.6 = (bf16[2,4,16512]{2,1,0:T(4,128)(2,1)S(1)}, bf16[2,4,16512]{2,1,0:T(4,128)(2,1)}, u32[]{:S(2)}, u32[]{:S(2)}) collective-permute-start(bf16[2,4,16512]{2,1,0:T(4,128)(2,1)S(1)} %collective-permute-done.4.refs_4_), channel_id=1, source_target_pairs={{0,1},{1,0},{2,3},{3,2},{4,5},{5,4},{6,7},{7,6},{8,9},{9,8},{10,11... | collective-permute-start | bytes 792584 | tf_op jit(solution)/shard_map/ppermute | solution.py:24
  34.8 4.9 %collective-permute-start.9 = (bf16[1,4,16512]{2,1,0:T(4,128)(2,1)S(1)}, bf16[1,4,16512]{2,1,0:T(4,128)(2,1)}, u32[]{:S(2)}, u32[]{:S(2)}) collective-permute-start(bf16[1,4,16512]{2,1,0:T(4,128)(2,1)S(1)} %shard_map.86.refs_7_), channel_id=1, source_target_pairs={{0,1},{1,0},{2,3},{3,2},{4,5},{5,4},{6,7},{7,6},{8,9},{9,8},{10,11... | collective-permute-start | bytes 396296 | tf_op jit(solution)/shard_map/ppermute | solution.py:24
  39.0 1.5 %collective-permute-start.10 = (bf16[1,4,16512]{2,1,0:T(4,128)(2,1)S(1)}, bf16[1,4,16512]{2,1,0:T(4,128)(2,1)}, u32[]{:S(2)}, u32[]{:S(2)}) collective-permute-start(bf16[1,4,16512]{2,1,0:T(4,128)(2,1)S(1)} %collective-permute-done.8.refs_8_), channel_id=1, source_target_pairs={{0,1},{1,0},{2,3},{3,2},{4,5},{5,4},{6,7},{7,6},{8,9},{9,8},{10,11... | collective-permute-start | bytes 396296 | tf_op jit(solution)/shard_map/ppermute | solution.py:24
  50.9 1.5 %collective-permute-start.12 = (f32[8,32,128]{2,1,0:T(8,128)S(1)}, f32[8,32,128]{2,1,0:T(8,128)S(1)}, u32[]{:S(2)}, u32[]{:S(2)}) collective-permute-start(f32[8,32,128]{2,1,0:T(8,128)S(1)} %get-tuple-element.28), channel_id=1, source_target_pairs={{0,1},{1,0},{2,3},{3,2},{4,5},{5,4},{6,7},{7,6},{8,9},{9,8},{10,11... | collective-permute-start | bytes 393224 | tf_op jit(solution)/shard_map/ppermute | solution.py:24
  67.9 4.9 %collective-permute-start.15 = (bf16[1,4,8192]{2,1,0:T(4,128)(2,1)S(1)}, bf16[1,4,8192]{2,1,0:T(4,128)(2,1)S(1)}, u32[]{:S(2)}, u32[]{:S(2)}) collective-permute-start(bf16[1,4,8192]{2,1,0:T(4,128)(2,1)S(1)} %bitcast.12), channel_id=1, source_target_pairs={{0,8},{1,9},{2,10},{3,11},{4,0},{5,1},{6,2},{7,3},{8,12},{9,13},{1... | collective-permute-start | bytes 196616 | tf_op jit(solution)/shard_map/ppermute | solution.py:24
  68.6 5.2 %collective-permute-start.16 = (bf16[1,4,8192]{2,1,0:T(4,128)(2,1)S(1)}, bf16[1,4,8192]{2,1,0:T(4,128)(2,1)S(1)}, u32[]{:S(2)}, u32[]{:S(2)}) collective-permute-start(bf16[1,4,8192]{2,1,0:T(4,128)(2,1)S(1)} %bitcast.13), channel_id=1, source_target_pairs={{0,4},{1,5},{2,6},{3,7},{4,12},{5,13},{6,14},{7,15},{8,0},{9,1},{1... | collective-permute-start | bytes 196616 | tf_op jit(solution)/shard_map/ppermute | solution.py:24
  70.0 5.4 %collective-permute-start.13 = (bf16[1,4,8192]{2,1,0:T(4,128)(2,1)S(1)}, bf16[1,4,8192]{2,1,0:T(4,128)(2,1)S(1)}, u32[]{:S(2)}, u32[]{:S(2)}) collective-permute-start(bf16[1,4,8192]{2,1,0:T(4,128)(2,1)S(1)} %bitcast.14), channel_id=1, source_target_pairs={{0,2},{1,3},{2,0},{3,1},{4,6},{5,7},{6,4},{7,5},{8,10},{9,11},{10,... | collective-permute-start | bytes 196616 | tf_op jit(solution)/shard_map/ppermute | solution.py:24
  73.8 9.5 %collective-permute-start.18 = (bf16[2,4,8192]{2,1,0:T(4,128)(2,1)S(1)}, bf16[2,4,8192]{2,1,0:T(4,128)(2,1)S(1)}, u32[]{:S(2)}, u32[]{:S(2)}) collective-permute-start(bf16[2,4,8192]{2,1,0:T(4,128)(2,1)S(1)} %constant_dynamic-update-slice_fusion.refs_3_), channel_id=1, source_target_pairs={{0,1},{1,0},{2,3},{3,2},{4,5},{5,4},{6,7},{7,6},{8,9},{9,8},{10,11... | collective-permute-start | bytes 393224 | tf_op jit(solution)/shard_map/ppermute | solution.py:24
  73.9 6.4 %collective-permute-start.17 = (bf16[2,4,8192]{2,1,0:T(4,128)(2,1)S(1)}, bf16[2,4,8192]{2,1,0:T(4,128)(2,1)S(1)}, u32[]{:S(2)}, u32[]{:S(2)}) collective-permute-start(bf16[2,4,8192]{2,1,0:T(4,128)(2,1)S(1)} %constant_dynamic-update-slice_fusion.refs_3_), channel_id=1, source_target_pairs={{0,2},{1,3},{2,0},{3,1},{4,6},{5,7},{6,4},{7,5},{8,10},{9,11},{10,... | collective-permute-start | bytes 393224 | tf_op jit(solution)/shard_map/ppermute | solution.py:24
  74.8 4.3 %collective-permute-start.20 = (bf16[1,4,8192]{2,1,0:T(4,128)(2,1)S(1)}, bf16[1,4,8192]{2,1,0:T(4,128)(2,1)S(1)}, u32[]{:S(2)}, u32[]{:S(2)}) collective-permute-start(bf16[1,4,8192]{2,1,0:T(4,128)(2,1)S(1)} %collective-permute-done.15), channel_id=1, source_target_pairs={{0,8},{1,9},{2,10},{3,11},{4,0},{5,1},{6,2},{7,3},{8,12},{9,13},{1... | collective-permute-start | bytes 196616 | tf_op jit(solution)/shard_map/ppermute | solution.py:24
  75.5 7.9 %collective-permute-start.14 = (bf16[2,4,8192]{2,1,0:T(4,128)(2,1)S(1)}, bf16[2,4,8192]{2,1,0:T(4,128)(2,1)S(1)}, u32[]{:S(2)}, u32[]{:S(2)}) collective-permute-start(bf16[2,4,8192]{2,1,0:T(4,128)(2,1)S(1)} %pad_maximum_fusion.1), channel_id=1, source_target_pairs={{0,1},{1,0},{2,3},{3,2},{4,5},{5,4},{6,7},{7,6},{8,9},{9,8},{10,11... | collective-permute-start | bytes 393224 | tf_op jit(solution)/shard_map/ppermute | solution.py:24
  79.1 4.3 %collective-permute-start.21 = (bf16[1,4,8192]{2,1,0:T(4,128)(2,1)S(1)}, bf16[1,4,8192]{2,1,0:T(4,128)(2,1)S(1)}, u32[]{:S(2)}, u32[]{:S(2)}) collective-permute-start(bf16[1,4,8192]{2,1,0:T(4,128)(2,1)S(1)} %collective-permute-done.20.refs_7_), channel_id=1, source_target_pairs={{0,2},{1,3},{2,0},{3,1},{4,6},{5,7},{6,4},{7,5},{8,10},{9,11},{10,... | collective-permute-start | bytes 196616 | tf_op jit(solution)/shard_map/ppermute | solution.py:24
  80.3 4.3 %collective-permute-start.19 = (bf16[2,4,8192]{2,1,0:T(4,128)(2,1)S(1)}, bf16[2,4,8192]{2,1,0:T(4,128)(2,1)S(1)}, u32[]{:S(2)}, u32[]{:S(2)}) collective-permute-start(bf16[2,4,8192]{2,1,0:T(4,128)(2,1)S(1)} %collective-permute-done.17.refs_4_), channel_id=1, source_target_pairs={{0,1},{1,0},{2,3},{3,2},{4,5},{5,4},{6,7},{7,6},{8,9},{9,8},{10,11... | collective-permute-start | bytes 393224 | tf_op jit(solution)/shard_map/ppermute | solution.py:24
  80.3 3.1 %collective-permute-start.22 = (bf16[1,4,8192]{2,1,0:T(4,128)(2,1)S(1)}, bf16[1,4,8192]{2,1,0:T(4,128)(2,1)S(1)}, u32[]{:S(2)}, u32[]{:S(2)}) collective-permute-start(bf16[1,4,8192]{2,1,0:T(4,128)(2,1)S(1)} %collective-permute-done.20.refs_7_), channel_id=1, source_target_pairs={{0,1},{1,0},{2,3},{3,2},{4,5},{5,4},{6,7},{7,6},{8,9},{9,8},{10,11... | collective-permute-start | bytes 196616 | tf_op jit(solution)/shard_map/ppermute | solution.py:24
  83.3 1.3 %collective-permute-start.23 = (bf16[1,4,8192]{2,1,0:T(4,128)(2,1)S(1)}, bf16[1,4,8192]{2,1,0:T(4,128)(2,1)S(1)}, u32[]{:S(2)}, u32[]{:S(2)}) collective-permute-start(bf16[1,4,8192]{2,1,0:T(4,128)(2,1)S(1)} %collective-permute-done.21.refs_8_), channel_id=1, source_target_pairs={{0,1},{1,0},{2,3},{3,2},{4,5},{5,4},{6,7},{7,6},{8,9},{9,8},{10,11... | collective-permute-start | bytes 196616 | tf_op jit(solution)/shard_map/ppermute | solution.py:24
  89.2 1.3 %collective-permute-start.24 = (bf16[8,4,1024]{2,1,0:T(4,128)(2,1)S(1)}, bf16[8,4,1024]{2,1,0:T(4,128)(2,1)S(1)}, u32[]{:S(2)}, u32[]{:S(2)}) collective-permute-start(bf16[8,4,1024]{2,1,0:T(4,128)(2,1)S(1)} %get-tuple-element.32), channel_id=1, source_target_pairs={{0,1},{1,0},{2,3},{3,2},{4,5},{5,4},{6,7},{7,6},{8,9},{9,8},{10,11... | collective-permute-start | bytes 196616 | tf_op jit(solution)/shard_map/ppermute | solution.py:24
  (8 other events, 94.6 us)
where the time goes:
time: 103 us
  Pallas kernels  25.7 us (25%)
  blocking collectives  23.8 us (23%)
  local copies, waits for them, and re-layouts  17.6 us (17%)
  starting transfers between devices  17.5 us (17%)
  waiting for transfers between devices  16.8 us (16%)
  other arithmetic  1.08 us (1%)
    all_to_all x2, blocking collectives, exchange(): lax.all_to_all(pieces, 'gx', 0, 0, axis_index_groups=same_core, tiled=True)  23.8 us
    ppermute x25, starting transfers between devices, permute(): lax.ppermute(block, 'gx', [(int(i), int(t)) for i, t in enumerate(target)])  17.5 us
    unnamed x15, local copies, waits for them, and re-layouts  16.8 us
    ppermute x25, waiting for transfers between devices, permute(): lax.ppermute(block, 'gx', [(int(i), int(t)) for i, t in enumerate(target)])  16.8 us
    pallas_call x2, Pallas kernels, fetch(): pl.pallas_call(functools.partial(fetch_kernel, [first for _, first, _ in...  11.2 us
    pallas_call x1, Pallas kernels, project(): pl.pallas_call(functools.partial(project_kernel, counts, crossed, width),...  4.66 us
    pallas_call x1, Pallas kernels, project_out(): pl.pallas_call(functools.partial(out_kernel, counts, crossed), out_shape=...  4.55 us
    pallas_call x1, Pallas kernels, attend(): pl.pallas_call(functools.partial(attend_kernel, devices, width // HD, til...  2.47 us
  transfers between devices with their start and end apart: 25, of which 9 were waited for; matrix products, arithmetic and copies ran while one was open for 2% of the time, Pallas kernels for 11%

commit v1 on v0

--- a/solution.py
+++ b/solution.py
@@ -14,7 +14,6 @@
 EPSILON = 1e-05
 TAG = 128
 VMEM_LIMIT = 8 * 1024 * 1024
-OUT_VMEM_LIMIT = 18 * 1024 * 1024
 VMEM = pl.BlockSpec(memory_space=pltpu.VMEM)
 SMEM = pl.BlockSpec(memory_space=pltpu.SMEM)
 HBM = pl.BlockSpec(memory_space=pltpu.HBM)
@@ -97,6 +96,8 @@
         else:
             chips = join(arrived)
         reached = [chips] + ring(chips, inner)
+        if step == size // 2 < len(meanwhile):
+            reached[-1:] = hold(reached[-1:], 0, meanwhile[step](chips.blocks))
         groups += reached + [group.send(core[1], crossed=True) for group in reached]
     return groups
 
@@ -136,7 +137,7 @@
     here = np.arange(devices)
     chips = [source // 2 for group in groups for source in group.sources]
     columns = [chip * 2 + (here % 2 ^ other) for chip in range(devices // 2) for other in range(2)]
-    return np.stack(chips + columns + [here], 1).astype(np.int32)
+    return np.stack(chips + columns, 1).astype(np.int32)
 
 
 def norm_kernel(lengths_far, hidden_far, gain_far, out, lengths, hidden, gain, arrived):
@@ -225,12 +226,10 @@
 def multiply(slots, weights, depth, total, kept):
     total[...] = jnp.zeros_like(total)
     chunk = 0
-    for part, copies in weights:
-        for at in range(part.shape[0] // depth):
+    for part in weights:
+        for at in range(0, part.shape[0], depth):
             kept[chunk] = assemble(slots, chunk * depth, depth)
-            if copies:
-                copies[at].wait()
-            total[...] += jnp.dot(kept[chunk], part[at * depth : (at + 1) * depth, :], preferred_element_type=jnp.float32)
+            total[...] += jnp.dot(kept[chunk], part[at : at + depth, :], preferred_element_type=jnp.float32)
             chunk += 1
 
 
@@ -251,21 +250,22 @@
 
 def project_kernel(counts, crossed, width, place, *refs):
     slots = slots_of(refs, counts)
-    weights, keyval, *outs = refs[len(counts) : len(counts) + 6]
-    kept, total, packed = refs[len(counts) + 6 :]
+    first, second, keyval, *outs = refs[len(counts) : len(counts) + 7]
+    kept, total, packed = refs[len(counts) + 7 :]
     queries, fresh = outs[:2], outs[2:]
     depth = keyval.shape[1]
     tags = jnp.concatenate([ref[at, :, width:].astype(jnp.float32) for ref, at in slots], 0)
     cosine, sine = turns(tags[:, 0:1] * 32.0 + tags[:, 1:2])
-    multiply(slots, [(weights, None)], depth, total, kept)
-    own = kept[place[2 * len(slots)]]
+    multiply(slots, [first, second], depth, total, kept)
+    me = lax.axis_index("gx")
+    own = kept[me]
     blocks = keyval.shape[2] // HD
     for which in range(2):
         term = jnp.dot(own, keyval[which], preferred_element_type=jnp.float32)
         for slot in range(len(slots)):
             for at in range(blocks):
                 row = (which * blocks + at) * 4
-                fresh[crossed[slot]][place[slot], row : row + 4, :] = term[
+                fresh[crossed[slot]][place[me, slot], row : row + 4, :] = term[
                     slot * 4 : slot * 4 + 4, at * HD : (at + 1) * HD
                 ]
     heads = total.shape[1] // HD
@@ -276,7 +276,7 @@
                 line, at = row * 2 * heads + head * 2, slot * 4 + row * 2
                 packed[slot, line : line + 2, :] = turned[at : at + 2, :]
     for slot in range(len(slots)):
-        queries[crossed[slot]][place[slot]] = packed[slot].astype(jnp.bfloat16)
+        queries[crossed[slot]][place[me, slot]] = packed[slot].astype(jnp.bfloat16)
 
 
 def group_shape(groups):
@@ -286,16 +286,16 @@
 
 def project(groups, w_query, w_keyval, place, devices):
     counts, crossed = group_shape(groups)
-    width, columns = w_query.shape
+    columns = w_query[0].shape[1]
     depth, kv_width = w_keyval.shape[1:]
-    own = groups[0].blocks.shape[1]
+    own, width = groups[0].blocks.shape[1], devices * depth
     rows, tile = devices * own, own * (columns // HD)
     query = jax.ShapeDtypeStruct((devices // 2, tile, HD), jnp.bfloat16)
     fresh = jax.ShapeDtypeStruct((devices // 2, own * 2 * kv_width // HD, HD), jnp.float32)
     return pl.pallas_call(
         functools.partial(project_kernel, counts, crossed, width),
         out_shape=[query, query, fresh, fresh],
-        in_specs=[SMEM] + [VMEM] * (len(groups) + 2),
+        in_specs=[SMEM] + [VMEM] * (len(groups) + 3),
         out_specs=[VMEM] * 4,
         scratch_shapes=[
             pltpu.VMEM((devices, rows, depth), jnp.bfloat16),
@@ -306,7 +306,7 @@
         cost_estimate=pl.CostEstimate(
             flops=2 * rows * columns * width, bytes_accessed=2 * columns * width, transcendentals=2 * rows * HD
         ),
-    )(place, *[group.blocks for group in groups], w_query, w_keyval)
+    )(place, *[group.blocks for group in groups], *w_query, w_keyval)
 
 
 def pack_kernel(near, far, near_sum, far_sum, out):
@@ -332,20 +332,14 @@
 
 def out_kernel(counts, crossed, place, *refs):
     slots = slots_of(refs, counts)
-    upper, weights, near, far, lower, kept, total, arrived = refs[len(counts) :]
-    depth, first = kept.shape[2], upper.shape[0]
-    copies = []
-    for at in range(lower.shape[0] // depth):
-        source = weights.at[pl.ds(first + at * depth, depth)]
-        copies.append(pltpu.make_async_copy(source, lower.at[pl.ds(at * depth, depth)], arrived.at[at]))
-        copies[-1].start()
-    multiply(slots, [(upper, None), (lower, copies)], depth, total, kept)
-    own = near.shape[1]
+    weights, near, far, kept, total = refs[len(counts) :]
+    multiply(slots, [weights], kept.shape[2], total, kept)
+    own, me = near.shape[1], lax.axis_index("gx")
     for slot in range(len(slots)):
-        (near, far)[crossed[slot]][place[slot]] = total[slot * own : (slot + 1) * own].astype(near.dtype)
-
-
-def project_out(groups, w_upper, w_out, place, devices):
+        (near, far)[crossed[slot]][place[me, slot]] = total[slot * own : (slot + 1) * own].astype(near.dtype)
+
+
+def project_out(groups, w_out, place, devices):
     counts, crossed = group_shape(groups)
     columns = w_out.shape[1]
     own, width = groups[0].blocks.shape[1:]
@@ -354,22 +348,20 @@
     return pl.pallas_call(
         functools.partial(out_kernel, counts, crossed),
         out_shape=[piece, piece],
-        in_specs=[SMEM] + [VMEM] * (len(groups) + 1) + [HBM],
+        in_specs=[SMEM] + [VMEM] * (len(groups) + 1),
         out_specs=[VMEM, VMEM],
         scratch_shapes=[
-            pltpu.VMEM((width - w_upper.shape[0], columns), w_out.dtype),
             pltpu.VMEM((chunks, devices * own, width // chunks), jnp.bfloat16),
             pltpu.VMEM((devices * own, columns), jnp.float32),
-            pltpu.SemaphoreType.DMA((chunks // 2,)),
         ],
-        compiler_params=pltpu.CompilerParams(vmem_limit_bytes=OUT_VMEM_LIMIT),
+        compiler_params=pltpu.CompilerParams(vmem_limit_bytes=VMEM_LIMIT),
         cost_estimate=pl.CostEstimate(
             flops=2 * devices * own * columns * width, bytes_accessed=2 * columns * width, transcendentals=0
         ),
-    )(place, *[group.blocks for group in groups], w_upper, pltpu.with_memory_space_constraint(w_out, pltpu.HBM))
-
-
-def attend_kernel(devices, kv_heads, tile, lengths, place, pieces, cache, out, fresh, queries, mixed):
+    )(place, *[group.blocks for group in groups], w_out)
+
+
+def attend_kernel(devices, kv_heads, tile, lengths, place, pieces, cache, _, out, fresh, queries, mixed):
     length, width = cache.shape[2:]
     extra = fresh.shape[2]
     half = tile // 2
@@ -378,7 +370,7 @@
     for chip in range(devices // 2):
         for other in range(2):
             piece = pieces[chip, other * tile : (other + 1) * tile, :]
-            queries[place[devices + 2 * chip + other]] = piece.astype(jnp.float32)
+            queries[place[lax.axis_index("gx"), devices + 2 * chip + other]] = piece.astype(jnp.float32)
     line = lax.broadcasted_iota(jnp.int32, (8, 1), 0)
     first = jnp.where(line % 4 < 2, lengths[0], lengths[1])
     cosine, sine = turns((first + line % 2).astype(jnp.float32))
@@ -426,13 +418,13 @@
     out[...] = mixed[...].astype(out.dtype)
 
 
-def attend(pieces, tile, cache, lengths, place, devices):
+def attend(pieces, tile, cache, lengths, place, after, devices):
     length, width = cache.shape[2], cache.shape[3]
     columns = devices * tile // 4 * HD
     return pl.pallas_call(
         functools.partial(attend_kernel, devices, width // HD, tile),
         out_shape=jax.ShapeDtypeStruct((4, columns), jnp.bfloat16),
-        in_specs=[SMEM, SMEM, VMEM, VMEM],
+        in_specs=[SMEM, SMEM, VMEM, VMEM, pl.BlockSpec(memory_space=pl.ANY)],
         out_specs=VMEM,
         scratch_shapes=[
             pltpu.VMEM((2, 2, HD, width), cache.dtype),
@@ -443,7 +435,7 @@
         cost_estimate=pl.CostEstimate(
             flops=8 * 128 * length * width, bytes_accessed=8 * length * width, transcendentals=256 * length
         ),
-    )(lengths, place, pieces, cache)
+    )(lengths, place, pieces, cache, after)
 
 
 def finish_kernel(devices, place, pieces, out):
@@ -451,7 +443,7 @@
     steps, rows = out.shape[:2]
     for chip in range(devices // 2):
         for other in range(2):
-            source = place[devices + 2 * chip + other]
+            source = place[lax.axis_index("gx"), devices + 2 * chip + other]
             lanes = pl.ds(pl.multiple_of(source * columns, columns), columns)
             piece = pieces[chip, other].astype(jnp.float32)
             for step in range(steps):
@@ -474,7 +466,7 @@
     devices = lax.axis_size("gx")
 
     normed = norm(hidden, norm_gain, lengths)
-    half = w_out.shape[0] // 2
+    first = w_query.shape[0] * 3 // 4
     fetched = []
 
     def bring(ranges, after):
@@ -486,18 +478,19 @@
         normed,
         devices,
         [
-            functools.partial(bring, [(w_query, 0, w_query.shape[0]), (w_keyval, 0, 2)]),
-            functools.partial(bring, [(kv_cache, 0, 2), (w_out, 0, half)]),
+            functools.partial(bring, [(w_query, 0, first)]),
+            functools.partial(bring, [(w_keyval, 0, 2), (kv_cache, 0, 2)]),
+            functools.partial(bring, [(w_query, first, w_query.shape[0] - first)]),
         ],
     )
-    (w_query, w_keyval), (kv_cache, w_upper) = fetched
-    table = jnp.asarray(places(groups, devices))
-    place = lax.dynamic_index_in_dim(table, lax.axis_index("gx"), 0, keepdims=False)
-    near, far, near_sum, far_sum = project(groups, w_query, w_keyval, place, devices)
+    (w_first,), (w_keyval, kv_cache), (w_second,) = fetched
+    place = jnp.asarray(places(groups, devices))
+    near, far, near_sum, far_sum = project(groups, [w_first, w_second], w_keyval, place, devices)
     pieces = pack(near, swap_cores(far, devices), near_sum, swap_cores(far_sum, devices))
-
-    mixed = attend(exchange(pieces, devices), near.shape[1], kv_cache, lengths, place, devices)
-    near, far = project_out(gather(mixed, devices), w_upper, w_out, place, devices)
+    w_out, done = fetch([(w_out, 0, w_out.shape[0])], pieces)
+
+    mixed = attend(exchange(pieces, devices), near.shape[1], kv_cache, lengths, place, done, devices)
+    near, far = project_out(gather(mixed, devices), w_out, place, devices)
     pieces = jnp.stack([near, swap_cores(far, devices)], 1)
     return finish(exchange(pieces, devices), place, steps, devices)
 

time: 103 us -> 97.1 us (0.943)
  blocking collectives: 23.8 us -> 10.2 us
  starting transfers between devices: 17.5 us -> 23.1 us
  Pallas kernels: 25.7 us -> 29.9 us
  local copies, waits for them, and re-layouts: 17.6 us -> 15.7 us
    all_to_all x2 -> x1, blocking collectives: 23.8 us -> 10.2 us  [exchange(): lax.all_to_all(pieces, 'gx', 0, 0, axis_index_groups=same_core, tiled=True)]
    pallas_call x2 -> x4, Pallas kernels: 11.2 us -> 15.9 us  [fetch(): pl.pallas_call(functools.partial(fetch_kernel, [first for _, first, _ in...]
    all_to_all x0 -> x1, starting transfers between devices: none -> 3.9 us  [exchange(): lax.all_to_all(pieces, 'gx', 0, 0, axis_index_groups=same_core, tiled=True)]
    ppermute x25, starting transfers between devices: 17.5 us -> 19.2 us  [permute(): lax.ppermute(block, 'gx', [(int(i), int(t)) for i, t in enumerate(target)])]
    unnamed x15 -> x13, local copies, waits for them, and re-layouts: 16.8 us -> 15.7 us
  transfers between devices with their start and end apart: 25 -> 26, of which waited for: 9 -> 9; matrix products, arithmetic and copies ran while one was open for 2% -> 0% of each run, Pallas kernels for 11% -> 16%
where the time goes in v1:
time: 97.1 us; the launch traced here: 96.7 us
  Pallas kernels  29.9 us (31%)
  starting transfers between devices  23.1 us (24%)
  waiting for transfers between devices  17.2 us (18%)
  local copies, waits for them, and re-layouts  15.7 us (16%)
  blocking collectives  10.2 us (11%)
    ppermute x25, starting transfers between devices, permute(): lax.ppermute(block, 'gx', [(int(i), int(t)) for i, t in enumerate(target)])  19.2 us
    ppermute x25, waiting for transfers between devices, permute(): lax.ppermute(block, 'gx', [(int(i), int(t)) for i, t in enumerate(target)])  17.2 us
    pallas_call x4, Pallas kernels, fetch(): pl.pallas_call(functools.partial(fetch_kernel, [first for _, first, _ in...  15.9 us
    unnamed x13, local copies, waits for them, and re-layouts  15.7 us
    all_to_all x1, blocking collectives, exchange(): lax.all_to_all(pieces, 'gx', 0, 0, axis_index_groups=same_core, tiled=True)  10.2 us
    pallas_call x1, Pallas kernels, project(): pl.pallas_call(functools.partial(project_kernel, counts, crossed, width),...  4.08 us
    all_to_all x1, starting transfers between devices, exchange(): lax.all_to_all(pieces, 'gx', 0, 0, axis_index_groups=same_core, tiled=True)  3.9 us
    pallas_call x1, Pallas kernels, project_out(): pl.pallas_call(functools.partial(out_kernel, counts, crossed), out_shape=...  3.7 us
  transfers between devices with their start and end apart: 26, of which 9 were waited for; matrix products, arithmetic and copies ran while one was open for 0% of the time, Pallas kernels for 16%

profile of v1, /device:TPU:0, one launch (start us, length us, event | category | flops | bytes accessed | tf_op | source)
XLA Modules:
  0.0 96.7 jit_solution(18250412587868809112)
XLA Ops:
  0.0 1.4 %shard_map.82 = bf16[4,16512]{1,0:T(4,128)(2,1)S(1)} custom-call(s32[2]{0:T(128)} %lengths.1, bf16[2,2,16384]{2,1,0:T(2,128)(2,1)} %hidden_far.1, bf16[16384]{0:T(1024)(128)(2,1)} %gain_far.1), custom_call_target="tpu_custom_call" | custom-call | flops 393216 | bytes 262144 | tf_op jit(solution)/shard_map/pallas_call | solution.py:170
  1.5 3.1 %collective-permute-start.3 = (bf16[1,4,16512]{2,1,0:T(4,128)(2,1)S(1)}, bf16[1,4,16512]{2,1,0:T(4,128)(2,1)S(1)}, u32[]{:S(2)}, u32[]{:S(2)}) collective-permute-start(bf16[1,4,16512]{2,1,0:T(4,128)(2,1)S(1)} %bitcast.4), channel_id=1, source_target_pairs={{0,4},{1,5},{2,6},{3,7},{4,12},{5,13},{6,14},{7,15},{8,0},{9,1},{1... | collective-permute-start | bytes 396296 | tf_op jit(solution)/shard_map/ppermute | solution.py:23
  5.6 1.8 %collective-permute-start = (bf16[1,4,16512]{2,1,0:T(4,128)(2,1)S(1)}, bf16[1,4,16512]{2,1,0:T(4,128)(2,1)S(1)}, u32[]{:S(2)}, u32[]{:S(2)}) collective-permute-start(bf16[1,4,16512]{2,1,0:T(4,128)(2,1)S(1)} %bitcast.6), channel_id=1, source_target_pairs={{0,2},{1,3},{2,0},{3,1},{4,6},{5,7},{6,4},{7,5},{8,10},{9,11},{10,... | collective-permute-start | bytes 396296 | tf_op jit(solution)/shard_map/ppermute | solution.py:23
  7.4 4.7 %shard_map.83 = (bf16[12288,512]{1,0:T(8,128)(2,1)S(1)}, f32[8,128]{1,0:T(8,128)S(1)}) custom-call(bf16[16384,512]{1,0:T(8,128)(2,1)} %refs_0_.6, bf16[1,4,16512]{2,1,0:T(4,128)(2,1)S(1)} %bitcast.7), custom_call_target="tpu_custom_call" | custom-call | bytes 12582912 | tf_op jit(solution)/shard_map/pallas_call | solution.py:203
  12.2 1.7 %collective-permute-start.7 = (bf16[1,4,16512]{2,1,0:T(4,128)(2,1)S(1)}, bf16[1,4,16512]{2,1,0:T(4,128)(2,1)S(1)}, u32[]{:S(2)}, u32[]{:S(2)}) collective-permute-start(bf16[1,4,16512]{2,1,0:T(4,128)(2,1)S(1)} %get-tuple-element.24.refs_2_), channel_id=1, source_target_pairs={{0,8},{1,9},{2,10},{3,11},{4,0},{5,1},{6,2},{7,3},{8,12},{9,13},{1... | collective-permute-start | bytes 396296 | tf_op jit(solution)/shard_map/ppermute | solution.py:23
  15.5 3.0 %shard_map.85 = (bf16[2,1024,512]{2,1,0:T(8,128)(2,1)S(1)}, bf16[2,2,1024,512]{3,2,1,0:T(8,128)(2,1)S(1)}, f32[8,128]{1,0:T(8,128)S(1)}) custom-call(bf16[2,1024,512]{2,1,0:T(8,128)(2,1)} %refs_0_.5, bf16[2,2,1024,512]{3,2,1,0:T(8,128)(2,1)} %refs_1_.1, bf16[1,4,16512]{2,1,0:T(4,128)(2,1)S(1)} %get-tuple-element.24.refs_2_), custom_call_target="tpu_custom_call" | custom-call | bytes 6291456 | tf_op jit(solution)/shard_map/pallas_call | solution.py:203
  18.5 2.0 %copy-done.2 = bf16[2,2,1024,512]{3,2,1,0:T(8,128)(2,1)} copy-done((bf16[2,2,1024,512]{3,2,1,0:T(8,128)(2,1)}, bf16[2,2,1024,512]{3,2,1,0:T(8,128)(2,1)S(1)}, u32[]{:S(2)}) %copy-start.2) | copy-done | bytes 4194328
  22.0 2.2 %shard_map.87 = (bf16[4096,512]{1,0:T(8,128)(2,1)S(1)}, f32[8,128]{1,0:T(8,128)S(1)}) custom-call(bf16[16384,512]{1,0:T(8,128)(2,1)} %refs_0_.6, bf16[1,4,16512]{2,1,0:T(4,128)(2,1)S(1)} %shard_map.86.refs_1_.refs_7_), custom_call_target="tpu_custom_call" | custom-call | bytes 4194304 | tf_op jit(solution)/shard_map/pallas_call | solution.py:203
  24.3 2.3 %collective-permute-done.8.refs_0_ = bf16[1,4,16512]{2,1,0:T(4,128)(2,1)S(1)} collective-permute-done((bf16[1,4,16512]{2,1,0:T(4,128)(2,1)S(1)}, bf16[1,4,16512]{2,1,0:T(4,128)(2,1)S(1)}, u32[]{:S(2)}, u32[]{:S(2)}) %collective-permute-start.8) | collective-permute-done | bytes 132128 | tf_op jit(solution)/shard_map/ppermute | solution.py:23
  28.0 4.1 %shard_map.89 = (bf16[8,16,128]{2,1,0:T(8,128)(2,1)S(1)}, bf16[8,16,128]{2,1,0:T(8,128)(2,1)S(1)}, f32[8,32,128]{2,1,0:T(8,128)S(1)}, f32[8,32,128]{2,1,0:T(8,128)S(1)}) custom-call(s32[16,32]{1,0:T(8,128)S(1)} %copy-done.4, bf16[1,4,16512]{2,1,0:T(4,128)(2,1)S(1)} %bitcast.9, bf16[1,4,16512]{2,1,0:T(4,128)(2,1)S(1)} %collective-permute-done.refs_1_, ...), custom_call_target="tpu_custom_call" | custom-call | flops 1073741824 | bytes 16777216 | tf_op jit(solution)/shard_map/pallas_call | solution.py:295
  34.2 3.9 %all-to-all-start = ((bf16[8,96,128]{2,1,0:T(8,128)(2,1)}), bf16[8,96,128]{2,1,0:T(8,128)(2,1)S(1)}, u32[]{:S(2)}, u32[]{:S(2)}) async-start(bf16[8,96,128]{2,1,0:T(8,128)(2,1)} %shard_map.90.refs_1_), calls=%async_computation | async-start | bytes 393216 | tf_op jit(solution)/shard_map/all_to_all | solution.py:133
  38.1 5.9 %shard_map.91 = (bf16[8192,1024]{1,0:T(8,128)(2,1)S(1)}, f32[8,128]{1,0:T(8,128)S(1)}) custom-call(bf16[8192,1024]{1,0:T(8,128)(2,1)} %refs_0_.7, bf16[8,96,128]{2,1,0:T(8,128)(2,1)} %shard_map.90.refs_1_), custom_call_target="tpu_custom_call" | custom-call | bytes 16777216 | tf_op jit(solution)/shard_map/pallas_call | solution.py:203
  44.1 5.7 %copy-done = bf16[8192,1024]{1,0:T(8,128)(2,1)} copy-done((bf16[8192,1024]{1,0:T(8,128)(2,1)}, bf16[8192,1024]{1,0:T(8,128)(2,1)S(1)}, u32[]{:S(2)}) %copy-start) | copy-done | bytes 16777240
  49.8 2.2 %copy-done.3 = bf16[2,2,1024,512]{3,2,1,0:T(8,128)(2,1)S(1)} copy-done((bf16[2,2,1024,512]{3,2,1,0:T(8,128)(2,1)S(1)}, bf16[2,2,1024,512]{3,2,1,0:T(8,128)(2,1)}, u32[]{:S(2)}) %copy-start.3) | copy-done | bytes 4194328
  52.0 2.6 %shard_map.92 = bf16[4,8192]{1,0:T(4,128)(2,1)S(1)} custom-call(s32[2]{0:T(128)S(1)} %copy-done.5, s32[16,32]{1,0:T(8,128)S(1)} %copy-done.4, bf16[8,96,128]{2,1,0:T(8,128)(2,1)S(1)} %all-to-all-done.pieces, bf16[2,2,1024,512]{3,2,1,0:T(8,128)(2,1)S(1)} %copy-done.3, f32[8,128]{1,0:T(8,128)S(1)} %get-tuple-element.35._), custom_call_target="tpu_custom_call" | custom-call | flops 536870912 | bytes 4194304 | tf_op jit(solution)/shard_map/pallas_call | solution.py:424
  54.7 3.0 %collective-permute-start.15 = (bf16[1,4,8192]{2,1,0:T(4,128)(2,1)S(1)}, bf16[1,4,8192]{2,1,0:T(4,128)(2,1)S(1)}, u32[]{:S(2)}, u32[]{:S(2)}) collective-permute-start(bf16[1,4,8192]{2,1,0:T(4,128)(2,1)S(1)} %bitcast.10), channel_id=1, source_target_pairs={{0,8},{1,9},{2,10},{3,11},{4,0},{5,1},{6,2},{7,3},{8,12},{9,13},{1... | collective-permute-start | bytes 196616 | tf_op jit(solution)/shard_map/ppermute | solution.py:23
  57.6 1.5 %collective-permute-start.13 = (bf16[1,4,8192]{2,1,0:T(4,128)(2,1)S(1)}, bf16[1,4,8192]{2,1,0:T(4,128)(2,1)S(1)}, u32[]{:S(2)}, u32[]{:S(2)}) collective-permute-start(bf16[1,4,8192]{2,1,0:T(4,128)(2,1)S(1)} %bitcast.12), channel_id=1, source_target_pairs={{0,2},{1,3},{2,0},{3,1},{4,6},{5,7},{6,4},{7,5},{8,10},{9,11},{10,... | collective-permute-start | bytes 196616 | tf_op jit(solution)/shard_map/ppermute | solution.py:23
  59.6 3.2 %collective-permute-done.16 = bf16[1,4,8192]{2,1,0:T(4,128)(2,1)S(1)} collective-permute-done((bf16[1,4,8192]{2,1,0:T(4,128)(2,1)S(1)}, bf16[1,4,8192]{2,1,0:T(4,128)(2,1)S(1)}, u32[]{:S(2)}, u32[]{:S(2)}) %collective-permute-start.16) | collective-permute-done | bytes 65568 | tf_op jit(solution)/shard_map/ppermute | solution.py:23
  62.9 1.5 %collective-permute-start.17 = (bf16[2,4,8192]{2,1,0:T(4,128)(2,1)S(1)}, bf16[2,4,8192]{2,1,0:T(4,128)(2,1)S(1)}, u32[]{:S(2)}, u32[]{:S(2)}) collective-permute-start(bf16[2,4,8192]{2,1,0:T(4,128)(2,1)S(1)} %constant_dynamic-update-slice_fusion.refs_3_), channel_id=1, source_target_pairs={{0,2},{1,3},{2,0},{3,1},{4,6},{5,7},{6,4},{7,5},{8,10},{9,11},{10,... | collective-permute-start | bytes 393224 | tf_op jit(solution)/shard_map/ppermute | solution.py:23
  65.2 3.5 %collective-permute-done.20.refs_7_ = bf16[1,4,8192]{2,1,0:T(4,128)(2,1)S(1)} collective-permute-done((bf16[1,4,8192]{2,1,0:T(4,128)(2,1)S(1)}, bf16[1,4,8192]{2,1,0:T(4,128)(2,1)S(1)}, u32[]{:S(2)}, u32[]{:S(2)}) %collective-permute-start.20) | collective-permute-done | bytes 65568 | tf_op jit(solution)/shard_map/ppermute | solution.py:23
  69.8 3.2 %collective-permute-done.21.refs_8_ = bf16[1,4,8192]{2,1,0:T(4,128)(2,1)S(1)} collective-permute-done((bf16[1,4,8192]{2,1,0:T(4,128)(2,1)S(1)}, bf16[1,4,8192]{2,1,0:T(4,128)(2,1)S(1)}, u32[]{:S(2)}, u32[]{:S(2)}) %collective-permute-start.21) | collective-permute-done | bytes 65568 | tf_op jit(solution)/shard_map/ppermute | solution.py:23
  74.2 5.8 %copy-done.1 = bf16[8192,1024]{1,0:T(8,128)(2,1)S(1)} copy-done((bf16[8192,1024]{1,0:T(8,128)(2,1)S(1)}, bf16[8192,1024]{1,0:T(8,128)(2,1)}, u32[]{:S(2)}) %copy-start.1) | copy-done | bytes 16777240
  80.0 3.7 %shard_map.93 = (bf16[8,4,1024]{2,1,0:T(4,128)(2,1)S(1)}, bf16[8,4,1024]{2,1,0:T(4,128)(2,1)S(1)}) custom-call(s32[16,32]{1,0:T(8,128)S(1)} %copy-done.4, bf16[1,4,8192]{2,1,0:T(4,128)(2,1)S(1)} %bitcast.14, bf16[1,4,8192]{2,1,0:T(4,128)(2,1)S(1)} %collective-permute-done.13.refs_1_, bf16[2,4,8192]{2,1,0:T(4,128)(2,1)S(1)} %collective-permute-done.14.refs_2_, ...), custom_call_target="tpu_custom_call" | custom-call | flops 1073741824 | bytes 16777216 | tf_op jit(solution)/shard_map/pallas_call | solution.py:348
  85.1 10.2 %all_to_all.10.pieces = bf16[8,2,4,1024]{3,2,1,0:T(4,128)(2,1)S(1)} all-to-all(bf16[8,2,4,1024]{3,2,1,0:T(4,128)(2,1)S(1)} %pad_maximum_fusion.2), channel_id=1, replica_groups={{0,2,4,6,8,10,12,14},{1,3,5,7,9,11,13,15},{16,18,20,22,24,26,28,30},{17..., dimensions={0} | all-to-all | bytes 262144 | tf_op jit(solution)/shard_map/all_to_all | solution.py:133
  (59 shorter events, 14.3 us)
Async XLA Ops:
  1.5 10.7 %collective-permute-start.3 = (bf16[1,4,16512]{2,1,0:T(4,128)(2,1)S(1)}, bf16[1,4,16512]{2,1,0:T(4,128)(2,1)S(1)}, u32[]{:S(2)}, u32[]{:S(2)}) collective-permute-start(bf16[1,4,16512]{2,1,0:T(4,128)(2,1)S(1)} %bitcast.4), channel_id=1, source_target_pairs={{0,4},{1,5},{2,6},{3,7},{4,12},{5,13},{6,14},{7,15},{8,0},{9,1},{1... | collective-permute-start | bytes 396296 | tf_op jit(solution)/shard_map/ppermute | solution.py:23
  4.5 7.6 %collective-permute-start.2 = (bf16[1,4,16512]{2,1,0:T(4,128)(2,1)S(1)}, bf16[1,4,16512]{2,1,0:T(4,128)(2,1)S(1)}, u32[]{:S(2)}, u32[]{:S(2)}) collective-permute-start(bf16[1,4,16512]{2,1,0:T(4,128)(2,1)S(1)} %bitcast.5), channel_id=1, source_target_pairs={{0,8},{1,9},{2,10},{3,11},{4,0},{5,1},{6,2},{7,3},{8,12},{9,13},{1... | collective-permute-start | bytes 396296 | tf_op jit(solution)/shard_map/ppermute | solution.py:23
  5.6 9.6 %collective-permute-start = (bf16[1,4,16512]{2,1,0:T(4,128)(2,1)S(1)}, bf16[1,4,16512]{2,1,0:T(4,128)(2,1)S(1)}, u32[]{:S(2)}, u32[]{:S(2)}) collective-permute-start(bf16[1,4,16512]{2,1,0:T(4,128)(2,1)S(1)} %bitcast.6), channel_id=1, source_target_pairs={{0,2},{1,3},{2,0},{3,1},{4,6},{5,7},{6,4},{7,5},{8,10},{9,11},{10,... | collective-permute-start | bytes 396296 | tf_op jit(solution)/shard_map/ppermute | solution.py:23
  12.2 8.3 %collective-permute-start.7 = (bf16[1,4,16512]{2,1,0:T(4,128)(2,1)S(1)}, bf16[1,4,16512]{2,1,0:T(4,128)(2,1)S(1)}, u32[]{:S(2)}, u32[]{:S(2)}) collective-permute-start(bf16[1,4,16512]{2,1,0:T(4,128)(2,1)S(1)} %get-tuple-element.24.refs_2_), channel_id=1, source_target_pairs={{0,8},{1,9},{2,10},{3,11},{4,0},{5,1},{6,2},{7,3},{8,12},{9,13},{1... | collective-permute-start | bytes 396296 | tf_op jit(solution)/shard_map/ppermute | solution.py:23
  13.9 7.6 %collective-permute-start.4 = (bf16[2,4,16512]{2,1,0:T(4,128)(2,1)S(1)}, bf16[2,4,16512]{2,1,0:T(4,128)(2,1)S(1)}, u32[]{:S(2)}, u32[]{:S(2)}) collective-permute-start(bf16[2,4,16512]{2,1,0:T(4,128)(2,1)S(1)} %get-tuple-element.23.refs_3_), channel_id=1, source_target_pairs={{0,2},{1,3},{2,0},{3,1},{4,6},{5,7},{6,4},{7,5},{8,10},{9,11},{10,... | collective-permute-start | bytes 792584 | tf_op jit(solution)/shard_map/ppermute | solution.py:23
  15.4 11.2 %collective-permute-start.1 = (bf16[2,4,16512]{2,1,0:T(4,128)(2,1)S(1)}, bf16[2,4,16512]{2,1,0:T(4,128)(2,1)S(1)}, u32[]{:S(2)}, u32[]{:S(2)}) collective-permute-start(bf16[2,4,16512]{2,1,0:T(4,128)(2,1)S(1)} %pad_maximum_fusion), channel_id=1, source_target_pairs={{0,1},{1,0},{2,3},{3,2},{4,5},{5,4},{6,7},{7,6},{8,9},{9,8},{10,11... | collective-permute-start | bytes 792584 | tf_op jit(solution)/shard_map/ppermute | solution.py:23
  20.5 6.0 %collective-permute-start.8 = (bf16[1,4,16512]{2,1,0:T(4,128)(2,1)S(1)}, bf16[1,4,16512]{2,1,0:T(4,128)(2,1)S(1)}, u32[]{:S(2)}, u32[]{:S(2)}) collective-permute-start(bf16[1,4,16512]{2,1,0:T(4,128)(2,1)S(1)} %shard_map.86.refs_1_.refs_7_), channel_id=1, source_target_pairs={{0,2},{1,3},{2,0},{3,1},{4,6},{5,7},{6,4},{7,5},{8,10},{9,11},{10,... | collective-permute-start | bytes 396296 | tf_op jit(solution)/shard_map/ppermute | solution.py:23
  21.3 5.3 %collective-permute-start.5 = (bf16[2,4,16512]{2,1,0:T(4,128)(2,1)S(1)}, bf16[2,4,16512]{2,1,0:T(4,128)(2,1)S(1)}, u32[]{:S(2)}, u32[]{:S(2)}) collective-permute-start(bf16[2,4,16512]{2,1,0:T(4,128)(2,1)S(1)} %get-tuple-element.23.refs_3_), channel_id=1, source_target_pairs={{0,1},{1,0},{2,3},{3,2},{4,5},{5,4},{6,7},{7,6},{8,9},{9,8},{10,11... | collective-permute-start | bytes 792584 | tf_op jit(solution)/shard_map/ppermute | solution.py:23
  21.5 6.4 %collective-permute-start.6 = (bf16[2,4,16512]{2,1,0:T(4,128)(2,1)S(1)}, bf16[2,4,16512]{2,1,0:T(4,128)(2,1)S(1)}, u32[]{:S(2)}, u32[]{:S(2)}) collective-permute-start(bf16[2,4,16512]{2,1,0:T(4,128)(2,1)S(1)} %collective-permute-done.4.refs_4_), channel_id=1, source_target_pairs={{0,1},{1,0},{2,3},{3,2},{4,5},{5,4},{6,7},{7,6},{8,9},{9,8},{10,11... | collective-permute-start | bytes 792584 | tf_op jit(solution)/shard_map/ppermute | solution.py:23
  21.8 4.8 %collective-permute-start.9 = (bf16[1,4,16512]{2,1,0:T(4,128)(2,1)S(1)}, bf16[1,4,16512]{2,1,0:T(4,128)(2,1)S(1)}, u32[]{:S(2)}, u32[]{:S(2)}) collective-permute-start(bf16[1,4,16512]{2,1,0:T(4,128)(2,1)S(1)} %shard_map.86.refs_1_.refs_7_), channel_id=1, source_target_pairs={{0,1},{1,0},{2,3},{3,2},{4,5},{5,4},{6,7},{7,6},{8,9},{9,8},{10,11... | collective-permute-start | bytes 396296 | tf_op jit(solution)/shard_map/ppermute | solution.py:23
  26.5 1.4 %collective-permute-start.10 = (bf16[1,4,16512]{2,1,0:T(4,128)(2,1)S(1)}, bf16[1,4,16512]{2,1,0:T(4,128)(2,1)S(1)}, u32[]{:S(2)}, u32[]{:S(2)}) collective-permute-start(bf16[1,4,16512]{2,1,0:T(4,128)(2,1)S(1)} %shard_map.88.refs_8_), channel_id=1, source_target_pairs={{0,1},{1,0},{2,3},{3,2},{4,5},{5,4},{6,7},{7,6},{8,9},{9,8},{10,11... | collective-permute-start | bytes 396296 | tf_op jit(solution)/shard_map/ppermute | solution.py:23
  32.0 1.5 %collective-permute-start.12 = (f32[8,32,128]{2,1,0:T(8,128)S(1)}, f32[8,32,128]{2,1,0:T(8,128)S(1)}, u32[]{:S(2)}, u32[]{:S(2)}) collective-permute-start(f32[8,32,128]{2,1,0:T(8,128)S(1)} %get-tuple-element.33), channel_id=1, source_target_pairs={{0,1},{1,0},{2,3},{3,2},{4,5},{5,4},{6,7},{7,6},{8,9},{9,8},{10,11... | collective-permute-start | bytes 393224 | tf_op jit(solution)/shard_map/ppermute | solution.py:23
  34.2 15.6 %all-to-all-start = ((bf16[8,96,128]{2,1,0:T(8,128)(2,1)}), bf16[8,96,128]{2,1,0:T(8,128)(2,1)S(1)}, u32[]{:S(2)}, u32[]{:S(2)}) async-start(bf16[8,96,128]{2,1,0:T(8,128)(2,1)} %shard_map.90.refs_1_), calls=%async_computation | async-start | bytes 393216 | tf_op jit(solution)/shard_map/all_to_all | solution.py:133
  54.7 5.0 %collective-permute-start.15 = (bf16[1,4,8192]{2,1,0:T(4,128)(2,1)S(1)}, bf16[1,4,8192]{2,1,0:T(4,128)(2,1)S(1)}, u32[]{:S(2)}, u32[]{:S(2)}) collective-permute-start(bf16[1,4,8192]{2,1,0:T(4,128)(2,1)S(1)} %bitcast.10), channel_id=1, source_target_pairs={{0,8},{1,9},{2,10},{3,11},{4,0},{5,1},{6,2},{7,3},{8,12},{9,13},{1... | collective-permute-start | bytes 196616 | tf_op jit(solution)/shard_map/ppermute | solution.py:23
  57.6 5.2 %collective-permute-start.16 = (bf16[1,4,8192]{2,1,0:T(4,128)(2,1)S(1)}, bf16[1,4,8192]{2,1,0:T(4,128)(2,1)S(1)}, u32[]{:S(2)}, u32[]{:S(2)}) collective-permute-start(bf16[1,4,8192]{2,1,0:T(4,128)(2,1)S(1)} %bitcast.11), channel_id=1, source_target_pairs={{0,4},{1,5},{2,6},{3,7},{4,12},{5,13},{6,14},{7,15},{8,0},{9,1},{1... | collective-permute-start | bytes 196616 | tf_op jit(solution)/shard_map/ppermute | solution.py:23
  57.6 7.4 %collective-permute-start.13 = (bf16[1,4,8192]{2,1,0:T(4,128)(2,1)S(1)}, bf16[1,4,8192]{2,1,0:T(4,128)(2,1)S(1)}, u32[]{:S(2)}, u32[]{:S(2)}) collective-permute-start(bf16[1,4,8192]{2,1,0:T(4,128)(2,1)S(1)} %bitcast.12), channel_id=1, source_target_pairs={{0,2},{1,3},{2,0},{3,1},{4,6},{5,7},{6,4},{7,5},{8,10},{9,11},{10,... | collective-permute-start | bytes 196616 | tf_op jit(solution)/shard_map/ppermute | solution.py:23
  62.8 10.1 %collective-permute-start.18 = (bf16[2,4,8192]{2,1,0:T(4,128)(2,1)S(1)}, bf16[2,4,8192]{2,1,0:T(4,128)(2,1)S(1)}, u32[]{:S(2)}, u32[]{:S(2)}) collective-permute-start(bf16[2,4,8192]{2,1,0:T(4,128)(2,1)S(1)} %constant_dynamic-update-slice_fusion.refs_3_), channel_id=1, source_target_pairs={{0,1},{1,0},{2,3},{3,2},{4,5},{5,4},{6,7},{7,6},{8,9},{9,8},{10,11... | collective-permute-start | bytes 393224 | tf_op jit(solution)/shard_map/ppermute | solution.py:23
  62.9 6.4 %collective-permute-start.17 = (bf16[2,4,8192]{2,1,0:T(4,128)(2,1)S(1)}, bf16[2,4,8192]{2,1,0:T(4,128)(2,1)S(1)}, u32[]{:S(2)}, u32[]{:S(2)}) collective-permute-start(bf16[2,4,8192]{2,1,0:T(4,128)(2,1)S(1)} %constant_dynamic-update-slice_fusion.refs_3_), channel_id=1, source_target_pairs={{0,2},{1,3},{2,0},{3,1},{4,6},{5,7},{6,4},{7,5},{8,10},{9,11},{10,... | collective-permute-start | bytes 393224 | tf_op jit(solution)/shard_map/ppermute | solution.py:23
  64.4 4.3 %collective-permute-start.20 = (bf16[1,4,8192]{2,1,0:T(4,128)(2,1)S(1)}, bf16[1,4,8192]{2,1,0:T(4,128)(2,1)S(1)}, u32[]{:S(2)}, u32[]{:S(2)}) collective-permute-start(bf16[1,4,8192]{2,1,0:T(4,128)(2,1)S(1)} %collective-permute-done.15), channel_id=1, source_target_pairs={{0,8},{1,9},{2,10},{3,11},{4,0},{5,1},{6,2},{7,3},{8,12},{9,13},{1... | collective-permute-start | bytes 196616 | tf_op jit(solution)/shard_map/ppermute | solution.py:23
  65.1 7.9 %collective-permute-start.14 = (bf16[2,4,8192]{2,1,0:T(4,128)(2,1)S(1)}, bf16[2,4,8192]{2,1,0:T(4,128)(2,1)S(1)}, u32[]{:S(2)}, u32[]{:S(2)}) collective-permute-start(bf16[2,4,8192]{2,1,0:T(4,128)(2,1)S(1)} %pad_maximum_fusion.1), channel_id=1, source_target_pairs={{0,1},{1,0},{2,3},{3,2},{4,5},{5,4},{6,7},{7,6},{8,9},{9,8},{10,11... | collective-permute-start | bytes 393224 | tf_op jit(solution)/shard_map/ppermute | solution.py:23
  68.7 4.3 %collective-permute-start.21 = (bf16[1,4,8192]{2,1,0:T(4,128)(2,1)S(1)}, bf16[1,4,8192]{2,1,0:T(4,128)(2,1)S(1)}, u32[]{:S(2)}, u32[]{:S(2)}) collective-permute-start(bf16[1,4,8192]{2,1,0:T(4,128)(2,1)S(1)} %collective-permute-done.20.refs_7_), channel_id=1, source_target_pairs={{0,2},{1,3},{2,0},{3,1},{4,6},{5,7},{6,4},{7,5},{8,10},{9,11},{10,... | collective-permute-start | bytes 196616 | tf_op jit(solution)/shard_map/ppermute | solution.py:23
  69.3 5.0 %collective-permute-start.19 = (bf16[2,4,8192]{2,1,0:T(4,128)(2,1)S(1)}, bf16[2,4,8192]{2,1,0:T(4,128)(2,1)S(1)}, u32[]{:S(2)}, u32[]{:S(2)}) collective-permute-start(bf16[2,4,8192]{2,1,0:T(4,128)(2,1)S(1)} %collective-permute-done.17.refs_4_), channel_id=1, source_target_pairs={{0,1},{1,0},{2,3},{3,2},{4,5},{5,4},{6,7},{7,6},{8,9},{9,8},{10,11... | collective-permute-start | bytes 393224 | tf_op jit(solution)/shard_map/ppermute | solution.py:23
  69.3 3.7 %collective-permute-start.22 = (bf16[1,4,8192]{2,1,0:T(4,128)(2,1)S(1)}, bf16[1,4,8192]{2,1,0:T(4,128)(2,1)S(1)}, u32[]{:S(2)}, u32[]{:S(2)}) collective-permute-start(bf16[1,4,8192]{2,1,0:T(4,128)(2,1)S(1)} %collective-permute-done.20.refs_7_), channel_id=1, source_target_pairs={{0,1},{1,0},{2,3},{3,2},{4,5},{5,4},{6,7},{7,6},{8,9},{9,8},{10,11... | collective-permute-start | bytes 196616 | tf_op jit(solution)/shard_map/ppermute | solution.py:23
  83.7 1.3 %collective-permute-start.24 = (bf16[8,4,1024]{2,1,0:T(4,128)(2,1)S(1)}, bf16[8,4,1024]{2,1,0:T(4,128)(2,1)S(1)}, u32[]{:S(2)}, u32[]{:S(2)}) collective-permute-start(bf16[8,4,1024]{2,1,0:T(4,128)(2,1)S(1)} %get-tuple-element.38), channel_id=1, source_target_pairs={{0,1},{1,0},{2,3},{3,2},{4,5},{5,4},{6,7},{7,6},{8,9},{9,8},{10,11... | collective-permute-start | bytes 196616 | tf_op jit(solution)/shard_map/ppermute | solution.py:23
  (8 other events, 37.3 us)

commit v2 on v1

--- a/solution.py
+++ b/solution.py
@@ -332,8 +332,8 @@
 
 def out_kernel(counts, crossed, place, *refs):
     slots = slots_of(refs, counts)
-    weights, near, far, kept, total = refs[len(counts) :]
-    multiply(slots, [weights], kept.shape[2], total, kept)
+    *weights, near, far, kept, total = refs[len(counts) :]
+    multiply(slots, weights, kept.shape[2], total, kept)
     own, me = near.shape[1], lax.axis_index("gx")
     for slot in range(len(slots)):
         (near, far)[crossed[slot]][place[me, slot]] = total[slot * own : (slot + 1) * own].astype(near.dtype)
@@ -341,14 +341,14 @@
 
 def project_out(groups, w_out, place, devices):
     counts, crossed = group_shape(groups)
-    columns = w_out.shape[1]
+    columns = w_out[0].shape[1]
     own, width = groups[0].blocks.shape[1:]
     chunks = devices // 2
     piece = jax.ShapeDtypeStruct((devices // 2, own, columns), jnp.bfloat16)
     return pl.pallas_call(
         functools.partial(out_kernel, counts, crossed),
         out_shape=[piece, piece],
-        in_specs=[SMEM] + [VMEM] * (len(groups) + 1),
+        in_specs=[SMEM] + [VMEM] * (len(groups) + len(w_out)),
         out_specs=[VMEM, VMEM],
         scratch_shapes=[
             pltpu.VMEM((chunks, devices * own, width // chunks), jnp.bfloat16),
@@ -358,10 +358,10 @@
         cost_estimate=pl.CostEstimate(
             flops=2 * devices * own * columns * width, bytes_accessed=2 * columns * width, transcendentals=0
         ),
-    )(place, *[group.blocks for group in groups], w_out)
-
-
-def attend_kernel(devices, kv_heads, tile, lengths, place, pieces, cache, _, out, fresh, queries, mixed):
+    )(place, *[group.blocks for group in groups], *w_out)
+
+
+def attend_kernel(devices, kv_heads, tile, lengths, place, pieces, cache, out, fresh, queries, mixed):
     length, width = cache.shape[2:]
     extra = fresh.shape[2]
     half = tile // 2
@@ -418,13 +418,13 @@
     out[...] = mixed[...].astype(out.dtype)
 
 
-def attend(pieces, tile, cache, lengths, place, after, devices):
+def attend(pieces, tile, cache, lengths, place, devices):
     length, width = cache.shape[2], cache.shape[3]
     columns = devices * tile // 4 * HD
     return pl.pallas_call(
         functools.partial(attend_kernel, devices, width // HD, tile),
         out_shape=jax.ShapeDtypeStruct((4, columns), jnp.bfloat16),
-        in_specs=[SMEM, SMEM, VMEM, VMEM, pl.BlockSpec(memory_space=pl.ANY)],
+        in_specs=[SMEM, SMEM, VMEM, VMEM],
         out_specs=VMEM,
         scratch_shapes=[
             pltpu.VMEM((2, 2, HD, width), cache.dtype),
@@ -435,7 +435,7 @@
         cost_estimate=pl.CostEstimate(
             flops=8 * 128 * length * width, bytes_accessed=8 * length * width, transcendentals=256 * length
         ),
-    )(lengths, place, pieces, cache, after)
+    )(lengths, place, pieces, cache)
 
 
 def finish_kernel(devices, place, pieces, out):
@@ -466,31 +466,30 @@
     devices = lax.axis_size("gx")
 
     normed = norm(hidden, norm_gain, lengths)
-    first = w_query.shape[0] * 3 // 4
+    cut = w_query.shape[0] * 3 // 4
     fetched = []
 
-    def bring(ranges, after):
-        *arrays, done = fetch(ranges, after)
-        fetched.append(arrays)
-        return done
-
-    groups = gather(
-        normed,
-        devices,
-        [
-            functools.partial(bring, [(w_query, 0, first)]),
-            functools.partial(bring, [(w_keyval, 0, 2), (kv_cache, 0, 2)]),
-            functools.partial(bring, [(w_query, first, w_query.shape[0] - first)]),
-        ],
-    )
-    (w_first,), (w_keyval, kv_cache), (w_second,) = fetched
+    def bring(*ranges):
+        def start(after):
+            *arrays, done = fetch(ranges, after)
+            fetched.extend(arrays)
+            return done
+
+        return start
+
+    waits = [bring((w_query, 0, cut)), bring((w_keyval, 0, 2), (kv_cache, 0, 2)), bring((w_query, cut, w_query.shape[0] - cut))]
+    groups = gather(normed, devices, waits)
+    w_first, w_keyval, kv_cache, w_second = fetched
     place = jnp.asarray(places(groups, devices))
     near, far, near_sum, far_sum = project(groups, [w_first, w_second], w_keyval, place, devices)
     pieces = pack(near, swap_cores(far, devices), near_sum, swap_cores(far_sum, devices))
-    w_out, done = fetch([(w_out, 0, w_out.shape[0])], pieces)
-
-    mixed = attend(exchange(pieces, devices), near.shape[1], kv_cache, lengths, place, done, devices)
-    near, far = project_out(gather(mixed, devices), w_out, place, devices)
+
+    mixed = attend(exchange(pieces, devices), near.shape[1], kv_cache, lengths, place, devices)
+    fetched = []
+    part = w_out.shape[0] // 8
+    waits = [bring((w_out, first * part, count * part)) for first, count in ((0, 3), (3, 3), (6, 2))]
+    groups = gather(mixed, devices, waits)
+    near, far = project_out(groups, fetched, place, devices)
     pieces = jnp.stack([near, swap_cores(far, devices)], 1)
     return finish(exchange(pieces, devices), place, steps, devices)
 

time: 97.1 us -> 81.2 us (0.84)
  local copies, waits for them, and re-layouts: 15.7 us -> 0.01 us
  blocking collectives: 10.2 us -> 22.2 us
  waiting for transfers between devices: 17.2 us -> 7.3 us
  starting transfers between devices: 23.1 us -> 19.6 us
  Pallas kernels: 29.9 us -> 31.2 us
    unnamed x13 -> x4, local copies, waits for them, and re-layouts: 15.7 us -> 0.01 us
    all_to_all x1 -> x2, blocking collectives: 10.2 us -> 22.2 us  [exchange(): lax.all_to_all(pieces, 'gx', 0, 0, axis_index_groups=same_core, tiled=True)]
    ppermute x25, waiting for transfers between devices: 17.2 us -> 7.3 us  [permute(): lax.ppermute(block, 'gx', [(int(i), int(t)) for i, t in enumerate(target)])]
    all_to_all x1 -> x0, starting transfers between devices: 3.9 us -> none  [exchange(): lax.all_to_all(pieces, 'gx', 0, 0, axis_index_groups=same_core, tiled=True)]
    pallas_call x4 -> x6, Pallas kernels: 15.9 us -> 17.9 us  [fetch(): pl.pallas_call(functools.partial(fetch_kernel, [first for _, first, _ in...]
  transfers between devices with their start and end apart: 26 -> 25, of which waited for: 9 -> 7; matrix products, arithmetic and copies ran while one was open for 0% -> 0% of each run, Pallas kernels for 16% -> 22%
where the time goes in v2:
time: 81.2 us; the launch traced here: 81 us
  Pallas kernels  31.2 us (38%)
  blocking collectives  22.2 us (27%)
  starting transfers between devices  19.6 us (24%)
  waiting for transfers between devices  7.3 us (9%)
    all_to_all x2, blocking collectives, exchange(): lax.all_to_all(pieces, 'gx', 0, 0, axis_index_groups=same_core, tiled=True)  22.2 us
    ppermute x25, starting transfers between devices, permute(): lax.ppermute(block, 'gx', [(int(i), int(t)) for i, t in enumerate(target)])  19.6 us
    pallas_call x6, Pallas kernels, fetch(): pl.pallas_call(functools.partial(fetch_kernel, [first for _, first, _ in...  17.9 us
    ppermute x25, waiting for transfers between devices, permute(): lax.ppermute(block, 'gx', [(int(i), int(t)) for i, t in enumerate(target)])  7.3 us
    pallas_call x1, Pallas kernels, project(): pl.pallas_call(functools.partial(project_kernel, counts, crossed, width),...  4.1 us
    pallas_call x1, Pallas kernels, project_out(): pl.pallas_call(functools.partial(out_kernel, counts, crossed), out_shape=...  3.7 us
    pallas_call x1, Pallas kernels, attend(): pl.pallas_call(functools.partial(attend_kernel, devices, width // HD, til...  2.6 us
  transfers between devices with their start and end apart: 25, of which 7 were waited for; matrix products, arithmetic and copies ran while one was open for 0% of the time, Pallas kernels for 22%

profile of v2, /device:TPU:0, one launch (start us, length us, event | category | flops | bytes accessed | tf_op | source)
XLA Modules:
  0.0 81.0 jit_solution(14761391053629100261)
XLA Ops:
  0.0 1.4 %shard_map.82 = bf16[4,16512]{1,0:T(4,128)(2,1)S(1)} custom-call(s32[2]{0:T(128)} %lengths.1, bf16[2,2,16384]{2,1,0:T(2,128)(2,1)} %hidden_far.1, bf16[16384]{0:T(1024)(128)(2,1)} %gain_far.1), custom_call_target="tpu_custom_call" | custom-call | flops 393216 | bytes 262144 | tf_op jit(solution)/shard_map/pallas_call | solution.py:170
  1.5 3.1 %collective-permute-start.3 = (bf16[1,4,16512]{2,1,0:T(4,128)(2,1)S(1)}, bf16[1,4,16512]{2,1,0:T(4,128)(2,1)S(1)}, u32[]{:S(2)}, u32[]{:S(2)}) collective-permute-start(bf16[1,4,16512]{2,1,0:T(4,128)(2,1)S(1)} %bitcast.4), channel_id=1, source_target_pairs={{0,4},{1,5},{2,6},{3,7},{4,12},{5,13},{6,14},{7,15},{8,0},{9,1},{1... | collective-permute-start | bytes 396296 | tf_op jit(solution)/shard_map/ppermute | solution.py:23
  5.6 1.8 %collective-permute-start = (bf16[1,4,16512]{2,1,0:T(4,128)(2,1)S(1)}, bf16[1,4,16512]{2,1,0:T(4,128)(2,1)S(1)}, u32[]{:S(2)}, u32[]{:S(2)}) collective-permute-start(bf16[1,4,16512]{2,1,0:T(4,128)(2,1)S(1)} %bitcast.6), channel_id=1, source_target_pairs={{0,2},{1,3},{2,0},{3,1},{4,6},{5,7},{6,4},{7,5},{8,10},{9,11},{10,... | collective-permute-start | bytes 396296 | tf_op jit(solution)/shard_map/ppermute | solution.py:23
  7.4 4.7 %shard_map.83 = (bf16[12288,512]{1,0:T(8,128)(2,1)S(1)}, f32[8,128]{1,0:T(8,128)S(1)}) custom-call(bf16[16384,512]{1,0:T(8,128)(2,1)} %refs_0_.8, bf16[1,4,16512]{2,1,0:T(4,128)(2,1)S(1)} %bitcast.7), custom_call_target="tpu_custom_call" | custom-call | bytes 12582912 | tf_op jit(solution)/shard_map/pallas_call | solution.py:203
  12.2 1.7 %collective-permute-start.7 = (bf16[1,4,16512]{2,1,0:T(4,128)(2,1)S(1)}, bf16[1,4,16512]{2,1,0:T(4,128)(2,1)S(1)}, u32[]{:S(2)}, u32[]{:S(2)}) collective-permute-start(bf16[1,4,16512]{2,1,0:T(4,128)(2,1)S(1)} %get-tuple-element.30.refs_2_), channel_id=1, source_target_pairs={{0,8},{1,9},{2,10},{3,11},{4,0},{5,1},{6,2},{7,3},{8,12},{9,13},{1... | collective-permute-start | bytes 396296 | tf_op jit(solution)/shard_map/ppermute | solution.py:23
  13.9 1.3 %collective-permute-start.4 = (bf16[2,4,16512]{2,1,0:T(4,128)(2,1)S(1)}, bf16[2,4,16512]{2,1,0:T(4,128)(2,1)S(1)}, u32[]{:S(2)}, u32[]{:S(2)}) collective-permute-start(bf16[2,4,16512]{2,1,0:T(4,128)(2,1)S(1)} %get-tuple-element.29.refs_3_), channel_id=1, source_target_pairs={{0,2},{1,3},{2,0},{3,1},{4,6},{5,7},{6,4},{7,5},{8,10},{9,11},{10,... | collective-permute-start | bytes 792584 | tf_op jit(solution)/shard_map/ppermute | solution.py:23
  15.5 3.0 %shard_map.85 = (bf16[2,1024,512]{2,1,0:T(8,128)(2,1)S(1)}, bf16[2,2,1024,512]{3,2,1,0:T(8,128)(2,1)S(1)}, f32[8,128]{1,0:T(8,128)S(1)}) custom-call(bf16[2,1024,512]{2,1,0:T(8,128)(2,1)} %refs_0_.7, bf16[2,2,1024,512]{3,2,1,0:T(8,128)(2,1)} %refs_1_.1, bf16[1,4,16512]{2,1,0:T(4,128)(2,1)S(1)} %get-tuple-element.30.refs_2_), custom_call_target="tpu_custom_call" | custom-call | bytes 6291456 | tf_op jit(solution)/shard_map/pallas_call | solution.py:203
  19.6 1.3 %collective-permute-done.4.refs_4_ = bf16[2,4,16512]{2,1,0:T(4,128)(2,1)S(1)} collective-permute-done((bf16[2,4,16512]{2,1,0:T(4,128)(2,1)S(1)}, bf16[2,4,16512]{2,1,0:T(4,128)(2,1)S(1)}, u32[]{:S(2)}, u32[]{:S(2)}) %collective-permute-start.4) | collective-permute-done | bytes 264224 | tf_op jit(solution)/shard_map/ppermute | solution.py:23
  21.4 2.2 %shard_map.87 = (bf16[4096,512]{1,0:T(8,128)(2,1)S(1)}, f32[8,128]{1,0:T(8,128)S(1)}) custom-call(bf16[16384,512]{1,0:T(8,128)(2,1)} %refs_0_.8, bf16[1,4,16512]{2,1,0:T(4,128)(2,1)S(1)} %shard_map.86.refs_1_.refs_7_), custom_call_target="tpu_custom_call" | custom-call | bytes 4194304 | tf_op jit(solution)/shard_map/pallas_call | solution.py:203
  24.7 1.3 %collective-permute-done.10.refs_10_ = bf16[1,4,16512]{2,1,0:T(4,128)(2,1)S(1)} collective-permute-done((bf16[1,4,16512]{2,1,0:T(4,128)(2,1)S(1)}, bf16[1,4,16512]{2,1,0:T(4,128)(2,1)S(1)}, u32[]{:S(2)}, u32[]{:S(2)}) %collective-permute-start.10) | collective-permute-done | bytes 132128 | tf_op jit(solution)/shard_map/ppermute | solution.py:23
  26.0 4.1 %shard_map.89 = (bf16[8,16,128]{2,1,0:T(8,128)(2,1)S(1)}, bf16[8,16,128]{2,1,0:T(8,128)(2,1)S(1)}, f32[8,32,128]{2,1,0:T(8,128)S(1)}, f32[8,32,128]{2,1,0:T(8,128)S(1)}) custom-call(s32[16,32]{1,0:T(8,128)S(1)} %copy-done, bf16[1,4,16512]{2,1,0:T(4,128)(2,1)S(1)} %bitcast.9, bf16[1,4,16512]{2,1,0:T(4,128)(2,1)S(1)} %collective-permute-done.refs_1_, ...), custom_call_target="tpu_custom_call" | custom-call | flops 1073741824 | bytes 16777216 | tf_op jit(solution)/shard_map/pallas_call | solution.py:295
  31.6 12.2 %all_to_all.10.pieces = bf16[8,96,128]{2,1,0:T(8,128)(2,1)S(1)} all-to-all(bf16[8,96,128]{2,1,0:T(8,128)(2,1)S(1)} %shard_map.90), channel_id=1, replica_groups={{0,2,4,6,8,10,12,14},{1,3,5,7,9,11,13,15},{16,18,20,22,24,26,28,30},{17..., dimensions={0} | all-to-all | bytes 393216 | tf_op jit(solution)/shard_map/all_to_all | solution.py:133
  43.8 2.6 %shard_map.91 = bf16[4,8192]{1,0:T(4,128)(2,1)S(1)} custom-call(s32[2]{0:T(128)S(1)} %copy-done.1, s32[16,32]{1,0:T(8,128)S(1)} %copy-done, bf16[8,96,128]{2,1,0:T(8,128)(2,1)S(1)} %all_to_all.10.pieces, bf16[2,2,1024,512]{3,2,1,0:T(8,128)(2,1)S(1)} %get-tuple-element.40.cache), custom_call_target="tpu_custom_call" | custom-call | flops 536870912 | bytes 4194304 | tf_op jit(solution)/shard_map/pallas_call | solution.py:424
  46.6 2.7 %collective-permute-start.15 = (bf16[1,4,8192]{2,1,0:T(4,128)(2,1)S(1)}, bf16[1,4,8192]{2,1,0:T(4,128)(2,1)S(1)}, u32[]{:S(2)}, u32[]{:S(2)}) collective-permute-start(bf16[1,4,8192]{2,1,0:T(4,128)(2,1)S(1)} %bitcast.11), channel_id=1, source_target_pairs={{0,8},{1,9},{2,10},{3,11},{4,0},{5,1},{6,2},{7,3},{8,12},{9,13},{1... | collective-permute-start | bytes 196616 | tf_op jit(solution)/shard_map/ppermute | solution.py:23
  50.3 2.9 %shard_map.92 = (bf16[3072,1024]{1,0:T(8,128)(2,1)S(1)}, f32[8,128]{1,0:T(8,128)S(1)}) custom-call(bf16[8192,1024]{1,0:T(8,128)(2,1)} %refs_0_.11, bf16[1,4,8192]{2,1,0:T(4,128)(2,1)S(1)} %bitcast.13), custom_call_target="tpu_custom_call" | custom-call | bytes 6291456 | tf_op jit(solution)/shard_map/pallas_call | solution.py:203
  53.3 1.3 %collective-permute-start.20 = (bf16[1,4,8192]{2,1,0:T(4,128)(2,1)S(1)}, bf16[1,4,8192]{2,1,0:T(4,128)(2,1)S(1)}, u32[]{:S(2)}, u32[]{:S(2)}) collective-permute-start(bf16[1,4,8192]{2,1,0:T(4,128)(2,1)S(1)} %get-tuple-element.43.refs_1_), channel_id=1, source_target_pairs={{0,8},{1,9},{2,10},{3,11},{4,0},{5,1},{6,2},{7,3},{8,12},{9,13},{1... | collective-permute-start | bytes 196616 | tf_op jit(solution)/shard_map/ppermute | solution.py:23
  55.7 2.9 %shard_map.94 = (bf16[3072,1024]{1,0:T(8,128)(2,1)S(1)}, f32[8,128]{1,0:T(8,128)S(1)}) custom-call(bf16[8192,1024]{1,0:T(8,128)(2,1)} %refs_0_.11, bf16[1,4,8192]{2,1,0:T(4,128)(2,1)S(1)} %get-tuple-element.43.refs_1_), custom_call_target="tpu_custom_call" | custom-call | bytes 6291456 | tf_op jit(solution)/shard_map/pallas_call | solution.py:203
  58.7 1.1 %collective-permute-start.21 = (bf16[1,4,8192]{2,1,0:T(4,128)(2,1)S(1)}, bf16[1,4,8192]{2,1,0:T(4,128)(2,1)S(1)}, u32[]{:S(2)}, u32[]{:S(2)}) collective-permute-start(bf16[1,4,8192]{2,1,0:T(4,128)(2,1)S(1)} %shard_map.95.refs_1_.refs_7_), channel_id=1, source_target_pairs={{0,2},{1,3},{2,0},{3,1},{4,6},{5,7},{6,4},{7,5},{8,10},{9,11},{10,... | collective-permute-start | bytes 196616 | tf_op jit(solution)/shard_map/ppermute | solution.py:23
  60.5 2.2 %shard_map.96 = (bf16[2048,1024]{1,0:T(8,128)(2,1)S(1)}, f32[8,128]{1,0:T(8,128)S(1)}) custom-call(bf16[8192,1024]{1,0:T(8,128)(2,1)} %refs_0_.11, bf16[1,4,8192]{2,1,0:T(4,128)(2,1)S(1)} %shard_map.95.refs_1_.refs_7_), custom_call_target="tpu_custom_call" | custom-call | bytes 4194304 | tf_op jit(solution)/shard_map/pallas_call | solution.py:203
  63.2 1.2 %collective-permute-done.23.refs_10_ = bf16[1,4,8192]{2,1,0:T(4,128)(2,1)S(1)} collective-permute-done((bf16[1,4,8192]{2,1,0:T(4,128)(2,1)S(1)}, bf16[1,4,8192]{2,1,0:T(4,128)(2,1)S(1)}, u32[]{:S(2)}, u32[]{:S(2)}) %collective-permute-start.23) | collective-permute-done | bytes 65568 | tf_op jit(solution)/shard_map/ppermute | solution.py:23
  64.5 3.7 %shard_map.98 = (bf16[8,4,1024]{2,1,0:T(4,128)(2,1)S(1)}, bf16[8,4,1024]{2,1,0:T(4,128)(2,1)S(1)}) custom-call(s32[16,32]{1,0:T(8,128)S(1)} %copy-done, bf16[1,4,8192]{2,1,0:T(4,128)(2,1)S(1)} %bitcast.15, bf16[1,4,8192]{2,1,0:T(4,128)(2,1)S(1)} %collective-permute-done.13.refs_1_, bf16[2,4,8192]{2,1,0:T(4,128)(2,1)S(1)} %collective-permute-done.14.refs_2_, ...), custom_call_target="tpu_custom_call" | custom-call | flops 1073741824 | bytes 16777216 | tf_op jit(solution)/shard_map/pallas_call | solution.py:348
  68.4 1.1 %collective-permute-done.24 = bf16[8,4,1024]{2,1,0:T(4,128)(2,1)S(1)} collective-permute-done((bf16[8,4,1024]{2,1,0:T(4,128)(2,1)S(1)}, bf16[8,4,1024]{2,1,0:T(4,128)(2,1)S(1)}, u32[]{:S(2)}, u32[]{:S(2)}) %collective-permute-start.24) | collective-permute-done | bytes 65568 | tf_op jit(solution)/shard_map/ppermute | solution.py:23
  69.6 10.0 %all_to_all.11.pieces = bf16[8,2,4,1024]{3,2,1,0:T(4,128)(2,1)S(1)} all-to-all(bf16[8,2,4,1024]{3,2,1,0:T(4,128)(2,1)S(1)} %pad_maximum_fusion.2), channel_id=1, replica_groups={{0,2,4,6,8,10,12,14},{1,3,5,7,9,11,13,15},{16,18,20,22,24,26,28,30},{17..., dimensions={0} | all-to-all | bytes 262144 | tf_op jit(solution)/shard_map/all_to_all | solution.py:133
  79.6 1.4 %shard_map.99 = bf16[2,2,16384]{2,1,0:T(2,128)(2,1)} custom-call(s32[16,32]{1,0:T(8,128)S(1)} %copy-done, bf16[8,2,4,1024]{3,2,1,0:T(4,128)(2,1)S(1)} %all_to_all.11.pieces), custom_call_target="tpu_custom_call" | custom-call | tf_op jit(solution)/shard_map/pallas_call | solution.py:455
  (53 shorter events, 9.4 us)
Async XLA Ops:
  1.5 10.7 %collective-permute-start.3 = (bf16[1,4,16512]{2,1,0:T(4,128)(2,1)S(1)}, bf16[1,4,16512]{2,1,0:T(4,128)(2,1)S(1)}, u32[]{:S(2)}, u32[]{:S(2)}) collective-permute-start(bf16[1,4,16512]{2,1,0:T(4,128)(2,1)S(1)} %bitcast.4), channel_id=1, source_target_pairs={{0,4},{1,5},{2,6},{3,7},{4,12},{5,13},{6,14},{7,15},{8,0},{9,1},{1... | collective-permute-start | bytes 396296 | tf_op jit(solution)/shard_map/ppermute | solution.py:23
  4.5 7.6 %collective-permute-start.2 = (bf16[1,4,16512]{2,1,0:T(4,128)(2,1)S(1)}, bf16[1,4,16512]{2,1,0:T(4,128)(2,1)S(1)}, u32[]{:S(2)}, u32[]{:S(2)}) collective-permute-start(bf16[1,4,16512]{2,1,0:T(4,128)(2,1)S(1)} %bitcast.5), channel_id=1, source_target_pairs={{0,8},{1,9},{2,10},{3,11},{4,0},{5,1},{6,2},{7,3},{8,12},{9,13},{1... | collective-permute-start | bytes 396296 | tf_op jit(solution)/shard_map/ppermute | solution.py:23
  5.6 9.6 %collective-permute-start = (bf16[1,4,16512]{2,1,0:T(4,128)(2,1)S(1)}, bf16[1,4,16512]{2,1,0:T(4,128)(2,1)S(1)}, u32[]{:S(2)}, u32[]{:S(2)}) collective-permute-start(bf16[1,4,16512]{2,1,0:T(4,128)(2,1)S(1)} %bitcast.6), channel_id=1, source_target_pairs={{0,2},{1,3},{2,0},{3,1},{4,6},{5,7},{6,4},{7,5},{8,10},{9,11},{10,... | collective-permute-start | bytes 396296 | tf_op jit(solution)/shard_map/ppermute | solution.py:23
  12.2 6.4 %collective-permute-start.7 = (bf16[1,4,16512]{2,1,0:T(4,128)(2,1)S(1)}, bf16[1,4,16512]{2,1,0:T(4,128)(2,1)S(1)}, u32[]{:S(2)}, u32[]{:S(2)}) collective-permute-start(bf16[1,4,16512]{2,1,0:T(4,128)(2,1)S(1)} %get-tuple-element.30.refs_2_), channel_id=1, source_target_pairs={{0,8},{1,9},{2,10},{3,11},{4,0},{5,1},{6,2},{7,3},{8,12},{9,13},{1... | collective-permute-start | bytes 396296 | tf_op jit(solution)/shard_map/ppermute | solution.py:23
  13.9 7.0 %collective-permute-start.4 = (bf16[2,4,16512]{2,1,0:T(4,128)(2,1)S(1)}, bf16[2,4,16512]{2,1,0:T(4,128)(2,1)S(1)}, u32[]{:S(2)}, u32[]{:S(2)}) collective-permute-start(bf16[2,4,16512]{2,1,0:T(4,128)(2,1)S(1)} %get-tuple-element.29.refs_3_), channel_id=1, source_target_pairs={{0,2},{1,3},{2,0},{3,1},{4,6},{5,7},{6,4},{7,5},{8,10},{9,11},{10,... | collective-permute-start | bytes 792584 | tf_op jit(solution)/shard_map/ppermute | solution.py:23
  15.4 9.2 %collective-permute-start.1 = (bf16[2,4,16512]{2,1,0:T(4,128)(2,1)S(1)}, bf16[2,4,16512]{2,1,0:T(4,128)(2,1)S(1)}, u32[]{:S(2)}, u32[]{:S(2)}) collective-permute-start(bf16[2,4,16512]{2,1,0:T(4,128)(2,1)S(1)} %pad_maximum_fusion), channel_id=1, source_target_pairs={{0,1},{1,0},{2,3},{3,2},{4,5},{5,4},{6,7},{7,6},{8,9},{9,8},{10,11... | collective-permute-start | bytes 792584 | tf_op jit(solution)/shard_map/ppermute | solution.py:23
  18.6 6.0 %collective-permute-start.8 = (bf16[1,4,16512]{2,1,0:T(4,128)(2,1)S(1)}, bf16[1,4,16512]{2,1,0:T(4,128)(2,1)S(1)}, u32[]{:S(2)}, u32[]{:S(2)}) collective-permute-start(bf16[1,4,16512]{2,1,0:T(4,128)(2,1)S(1)} %shard_map.86.refs_1_.refs_7_), channel_id=1, source_target_pairs={{0,2},{1,3},{2,0},{3,1},{4,6},{5,7},{6,4},{7,5},{8,10},{9,11},{10,... | collective-permute-start | bytes 396296 | tf_op jit(solution)/shard_map/ppermute | solution.py:23
  19.3 5.3 %collective-permute-start.5 = (bf16[2,4,16512]{2,1,0:T(4,128)(2,1)S(1)}, bf16[2,4,16512]{2,1,0:T(4,128)(2,1)S(1)}, u32[]{:S(2)}, u32[]{:S(2)}) collective-permute-start(bf16[2,4,16512]{2,1,0:T(4,128)(2,1)S(1)} %get-tuple-element.29.refs_3_), channel_id=1, source_target_pairs={{0,1},{1,0},{2,3},{3,2},{4,5},{5,4},{6,7},{7,6},{8,9},{9,8},{10,11... | collective-permute-start | bytes 792584 | tf_op jit(solution)/shard_map/ppermute | solution.py:23
  20.9 5.1 %collective-permute-start.6 = (bf16[2,4,16512]{2,1,0:T(4,128)(2,1)S(1)}, bf16[2,4,16512]{2,1,0:T(4,128)(2,1)S(1)}, u32[]{:S(2)}, u32[]{:S(2)}) collective-permute-start(bf16[2,4,16512]{2,1,0:T(4,128)(2,1)S(1)} %collective-permute-done.4.refs_4_), channel_id=1, source_target_pairs={{0,1},{1,0},{2,3},{3,2},{4,5},{5,4},{6,7},{7,6},{8,9},{9,8},{10,11... | collective-permute-start | bytes 792584 | tf_op jit(solution)/shard_map/ppermute | solution.py:23
  20.9 3.8 %collective-permute-start.9 = (bf16[1,4,16512]{2,1,0:T(4,128)(2,1)S(1)}, bf16[1,4,16512]{2,1,0:T(4,128)(2,1)S(1)}, u32[]{:S(2)}, u32[]{:S(2)}) collective-permute-start(bf16[1,4,16512]{2,1,0:T(4,128)(2,1)S(1)} %shard_map.86.refs_1_.refs_7_), channel_id=1, source_target_pairs={{0,1},{1,0},{2,3},{3,2},{4,5},{5,4},{6,7},{7,6},{8,9},{9,8},{10,11... | collective-permute-start | bytes 396296 | tf_op jit(solution)/shard_map/ppermute | solution.py:23
  24.6 1.4 %collective-permute-start.10 = (bf16[1,4,16512]{2,1,0:T(4,128)(2,1)S(1)}, bf16[1,4,16512]{2,1,0:T(4,128)(2,1)S(1)}, u32[]{:S(2)}, u32[]{:S(2)}) collective-permute-start(bf16[1,4,16512]{2,1,0:T(4,128)(2,1)S(1)} %shard_map.88.refs_8_), channel_id=1, source_target_pairs={{0,1},{1,0},{2,3},{3,2},{4,5},{5,4},{6,7},{7,6},{8,9},{9,8},{10,11... | collective-permute-start | bytes 396296 | tf_op jit(solution)/shard_map/ppermute | solution.py:23
  30.1 1.5 %collective-permute-start.12 = (f32[8,32,128]{2,1,0:T(8,128)S(1)}, f32[8,32,128]{2,1,0:T(8,128)S(1)}, u32[]{:S(2)}, u32[]{:S(2)}) collective-permute-start(f32[8,32,128]{2,1,0:T(8,128)S(1)} %get-tuple-element.39), channel_id=1, source_target_pairs={{0,1},{1,0},{2,3},{3,2},{4,5},{5,4},{6,7},{7,6},{8,9},{9,8},{10,11... | collective-permute-start | bytes 393224 | tf_op jit(solution)/shard_map/ppermute | solution.py:23
  30.3 1.3 %collective-permute-start.11 = (bf16[8,16,128]{2,1,0:T(8,128)(2,1)S(1)}, bf16[8,16,128]{2,1,0:T(8,128)(2,1)S(1)}, u32[]{:S(2)}, u32[]{:S(2)}) collective-permute-start(bf16[8,16,128]{2,1,0:T(8,128)(2,1)S(1)} %get-tuple-element.37), channel_id=1, source_target_pairs={{0,1},{1,0},{2,3},{3,2},{4,5},{5,4},{6,7},{7,6},{8,9},{9,8},{10,11... | collective-permute-start | bytes 98312 | tf_op jit(solution)/shard_map/ppermute | solution.py:23
  46.4 6.8 %collective-permute-start.16 = (bf16[1,4,8192]{2,1,0:T(4,128)(2,1)S(1)}, bf16[1,4,8192]{2,1,0:T(4,128)(2,1)S(1)}, u32[]{:S(2)}, u32[]{:S(2)}) collective-permute-start(bf16[1,4,8192]{2,1,0:T(4,128)(2,1)S(1)} %bitcast.10), channel_id=1, source_target_pairs={{0,4},{1,5},{2,6},{3,7},{4,12},{5,13},{6,14},{7,15},{8,0},{9,1},{1... | collective-permute-start | bytes 196616 | tf_op jit(solution)/shard_map/ppermute | solution.py:23
  46.6 6.6 %collective-permute-start.15 = (bf16[1,4,8192]{2,1,0:T(4,128)(2,1)S(1)}, bf16[1,4,8192]{2,1,0:T(4,128)(2,1)S(1)}, u32[]{:S(2)}, u32[]{:S(2)}) collective-permute-start(bf16[1,4,8192]{2,1,0:T(4,128)(2,1)S(1)} %bitcast.11), channel_id=1, source_target_pairs={{0,8},{1,9},{2,10},{3,11},{4,0},{5,1},{6,2},{7,3},{8,12},{9,13},{1... | collective-permute-start | bytes 196616 | tf_op jit(solution)/shard_map/ppermute | solution.py:23
  49.4 6.2 %collective-permute-start.13 = (bf16[1,4,8192]{2,1,0:T(4,128)(2,1)S(1)}, bf16[1,4,8192]{2,1,0:T(4,128)(2,1)S(1)}, u32[]{:S(2)}, u32[]{:S(2)}) collective-permute-start(bf16[1,4,8192]{2,1,0:T(4,128)(2,1)S(1)} %bitcast.12), channel_id=1, source_target_pairs={{0,2},{1,3},{2,0},{3,1},{4,6},{5,7},{6,4},{7,5},{8,10},{9,11},{10,... | collective-permute-start | bytes 196616 | tf_op jit(solution)/shard_map/ppermute | solution.py:23
  53.3 5.4 %collective-permute-start.20 = (bf16[1,4,8192]{2,1,0:T(4,128)(2,1)S(1)}, bf16[1,4,8192]{2,1,0:T(4,128)(2,1)S(1)}, u32[]{:S(2)}, u32[]{:S(2)}) collective-permute-start(bf16[1,4,8192]{2,1,0:T(4,128)(2,1)S(1)} %get-tuple-element.43.refs_1_), channel_id=1, source_target_pairs={{0,8},{1,9},{2,10},{3,11},{4,0},{5,1},{6,2},{7,3},{8,12},{9,13},{1... | collective-permute-start | bytes 196616 | tf_op jit(solution)/shard_map/ppermute | solution.py:23
  54.6 5.4 %collective-permute-start.17 = (bf16[2,4,8192]{2,1,0:T(4,128)(2,1)S(1)}, bf16[2,4,8192]{2,1,0:T(4,128)(2,1)S(1)}, u32[]{:S(2)}, u32[]{:S(2)}) collective-permute-start(bf16[2,4,8192]{2,1,0:T(4,128)(2,1)S(1)} %get-tuple-element.42.refs_3_), channel_id=1, source_target_pairs={{0,2},{1,3},{2,0},{3,1},{4,6},{5,7},{6,4},{7,5},{8,10},{9,11},{10,... | collective-permute-start | bytes 393224 | tf_op jit(solution)/shard_map/ppermute | solution.py:23
  58.6 4.7 %collective-permute-start.14 = (bf16[2,4,8192]{2,1,0:T(4,128)(2,1)S(1)}, bf16[2,4,8192]{2,1,0:T(4,128)(2,1)S(1)}, u32[]{:S(2)}, u32[]{:S(2)}) collective-permute-start(bf16[2,4,8192]{2,1,0:T(4,128)(2,1)S(1)} %pad_maximum_fusion.1), channel_id=1, source_target_pairs={{0,1},{1,0},{2,3},{3,2},{4,5},{5,4},{6,7},{7,6},{8,9},{9,8},{10,11... | collective-permute-start | bytes 393224 | tf_op jit(solution)/shard_map/ppermute | solution.py:23
  58.7 4.5 %collective-permute-start.21 = (bf16[1,4,8192]{2,1,0:T(4,128)(2,1)S(1)}, bf16[1,4,8192]{2,1,0:T(4,128)(2,1)S(1)}, u32[]{:S(2)}, u32[]{:S(2)}) collective-permute-start(bf16[1,4,8192]{2,1,0:T(4,128)(2,1)S(1)} %shard_map.95.refs_1_.refs_7_), channel_id=1, source_target_pairs={{0,2},{1,3},{2,0},{3,1},{4,6},{5,7},{6,4},{7,5},{8,10},{9,11},{10,... | collective-permute-start | bytes 196616 | tf_op jit(solution)/shard_map/ppermute | solution.py:23
  59.8 3.5 %collective-permute-start.18 = (bf16[2,4,8192]{2,1,0:T(4,128)(2,1)S(1)}, bf16[2,4,8192]{2,1,0:T(4,128)(2,1)S(1)}, u32[]{:S(2)}, u32[]{:S(2)}) collective-permute-start(bf16[2,4,8192]{2,1,0:T(4,128)(2,1)S(1)} %get-tuple-element.42.refs_3_), channel_id=1, source_target_pairs={{0,1},{1,0},{2,3},{3,2},{4,5},{5,4},{6,7},{7,6},{8,9},{9,8},{10,11... | collective-permute-start | bytes 393224 | tf_op jit(solution)/shard_map/ppermute | solution.py:23
  60.0 4.5 %collective-permute-start.19 = (bf16[2,4,8192]{2,1,0:T(4,128)(2,1)S(1)}, bf16[2,4,8192]{2,1,0:T(4,128)(2,1)S(1)}, u32[]{:S(2)}, u32[]{:S(2)}) collective-permute-start(bf16[2,4,8192]{2,1,0:T(4,128)(2,1)S(1)} %collective-permute-done.17.refs_4_), channel_id=1, source_target_pairs={{0,1},{1,0},{2,3},{3,2},{4,5},{5,4},{6,7},{7,6},{8,9},{9,8},{10,11... | collective-permute-start | bytes 393224 | tf_op jit(solution)/shard_map/ppermute | solution.py:23
  60.3 3.0 %collective-permute-start.22 = (bf16[1,4,8192]{2,1,0:T(4,128)(2,1)S(1)}, bf16[1,4,8192]{2,1,0:T(4,128)(2,1)S(1)}, u32[]{:S(2)}, u32[]{:S(2)}) collective-permute-start(bf16[1,4,8192]{2,1,0:T(4,128)(2,1)S(1)} %shard_map.95.refs_1_.refs_7_), channel_id=1, source_target_pairs={{0,1},{1,0},{2,3},{3,2},{4,5},{5,4},{6,7},{7,6},{8,9},{9,8},{10,11... | collective-permute-start | bytes 196616 | tf_op jit(solution)/shard_map/ppermute | solution.py:23
  68.2 1.3 %collective-permute-start.24 = (bf16[8,4,1024]{2,1,0:T(4,128)(2,1)S(1)}, bf16[8,4,1024]{2,1,0:T(4,128)(2,1)S(1)}, u32[]{:S(2)}, u32[]{:S(2)}) collective-permute-start(bf16[8,4,1024]{2,1,0:T(4,128)(2,1)S(1)} %get-tuple-element.50), channel_id=1, source_target_pairs={{0,1},{1,0},{2,3},{3,2},{4,5},{5,4},{6,7},{7,6},{8,9},{9,8},{10,11... | collective-permute-start | bytes 196616 | tf_op jit(solution)/shard_map/ppermute | solution.py:23
  (3 other events, 26.5 us)

commit v3 on v2

--- a/solution.py
+++ b/solution.py
@@ -128,16 +128,18 @@
     return permute(block, np.arange(devices) ^ 1)
 
 
-def exchange(pieces, devices):
-    same_core = [list(range(core, devices, 2)) for core in range(2)]
-    return lax.all_to_all(pieces, "gx", 0, 0, axis_index_groups=same_core, tiled=True)
+def origins(groups):
+    return [source for group in groups if not group.crossed for source in group.sources]
+
+
+def give_back(pieces, groups):
+    return [pieces[0]] + [permute(piece, origin) for piece, origin in zip(pieces[1:], origins(groups)[1:])]
 
 
 def places(groups, devices):
     here = np.arange(devices)
-    chips = [source // 2 for group in groups for source in group.sources]
-    columns = [chip * 2 + (here % 2 ^ other) for chip in range(devices // 2) for other in range(2)]
-    return np.stack(chips + columns, 1).astype(np.int32)
+    senders = [moved(here, origin) for origin in origins(groups)]
+    return np.stack([sender ^ other for sender in senders for other in range(2)], 1).astype(np.int32)
 
 
 def norm_kernel(lengths_far, hidden_far, gain_far, out, lengths, hidden, gain, arrived):
@@ -248,7 +250,7 @@
     return values * cosine + swapped * sine
 
 
-def project_kernel(counts, crossed, width, place, *refs):
+def project_kernel(counts, crossed, width, *refs):
     slots = slots_of(refs, counts)
     first, second, keyval, *outs = refs[len(counts) : len(counts) + 7]
     kept, total, packed = refs[len(counts) + 7 :]
@@ -257,15 +259,14 @@
     tags = jnp.concatenate([ref[at, :, width:].astype(jnp.float32) for ref, at in slots], 0)
     cosine, sine = turns(tags[:, 0:1] * 32.0 + tags[:, 1:2])
     multiply(slots, [first, second], depth, total, kept)
-    me = lax.axis_index("gx")
-    own = kept[me]
+    own = kept[lax.axis_index("gx")]
     blocks = keyval.shape[2] // HD
     for which in range(2):
         term = jnp.dot(own, keyval[which], preferred_element_type=jnp.float32)
         for slot in range(len(slots)):
             for at in range(blocks):
                 row = (which * blocks + at) * 4
-                fresh[crossed[slot]][place[me, slot], row : row + 4, :] = term[
+                fresh[crossed[slot][0]][crossed[slot][1], row : row + 4, :] = term[
                     slot * 4 : slot * 4 + 4, at * HD : (at + 1) * HD
                 ]
     heads = total.shape[1] // HD
@@ -276,15 +277,20 @@
                 line, at = row * 2 * heads + head * 2, slot * 4 + row * 2
                 packed[slot, line : line + 2, :] = turned[at : at + 2, :]
     for slot in range(len(slots)):
-        queries[crossed[slot]][place[me, slot]] = packed[slot].astype(jnp.bfloat16)
+        queries[crossed[slot][0]][crossed[slot][1]] = packed[slot].astype(jnp.bfloat16)
 
 
 def group_shape(groups):
     counts = [len(group.sources) for group in groups]
-    return counts, [int(group.crossed) for group, count in zip(groups, counts) for _ in range(count)]
-
-
-def project(groups, w_query, w_keyval, place, devices):
+    seen, order = [0, 0], []
+    for group, count in zip(groups, counts):
+        for _ in range(count):
+            order.append((int(group.crossed), seen[group.crossed]))
+            seen[group.crossed] += 1
+    return counts, order
+
+
+def project(groups, w_query, w_keyval, devices):
     counts, crossed = group_shape(groups)
     columns = w_query[0].shape[1]
     depth, kv_width = w_keyval.shape[1:]
@@ -295,7 +301,7 @@
     return pl.pallas_call(
         functools.partial(project_kernel, counts, crossed, width),
         out_shape=[query, query, fresh, fresh],
-        in_specs=[SMEM] + [VMEM] * (len(groups) + 3),
+        in_specs=[VMEM] * (len(groups) + 3),
         out_specs=[VMEM] * 4,
         scratch_shapes=[
             pltpu.VMEM((devices, rows, depth), jnp.bfloat16),
@@ -306,40 +312,59 @@
         cost_estimate=pl.CostEstimate(
             flops=2 * rows * columns * width, bytes_accessed=2 * columns * width, transcendentals=2 * rows * HD
         ),
-    )(place, *[group.blocks for group in groups], *w_query, w_keyval)
-
-
-def pack_kernel(near, far, near_sum, far_sum, out):
+    )(*[group.blocks for group in groups], *w_query, w_keyval)
+
+
+def pack_kernel(near, far, near_sum, far_sum, *outs):
     tile, lines = near.shape[1], near_sum.shape[1]
-    out[:, :tile, :] = near[...]
-    out[:, tile : 2 * tile, :] = far[...]
-    total = near_sum[...] + far_sum[...]
-    high = total.astype(jnp.bfloat16)
-    out[:, 2 * tile : 2 * tile + lines, :] = high
-    out[:, 2 * tile + lines :, :] = (total - high.astype(jnp.float32)).astype(jnp.bfloat16)
+    for chip, out in enumerate(outs):
+        out[:tile, :] = near[chip]
+        out[tile : 2 * tile, :] = far[chip]
+        total = near_sum[chip] + far_sum[chip]
+        high = total.astype(jnp.bfloat16)
+        out[2 * tile : 2 * tile + lines, :] = high
+        out[2 * tile + lines :, :] = (total - high.astype(jnp.float32)).astype(jnp.bfloat16)
 
 
 def pack(near, far, near_sum, far_sum):
     chips, tile, _ = near.shape
+    piece = jax.ShapeDtypeStruct((2 * tile + 2 * near_sum.shape[1], HD), jnp.bfloat16)
     return pl.pallas_call(
         pack_kernel,
-        out_shape=jax.ShapeDtypeStruct((chips, 2 * tile + 2 * near_sum.shape[1], HD), jnp.bfloat16),
+        out_shape=[piece] * chips,
         in_specs=[VMEM] * 4,
-        out_specs=VMEM,
+        out_specs=[VMEM] * chips,
         compiler_params=pltpu.CompilerParams(vmem_limit_bytes=VMEM_LIMIT),
     )(near, far, near_sum, far_sum)
 
 
-def out_kernel(counts, crossed, place, *refs):
+def pair_kernel(near, far, *outs):
+    for chip, out in enumerate(outs):
+        out[0] = near[chip]
+        out[1] = far[chip]
+
+
+def pair(near, far):
+    chips = near.shape[0]
+    return pl.pallas_call(
+        pair_kernel,
+        out_shape=[jax.ShapeDtypeStruct((2, *near.shape[1:]), near.dtype)] * chips,
+        in_specs=[VMEM] * 2,
+        out_specs=[VMEM] * chips,
+        compiler_params=pltpu.CompilerParams(vmem_limit_bytes=VMEM_LIMIT),
+    )(near, far)
+
+
+def out_kernel(counts, crossed, *refs):
     slots = slots_of(refs, counts)
     *weights, near, far, kept, total = refs[len(counts) :]
     multiply(slots, weights, kept.shape[2], total, kept)
-    own, me = near.shape[1], lax.axis_index("gx")
+    own = near.shape[1]
     for slot in range(len(slots)):
-        (near, far)[crossed[slot]][place[me, slot]] = total[slot * own : (slot + 1) * own].astype(near.dtype)
-
-
-def project_out(groups, w_out, place, devices):
+        (near, far)[crossed[slot][0]][crossed[slot][1]] = total[slot * own : (slot + 1) * own].astype(near.dtype)
+
+
+def project_out(groups, w_out, devices):
     counts, crossed = group_shape(groups)
     columns = w_out[0].shape[1]
     own, width = groups[0].blocks.shape[1:]
@@ -348,7 +373,7 @@
     return pl.pallas_call(
         functools.partial(out_kernel, counts, crossed),
         out_shape=[piece, piece],
-        in_specs=[SMEM] + [VMEM] * (len(groups) + len(w_out)),
+        in_specs=[VMEM] * (len(groups) + len(w_out)),
         out_specs=[VMEM, VMEM],
         scratch_shapes=[
             pltpu.VMEM((chunks, devices * own, width // chunks), jnp.bfloat16),
@@ -358,10 +383,11 @@
         cost_estimate=pl.CostEstimate(
             flops=2 * devices * own * columns * width, bytes_accessed=2 * columns * width, transcendentals=0
         ),
-    )(place, *[group.blocks for group in groups], *w_out)
-
-
-def attend_kernel(devices, kv_heads, tile, lengths, place, pieces, cache, out, fresh, queries, mixed):
+    )(*[group.blocks for group in groups], *w_out)
+
+
+def attend_kernel(devices, kv_heads, tile, lengths, place, cache, *refs):
+    pieces, (out, fresh, queries, mixed) = refs[:-4], refs[-4:]
     length, width = cache.shape[2:]
     extra = fresh.shape[2]
     half = tile // 2
@@ -369,13 +395,14 @@
     scale = 1.0 / math.sqrt(HD)
     for chip in range(devices // 2):
         for other in range(2):
-            piece = pieces[chip, other * tile : (other + 1) * tile, :]
-            queries[place[lax.axis_index("gx"), devices + 2 * chip + other]] = piece.astype(jnp.float32)
+            piece = pieces[chip][other * tile : (other + 1) * tile, :]
+            queries[place[lax.axis_index("gx"), 2 * chip + other]] = piece.astype(jnp.float32)
     line = lax.broadcasted_iota(jnp.int32, (8, 1), 0)
     first = jnp.where(line % 4 < 2, lengths[0], lengths[1])
     cosine, sine = turns((first + line % 2).astype(jnp.float32))
-    terms = pieces[:, 2 * tile :, :].astype(jnp.float32)
-    total = jnp.sum(terms, 0)
+    total = pieces[0][2 * tile :, :].astype(jnp.float32)
+    for piece in pieces[1:]:
+        total += piece[2 * tile :, :].astype(jnp.float32)
     total = total[: total.shape[0] // 2] + total[total.shape[0] // 2 :]
     twice = [jnp.concatenate([total[4 * at : 4 * at + 4]] * 2, 0) for at in range(2 * kv_heads)]
     new_keys = jnp.concatenate([turn(part, cosine, sine) for part in twice[:kv_heads]], 1)
@@ -424,7 +451,7 @@
     return pl.pallas_call(
         functools.partial(attend_kernel, devices, width // HD, tile),
         out_shape=jax.ShapeDtypeStruct((4, columns), jnp.bfloat16),
-        in_specs=[SMEM, SMEM, VMEM, VMEM],
+        in_specs=[SMEM, SMEM] + [VMEM] * (len(pieces) + 1),
         out_specs=VMEM,
         scratch_shapes=[
             pltpu.VMEM((2, 2, HD, width), cache.dtype),
@@ -435,30 +462,31 @@
         cost_estimate=pl.CostEstimate(
             flops=8 * 128 * length * width, bytes_accessed=8 * length * width, transcendentals=256 * length
         ),
-    )(lengths, place, pieces, cache)
-
-
-def finish_kernel(devices, place, pieces, out):
-    columns = pieces.shape[3]
+    )(lengths, place, cache, *pieces)
+
+
+def finish_kernel(devices, place, *refs):
+    *pieces, out = refs
+    columns = pieces[0].shape[2]
     steps, rows = out.shape[:2]
     for chip in range(devices // 2):
         for other in range(2):
-            source = place[lax.axis_index("gx"), devices + 2 * chip + other]
+            source = place[lax.axis_index("gx"), 2 * chip + other]
             lanes = pl.ds(pl.multiple_of(source * columns, columns), columns)
-            piece = pieces[chip, other].astype(jnp.float32)
+            piece = pieces[chip][other].astype(jnp.float32)
             for step in range(steps):
                 out[step, :, lanes] = piece[step * rows : (step + 1) * rows].astype(out.dtype)
 
 
 def finish(pieces, place, steps, devices):
-    own, columns = pieces.shape[2:]
+    own, columns = pieces[0].shape[1:]
     return pl.pallas_call(
         functools.partial(finish_kernel, devices),
         out_shape=jax.ShapeDtypeStruct((steps, own // steps, devices * columns), jnp.bfloat16),
-        in_specs=[SMEM, VMEM],
+        in_specs=[SMEM] + [VMEM] * len(pieces),
         out_specs=VMEM,
         compiler_params=pltpu.CompilerParams(vmem_limit_bytes=VMEM_LIMIT),
-    )(place, pieces)
+    )(place, *pieces)
 
 
 def body(hidden, norm_gain, w_query, w_keyval, w_out, kv_cache, lengths):
@@ -481,17 +509,17 @@
     groups = gather(normed, devices, waits)
     w_first, w_keyval, kv_cache, w_second = fetched
     place = jnp.asarray(places(groups, devices))
-    near, far, near_sum, far_sum = project(groups, [w_first, w_second], w_keyval, place, devices)
+    near, far, near_sum, far_sum = project(groups, [w_first, w_second], w_keyval, devices)
     pieces = pack(near, swap_cores(far, devices), near_sum, swap_cores(far_sum, devices))
 
-    mixed = attend(exchange(pieces, devices), near.shape[1], kv_cache, lengths, place, devices)
+    mixed = attend(give_back(pieces, groups), near.shape[1], kv_cache, lengths, place, devices)
     fetched = []
     part = w_out.shape[0] // 8
     waits = [bring((w_out, first * part, count * part)) for first, count in ((0, 3), (3, 3), (6, 2))]
     groups = gather(mixed, devices, waits)
-    near, far = project_out(groups, fetched, place, devices)
-    pieces = jnp.stack([near, swap_cores(far, devices)], 1)
-    return finish(exchange(pieces, devices), place, steps, devices)
+    near, far = project_out(groups, fetched, devices)
+    pieces = pair(near, swap_cores(far, devices))
+    return finish(give_back(pieces, groups), place, steps, devices)
 
 
 def rotate(values, positions):

time: 81.2 us -> 90 us (1.11)
  starting transfers between devices: 19.6 us -> 44.2 us
  blocking collectives: 22.2 us -> 0 us
  waiting for transfers between devices: 7.3 us -> 15.3 us
  Pallas kernels: 31.2 us -> 29.8 us
    ppermute x25 -> x39, starting transfers between devices: 19.6 us -> 44.2 us  [permute(): lax.ppermute(block, 'gx', [(int(i), int(t)) for i, t in enumerate(target)])]
    all_to_all x2 -> x0, blocking collectives: 22.2 us -> none  [exchange(): lax.all_to_all(pieces, 'gx', 0, 0, axis_index_groups=same_core, tiled=True)]
    ppermute x25 -> x39, waiting for transfers between devices: 7.3 us -> 15.3 us  [permute(): lax.ppermute(block, 'gx', [(int(i), int(t)) for i, t in enumerate(target)])]
  transfers between devices with their start and end apart: 25 -> 39, of which waited for: 7 -> 11; matrix products, arithmetic and copies ran while one was open for 0% -> 0% of each run, Pallas kernels for 22% -> 20%
where the time goes in v3:
time: 90 us; the launch traced here: 89.9 us
  starting transfers between devices  44.2 us (49%)
  Pallas kernels  29.8 us (33%)
  waiting for transfers between devices  15.3 us (17%)
    ppermute x39, starting transfers between devices, permute(): lax.ppermute(block, 'gx', [(int(i), int(t)) for i, t in enumerate(target)])  44.2 us
    pallas_call x6, Pallas kernels, fetch(): pl.pallas_call(functools.partial(fetch_kernel, [first for _, first, _ in...  17.9 us
    ppermute x39, waiting for transfers between devices, permute(): lax.ppermute(block, 'gx', [(int(i), int(t)) for i, t in enumerate(target)])  15.3 us
    pallas_call x1, Pallas kernels, project(): pl.pallas_call(functools.partial(project_kernel, counts, crossed, width),...  3.39 us
    pallas_call x1, Pallas kernels, project_out(): pl.pallas_call(functools.partial(out_kernel, counts, crossed), out_shape=...  3.04 us
    pallas_call x1, Pallas kernels, attend(): pl.pallas_call(functools.partial(attend_kernel, devices, width // HD, til...  2.59 us
  transfers between devices with their start and end apart: 39, of which 11 were waited for; matrix products, arithmetic and copies ran while one was open for 0% of the time, Pallas kernels for 20%

profile of v3, /device:TPU:0, one launch (start us, length us, event | category | flops | bytes accessed | tf_op | source)
XLA Modules:
  0.0 89.9 jit_solution(12298836193560870143)
XLA Ops:
  0.0 1.4 %shard_map.82 = bf16[4,16512]{1,0:T(4,128)(2,1)S(1)} custom-call(s32[2]{0:T(128)} %lengths.1, bf16[2,2,16384]{2,1,0:T(2,128)(2,1)} %hidden_far.1, bf16[16384]{0:T(1024)(128)(2,1)} %gain_far.1), custom_call_target="tpu_custom_call" | custom-call | flops 393216 | bytes 262144 | tf_op jit(solution)/shard_map/pallas_call | solution.py:172
  1.5 3.1 %collective-permute-start.1 = (bf16[1,4,16512]{2,1,0:T(4,128)(2,1)S(1)}, bf16[1,4,16512]{2,1,0:T(4,128)(2,1)S(1)}, u32[]{:S(2)}, u32[]{:S(2)}) collective-permute-start(bf16[1,4,16512]{2,1,0:T(4,128)(2,1)S(1)} %bitcast.2), channel_id=1, source_target_pairs={{0,4},{1,5},{2,6},{3,7},{4,12},{5,13},{6,14},{7,15},{8,0},{9,1},{1... | collective-permute-start | bytes 396296 | tf_op jit(solution)/shard_map/ppermute | solution.py:23
  5.6 1.8 %collective-permute-start.2 = (bf16[1,4,16512]{2,1,0:T(4,128)(2,1)S(1)}, bf16[1,4,16512]{2,1,0:T(4,128)(2,1)S(1)}, u32[]{:S(2)}, u32[]{:S(2)}) collective-permute-start(bf16[1,4,16512]{2,1,0:T(4,128)(2,1)S(1)} %bitcast.4), channel_id=1, source_target_pairs={{0,2},{1,3},{2,0},{3,1},{4,6},{5,7},{6,4},{7,5},{8,10},{9,11},{10,... | collective-permute-start | bytes 396296 | tf_op jit(solution)/shard_map/ppermute | solution.py:23
  7.4 4.7 %shard_map.83 = (bf16[12288,512]{1,0:T(8,128)(2,1)S(1)}, f32[8,128]{1,0:T(8,128)S(1)}) custom-call(bf16[16384,512]{1,0:T(8,128)(2,1)} %refs_0_.8, bf16[1,4,16512]{2,1,0:T(4,128)(2,1)S(1)} %bitcast.5), custom_call_target="tpu_custom_call" | custom-call | bytes 12582912 | tf_op jit(solution)/shard_map/pallas_call | solution.py:205
  12.2 1.7 %collective-permute-start.7 = (bf16[1,4,16512]{2,1,0:T(4,128)(2,1)S(1)}, bf16[1,4,16512]{2,1,0:T(4,128)(2,1)S(1)}, u32[]{:S(2)}, u32[]{:S(2)}) collective-permute-start(bf16[1,4,16512]{2,1,0:T(4,128)(2,1)S(1)} %get-tuple-element.45.refs_2_), channel_id=1, source_target_pairs={{0,8},{1,9},{2,10},{3,11},{4,0},{5,1},{6,2},{7,3},{8,12},{9,13},{1... | collective-permute-start | bytes 396296 | tf_op jit(solution)/shard_map/ppermute | solution.py:23
  15.5 3.0 %shard_map.85 = (bf16[2,1024,512]{2,1,0:T(8,128)(2,1)S(1)}, bf16[2,2,1024,512]{3,2,1,0:T(8,128)(2,1)S(1)}, f32[8,128]{1,0:T(8,128)S(1)}) custom-call(bf16[2,1024,512]{2,1,0:T(8,128)(2,1)} %refs_0_.7, bf16[2,2,1024,512]{3,2,1,0:T(8,128)(2,1)} %refs_1_.1, bf16[1,4,16512]{2,1,0:T(4,128)(2,1)S(1)} %get-tuple-element.45.refs_2_), custom_call_target="tpu_custom_call" | custom-call | bytes 6291456 | tf_op jit(solution)/shard_map/pallas_call | solution.py:205
  21.4 2.2 %shard_map.87 = (bf16[4096,512]{1,0:T(8,128)(2,1)S(1)}, f32[8,128]{1,0:T(8,128)S(1)}) custom-call(bf16[16384,512]{1,0:T(8,128)(2,1)} %refs_0_.8, bf16[1,4,16512]{2,1,0:T(4,128)(2,1)S(1)} %shard_map.86.refs_1_.refs_7_), custom_call_target="tpu_custom_call" | custom-call | bytes 4194304 | tf_op jit(solution)/shard_map/pallas_call | solution.py:205
  26.0 3.4 %shard_map.89 = (bf16[8,16,128]{2,1,0:T(8,128)(2,1)S(1)}, bf16[8,16,128]{2,1,0:T(8,128)(2,1)S(1)}, f32[8,32,128]{2,1,0:T(8,128)S(1)}, f32[8,32,128]{2,1,0:T(8,128)S(1)}) custom-call(bf16[1,4,16512]{2,1,0:T(4,128)(2,1)S(1)} %bitcast.7, bf16[1,4,16512]{2,1,0:T(4,128)(2,1)S(1)} %collective-permute-done.2.refs_1_, ...), custom_call_target="tpu_custom_call" | custom-call | flops 1073741824 | bytes 16777216 | tf_op jit(solution)/shard_map/pallas_call | solution.py:301
  31.6 1.8 %collective-permute-start.14 = (bf16[96,128]{1,0:T(8,128)(2,1)S(1)}, bf16[96,128]{1,0:T(8,128)(2,1)S(1)}, u32[]{:S(2)}, u32[]{:S(2)}) collective-permute-start(bf16[96,128]{1,0:T(8,128)(2,1)S(1)} %get-tuple-element.59), channel_id=1, source_target_pairs={{0,4},{1,5},{2,6},{3,7},{4,12},{5,13},{6,14},{7,15},{8,0},{9,1},{1... | collective-permute-start | bytes 73736 | tf_op jit(solution)/shard_map/ppermute | solution.py:23
  35.3 3.1 %collective-permute-start.17 = (bf16[96,128]{1,0:T(8,128)(2,1)S(1)}, bf16[96,128]{1,0:T(8,128)(2,1)S(1)}, u32[]{:S(2)}, u32[]{:S(2)}) collective-permute-start(bf16[96,128]{1,0:T(8,128)(2,1)S(1)} %get-tuple-element.62), channel_id=1, source_target_pairs={{0,10},{1,11},{2,8},{3,9},{4,2},{5,3},{6,0},{7,1},{8,14},{9,15},{1... | collective-permute-start | bytes 73736 | tf_op jit(solution)/shard_map/ppermute | solution.py:23
  38.4 2.5 %collective-permute-start.18 = (bf16[96,128]{1,0:T(8,128)(2,1)S(1)}, bf16[96,128]{1,0:T(8,128)(2,1)S(1)}, u32[]{:S(2)}, u32[]{:S(2)}) collective-permute-start(bf16[96,128]{1,0:T(8,128)(2,1)S(1)} %get-tuple-element.63), channel_id=1, source_target_pairs={{0,12},{1,13},{2,14},{3,15},{4,8},{5,9},{6,10},{7,11},{8,4},{9,5},... | collective-permute-start | bytes 73736 | tf_op jit(solution)/shard_map/ppermute | solution.py:23
  40.9 2.0 %collective-permute-start.19 = (bf16[96,128]{1,0:T(8,128)(2,1)S(1)}, bf16[96,128]{1,0:T(8,128)(2,1)S(1)}, u32[]{:S(2)}, u32[]{:S(2)}) collective-permute-start(bf16[96,128]{1,0:T(8,128)(2,1)S(1)} %get-tuple-element.64), channel_id=1, source_target_pairs={{0,14},{1,15},{2,12},{3,13},{4,10},{5,11},{6,8},{7,9},{8,6},{9,7},... | collective-permute-start | bytes 73736 | tf_op jit(solution)/shard_map/ppermute | solution.py:23
  44.0 3.4 %collective-permute-done.19.refs_7_ = bf16[96,128]{1,0:T(8,128)(2,1)S(1)} collective-permute-done((bf16[96,128]{1,0:T(8,128)(2,1)S(1)}, bf16[96,128]{1,0:T(8,128)(2,1)S(1)}, u32[]{:S(2)}, u32[]{:S(2)}) %collective-permute-start.19) | collective-permute-done | bytes 24608 | tf_op jit(solution)/shard_map/ppermute | solution.py:23
  47.5 2.6 %shard_map.91 = bf16[4,8192]{1,0:T(4,128)(2,1)S(1)} custom-call(s32[2]{0:T(128)S(1)} %copy-done.1, s32[16,16]{1,0:T(8,128)S(1)} %copy-done, bf16[2,2,1024,512]{3,2,1,0:T(8,128)(2,1)S(1)} %get-tuple-element.46.cache, bf16[96,128]{1,0:T(8,128)(2,1)S(1)} %get-tuple-element.57.refs_0_, bf16[96,128]{1,0:T(8,128)(2,1)S(1)} %collective-permute-done.13.refs_1_, ...), custom_call_target="tpu_custom_call" | custom-call | flops 536870912 | bytes 4194304 | tf_op jit(solution)/shard_map/pallas_call | solution.py:451
  50.1 2.9 %collective-permute-start.22 = (bf16[1,4,8192]{2,1,0:T(4,128)(2,1)S(1)}, bf16[1,4,8192]{2,1,0:T(4,128)(2,1)S(1)}, u32[]{:S(2)}, u32[]{:S(2)}) collective-permute-start(bf16[1,4,8192]{2,1,0:T(4,128)(2,1)S(1)} %bitcast.9), channel_id=1, source_target_pairs={{0,8},{1,9},{2,10},{3,11},{4,0},{5,1},{6,2},{7,3},{8,12},{9,13},{1... | collective-permute-start | bytes 196616 | tf_op jit(solution)/shard_map/ppermute | solution.py:23
  54.2 2.9 %shard_map.92 = (bf16[3072,1024]{1,0:T(8,128)(2,1)S(1)}, f32[8,128]{1,0:T(8,128)S(1)}) custom-call(bf16[8192,1024]{1,0:T(8,128)(2,1)} %refs_0_.11, bf16[1,4,8192]{2,1,0:T(4,128)(2,1)S(1)} %bitcast.11), custom_call_target="tpu_custom_call" | custom-call | bytes 6291456 | tf_op jit(solution)/shard_map/pallas_call | solution.py:205
  57.1 1.5 %collective-permute-start.27 = (bf16[1,4,8192]{2,1,0:T(4,128)(2,1)S(1)}, bf16[1,4,8192]{2,1,0:T(4,128)(2,1)S(1)}, u32[]{:S(2)}, u32[]{:S(2)}) collective-permute-start(bf16[1,4,8192]{2,1,0:T(4,128)(2,1)S(1)} %get-tuple-element.67.refs_1_), channel_id=1, source_target_pairs={{0,8},{1,9},{2,10},{3,11},{4,0},{5,1},{6,2},{7,3},{8,12},{9,13},{1... | collective-permute-start | bytes 196616 | tf_op jit(solution)/shard_map/ppermute | solution.py:23
  59.9 2.9 %shard_map.94 = (bf16[3072,1024]{1,0:T(8,128)(2,1)S(1)}, f32[8,128]{1,0:T(8,128)S(1)}) custom-call(bf16[8192,1024]{1,0:T(8,128)(2,1)} %refs_0_.11, bf16[1,4,8192]{2,1,0:T(4,128)(2,1)S(1)} %get-tuple-element.67.refs_1_), custom_call_target="tpu_custom_call" | custom-call | bytes 6291456 | tf_op jit(solution)/shard_map/pallas_call | solution.py:205
  64.5 2.2 %shard_map.96 = (bf16[2048,1024]{1,0:T(8,128)(2,1)S(1)}, f32[8,128]{1,0:T(8,128)S(1)}) custom-call(bf16[8192,1024]{1,0:T(8,128)(2,1)} %refs_0_.11, bf16[1,4,8192]{2,1,0:T(4,128)(2,1)S(1)} %shard_map.95.refs_1_.refs_7_), custom_call_target="tpu_custom_call" | custom-call | bytes 4194304 | tf_op jit(solution)/shard_map/pallas_call | solution.py:205
  68.7 3.0 %shard_map.98 = (bf16[8,4,1024]{2,1,0:T(4,128)(2,1)S(1)}, bf16[8,4,1024]{2,1,0:T(4,128)(2,1)S(1)}) custom-call(bf16[1,4,8192]{2,1,0:T(4,128)(2,1)S(1)} %bitcast.13, bf16[1,4,8192]{2,1,0:T(4,128)(2,1)S(1)} %collective-permute-done.20.refs_1_, bf16[2,4,8192]{2,1,0:T(4,128)(2,1)S(1)} %collective-permute-done.21.refs_2_, ...), custom_call_target="tpu_custom_call" | custom-call | flops 1073741824 | bytes 16777216 | tf_op jit(solution)/shard_map/pallas_call | solution.py:373
  74.5 2.4 %collective-permute-start.34 = (bf16[2,4,1024]{2,1,0:T(4,128)(2,1)S(1)}, bf16[2,4,1024]{2,1,0:T(4,128)(2,1)S(1)}, u32[]{:S(2)}, u32[]{:S(2)}) collective-permute-start(bf16[2,4,1024]{2,1,0:T(4,128)(2,1)S(1)} %get-tuple-element.78), channel_id=1, source_target_pairs={{0,8},{1,9},{2,10},{3,11},{4,0},{5,1},{6,2},{7,3},{8,12},{9,13},{1... | collective-permute-start | bytes 49160 | tf_op jit(solution)/shard_map/ppermute | solution.py:23
  76.9 3.8 %collective-permute-start.36 = (bf16[2,4,1024]{2,1,0:T(4,128)(2,1)S(1)}, bf16[2,4,1024]{2,1,0:T(4,128)(2,1)S(1)}, u32[]{:S(2)}, u32[]{:S(2)}) collective-permute-start(bf16[2,4,1024]{2,1,0:T(4,128)(2,1)S(1)} %get-tuple-element.80), channel_id=1, source_target_pairs={{0,10},{1,11},{2,8},{3,9},{4,2},{5,3},{6,0},{7,1},{8,14},{9,15},{1... | collective-permute-start | bytes 49160 | tf_op jit(solution)/shard_map/ppermute | solution.py:23
  82.0 3.1 %collective-permute-start.38 = (bf16[2,4,1024]{2,1,0:T(4,128)(2,1)S(1)}, bf16[2,4,1024]{2,1,0:T(4,128)(2,1)S(1)}, u32[]{:S(2)}, u32[]{:S(2)}) collective-permute-start(bf16[2,4,1024]{2,1,0:T(4,128)(2,1)S(1)} %get-tuple-element.82), channel_id=1, source_target_pairs={{0,14},{1,15},{2,12},{3,13},{4,10},{5,11},{6,8},{7,9},{8,6},{9,7},... | collective-permute-start | bytes 49160 | tf_op jit(solution)/shard_map/ppermute | solution.py:23
  86.3 2.2 %collective-permute-done.38.refs_7_ = bf16[2,4,1024]{2,1,0:T(4,128)(2,1)S(1)} collective-permute-done((bf16[2,4,1024]{2,1,0:T(4,128)(2,1)S(1)}, bf16[2,4,1024]{2,1,0:T(4,128)(2,1)S(1)}, u32[]{:S(2)}, u32[]{:S(2)}) %collective-permute-start.38) | collective-permute-done | bytes 16416 | tf_op jit(solution)/shard_map/ppermute | solution.py:23
  (79 shorter events, 25.8 us)
Async XLA Ops:
  1.5 10.7 %collective-permute-start.1 = (bf16[1,4,16512]{2,1,0:T(4,128)(2,1)S(1)}, bf16[1,4,16512]{2,1,0:T(4,128)(2,1)S(1)}, u32[]{:S(2)}, u32[]{:S(2)}) collective-permute-start(bf16[1,4,16512]{2,1,0:T(4,128)(2,1)S(1)} %bitcast.2), channel_id=1, source_target_pairs={{0,4},{1,5},{2,6},{3,7},{4,12},{5,13},{6,14},{7,15},{8,0},{9,1},{1... | collective-permute-start | bytes 396296 | tf_op jit(solution)/shard_map/ppermute | solution.py:23
  4.5 7.6 %collective-permute-start = (bf16[1,4,16512]{2,1,0:T(4,128)(2,1)S(1)}, bf16[1,4,16512]{2,1,0:T(4,128)(2,1)S(1)}, u32[]{:S(2)}, u32[]{:S(2)}) collective-permute-start(bf16[1,4,16512]{2,1,0:T(4,128)(2,1)S(1)} %bitcast.3), channel_id=1, source_target_pairs={{0,8},{1,9},{2,10},{3,11},{4,0},{5,1},{6,2},{7,3},{8,12},{9,13},{1... | collective-permute-start | bytes 396296 | tf_op jit(solution)/shard_map/ppermute | solution.py:23
  5.6 9.6 %collective-permute-start.2 = (bf16[1,4,16512]{2,1,0:T(4,128)(2,1)S(1)}, bf16[1,4,16512]{2,1,0:T(4,128)(2,1)S(1)}, u32[]{:S(2)}, u32[]{:S(2)}) collective-permute-start(bf16[1,4,16512]{2,1,0:T(4,128)(2,1)S(1)} %bitcast.4), channel_id=1, source_target_pairs={{0,2},{1,3},{2,0},{3,1},{4,6},{5,7},{6,4},{7,5},{8,10},{9,11},{10,... | collective-permute-start | bytes 396296 | tf_op jit(solution)/shard_map/ppermute | solution.py:23
  12.2 6.4 %collective-permute-start.7 = (bf16[1,4,16512]{2,1,0:T(4,128)(2,1)S(1)}, bf16[1,4,16512]{2,1,0:T(4,128)(2,1)S(1)}, u32[]{:S(2)}, u32[]{:S(2)}) collective-permute-start(bf16[1,4,16512]{2,1,0:T(4,128)(2,1)S(1)} %get-tuple-element.45.refs_2_), channel_id=1, source_target_pairs={{0,8},{1,9},{2,10},{3,11},{4,0},{5,1},{6,2},{7,3},{8,12},{9,13},{1... | collective-permute-start | bytes 396296 | tf_op jit(solution)/shard_map/ppermute | solution.py:23
  13.9 7.0 %collective-permute-start.4 = (bf16[2,4,16512]{2,1,0:T(4,128)(2,1)S(1)}, bf16[2,4,16512]{2,1,0:T(4,128)(2,1)S(1)}, u32[]{:S(2)}, u32[]{:S(2)}) collective-permute-start(bf16[2,4,16512]{2,1,0:T(4,128)(2,1)S(1)} %get-tuple-element.47.refs_3_), channel_id=1, source_target_pairs={{0,2},{1,3},{2,0},{3,1},{4,6},{5,7},{6,4},{7,5},{8,10},{9,11},{10,... | collective-permute-start | bytes 792584 | tf_op jit(solution)/shard_map/ppermute | solution.py:23
  15.4 9.2 %collective-permute-start.3 = (bf16[2,4,16512]{2,1,0:T(4,128)(2,1)S(1)}, bf16[2,4,16512]{2,1,0:T(4,128)(2,1)S(1)}, u32[]{:S(2)}, u32[]{:S(2)}) collective-permute-start(bf16[2,4,16512]{2,1,0:T(4,128)(2,1)S(1)} %pad_maximum_fusion), channel_id=1, source_target_pairs={{0,1},{1,0},{2,3},{3,2},{4,5},{5,4},{6,7},{7,6},{8,9},{9,8},{10,11... | collective-permute-start | bytes 792584 | tf_op jit(solution)/shard_map/ppermute | solution.py:23
  18.6 6.0 %collective-permute-start.8 = (bf16[1,4,16512]{2,1,0:T(4,128)(2,1)S(1)}, bf16[1,4,16512]{2,1,0:T(4,128)(2,1)S(1)}, u32[]{:S(2)}, u32[]{:S(2)}) collective-permute-start(bf16[1,4,16512]{2,1,0:T(4,128)(2,1)S(1)} %shard_map.86.refs_1_.refs_7_), channel_id=1, source_target_pairs={{0,2},{1,3},{2,0},{3,1},{4,6},{5,7},{6,4},{7,5},{8,10},{9,11},{10,... | collective-permute-start | bytes 396296 | tf_op jit(solution)/shard_map/ppermute | solution.py:23
  30.9 7.5 %collective-permute-start.13 = (bf16[96,128]{1,0:T(8,128)(2,1)S(1)}, bf16[96,128]{1,0:T(8,128)(2,1)S(1)}, u32[]{:S(2)}, u32[]{:S(2)}) collective-permute-start(bf16[96,128]{1,0:T(8,128)(2,1)S(1)} %get-tuple-element.58), channel_id=1, source_target_pairs={{0,2},{1,3},{2,0},{3,1},{4,6},{5,7},{6,4},{7,5},{8,10},{9,11},{10,... | collective-permute-start | bytes 73736 | tf_op jit(solution)/shard_map/ppermute | solution.py:23
  31.6 9.3 %collective-permute-start.14 = (bf16[96,128]{1,0:T(8,128)(2,1)S(1)}, bf16[96,128]{1,0:T(8,128)(2,1)S(1)}, u32[]{:S(2)}, u32[]{:S(2)}) collective-permute-start(bf16[96,128]{1,0:T(8,128)(2,1)S(1)} %get-tuple-element.59), channel_id=1, source_target_pairs={{0,4},{1,5},{2,6},{3,7},{4,12},{5,13},{6,14},{7,15},{8,0},{9,1},{1... | collective-permute-start | bytes 73736 | tf_op jit(solution)/shard_map/ppermute | solution.py:23
  33.4 9.5 %collective-permute-start.15 = (bf16[96,128]{1,0:T(8,128)(2,1)S(1)}, bf16[96,128]{1,0:T(8,128)(2,1)S(1)}, u32[]{:S(2)}, u32[]{:S(2)}) collective-permute-start(bf16[96,128]{1,0:T(8,128)(2,1)S(1)} %get-tuple-element.60), channel_id=1, source_target_pairs={{0,8},{1,9},{2,10},{3,11},{4,0},{5,1},{6,2},{7,3},{8,12},{9,13},{1... | collective-permute-start | bytes 73736 | tf_op jit(solution)/shard_map/ppermute | solution.py:23
  34.6 8.4 %collective-permute-start.16 = (bf16[96,128]{1,0:T(8,128)(2,1)S(1)}, bf16[96,128]{1,0:T(8,128)(2,1)S(1)}, u32[]{:S(2)}, u32[]{:S(2)}) collective-permute-start(bf16[96,128]{1,0:T(8,128)(2,1)S(1)} %get-tuple-element.61), channel_id=1, source_target_pairs={{0,6},{1,7},{2,4},{3,5},{4,14},{5,15},{6,12},{7,13},{8,2},{9,3},{1... | collective-permute-start | bytes 73736 | tf_op jit(solution)/shard_map/ppermute | solution.py:23
  35.3 7.6 %collective-permute-start.17 = (bf16[96,128]{1,0:T(8,128)(2,1)S(1)}, bf16[96,128]{1,0:T(8,128)(2,1)S(1)}, u32[]{:S(2)}, u32[]{:S(2)}) collective-permute-start(bf16[96,128]{1,0:T(8,128)(2,1)S(1)} %get-tuple-element.62), channel_id=1, source_target_pairs={{0,10},{1,11},{2,8},{3,9},{4,2},{5,3},{6,0},{7,1},{8,14},{9,15},{1... | collective-permute-start | bytes 73736 | tf_op jit(solution)/shard_map/ppermute | solution.py:23
  38.4 5.6 %collective-permute-start.18 = (bf16[96,128]{1,0:T(8,128)(2,1)S(1)}, bf16[96,128]{1,0:T(8,128)(2,1)S(1)}, u32[]{:S(2)}, u32[]{:S(2)}) collective-permute-start(bf16[96,128]{1,0:T(8,128)(2,1)S(1)} %get-tuple-element.63), channel_id=1, source_target_pairs={{0,12},{1,13},{2,14},{3,15},{4,8},{5,9},{6,10},{7,11},{8,4},{9,5},... | collective-permute-start | bytes 73736 | tf_op jit(solution)/shard_map/ppermute | solution.py:23
  40.9 6.5 %collective-permute-start.19 = (bf16[96,128]{1,0:T(8,128)(2,1)S(1)}, bf16[96,128]{1,0:T(8,128)(2,1)S(1)}, u32[]{:S(2)}, u32[]{:S(2)}) collective-permute-start(bf16[96,128]{1,0:T(8,128)(2,1)S(1)} %get-tuple-element.64), channel_id=1, source_target_pairs={{0,14},{1,15},{2,12},{3,13},{4,10},{5,11},{6,8},{7,9},{8,6},{9,7},... | collective-permute-start | bytes 73736 | tf_op jit(solution)/shard_map/ppermute | solution.py:23
  50.1 7.0 %collective-permute-start.23 = (bf16[1,4,8192]{2,1,0:T(4,128)(2,1)S(1)}, bf16[1,4,8192]{2,1,0:T(4,128)(2,1)S(1)}, u32[]{:S(2)}, u32[]{:S(2)}) collective-permute-start(bf16[1,4,8192]{2,1,0:T(4,128)(2,1)S(1)} %bitcast.8), channel_id=1, source_target_pairs={{0,4},{1,5},{2,6},{3,7},{4,12},{5,13},{6,14},{7,15},{8,0},{9,1},{1... | collective-permute-start | bytes 196616 | tf_op jit(solution)/shard_map/ppermute | solution.py:23
  50.1 6.9 %collective-permute-start.22 = (bf16[1,4,8192]{2,1,0:T(4,128)(2,1)S(1)}, bf16[1,4,8192]{2,1,0:T(4,128)(2,1)S(1)}, u32[]{:S(2)}, u32[]{:S(2)}) collective-permute-start(bf16[1,4,8192]{2,1,0:T(4,128)(2,1)S(1)} %bitcast.9), channel_id=1, source_target_pairs={{0,8},{1,9},{2,10},{3,11},{4,0},{5,1},{6,2},{7,3},{8,12},{9,13},{1... | collective-permute-start | bytes 196616 | tf_op jit(solution)/shard_map/ppermute | solution.py:23
  53.0 6.8 %collective-permute-start.20 = (bf16[1,4,8192]{2,1,0:T(4,128)(2,1)S(1)}, bf16[1,4,8192]{2,1,0:T(4,128)(2,1)S(1)}, u32[]{:S(2)}, u32[]{:S(2)}) collective-permute-start(bf16[1,4,8192]{2,1,0:T(4,128)(2,1)S(1)} %bitcast.10), channel_id=1, source_target_pairs={{0,2},{1,3},{2,0},{3,1},{4,6},{5,7},{6,4},{7,5},{8,10},{9,11},{10,... | collective-permute-start | bytes 196616 | tf_op jit(solution)/shard_map/ppermute | solution.py:23
  57.1 5.7 %collective-permute-start.27 = (bf16[1,4,8192]{2,1,0:T(4,128)(2,1)S(1)}, bf16[1,4,8192]{2,1,0:T(4,128)(2,1)S(1)}, u32[]{:S(2)}, u32[]{:S(2)}) collective-permute-start(bf16[1,4,8192]{2,1,0:T(4,128)(2,1)S(1)} %get-tuple-element.67.refs_1_), channel_id=1, source_target_pairs={{0,8},{1,9},{2,10},{3,11},{4,0},{5,1},{6,2},{7,3},{8,12},{9,13},{1... | collective-permute-start | bytes 196616 | tf_op jit(solution)/shard_map/ppermute | solution.py:23
  73.1 7.7 %collective-permute-start.32 = (bf16[2,4,1024]{2,1,0:T(4,128)(2,1)S(1)}, bf16[2,4,1024]{2,1,0:T(4,128)(2,1)S(1)}, u32[]{:S(2)}, u32[]{:S(2)}) collective-permute-start(bf16[2,4,1024]{2,1,0:T(4,128)(2,1)S(1)} %get-tuple-element.76), channel_id=1, source_target_pairs={{0,2},{1,3},{2,0},{3,1},{4,6},{5,7},{6,4},{7,5},{8,10},{9,11},{10,... | collective-permute-start | bytes 49160 | tf_op jit(solution)/shard_map/ppermute | solution.py:23
  74.0 8.0 %collective-permute-start.33 = (bf16[2,4,1024]{2,1,0:T(4,128)(2,1)S(1)}, bf16[2,4,1024]{2,1,0:T(4,128)(2,1)S(1)}, u32[]{:S(2)}, u32[]{:S(2)}) collective-permute-start(bf16[2,4,1024]{2,1,0:T(4,128)(2,1)S(1)} %get-tuple-element.77), channel_id=1, source_target_pairs={{0,4},{1,5},{2,6},{3,7},{4,12},{5,13},{6,14},{7,15},{8,0},{9,1},{1... | collective-permute-start | bytes 49160 | tf_op jit(solution)/shard_map/ppermute | solution.py:23
  74.5 10.6 %collective-permute-start.34 = (bf16[2,4,1024]{2,1,0:T(4,128)(2,1)S(1)}, bf16[2,4,1024]{2,1,0:T(4,128)(2,1)S(1)}, u32[]{:S(2)}, u32[]{:S(2)}) collective-permute-start(bf16[2,4,1024]{2,1,0:T(4,128)(2,1)S(1)} %get-tuple-element.78), channel_id=1, source_target_pairs={{0,8},{1,9},{2,10},{3,11},{4,0},{5,1},{6,2},{7,3},{8,12},{9,13},{1... | collective-permute-start | bytes 49160 | tf_op jit(solution)/shard_map/ppermute | solution.py:23
  76.9 8.2 %collective-permute-start.35 = (bf16[2,4,1024]{2,1,0:T(4,128)(2,1)S(1)}, bf16[2,4,1024]{2,1,0:T(4,128)(2,1)S(1)}, u32[]{:S(2)}, u32[]{:S(2)}) collective-permute-start(bf16[2,4,1024]{2,1,0:T(4,128)(2,1)S(1)} %get-tuple-element.79), channel_id=1, source_target_pairs={{0,6},{1,7},{2,4},{3,5},{4,14},{5,15},{6,12},{7,13},{8,2},{9,3},{1... | collective-permute-start | bytes 49160 | tf_op jit(solution)/shard_map/ppermute | solution.py:23
  76.9 8.2 %collective-permute-start.36 = (bf16[2,4,1024]{2,1,0:T(4,128)(2,1)S(1)}, bf16[2,4,1024]{2,1,0:T(4,128)(2,1)S(1)}, u32[]{:S(2)}, u32[]{:S(2)}) collective-permute-start(bf16[2,4,1024]{2,1,0:T(4,128)(2,1)S(1)} %get-tuple-element.80), channel_id=1, source_target_pairs={{0,10},{1,11},{2,8},{3,9},{4,2},{5,3},{6,0},{7,1},{8,14},{9,15},{1... | collective-permute-start | bytes 49160 | tf_op jit(solution)/shard_map/ppermute | solution.py:23
  82.0 6.4 %collective-permute-start.38 = (bf16[2,4,1024]{2,1,0:T(4,128)(2,1)S(1)}, bf16[2,4,1024]{2,1,0:T(4,128)(2,1)S(1)}, u32[]{:S(2)}, u32[]{:S(2)}) collective-permute-start(bf16[2,4,1024]{2,1,0:T(4,128)(2,1)S(1)} %get-tuple-element.82), channel_id=1, source_target_pairs={{0,14},{1,15},{2,12},{3,13},{4,10},{5,11},{6,8},{7,9},{8,6},{9,7},... | collective-permute-start | bytes 49160 | tf_op jit(solution)/shard_map/ppermute | solution.py:23
  (17 other events, 95.4 us)

commit v4 on v3

--- a/solution.py
+++ b/solution.py
@@ -128,18 +128,14 @@
     return permute(block, np.arange(devices) ^ 1)
 
 
-def origins(groups):
-    return [source for group in groups if not group.crossed for source in group.sources]
-
-
-def give_back(pieces, groups):
-    return [pieces[0]] + [permute(piece, origin) for piece, origin in zip(pieces[1:], origins(groups)[1:])]
-
-
-def places(groups, devices):
-    here = np.arange(devices)
-    senders = [moved(here, origin) for origin in origins(groups)]
-    return np.stack([sender ^ other for sender in senders for other in range(2)], 1).astype(np.int32)
+def exchange(pieces, devices):
+    same_core = [list(range(core, devices, 2)) for core in range(2)]
+    return lax.all_to_all(pieces, "gx", 0, 0, axis_index_groups=same_core, tiled=True)
+
+
+def places(groups):
+    origins = [source // 2 for group in groups if not group.crossed for source in group.sources]
+    return np.stack(origins, 1).astype(np.int32)
 
 
 def norm_kernel(lengths_far, hidden_far, gain_far, out, lengths, hidden, gain, arrived):
@@ -222,7 +218,7 @@
 
 def assemble(slots, first, width):
     lanes = slice(first, first + width)
-    return jnp.concatenate([ref[at, :, lanes].astype(jnp.float32) for ref, at in slots], 0).astype(jnp.bfloat16)
+    return jnp.concatenate([ref[at, :, lanes] for ref, at in slots], 0)
 
 
 def multiply(slots, weights, depth, total, kept):
@@ -315,44 +311,44 @@
     )(*[group.blocks for group in groups], *w_query, w_keyval)
 
 
-def pack_kernel(near, far, near_sum, far_sum, *outs):
+def pack_kernel(place, near, far, near_sum, far_sum, out):
     tile, lines = near.shape[1], near_sum.shape[1]
-    for chip, out in enumerate(outs):
-        out[:tile, :] = near[chip]
-        out[tile : 2 * tile, :] = far[chip]
-        total = near_sum[chip] + far_sum[chip]
+    for slot in range(near.shape[0]):
+        chip = place[lax.axis_index("gx"), slot]
+        out[chip, :tile, :] = near[slot]
+        out[chip, tile : 2 * tile, :] = far[slot]
+        total = near_sum[slot] + far_sum[slot]
         high = total.astype(jnp.bfloat16)
-        out[2 * tile : 2 * tile + lines, :] = high
-        out[2 * tile + lines :, :] = (total - high.astype(jnp.float32)).astype(jnp.bfloat16)
-
-
-def pack(near, far, near_sum, far_sum):
+        out[chip, 2 * tile : 2 * tile + lines, :] = high
+        out[chip, 2 * tile + lines :, :] = (total - high.astype(jnp.float32)).astype(jnp.bfloat16)
+
+
+def pack(place, near, far, near_sum, far_sum):
     chips, tile, _ = near.shape
-    piece = jax.ShapeDtypeStruct((2 * tile + 2 * near_sum.shape[1], HD), jnp.bfloat16)
     return pl.pallas_call(
         pack_kernel,
-        out_shape=[piece] * chips,
-        in_specs=[VMEM] * 4,
-        out_specs=[VMEM] * chips,
-        compiler_params=pltpu.CompilerParams(vmem_limit_bytes=VMEM_LIMIT),
-    )(near, far, near_sum, far_sum)
-
-
-def pair_kernel(near, far, *outs):
-    for chip, out in enumerate(outs):
-        out[0] = near[chip]
-        out[1] = far[chip]
-
-
-def pair(near, far):
-    chips = near.shape[0]
+        out_shape=jax.ShapeDtypeStruct((chips, 2 * tile + 2 * near_sum.shape[1], HD), jnp.bfloat16),
+        in_specs=[SMEM] + [VMEM] * 4,
+        out_specs=VMEM,
+        compiler_params=pltpu.CompilerParams(vmem_limit_bytes=VMEM_LIMIT),
+    )(place, near, far, near_sum, far_sum)
+
+
+def pair_kernel(place, near, far, out):
+    for slot in range(near.shape[0]):
+        chip = place[lax.axis_index("gx"), slot]
+        out[chip, 0] = near[slot]
+        out[chip, 1] = far[slot]
+
+
+def pair(place, near, far):
     return pl.pallas_call(
         pair_kernel,
-        out_shape=[jax.ShapeDtypeStruct((2, *near.shape[1:]), near.dtype)] * chips,
-        in_specs=[VMEM] * 2,
-        out_specs=[VMEM] * chips,
-        compiler_params=pltpu.CompilerParams(vmem_limit_bytes=VMEM_LIMIT),
-    )(near, far)
+        out_shape=jax.ShapeDtypeStruct((near.shape[0], 2, *near.shape[1:]), near.dtype),
+        in_specs=[SMEM] + [VMEM] * 2,
+        out_specs=VMEM,
+        compiler_params=pltpu.CompilerParams(vmem_limit_bytes=VMEM_LIMIT),
+    )(place, near, far)
 
 
 def out_kernel(counts, crossed, *refs):
@@ -386,8 +382,7 @@
     )(*[group.blocks for group in groups], *w_out)
 
 
-def attend_kernel(devices, kv_heads, tile, lengths, place, cache, *refs):
-    pieces, (out, fresh, queries, mixed) = refs[:-4], refs[-4:]
+def attend_kernel(devices, kv_heads, tile, lengths, pieces, cache, out, fresh, queries, mixed):
     length, width = cache.shape[2:]
     extra = fresh.shape[2]
     half = tile // 2
@@ -395,14 +390,12 @@
     scale = 1.0 / math.sqrt(HD)
     for chip in range(devices // 2):
         for other in range(2):
-            piece = pieces[chip][other * tile : (other + 1) * tile, :]
-            queries[place[lax.axis_index("gx"), 2 * chip + other]] = piece.astype(jnp.float32)
+            piece = pieces[chip, other * tile : (other + 1) * tile, :]
+            queries[2 * chip + (lax.axis_index("gx") % 2 + other) % 2] = piece.astype(jnp.float32)
     line = lax.broadcasted_iota(jnp.int32, (8, 1), 0)
     first = jnp.where(line % 4 < 2, lengths[0], lengths[1])
     cosine, sine = turns((first + line % 2).astype(jnp.float32))
-    total = pieces[0][2 * tile :, :].astype(jnp.float32)
-    for piece in pieces[1:]:
-        total += piece[2 * tile :, :].astype(jnp.float32)
+    total = jnp.sum(pieces[:, 2 * tile :, :].astype(jnp.float32), 0)
     total = total[: total.shape[0] // 2] + total[total.shape[0] // 2 :]
     twice = [jnp.concatenate([total[4 * at : 4 * at + 4]] * 2, 0) for at in range(2 * kv_heads)]
     new_keys = jnp.concatenate([turn(part, cosine, sine) for part in twice[:kv_heads]], 1)
@@ -445,13 +438,13 @@
     out[...] = mixed[...].astype(out.dtype)
 
 
-def attend(pieces, tile, cache, lengths, place, devices):
+def attend(pieces, tile, cache, lengths, devices):
     length, width = cache.shape[2], cache.shape[3]
     columns = devices * tile // 4 * HD
     return pl.pallas_call(
         functools.partial(attend_kernel, devices, width // HD, tile),
         out_shape=jax.ShapeDtypeStruct((4, columns), jnp.bfloat16),
-        in_specs=[SMEM, SMEM] + [VMEM] * (len(pieces) + 1),
+        in_specs=[SMEM, VMEM, VMEM],
         out_specs=VMEM,
         scratch_shapes=[
             pltpu.VMEM((2, 2, HD, width), cache.dtype),
@@ -462,31 +455,30 @@
         cost_estimate=pl.CostEstimate(
             flops=8 * 128 * length * width, bytes_accessed=8 * length * width, transcendentals=256 * length
         ),
-    )(lengths, place, cache, *pieces)
-
-
-def finish_kernel(devices, place, *refs):
-    *pieces, out = refs
-    columns = pieces[0].shape[2]
+    )(lengths, pieces, cache)
+
+
+def finish_kernel(devices, pieces, out):
+    columns = pieces.shape[3]
     steps, rows = out.shape[:2]
     for chip in range(devices // 2):
         for other in range(2):
-            source = place[lax.axis_index("gx"), 2 * chip + other]
+            source = 2 * chip + (lax.axis_index("gx") % 2 + other) % 2
             lanes = pl.ds(pl.multiple_of(source * columns, columns), columns)
-            piece = pieces[chip][other].astype(jnp.float32)
+            piece = pieces[chip, other].astype(jnp.float32)
             for step in range(steps):
                 out[step, :, lanes] = piece[step * rows : (step + 1) * rows].astype(out.dtype)
 
 
-def finish(pieces, place, steps, devices):
-    own, columns = pieces[0].shape[1:]
+def finish(pieces, steps, devices):
+    own, columns = pieces.shape[2:]
     return pl.pallas_call(
         functools.partial(finish_kernel, devices),
         out_shape=jax.ShapeDtypeStruct((steps, own // steps, devices * columns), jnp.bfloat16),
-        in_specs=[SMEM] + [VMEM] * len(pieces),
+        in_specs=[VMEM],
         out_specs=VMEM,
         compiler_params=pltpu.CompilerParams(vmem_limit_bytes=VMEM_LIMIT),
-    )(place, *pieces)
+    )(pieces)
 
 
 def body(hidden, norm_gain, w_query, w_keyval, w_out, kv_cache, lengths):
@@ -505,21 +497,25 @@
 
         return start
 
-    waits = [bring((w_query, 0, cut)), bring((w_keyval, 0, 2), (kv_cache, 0, 2)), bring((w_query, cut, w_query.shape[0] - cut))]
+    part = w_out.shape[0] // 8
+    waits = [
+        bring((w_query, 0, cut)),
+        bring((w_keyval, 0, 2), (kv_cache, 0, 2)),
+        bring((w_query, cut, w_query.shape[0] - cut), (w_out, 0, part)),
+    ]
     groups = gather(normed, devices, waits)
-    w_first, w_keyval, kv_cache, w_second = fetched
-    place = jnp.asarray(places(groups, devices))
+    w_first, w_keyval, kv_cache, w_second, w_out_first = fetched
+    place = jnp.asarray(places(groups))
     near, far, near_sum, far_sum = project(groups, [w_first, w_second], w_keyval, devices)
-    pieces = pack(near, swap_cores(far, devices), near_sum, swap_cores(far_sum, devices))
-
-    mixed = attend(give_back(pieces, groups), near.shape[1], kv_cache, lengths, place, devices)
-    fetched = []
-    part = w_out.shape[0] // 8
-    waits = [bring((w_out, first * part, count * part)) for first, count in ((0, 3), (3, 3), (6, 2))]
+    pieces = pack(place, near, swap_cores(far, devices), near_sum, swap_cores(far_sum, devices))
+
+    mixed = attend(exchange(pieces, devices), near.shape[1], kv_cache, lengths, devices)
+    fetched = [w_out_first]
+    waits = [bring((w_out, first * part, count * part)) for first, count in ((1, 2), (3, 3), (6, 2))]
     groups = gather(mixed, devices, waits)
     near, far = project_out(groups, fetched, devices)
-    pieces = pair(near, swap_cores(far, devices))
-    return finish(give_back(pieces, groups), place, steps, devices)
+    pieces = pair(place, near, swap_cores(far, devices))
+    return finish(exchange(pieces, devices), steps, devices)
 
 
 def rotate(values, positions):

time: 90 us -> 81 us (0.900)
  starting transfers between devices: 44.2 us -> 20.3 us
  blocking collectives: 0 us -> 22.9 us
  waiting for transfers between devices: 15.3 us -> 6.62 us
    ppermute x39 -> x25, starting transfers between devices: 44.2 us -> 20.3 us  [permute(): lax.ppermute(block, 'gx', [(int(i), int(t)) for i, t in enumerate(target)])]
    all_to_all x0 -> x2, blocking collectives: none -> 22.9 us  [exchange(): lax.all_to_all(pieces, 'gx', 0, 0, axis_index_groups=same_core, tiled=True)]
    ppermute x39 -> x25, waiting for transfers between devices: 15.3 us -> 6.62 us  [permute(): lax.ppermute(block, 'gx', [(int(i), int(t)) for i, t in enumerate(target)])]
    pallas_call x2, Pallas kernels: 0.03 us -> 1.39 us  [the longest x1 0.7 us: pack(): pl.pallas_call(pack_kernel, out_shape=jax.ShapeDtypeStruct((chips, 2 * ti...]
  transfers between devices with their start and end apart: 39 -> 25, of which waited for: 11 -> 7; matrix products, arithmetic and copies ran while one was open for 0% -> 0% of each run, Pallas kernels for 20% -> 22%
where the time goes in v4:
time: 81 us; the launch traced here: 80.8 us
  Pallas kernels  30.5 us (38%)
  blocking collectives  22.9 us (28%)
  starting transfers between devices  20.3 us (25%)
  waiting for transfers between devices  6.62 us (8%)
    all_to_all x2, blocking collectives, exchange(): lax.all_to_all(pieces, 'gx', 0, 0, axis_index_groups=same_core, tiled=True)  22.9 us
    ppermute x25, starting transfers between devices, permute(): lax.ppermute(block, 'gx', [(int(i), int(t)) for i, t in enumerate(target)])  20.3 us
    pallas_call x6, Pallas kernels, fetch(): pl.pallas_call(functools.partial(fetch_kernel, [first for _, first, _ in...  17.9 us
    ppermute x25, waiting for transfers between devices, permute(): lax.ppermute(block, 'gx', [(int(i), int(t)) for i, t in enumerate(target)])  6.62 us
    pallas_call x1, Pallas kernels, project(): pl.pallas_call(functools.partial(project_kernel, counts, crossed, width),...  3.44 us
    pallas_call x1, Pallas kernels, project_out(): pl.pallas_call(functools.partial(out_kernel, counts, crossed), out_shape=...  3.05 us
    pallas_call x1, Pallas kernels, attend(): pl.pallas_call(functools.partial(attend_kernel, devices, width // HD, til...  2.47 us
  transfers between devices with their start and end apart: 25, of which 7 were waited for; matrix products, arithmetic and copies ran while one was open for 0% of the time, Pallas kernels for 22%

profile of v4, /device:TPU:0, one launch (start us, length us, event | category | flops | bytes accessed | tf_op | source)
XLA Modules:
  0.0 80.8 jit_solution(8739737155872326085)
XLA Ops:
  0.0 1.4 %shard_map.82 = bf16[4,16512]{1,0:T(4,128)(2,1)S(1)} custom-call(s32[2]{0:T(128)} %lengths.1, bf16[2,2,16384]{2,1,0:T(2,128)(2,1)} %hidden_far.1, bf16[16384]{0:T(1024)(128)(2,1)} %gain_far.1), custom_call_target="tpu_custom_call" | custom-call | flops 393216 | bytes 262144 | tf_op jit(solution)/shard_map/pallas_call | solution.py:168
  1.5 3.1 %collective-permute-start.3 = (bf16[1,4,16512]{2,1,0:T(4,128)(2,1)S(1)}, bf16[1,4,16512]{2,1,0:T(4,128)(2,1)S(1)}, u32[]{:S(2)}, u32[]{:S(2)}) collective-permute-start(bf16[1,4,16512]{2,1,0:T(4,128)(2,1)S(1)} %bitcast.2), channel_id=1, source_target_pairs={{0,4},{1,5},{2,6},{3,7},{4,12},{5,13},{6,14},{7,15},{8,0},{9,1},{1... | collective-permute-start | bytes 396296 | tf_op jit(solution)/shard_map/ppermute | solution.py:23
  4.5 1.1 %collective-permute-start.2 = (bf16[1,4,16512]{2,1,0:T(4,128)(2,1)S(1)}, bf16[1,4,16512]{2,1,0:T(4,128)(2,1)S(1)}, u32[]{:S(2)}, u32[]{:S(2)}) collective-permute-start(bf16[1,4,16512]{2,1,0:T(4,128)(2,1)S(1)} %bitcast.3), channel_id=1, source_target_pairs={{0,8},{1,9},{2,10},{3,11},{4,0},{5,1},{6,2},{7,3},{8,12},{9,13},{1... | collective-permute-start | bytes 396296 | tf_op jit(solution)/shard_map/ppermute | solution.py:23
  5.6 1.8 %collective-permute-start = (bf16[1,4,16512]{2,1,0:T(4,128)(2,1)S(1)}, bf16[1,4,16512]{2,1,0:T(4,128)(2,1)S(1)}, u32[]{:S(2)}, u32[]{:S(2)}) collective-permute-start(bf16[1,4,16512]{2,1,0:T(4,128)(2,1)S(1)} %bitcast.4), channel_id=1, source_target_pairs={{0,2},{1,3},{2,0},{3,1},{4,6},{5,7},{6,4},{7,5},{8,10},{9,11},{10,... | collective-permute-start | bytes 396296 | tf_op jit(solution)/shard_map/ppermute | solution.py:23
  7.4 4.7 %shard_map.83 = (bf16[12288,512]{1,0:T(8,128)(2,1)S(1)}, f32[8,128]{1,0:T(8,128)S(1)}) custom-call(bf16[16384,512]{1,0:T(8,128)(2,1)} %refs_0_.8, bf16[1,4,16512]{2,1,0:T(4,128)(2,1)S(1)} %bitcast.5), custom_call_target="tpu_custom_call" | custom-call | bytes 12582912 | tf_op jit(solution)/shard_map/pallas_call | solution.py:201
  12.2 1.7 %collective-permute-start.7 = (bf16[1,4,16512]{2,1,0:T(4,128)(2,1)S(1)}, bf16[1,4,16512]{2,1,0:T(4,128)(2,1)S(1)}, u32[]{:S(2)}, u32[]{:S(2)}) collective-permute-start(bf16[1,4,16512]{2,1,0:T(4,128)(2,1)S(1)} %get-tuple-element.31.refs_2_), channel_id=1, source_target_pairs={{0,8},{1,9},{2,10},{3,11},{4,0},{5,1},{6,2},{7,3},{8,12},{9,13},{1... | collective-permute-start | bytes 396296 | tf_op jit(solution)/shard_map/ppermute | solution.py:23
  13.9 1.3 %collective-permute-start.4 = (bf16[2,4,16512]{2,1,0:T(4,128)(2,1)S(1)}, bf16[2,4,16512]{2,1,0:T(4,128)(2,1)S(1)}, u32[]{:S(2)}, u32[]{:S(2)}) collective-permute-start(bf16[2,4,16512]{2,1,0:T(4,128)(2,1)S(1)} %get-tuple-element.30.refs_3_), channel_id=1, source_target_pairs={{0,2},{1,3},{2,0},{3,1},{4,6},{5,7},{6,4},{7,5},{8,10},{9,11},{10,... | collective-permute-start | bytes 792584 | tf_op jit(solution)/shard_map/ppermute | solution.py:23
  15.5 3.0 %shard_map.85 = (bf16[2,1024,512]{2,1,0:T(8,128)(2,1)S(1)}, bf16[2,2,1024,512]{3,2,1,0:T(8,128)(2,1)S(1)}, f32[8,128]{1,0:T(8,128)S(1)}) custom-call(bf16[2,1024,512]{2,1,0:T(8,128)(2,1)} %refs_0_.7, bf16[2,2,1024,512]{3,2,1,0:T(8,128)(2,1)} %refs_1_.2, bf16[1,4,16512]{2,1,0:T(4,128)(2,1)S(1)} %get-tuple-element.31.refs_2_), custom_call_target="tpu_custom_call" | custom-call | bytes 6291456 | tf_op jit(solution)/shard_map/pallas_call | solution.py:201
  19.5 1.3 %collective-permute-done.4.refs_4_ = bf16[2,4,16512]{2,1,0:T(4,128)(2,1)S(1)} collective-permute-done((bf16[2,4,16512]{2,1,0:T(4,128)(2,1)S(1)}, bf16[2,4,16512]{2,1,0:T(4,128)(2,1)S(1)}, u32[]{:S(2)}, u32[]{:S(2)}) %collective-permute-start.4) | collective-permute-done | bytes 264224 | tf_op jit(solution)/shard_map/ppermute | solution.py:23
  21.4 2.9 %shard_map.87 = (bf16[4096,512]{1,0:T(8,128)(2,1)S(1)}, bf16[1024,1024]{1,0:T(8,128)(2,1)S(1)}, f32[8,128]{1,0:T(8,128)S(1)}) custom-call(bf16[16384,512]{1,0:T(8,128)(2,1)} %refs_0_.8, bf16[8192,1024]{1,0:T(8,128)(2,1)} %refs_0_.11, bf16[1,4,16512]{2,1,0:T(4,128)(2,1)S(1)} %shard_map.86.refs_2_.refs_7_), custom_call_target="tpu_custom_call" | custom-call | bytes 6291456 | tf_op jit(solution)/shard_map/pallas_call | solution.py:201
  24.7 1.3 %collective-permute-done.10.refs_10_ = bf16[1,4,16512]{2,1,0:T(4,128)(2,1)S(1)} collective-permute-done((bf16[1,4,16512]{2,1,0:T(4,128)(2,1)S(1)}, bf16[1,4,16512]{2,1,0:T(4,128)(2,1)S(1)}, u32[]{:S(2)}, u32[]{:S(2)}) %collective-permute-start.10) | collective-permute-done | bytes 132128 | tf_op jit(solution)/shard_map/ppermute | solution.py:23
  26.0 3.4 %shard_map.89 = (bf16[8,16,128]{2,1,0:T(8,128)(2,1)S(1)}, bf16[8,16,128]{2,1,0:T(8,128)(2,1)S(1)}, f32[8,32,128]{2,1,0:T(8,128)S(1)}, f32[8,32,128]{2,1,0:T(8,128)S(1)}) custom-call(bf16[1,4,16512]{2,1,0:T(4,128)(2,1)S(1)} %bitcast.7, bf16[1,4,16512]{2,1,0:T(4,128)(2,1)S(1)} %collective-permute-done.refs_1_, ...), custom_call_target="tpu_custom_call" | custom-call | flops 1073741824 | bytes 16777216 | tf_op jit(solution)/shard_map/pallas_call | solution.py:297
  31.6 12.9 %all_to_all.10.pieces = bf16[8,96,128]{2,1,0:T(8,128)(2,1)S(1)} all-to-all(bf16[8,96,128]{2,1,0:T(8,128)(2,1)S(1)} %shard_map.90), channel_id=1, replica_groups={{0,2,4,6,8,10,12,14},{1,3,5,7,9,11,13,15},{16,18,20,22,24,26,28,30},{17..., dimensions={0} | all-to-all | bytes 393216 | tf_op jit(solution)/shard_map/all_to_all | solution.py:133
  44.5 2.5 %shard_map.91 = bf16[4,8192]{1,0:T(4,128)(2,1)S(1)} custom-call(s32[2]{0:T(128)S(1)} %copy-done.1, bf16[8,96,128]{2,1,0:T(8,128)(2,1)S(1)} %all_to_all.10.pieces, bf16[2,2,1024,512]{3,2,1,0:T(8,128)(2,1)S(1)} %get-tuple-element.41.cache), custom_call_target="tpu_custom_call" | custom-call | flops 536870912 | bytes 4194304 | tf_op jit(solution)/shard_map/pallas_call | solution.py:444
  47.2 2.7 %collective-permute-start.15 = (bf16[1,4,8192]{2,1,0:T(4,128)(2,1)S(1)}, bf16[1,4,8192]{2,1,0:T(4,128)(2,1)S(1)}, u32[]{:S(2)}, u32[]{:S(2)}) collective-permute-start(bf16[1,4,8192]{2,1,0:T(4,128)(2,1)S(1)} %bitcast.9), channel_id=1, source_target_pairs={{0,8},{1,9},{2,10},{3,11},{4,0},{5,1},{6,2},{7,3},{8,12},{9,13},{1... | collective-permute-start | bytes 196616 | tf_op jit(solution)/shard_map/ppermute | solution.py:23
  50.9 2.2 %shard_map.92 = (bf16[2048,1024]{1,0:T(8,128)(2,1)S(1)}, f32[8,128]{1,0:T(8,128)S(1)}) custom-call(bf16[8192,1024]{1,0:T(8,128)(2,1)} %refs_0_.11, bf16[1,4,8192]{2,1,0:T(4,128)(2,1)S(1)} %bitcast.11), custom_call_target="tpu_custom_call" | custom-call | bytes 4194304 | tf_op jit(solution)/shard_map/pallas_call | solution.py:201
  53.2 2.0 %collective-permute-start.20 = (bf16[1,4,8192]{2,1,0:T(4,128)(2,1)S(1)}, bf16[1,4,8192]{2,1,0:T(4,128)(2,1)S(1)}, u32[]{:S(2)}, u32[]{:S(2)}) collective-permute-start(bf16[1,4,8192]{2,1,0:T(4,128)(2,1)S(1)} %get-tuple-element.44.refs_1_), channel_id=1, source_target_pairs={{0,8},{1,9},{2,10},{3,11},{4,0},{5,1},{6,2},{7,3},{8,12},{9,13},{1... | collective-permute-start | bytes 196616 | tf_op jit(solution)/shard_map/ppermute | solution.py:23
  56.2 2.9 %shard_map.94 = (bf16[3072,1024]{1,0:T(8,128)(2,1)S(1)}, f32[8,128]{1,0:T(8,128)S(1)}) custom-call(bf16[8192,1024]{1,0:T(8,128)(2,1)} %refs_0_.11, bf16[1,4,8192]{2,1,0:T(4,128)(2,1)S(1)} %get-tuple-element.44.refs_1_), custom_call_target="tpu_custom_call" | custom-call | bytes 6291456 | tf_op jit(solution)/shard_map/pallas_call | solution.py:201
  59.2 1.1 %collective-permute-start.21 = (bf16[1,4,8192]{2,1,0:T(4,128)(2,1)S(1)}, bf16[1,4,8192]{2,1,0:T(4,128)(2,1)S(1)}, u32[]{:S(2)}, u32[]{:S(2)}) collective-permute-start(bf16[1,4,8192]{2,1,0:T(4,128)(2,1)S(1)} %shard_map.95.refs_1_.refs_7_), channel_id=1, source_target_pairs={{0,2},{1,3},{2,0},{3,1},{4,6},{5,7},{6,4},{7,5},{8,10},{9,11},{10,... | collective-permute-start | bytes 196616 | tf_op jit(solution)/shard_map/ppermute | solution.py:23
  61.1 2.2 %shard_map.96 = (bf16[2048,1024]{1,0:T(8,128)(2,1)S(1)}, f32[8,128]{1,0:T(8,128)S(1)}) custom-call(bf16[8192,1024]{1,0:T(8,128)(2,1)} %refs_0_.11, bf16[1,4,8192]{2,1,0:T(4,128)(2,1)S(1)} %shard_map.95.refs_1_.refs_7_), custom_call_target="tpu_custom_call" | custom-call | bytes 4194304 | tf_op jit(solution)/shard_map/pallas_call | solution.py:201
  63.8 1.2 %collective-permute-done.23.refs_10_ = bf16[1,4,8192]{2,1,0:T(4,128)(2,1)S(1)} collective-permute-done((bf16[1,4,8192]{2,1,0:T(4,128)(2,1)S(1)}, bf16[1,4,8192]{2,1,0:T(4,128)(2,1)S(1)}, u32[]{:S(2)}, u32[]{:S(2)}) %collective-permute-start.23) | collective-permute-done | bytes 65568 | tf_op jit(solution)/shard_map/ppermute | solution.py:23
  65.0 3.1 %shard_map.98 = (bf16[8,4,1024]{2,1,0:T(4,128)(2,1)S(1)}, bf16[8,4,1024]{2,1,0:T(4,128)(2,1)S(1)}) custom-call(bf16[1,4,8192]{2,1,0:T(4,128)(2,1)S(1)} %bitcast.13, bf16[1,4,8192]{2,1,0:T(4,128)(2,1)S(1)} %collective-permute-done.13.refs_1_, bf16[2,4,8192]{2,1,0:T(4,128)(2,1)S(1)} %collective-permute-done.14.refs_2_, ...), custom_call_target="tpu_custom_call" | custom-call | flops 1073741824 | bytes 16777216 | tf_op jit(solution)/shard_map/pallas_call | solution.py:369
  68.3 1.1 %collective-permute-done.24.far = bf16[8,4,1024]{2,1,0:T(4,128)(2,1)S(1)} collective-permute-done((bf16[8,4,1024]{2,1,0:T(4,128)(2,1)S(1)}, bf16[8,4,1024]{2,1,0:T(4,128)(2,1)S(1)}, u32[]{:S(2)}, u32[]{:S(2)}) %collective-permute-start.24) | collective-permute-done | bytes 65568 | tf_op jit(solution)/shard_map/ppermute | solution.py:23
  70.1 10.0 %all_to_all.11.pieces = bf16[8,2,4,1024]{3,2,1,0:T(4,128)(2,1)S(1)} all-to-all(bf16[8,2,4,1024]{3,2,1,0:T(4,128)(2,1)S(1)} %shard_map.99), channel_id=1, replica_groups={{0,2,4,6,8,10,12,14},{1,3,5,7,9,11,13,15},{16,18,20,22,24,26,28,30},{17..., dimensions={0} | all-to-all | bytes 262144 | tf_op jit(solution)/shard_map/all_to_all | solution.py:133
  (53 shorter events, 9.6 us)
Async XLA Ops:
  1.5 10.7 %collective-permute-start.3 = (bf16[1,4,16512]{2,1,0:T(4,128)(2,1)S(1)}, bf16[1,4,16512]{2,1,0:T(4,128)(2,1)S(1)}, u32[]{:S(2)}, u32[]{:S(2)}) collective-permute-start(bf16[1,4,16512]{2,1,0:T(4,128)(2,1)S(1)} %bitcast.2), channel_id=1, source_target_pairs={{0,4},{1,5},{2,6},{3,7},{4,12},{5,13},{6,14},{7,15},{8,0},{9,1},{1... | collective-permute-start | bytes 396296 | tf_op jit(solution)/shard_map/ppermute | solution.py:23
  4.5 7.6 %collective-permute-start.2 = (bf16[1,4,16512]{2,1,0:T(4,128)(2,1)S(1)}, bf16[1,4,16512]{2,1,0:T(4,128)(2,1)S(1)}, u32[]{:S(2)}, u32[]{:S(2)}) collective-permute-start(bf16[1,4,16512]{2,1,0:T(4,128)(2,1)S(1)} %bitcast.3), channel_id=1, source_target_pairs={{0,8},{1,9},{2,10},{3,11},{4,0},{5,1},{6,2},{7,3},{8,12},{9,13},{1... | collective-permute-start | bytes 396296 | tf_op jit(solution)/shard_map/ppermute | solution.py:23
  5.6 9.6 %collective-permute-start = (bf16[1,4,16512]{2,1,0:T(4,128)(2,1)S(1)}, bf16[1,4,16512]{2,1,0:T(4,128)(2,1)S(1)}, u32[]{:S(2)}, u32[]{:S(2)}) collective-permute-start(bf16[1,4,16512]{2,1,0:T(4,128)(2,1)S(1)} %bitcast.4), channel_id=1, source_target_pairs={{0,2},{1,3},{2,0},{3,1},{4,6},{5,7},{6,4},{7,5},{8,10},{9,11},{10,... | collective-permute-start | bytes 396296 | tf_op jit(solution)/shard_map/ppermute | solution.py:23
  12.2 6.4 %collective-permute-start.7 = (bf16[1,4,16512]{2,1,0:T(4,128)(2,1)S(1)}, bf16[1,4,16512]{2,1,0:T(4,128)(2,1)S(1)}, u32[]{:S(2)}, u32[]{:S(2)}) collective-permute-start(bf16[1,4,16512]{2,1,0:T(4,128)(2,1)S(1)} %get-tuple-element.31.refs_2_), channel_id=1, source_target_pairs={{0,8},{1,9},{2,10},{3,11},{4,0},{5,1},{6,2},{7,3},{8,12},{9,13},{1... | collective-permute-start | bytes 396296 | tf_op jit(solution)/shard_map/ppermute | solution.py:23
  13.9 7.0 %collective-permute-start.4 = (bf16[2,4,16512]{2,1,0:T(4,128)(2,1)S(1)}, bf16[2,4,16512]{2,1,0:T(4,128)(2,1)S(1)}, u32[]{:S(2)}, u32[]{:S(2)}) collective-permute-start(bf16[2,4,16512]{2,1,0:T(4,128)(2,1)S(1)} %get-tuple-element.30.refs_3_), channel_id=1, source_target_pairs={{0,2},{1,3},{2,0},{3,1},{4,6},{5,7},{6,4},{7,5},{8,10},{9,11},{10,... | collective-permute-start | bytes 792584 | tf_op jit(solution)/shard_map/ppermute | solution.py:23
  15.4 9.2 %collective-permute-start.1 = (bf16[2,4,16512]{2,1,0:T(4,128)(2,1)S(1)}, bf16[2,4,16512]{2,1,0:T(4,128)(2,1)S(1)}, u32[]{:S(2)}, u32[]{:S(2)}) collective-permute-start(bf16[2,4,16512]{2,1,0:T(4,128)(2,1)S(1)} %pad_maximum_fusion), channel_id=1, source_target_pairs={{0,1},{1,0},{2,3},{3,2},{4,5},{5,4},{6,7},{7,6},{8,9},{9,8},{10,11... | collective-permute-start | bytes 792584 | tf_op jit(solution)/shard_map/ppermute | solution.py:23
  18.6 6.0 %collective-permute-start.8 = (bf16[1,4,16512]{2,1,0:T(4,128)(2,1)S(1)}, bf16[1,4,16512]{2,1,0:T(4,128)(2,1)S(1)}, u32[]{:S(2)}, u32[]{:S(2)}) collective-permute-start(bf16[1,4,16512]{2,1,0:T(4,128)(2,1)S(1)} %shard_map.86.refs_2_.refs_7_), channel_id=1, source_target_pairs={{0,2},{1,3},{2,0},{3,1},{4,6},{5,7},{6,4},{7,5},{8,10},{9,11},{10,... | collective-permute-start | bytes 396296 | tf_op jit(solution)/shard_map/ppermute | solution.py:23
  19.3 5.3 %collective-permute-start.5 = (bf16[2,4,16512]{2,1,0:T(4,128)(2,1)S(1)}, bf16[2,4,16512]{2,1,0:T(4,128)(2,1)S(1)}, u32[]{:S(2)}, u32[]{:S(2)}) collective-permute-start(bf16[2,4,16512]{2,1,0:T(4,128)(2,1)S(1)} %get-tuple-element.30.refs_3_), channel_id=1, source_target_pairs={{0,1},{1,0},{2,3},{3,2},{4,5},{5,4},{6,7},{7,6},{8,9},{9,8},{10,11... | collective-permute-start | bytes 792584 | tf_op jit(solution)/shard_map/ppermute | solution.py:23
  20.9 5.1 %collective-permute-start.6 = (bf16[2,4,16512]{2,1,0:T(4,128)(2,1)S(1)}, bf16[2,4,16512]{2,1,0:T(4,128)(2,1)S(1)}, u32[]{:S(2)}, u32[]{:S(2)}) collective-permute-start(bf16[2,4,16512]{2,1,0:T(4,128)(2,1)S(1)} %collective-permute-done.4.refs_4_), channel_id=1, source_target_pairs={{0,1},{1,0},{2,3},{3,2},{4,5},{5,4},{6,7},{7,6},{8,9},{9,8},{10,11... | collective-permute-start | bytes 792584 | tf_op jit(solution)/shard_map/ppermute | solution.py:23
  20.9 3.8 %collective-permute-start.9 = (bf16[1,4,16512]{2,1,0:T(4,128)(2,1)S(1)}, bf16[1,4,16512]{2,1,0:T(4,128)(2,1)S(1)}, u32[]{:S(2)}, u32[]{:S(2)}) collective-permute-start(bf16[1,4,16512]{2,1,0:T(4,128)(2,1)S(1)} %shard_map.86.refs_2_.refs_7_), channel_id=1, source_target_pairs={{0,1},{1,0},{2,3},{3,2},{4,5},{5,4},{6,7},{7,6},{8,9},{9,8},{10,11... | collective-permute-start | bytes 396296 | tf_op jit(solution)/shard_map/ppermute | solution.py:23
  24.6 1.4 %collective-permute-start.10 = (bf16[1,4,16512]{2,1,0:T(4,128)(2,1)S(1)}, bf16[1,4,16512]{2,1,0:T(4,128)(2,1)S(1)}, u32[]{:S(2)}, u32[]{:S(2)}) collective-permute-start(bf16[1,4,16512]{2,1,0:T(4,128)(2,1)S(1)} %shard_map.88.refs_8_), channel_id=1, source_target_pairs={{0,1},{1,0},{2,3},{3,2},{4,5},{5,4},{6,7},{7,6},{8,9},{9,8},{10,11... | collective-permute-start | bytes 396296 | tf_op jit(solution)/shard_map/ppermute | solution.py:23
  29.4 1.5 %collective-permute-start.12 = (f32[8,32,128]{2,1,0:T(8,128)S(1)}, f32[8,32,128]{2,1,0:T(8,128)S(1)}, u32[]{:S(2)}, u32[]{:S(2)}) collective-permute-start(f32[8,32,128]{2,1,0:T(8,128)S(1)} %get-tuple-element.40), channel_id=1, source_target_pairs={{0,1},{1,0},{2,3},{3,2},{4,5},{5,4},{6,7},{7,6},{8,9},{9,8},{10,11... | collective-permute-start | bytes 393224 | tf_op jit(solution)/shard_map/ppermute | solution.py:23
  47.0 6.2 %collective-permute-start.16 = (bf16[1,4,8192]{2,1,0:T(4,128)(2,1)S(1)}, bf16[1,4,8192]{2,1,0:T(4,128)(2,1)S(1)}, u32[]{:S(2)}, u32[]{:S(2)}) collective-permute-start(bf16[1,4,8192]{2,1,0:T(4,128)(2,1)S(1)} %bitcast.8), channel_id=1, source_target_pairs={{0,4},{1,5},{2,6},{3,7},{4,12},{5,13},{6,14},{7,15},{8,0},{9,1},{1... | collective-permute-start | bytes 196616 | tf_op jit(solution)/shard_map/ppermute | solution.py:23
  47.2 6.0 %collective-permute-start.15 = (bf16[1,4,8192]{2,1,0:T(4,128)(2,1)S(1)}, bf16[1,4,8192]{2,1,0:T(4,128)(2,1)S(1)}, u32[]{:S(2)}, u32[]{:S(2)}) collective-permute-start(bf16[1,4,8192]{2,1,0:T(4,128)(2,1)S(1)} %bitcast.9), channel_id=1, source_target_pairs={{0,8},{1,9},{2,10},{3,11},{4,0},{5,1},{6,2},{7,3},{8,12},{9,13},{1... | collective-permute-start | bytes 196616 | tf_op jit(solution)/shard_map/ppermute | solution.py:23
  49.9 6.2 %collective-permute-start.13 = (bf16[1,4,8192]{2,1,0:T(4,128)(2,1)S(1)}, bf16[1,4,8192]{2,1,0:T(4,128)(2,1)S(1)}, u32[]{:S(2)}, u32[]{:S(2)}) collective-permute-start(bf16[1,4,8192]{2,1,0:T(4,128)(2,1)S(1)} %bitcast.10), channel_id=1, source_target_pairs={{0,2},{1,3},{2,0},{3,1},{4,6},{5,7},{6,4},{7,5},{8,10},{9,11},{10,... | collective-permute-start | bytes 196616 | tf_op jit(solution)/shard_map/ppermute | solution.py:23
  53.2 6.0 %collective-permute-start.20 = (bf16[1,4,8192]{2,1,0:T(4,128)(2,1)S(1)}, bf16[1,4,8192]{2,1,0:T(4,128)(2,1)S(1)}, u32[]{:S(2)}, u32[]{:S(2)}) collective-permute-start(bf16[1,4,8192]{2,1,0:T(4,128)(2,1)S(1)} %get-tuple-element.44.refs_1_), channel_id=1, source_target_pairs={{0,8},{1,9},{2,10},{3,11},{4,0},{5,1},{6,2},{7,3},{8,12},{9,13},{1... | collective-permute-start | bytes 196616 | tf_op jit(solution)/shard_map/ppermute | solution.py:23
  55.2 5.4 %collective-permute-start.17 = (bf16[2,4,8192]{2,1,0:T(4,128)(2,1)S(1)}, bf16[2,4,8192]{2,1,0:T(4,128)(2,1)S(1)}, u32[]{:S(2)}, u32[]{:S(2)}) collective-permute-start(bf16[2,4,8192]{2,1,0:T(4,128)(2,1)S(1)} %get-tuple-element.43.refs_3_), channel_id=1, source_target_pairs={{0,2},{1,3},{2,0},{3,1},{4,6},{5,7},{6,4},{7,5},{8,10},{9,11},{10,... | collective-permute-start | bytes 393224 | tf_op jit(solution)/shard_map/ppermute | solution.py:23
  59.1 4.7 %collective-permute-start.14 = (bf16[2,4,8192]{2,1,0:T(4,128)(2,1)S(1)}, bf16[2,4,8192]{2,1,0:T(4,128)(2,1)S(1)}, u32[]{:S(2)}, u32[]{:S(2)}) collective-permute-start(bf16[2,4,8192]{2,1,0:T(4,128)(2,1)S(1)} %pad_maximum_fusion.1), channel_id=1, source_target_pairs={{0,1},{1,0},{2,3},{3,2},{4,5},{5,4},{6,7},{7,6},{8,9},{9,8},{10,11... | collective-permute-start | bytes 393224 | tf_op jit(solution)/shard_map/ppermute | solution.py:23
  59.2 4.5 %collective-permute-start.21 = (bf16[1,4,8192]{2,1,0:T(4,128)(2,1)S(1)}, bf16[1,4,8192]{2,1,0:T(4,128)(2,1)S(1)}, u32[]{:S(2)}, u32[]{:S(2)}) collective-permute-start(bf16[1,4,8192]{2,1,0:T(4,128)(2,1)S(1)} %shard_map.95.refs_1_.refs_7_), channel_id=1, source_target_pairs={{0,2},{1,3},{2,0},{3,1},{4,6},{5,7},{6,4},{7,5},{8,10},{9,11},{10,... | collective-permute-start | bytes 196616 | tf_op jit(solution)/shard_map/ppermute | solution.py:23
  60.3 3.5 %collective-permute-start.18 = (bf16[2,4,8192]{2,1,0:T(4,128)(2,1)S(1)}, bf16[2,4,8192]{2,1,0:T(4,128)(2,1)S(1)}, u32[]{:S(2)}, u32[]{:S(2)}) collective-permute-start(bf16[2,4,8192]{2,1,0:T(4,128)(2,1)S(1)} %get-tuple-element.43.refs_3_), channel_id=1, source_target_pairs={{0,1},{1,0},{2,3},{3,2},{4,5},{5,4},{6,7},{7,6},{8,9},{9,8},{10,11... | collective-permute-start | bytes 393224 | tf_op jit(solution)/shard_map/ppermute | solution.py:23
  60.5 4.5 %collective-permute-start.19 = (bf16[2,4,8192]{2,1,0:T(4,128)(2,1)S(1)}, bf16[2,4,8192]{2,1,0:T(4,128)(2,1)S(1)}, u32[]{:S(2)}, u32[]{:S(2)}) collective-permute-start(bf16[2,4,8192]{2,1,0:T(4,128)(2,1)S(1)} %collective-permute-done.17.refs_4_), channel_id=1, source_target_pairs={{0,1},{1,0},{2,3},{3,2},{4,5},{5,4},{6,7},{7,6},{8,9},{9,8},{10,11... | collective-permute-start | bytes 393224 | tf_op jit(solution)/shard_map/ppermute | solution.py:23
  60.9 3.0 %collective-permute-start.22 = (bf16[1,4,8192]{2,1,0:T(4,128)(2,1)S(1)}, bf16[1,4,8192]{2,1,0:T(4,128)(2,1)S(1)}, u32[]{:S(2)}, u32[]{:S(2)}) collective-permute-start(bf16[1,4,8192]{2,1,0:T(4,128)(2,1)S(1)} %shard_map.95.refs_1_.refs_7_), channel_id=1, source_target_pairs={{0,1},{1,0},{2,3},{3,2},{4,5},{5,4},{6,7},{7,6},{8,9},{9,8},{10,11... | collective-permute-start | bytes 196616 | tf_op jit(solution)/shard_map/ppermute | solution.py:23
  63.8 1.3 %collective-permute-start.23 = (bf16[1,4,8192]{2,1,0:T(4,128)(2,1)S(1)}, bf16[1,4,8192]{2,1,0:T(4,128)(2,1)S(1)}, u32[]{:S(2)}, u32[]{:S(2)}) collective-permute-start(bf16[1,4,8192]{2,1,0:T(4,128)(2,1)S(1)} %shard_map.97.refs_8_), channel_id=1, source_target_pairs={{0,1},{1,0},{2,3},{3,2},{4,5},{5,4},{6,7},{7,6},{8,9},{9,8},{10,11... | collective-permute-start | bytes 196616 | tf_op jit(solution)/shard_map/ppermute | solution.py:23
  68.1 1.3 %collective-permute-start.24 = (bf16[8,4,1024]{2,1,0:T(4,128)(2,1)S(1)}, bf16[8,4,1024]{2,1,0:T(4,128)(2,1)S(1)}, u32[]{:S(2)}, u32[]{:S(2)}) collective-permute-start(bf16[8,4,1024]{2,1,0:T(4,128)(2,1)S(1)} %get-tuple-element.52), channel_id=1, source_target_pairs={{0,1},{1,0},{2,3},{3,2},{4,5},{5,4},{6,7},{7,6},{8,9},{9,8},{10,11... | collective-permute-start | bytes 196616 | tf_op jit(solution)/shard_map/ppermute | solution.py:23
  (3 other events, 24.7 us)

commit v5 on v4

--- a/solution.py
+++ b/solution.py
@@ -13,7 +13,7 @@
 ROPE_BASE = 500000.0
 EPSILON = 1e-05
 TAG = 128
-VMEM_LIMIT = 8 * 1024 * 1024
+VMEM_LIMIT = 10 * 1024 * 1024
 VMEM = pl.BlockSpec(memory_space=pltpu.VMEM)
 SMEM = pl.BlockSpec(memory_space=pltpu.SMEM)
 HBM = pl.BlockSpec(memory_space=pltpu.HBM)
@@ -79,11 +79,12 @@
     return groups
 
 
-def gather(block, devices, meanwhile=()):
+def gather(block, devices, meanwhile=(), inner_first=False):
     (size, following, preceding), inner, core = axes_of(devices)
     own = Group(block[None], [np.arange(devices)])
     near = ring(own, inner)
-    groups = [own] + near + [join([own] + near).send(core[1], crossed=True)]
+    chip_pair = join([own] + near)
+    groups = [own] + near + [chip_pair.send(core[1], crossed=True)]
     forward = backward = own
     for step in range(1, size // 2 + 1):
         before = forward.blocks
@@ -91,7 +92,9 @@
         forward, backward = arrived[0], arrived[-1]
         if step <= len(meanwhile):
             onward = (step < size // 2) + (2 * step + 2 < size)
-            chips, *alone = hold(arrived, onward, meanwhile[step - 1](before))
+            chips, *alone = hold(arrived, 0 if inner_first else onward, meanwhile[step - 1](before))
+            if inner_first:
+                alone = [hold([group], 0, chip_pair.blocks)[0] for group in arrived[:onward]]
             forward, backward = (alone + [forward])[0], (alone + [backward])[-1]
         else:
             chips = join(arrived)
@@ -134,11 +137,18 @@
 
 
 def places(groups):
-    origins = [source // 2 for group in groups if not group.crossed for source in group.sources]
-    return np.stack(origins, 1).astype(np.int32)
-
-
-def norm_kernel(lengths_far, hidden_far, gain_far, out, lengths, hidden, gain, arrived):
+    return [(source // 2)[::2] for group in groups if not group.crossed for source in group.sources]
+
+
+def look_up(values):
+    chip = lax.axis_index("gx") // 2
+    found = jnp.int32(int(values[0]))
+    for at in range(1, len(values)):
+        found = jnp.where(chip == at, jnp.int32(int(values[at])), found)
+    return found
+
+
+def norm_kernel(lengths_far, hidden_far, gain_far, out, spread, lengths, hidden, gain, arrived):
     copies = [
         pltpu.make_async_copy(far, near, arrived.at[at])
         for at, (far, near) in enumerate(((hidden_far, hidden), (gain_far, gain), (lengths_far, lengths)))
@@ -161,15 +171,20 @@
         position = jnp.where(line // steps == row, position + lengths[row], position)
     tag = jnp.where(lane == 0, position // 32, position % 32)
     out[:, width:] = tag.astype(jnp.float32).astype(out.dtype)
+    for row in range(spread.shape[0]):
+        spread[row] = jnp.full(spread.shape[1:], lengths[row], spread.dtype)
 
 
 def norm(hidden, gain, lengths):
     steps, rows, width = hidden.shape
     return pl.pallas_call(
         norm_kernel,
-        out_shape=jax.ShapeDtypeStruct((steps * rows, width + TAG), jnp.bfloat16),
+        out_shape=[
+            jax.ShapeDtypeStruct((steps * rows, width + TAG), jnp.bfloat16),
+            jax.ShapeDtypeStruct((rows, 8, HD), jnp.int32),
+        ],
         in_specs=[HBM] * 3,
-        out_specs=VMEM,
+        out_specs=[VMEM] * 2,
         scratch_shapes=[
             pltpu.SMEM(lengths.shape, lengths.dtype),
             pltpu.VMEM(hidden.shape, hidden.dtype),
@@ -221,10 +236,12 @@
     return jnp.concatenate([ref[at, :, lanes] for ref, at in slots], 0)
 
 
-def multiply(slots, weights, depth, total, kept):
+def multiply(slots, weights, depth, total, kept, copy=None):
     total[...] = jnp.zeros_like(total)
     chunk = 0
     for part in weights:
+        if copy is not None and part is weights[-1]:
+            copy.wait()
         for at in range(0, part.shape[0], depth):
             kept[chunk] = assemble(slots, chunk * depth, depth)
             total[...] += jnp.dot(kept[chunk], part[at : at + depth, :], preferred_element_type=jnp.float32)
@@ -314,7 +331,7 @@
 def pack_kernel(place, near, far, near_sum, far_sum, out):
     tile, lines = near.shape[1], near_sum.shape[1]
     for slot in range(near.shape[0]):
-        chip = place[lax.axis_index("gx"), slot]
+        chip = look_up(place[slot])
         out[chip, :tile, :] = near[slot]
         out[chip, tile : 2 * tile, :] = far[slot]
         total = near_sum[slot] + far_sum[slot]
@@ -326,60 +343,64 @@
 def pack(place, near, far, near_sum, far_sum):
     chips, tile, _ = near.shape
     return pl.pallas_call(
-        pack_kernel,
+        functools.partial(pack_kernel, place),
         out_shape=jax.ShapeDtypeStruct((chips, 2 * tile + 2 * near_sum.shape[1], HD), jnp.bfloat16),
-        in_specs=[SMEM] + [VMEM] * 4,
+        in_specs=[VMEM] * 4,
         out_specs=VMEM,
         compiler_params=pltpu.CompilerParams(vmem_limit_bytes=VMEM_LIMIT),
-    )(place, near, far, near_sum, far_sum)
+    )(near, far, near_sum, far_sum)
 
 
 def pair_kernel(place, near, far, out):
     for slot in range(near.shape[0]):
-        chip = place[lax.axis_index("gx"), slot]
+        chip = look_up(place[slot])
         out[chip, 0] = near[slot]
         out[chip, 1] = far[slot]
 
 
 def pair(place, near, far):
     return pl.pallas_call(
-        pair_kernel,
+        functools.partial(pair_kernel, place),
         out_shape=jax.ShapeDtypeStruct((near.shape[0], 2, *near.shape[1:]), near.dtype),
-        in_specs=[SMEM] + [VMEM] * 2,
+        in_specs=[VMEM] * 2,
         out_specs=VMEM,
         compiler_params=pltpu.CompilerParams(vmem_limit_bytes=VMEM_LIMIT),
-    )(place, near, far)
+    )(near, far)
 
 
 def out_kernel(counts, crossed, *refs):
     slots = slots_of(refs, counts)
-    *weights, near, far, kept, total = refs[len(counts) :]
-    multiply(slots, weights, kept.shape[2], total, kept)
+    *weights, rest, near, far, last, kept, total, arrived = refs[len(counts) :]
+    copy = pltpu.make_async_copy(rest.at[pl.ds(rest.shape[0] - last.shape[0], last.shape[0])], last, arrived)
+    copy.start()
+    multiply(slots, weights + [last], kept.shape[2], total, kept, copy)
     own = near.shape[1]
     for slot in range(len(slots)):
         (near, far)[crossed[slot][0]][crossed[slot][1]] = total[slot * own : (slot + 1) * own].astype(near.dtype)
 
 
-def project_out(groups, w_out, devices):
+def project_out(groups, fetched, w_out, devices):
     counts, crossed = group_shape(groups)
-    columns = w_out[0].shape[1]
+    columns = w_out.shape[1]
     own, width = groups[0].blocks.shape[1:]
     chunks = devices // 2
     piece = jax.ShapeDtypeStruct((devices // 2, own, columns), jnp.bfloat16)
     return pl.pallas_call(
         functools.partial(out_kernel, counts, crossed),
         out_shape=[piece, piece],
-        in_specs=[VMEM] * (len(groups) + len(w_out)),
+        in_specs=[VMEM] * (len(groups) + len(fetched)) + [HBM],
         out_specs=[VMEM, VMEM],
         scratch_shapes=[
+            pltpu.VMEM((width - sum(part.shape[0] for part in fetched), columns), w_out.dtype),
             pltpu.VMEM((chunks, devices * own, width // chunks), jnp.bfloat16),
             pltpu.VMEM((devices * own, columns), jnp.float32),
+            pltpu.SemaphoreType.DMA(()),
         ],
         compiler_params=pltpu.CompilerParams(vmem_limit_bytes=VMEM_LIMIT),
         cost_estimate=pl.CostEstimate(
             flops=2 * devices * own * columns * width, bytes_accessed=2 * columns * width, transcendentals=0
         ),
-    )(*[group.blocks for group in groups], *w_out)
+    )(*[group.blocks for group in groups], *fetched, pltpu.with_memory_space_constraint(w_out, pltpu.HBM))
 
 
 def attend_kernel(devices, kv_heads, tile, lengths, pieces, cache, out, fresh, queries, mixed):
@@ -393,7 +414,7 @@
             piece = pieces[chip, other * tile : (other + 1) * tile, :]
             queries[2 * chip + (lax.axis_index("gx") % 2 + other) % 2] = piece.astype(jnp.float32)
     line = lax.broadcasted_iota(jnp.int32, (8, 1), 0)
-    first = jnp.where(line % 4 < 2, lengths[0], lengths[1])
+    first = jnp.where(line % 4 < 2, lengths[0, :, :1], lengths[1, :, :1])
     cosine, sine = turns((first + line % 2).astype(jnp.float32))
     total = jnp.sum(pieces[:, 2 * tile :, :].astype(jnp.float32), 0)
     total = total[: total.shape[0] // 2] + total[total.shape[0] // 2 :]
@@ -419,7 +440,7 @@
         own_lane = lax.broadcasted_iota(jnp.int32, spread.shape, 1) // HD
         spread = jnp.where(own_row == own_lane, spread, 0.0).astype(jnp.bfloat16)
         scores = lax.dot_general(spread, cache[0, row], across, preferred_element_type=jnp.float32) * scale
-        scores = jnp.where(column < lengths[row], scores, -jnp.inf)
+        scores = jnp.where(column < lengths[row, :1, :1], scores, -jnp.inf)
         new_scores = lax.dot_general(spread, fresh[0, row], across, preferred_element_type=jnp.float32) * scale
         new_scores = jnp.where(new_column <= step, new_scores, -jnp.inf)
         peak = jnp.maximum(jnp.max(scores, 1, keepdims=True), jnp.max(new_scores, 1, keepdims=True))
@@ -444,7 +465,7 @@
     return pl.pallas_call(
         functools.partial(attend_kernel, devices, width // HD, tile),
         out_shape=jax.ShapeDtypeStruct((4, columns), jnp.bfloat16),
-        in_specs=[SMEM, VMEM, VMEM],
+        in_specs=[VMEM] * 3,
         out_specs=VMEM,
         scratch_shapes=[
             pltpu.VMEM((2, 2, HD, width), cache.dtype),
@@ -485,7 +506,7 @@
     steps = hidden.shape[0]
     devices = lax.axis_size("gx")
 
-    normed = norm(hidden, norm_gain, lengths)
+    normed, lengths = norm(hidden, norm_gain, lengths)
     cut = w_query.shape[0] * 3 // 4
     fetched = []
 
@@ -503,17 +524,17 @@
         bring((w_keyval, 0, 2), (kv_cache, 0, 2)),
         bring((w_query, cut, w_query.shape[0] - cut), (w_out, 0, part)),
     ]
-    groups = gather(normed, devices, waits)
+    groups = gather(normed, devices, waits, inner_first=True)
     w_first, w_keyval, kv_cache, w_second, w_out_first = fetched
-    place = jnp.asarray(places(groups))
+    place = places(groups)
     near, far, near_sum, far_sum = project(groups, [w_first, w_second], w_keyval, devices)
     pieces = pack(place, near, swap_cores(far, devices), near_sum, swap_cores(far_sum, devices))
 
     mixed = attend(exchange(pieces, devices), near.shape[1], kv_cache, lengths, devices)
     fetched = [w_out_first]
-    waits = [bring((w_out, first * part, count * part)) for first, count in ((1, 2), (3, 3), (6, 2))]
+    waits = [bring((w_out, first * part, count * part)) for first, count in ((1, 2), (3, 1), (4, 2))]
     groups = gather(mixed, devices, waits)
-    near, far = project_out(groups, fetched, devices)
+    near, far = project_out(groups, fetched, w_out, devices)
     pieces = pair(place, near, swap_cores(far, devices))
     return finish(exchange(pieces, devices), steps, devices)
 

time: 81 us -> 79.7 us (0.984)
  Pallas kernels: 30.5 us -> 28.5 us
  waiting for transfers between devices: 6.62 us -> 7.44 us
    pallas_call x3, Pallas kernels: 2.84 us -> 1.51 us  [the longest x1 1.45 us: norm(): pl.pallas_call(norm_kernel, out_shape=[jax.ShapeDtypeStruct((steps * rows...]
    pallas_call x6, Pallas kernels: 17.9 us -> 16.6 us  [fetch(): pl.pallas_call(functools.partial(fetch_kernel, [first for _, first, _ in...]
    pallas_call x1, Pallas kernels: 3.05 us -> 4.14 us  [project_out(): pl.pallas_call(functools.partial(out_kernel, counts, crossed), out_shape=...]
    ppermute x25, waiting for transfers between devices: 6.62 us -> 7.44 us  [permute(): lax.ppermute(block, 'gx', [(int(i), int(t)) for i, t in enumerate(target)])]
  transfers between devices with their start and end apart: 25 -> 25, of which waited for: 7 -> 8; matrix products, arithmetic and copies ran while one was open for 0% -> 0% of each run, Pallas kernels for 22% -> 21%
where the time goes in v5:
time: 79.7 us; the launch traced here: 79.4 us
  Pallas kernels  28.5 us (36%)
  blocking collectives  23 us (29%)
  starting transfers between devices  19.9 us (25%)
  waiting for transfers between devices  7.44 us (9%)
    all_to_all x2, blocking collectives, exchange(): lax.all_to_all(pieces, 'gx', 0, 0, axis_index_groups=same_core, tiled=True)  23 us
    ppermute x25, starting transfers between devices, permute(): lax.ppermute(block, 'gx', [(int(i), int(t)) for i, t in enumerate(target)])  19.9 us
    pallas_call x6, Pallas kernels, fetch(): pl.pallas_call(functools.partial(fetch_kernel, [first for _, first, _ in...  16.6 us
    ppermute x25, waiting for transfers between devices, permute(): lax.ppermute(block, 'gx', [(int(i), int(t)) for i, t in enumerate(target)])  7.44 us
    pallas_call x1, Pallas kernels, project_out(): pl.pallas_call(functools.partial(out_kernel, counts, crossed), out_shape=...  4.14 us
    pallas_call x1, Pallas kernels, project(): pl.pallas_call(functools.partial(project_kernel, counts, crossed, width),...  3.44 us
    pallas_call x1, Pallas kernels, attend(): pl.pallas_call(functools.partial(attend_kernel, devices, width // HD, til...  1.93 us
  transfers between devices with their start and end apart: 25, of which 8 were waited for; matrix products, arithmetic and copies ran while one was open for 0% of the time, Pallas kernels for 21%

profile of v5, /device:TPU:0, one launch (start us, length us, event | category | flops | bytes accessed | tf_op | source)
XLA Modules:
  0.0 79.4 jit_solution(12168945084390803917)
XLA Ops:
  0.0 1.4 %shard_map.73 = (bf16[4,16512]{1,0:T(4,128)(2,1)S(1)}, s32[2,8,128]{2,1,0:T(8,128)S(1)}) custom-call(s32[2]{0:T(128)} %lengths_far.1, bf16[2,2,16384]{2,1,0:T(2,128)(2,1)} %hidden_far.1, bf16[16384]{0:T(1024)(128)(2,1)} %gain_far.1), custom_call_target="tpu_custom_call" | custom-call | flops 393216 | bytes 262144 | tf_op jit(solution)/shard_map/pallas_call | solution.py:180
  1.5 3.1 %collective-permute-start.3 = (bf16[1,4,16512]{2,1,0:T(4,128)(2,1)S(1)}, bf16[1,4,16512]{2,1,0:T(4,128)(2,1)S(1)}, u32[]{:S(2)}, u32[]{:S(2)}) collective-permute-start(bf16[1,4,16512]{2,1,0:T(4,128)(2,1)S(1)} %bitcast.2), channel_id=1, source_target_pairs={{0,4},{1,5},{2,6},{3,7},{4,12},{5,13},{6,14},{7,15},{8,0},{9,1},{1... | collective-permute-start | bytes 396296 | tf_op jit(solution)/shard_map/ppermute | solution.py:23
  4.5 1.1 %collective-permute-start.2 = (bf16[1,4,16512]{2,1,0:T(4,128)(2,1)S(1)}, bf16[1,4,16512]{2,1,0:T(4,128)(2,1)S(1)}, u32[]{:S(2)}, u32[]{:S(2)}) collective-permute-start(bf16[1,4,16512]{2,1,0:T(4,128)(2,1)S(1)} %bitcast.3), channel_id=1, source_target_pairs={{0,8},{1,9},{2,10},{3,11},{4,0},{5,1},{6,2},{7,3},{8,12},{9,13},{1... | collective-permute-start | bytes 396296 | tf_op jit(solution)/shard_map/ppermute | solution.py:23
  5.6 1.8 %collective-permute-start = (bf16[1,4,16512]{2,1,0:T(4,128)(2,1)S(1)}, bf16[1,4,16512]{2,1,0:T(4,128)(2,1)S(1)}, u32[]{:S(2)}, u32[]{:S(2)}) collective-permute-start(bf16[1,4,16512]{2,1,0:T(4,128)(2,1)S(1)} %bitcast.4), channel_id=1, source_target_pairs={{0,2},{1,3},{2,0},{3,1},{4,6},{5,7},{6,4},{7,5},{8,10},{9,11},{10,... | collective-permute-start | bytes 396296 | tf_op jit(solution)/shard_map/ppermute | solution.py:23
  7.4 4.7 %shard_map.74 = (bf16[12288,512]{1,0:T(8,128)(2,1)S(1)}, f32[8,128]{1,0:T(8,128)S(1)}) custom-call(bf16[16384,512]{1,0:T(8,128)(2,1)} %refs_0_.8, bf16[1,4,16512]{2,1,0:T(4,128)(2,1)S(1)} %bitcast.5), custom_call_target="tpu_custom_call" | custom-call | bytes 12582912 | tf_op jit(solution)/shard_map/pallas_call | solution.py:216
  12.2 1.4 %collective-permute-start.4 = (bf16[2,4,16512]{2,1,0:T(4,128)(2,1)S(1)}, bf16[2,4,16512]{2,1,0:T(4,128)(2,1)S(1)}, u32[]{:S(2)}, u32[]{:S(2)}) collective-permute-start(bf16[2,4,16512]{2,1,0:T(4,128)(2,1)S(1)} %shard_map.75.refs_3_), channel_id=1, source_target_pairs={{0,2},{1,3},{2,0},{3,1},{4,6},{5,7},{6,4},{7,5},{8,10},{9,11},{10,... | collective-permute-start | bytes 792584 | tf_op jit(solution)/shard_map/ppermute | solution.py:23
  13.8 1.7 %collective-permute-start.7 = (bf16[1,4,16512]{2,1,0:T(4,128)(2,1)S(1)}, bf16[1,4,16512]{2,1,0:T(4,128)(2,1)S(1)}, u32[]{:S(2)}, u32[]{:S(2)}) collective-permute-start(bf16[1,4,16512]{2,1,0:T(4,128)(2,1)S(1)} %shard_map.76.refs_2_), channel_id=1, source_target_pairs={{0,8},{1,9},{2,10},{3,11},{4,0},{5,1},{6,2},{7,3},{8,12},{9,13},{1... | collective-permute-start | bytes 396296 | tf_op jit(solution)/shard_map/ppermute | solution.py:23
  15.5 3.0 %shard_map.77 = (bf16[2,1024,512]{2,1,0:T(8,128)(2,1)S(1)}, bf16[2,2,1024,512]{3,2,1,0:T(8,128)(2,1)S(1)}, f32[8,128]{1,0:T(8,128)S(1)}) custom-call(bf16[2,1024,512]{2,1,0:T(8,128)(2,1)} %refs_0_.7, bf16[2,2,1024,512]{3,2,1,0:T(8,128)(2,1)} %refs_1_.2, bf16[1,4,16512]{2,1,0:T(4,128)(2,1)S(1)} %shard_map.76.refs_2_), custom_call_target="tpu_custom_call" | custom-call | bytes 6291456 | tf_op jit(solution)/shard_map/pallas_call | solution.py:216
  20.8 2.9 %shard_map.79 = (bf16[4096,512]{1,0:T(8,128)(2,1)S(1)}, bf16[1024,1024]{1,0:T(8,128)(2,1)S(1)}, f32[8,128]{1,0:T(8,128)S(1)}) custom-call(bf16[16384,512]{1,0:T(8,128)(2,1)} %refs_0_.8, bf16[8192,1024]{1,0:T(8,128)(2,1)} %refs_15_.1, bf16[1,4,16512]{2,1,0:T(4,128)(2,1)S(1)} %shard_map.78.refs_2_.refs_7_), custom_call_target="tpu_custom_call" | custom-call | bytes 6291456 | tf_op jit(solution)/shard_map/pallas_call | solution.py:216
  24.7 1.3 %collective-permute-done.10.refs_10_ = bf16[1,4,16512]{2,1,0:T(4,128)(2,1)S(1)} collective-permute-done((bf16[1,4,16512]{2,1,0:T(4,128)(2,1)S(1)}, bf16[1,4,16512]{2,1,0:T(4,128)(2,1)S(1)}, u32[]{:S(2)}, u32[]{:S(2)}) %collective-permute-start.10) | collective-permute-done | bytes 132128 | tf_op jit(solution)/shard_map/ppermute | solution.py:23
  26.0 3.4 %shard_map.81 = (bf16[8,16,128]{2,1,0:T(8,128)(2,1)S(1)}, bf16[8,16,128]{2,1,0:T(8,128)(2,1)S(1)}, f32[8,32,128]{2,1,0:T(8,128)S(1)}, f32[8,32,128]{2,1,0:T(8,128)S(1)}) custom-call(bf16[1,4,16512]{2,1,0:T(4,128)(2,1)S(1)} %bitcast.7, bf16[1,4,16512]{2,1,0:T(4,128)(2,1)S(1)} %collective-permute-done.refs_1_, ...), custom_call_target="tpu_custom_call" | custom-call | flops 1073741824 | bytes 16777216 | tf_op jit(solution)/shard_map/pallas_call | solution.py:314
  30.9 12.6 %all_to_all.10.pieces = bf16[8,96,128]{2,1,0:T(8,128)(2,1)S(1)} all-to-all(bf16[8,96,128]{2,1,0:T(8,128)(2,1)S(1)} %shard_map.82), channel_id=1, replica_groups={{0,2,4,6,8,10,12,14},{1,3,5,7,9,11,13,15},{16,18,20,22,24,26,28,30},{17..., dimensions={0} | all-to-all | bytes 393216 | tf_op jit(solution)/shard_map/all_to_all | solution.py:136
  43.5 1.9 %shard_map.83 = bf16[4,8192]{1,0:T(4,128)(2,1)S(1)} custom-call(s32[2,8,128]{2,1,0:T(8,128)S(1)} %get-tuple-element.29.lengths, bf16[8,96,128]{2,1,0:T(8,128)(2,1)S(1)} %all_to_all.10.pieces, bf16[2,2,1024,512]{3,2,1,0:T(8,128)(2,1)S(1)} %get-tuple-element.41.cache), custom_call_target="tpu_custom_call" | custom-call | flops 536870912 | bytes 4194304 | tf_op jit(solution)/shard_map/pallas_call | solution.py:465
  45.7 2.7 %collective-permute-start.15 = (bf16[1,4,8192]{2,1,0:T(4,128)(2,1)S(1)}, bf16[1,4,8192]{2,1,0:T(4,128)(2,1)S(1)}, u32[]{:S(2)}, u32[]{:S(2)}) collective-permute-start(bf16[1,4,8192]{2,1,0:T(4,128)(2,1)S(1)} %bitcast.9), channel_id=1, source_target_pairs={{0,8},{1,9},{2,10},{3,11},{4,0},{5,1},{6,2},{7,3},{8,12},{9,13},{1... | collective-permute-start | bytes 196616 | tf_op jit(solution)/shard_map/ppermute | solution.py:23
  48.4 1.0 %collective-permute-start.13 = (bf16[1,4,8192]{2,1,0:T(4,128)(2,1)S(1)}, bf16[1,4,8192]{2,1,0:T(4,128)(2,1)S(1)}, u32[]{:S(2)}, u32[]{:S(2)}) collective-permute-start(bf16[1,4,8192]{2,1,0:T(4,128)(2,1)S(1)} %bitcast.10), channel_id=1, source_target_pairs={{0,2},{1,3},{2,0},{3,1},{4,6},{5,7},{6,4},{7,5},{8,10},{9,11},{10,... | collective-permute-start | bytes 196616 | tf_op jit(solution)/shard_map/ppermute | solution.py:23
  49.4 2.2 %shard_map.84 = (bf16[2048,1024]{1,0:T(8,128)(2,1)S(1)}, f32[8,128]{1,0:T(8,128)S(1)}) custom-call(bf16[8192,1024]{1,0:T(8,128)(2,1)} %refs_15_.1, bf16[1,4,8192]{2,1,0:T(4,128)(2,1)S(1)} %bitcast.11), custom_call_target="tpu_custom_call" | custom-call | bytes 4194304 | tf_op jit(solution)/shard_map/pallas_call | solution.py:216
  51.7 2.0 %collective-permute-start.20 = (bf16[1,4,8192]{2,1,0:T(4,128)(2,1)S(1)}, bf16[1,4,8192]{2,1,0:T(4,128)(2,1)S(1)}, u32[]{:S(2)}, u32[]{:S(2)}) collective-permute-start(bf16[1,4,8192]{2,1,0:T(4,128)(2,1)S(1)} %get-tuple-element.44.refs_1_), channel_id=1, source_target_pairs={{0,8},{1,9},{2,10},{3,11},{4,0},{5,1},{6,2},{7,3},{8,12},{9,13},{1... | collective-permute-start | bytes 196616 | tf_op jit(solution)/shard_map/ppermute | solution.py:23
  54.7 1.6 %shard_map.86 = (bf16[1024,1024]{1,0:T(8,128)(2,1)S(1)}, f32[8,128]{1,0:T(8,128)S(1)}) custom-call(bf16[8192,1024]{1,0:T(8,128)(2,1)} %refs_15_.1, bf16[1,4,8192]{2,1,0:T(4,128)(2,1)S(1)} %get-tuple-element.44.refs_1_), custom_call_target="tpu_custom_call" | custom-call | bytes 2097152 | tf_op jit(solution)/shard_map/pallas_call | solution.py:216
  56.4 1.1 %collective-permute-start.21 = (bf16[1,4,8192]{2,1,0:T(4,128)(2,1)S(1)}, bf16[1,4,8192]{2,1,0:T(4,128)(2,1)S(1)}, u32[]{:S(2)}, u32[]{:S(2)}) collective-permute-start(bf16[1,4,8192]{2,1,0:T(4,128)(2,1)S(1)} %shard_map.87.refs_1_.refs_7_), channel_id=1, source_target_pairs={{0,2},{1,3},{2,0},{3,1},{4,6},{5,7},{6,4},{7,5},{8,10},{9,11},{10,... | collective-permute-start | bytes 196616 | tf_op jit(solution)/shard_map/ppermute | solution.py:23
  59.1 2.2 %shard_map.88 = (bf16[2048,1024]{1,0:T(8,128)(2,1)S(1)}, f32[8,128]{1,0:T(8,128)S(1)}) custom-call(bf16[8192,1024]{1,0:T(8,128)(2,1)} %refs_15_.1, bf16[1,4,8192]{2,1,0:T(4,128)(2,1)S(1)} %shard_map.87.refs_1_.refs_7_), custom_call_target="tpu_custom_call" | custom-call | bytes 4194304 | tf_op jit(solution)/shard_map/pallas_call | solution.py:216
  61.5 1.2 %collective-permute-done.23.refs_10_ = bf16[1,4,8192]{2,1,0:T(4,128)(2,1)S(1)} collective-permute-done((bf16[1,4,8192]{2,1,0:T(4,128)(2,1)S(1)}, bf16[1,4,8192]{2,1,0:T(4,128)(2,1)S(1)}, u32[]{:S(2)}, u32[]{:S(2)}) %collective-permute-start.23) | collective-permute-done | bytes 65568 | tf_op jit(solution)/shard_map/ppermute | solution.py:23
  62.7 4.1 %shard_map.90 = (bf16[8,4,1024]{2,1,0:T(4,128)(2,1)S(1)}, bf16[8,4,1024]{2,1,0:T(4,128)(2,1)S(1)}) custom-call(bf16[1,4,8192]{2,1,0:T(4,128)(2,1)S(1)} %bitcast.13, bf16[1,4,8192]{2,1,0:T(4,128)(2,1)S(1)} %collective-permute-done.13.refs_1_, bf16[2,4,8192]{2,1,0:T(4,128)(2,1)S(1)} %collective-permute-done.14.refs_2_, ...), custom_call_target="tpu_custom_call" | custom-call | flops 1073741824 | bytes 16777216 | tf_op jit(solution)/shard_map/pallas_call | solution.py:388
  67.1 1.1 %collective-permute-done.24.far = bf16[8,4,1024]{2,1,0:T(4,128)(2,1)S(1)} collective-permute-done((bf16[8,4,1024]{2,1,0:T(4,128)(2,1)S(1)}, bf16[8,4,1024]{2,1,0:T(4,128)(2,1)S(1)}, u32[]{:S(2)}, u32[]{:S(2)}) %collective-permute-start.24) | collective-permute-done | bytes 65568 | tf_op jit(solution)/shard_map/ppermute | solution.py:23
  68.2 10.5 %all_to_all.11.pieces = bf16[8,2,4,1024]{3,2,1,0:T(4,128)(2,1)S(1)} all-to-all(bf16[8,2,4,1024]{3,2,1,0:T(4,128)(2,1)S(1)} %shard_map.91), channel_id=1, replica_groups={{0,2,4,6,8,10,12,14},{1,3,5,7,9,11,13,15},{16,18,20,22,24,26,28,30},{17..., dimensions={0} | all-to-all | bytes 262144 | tf_op jit(solution)/shard_map/all_to_all | solution.py:136
  (50 shorter events, 9.0 us)
Async XLA Ops:
  1.5 10.7 %collective-permute-start.3 = (bf16[1,4,16512]{2,1,0:T(4,128)(2,1)S(1)}, bf16[1,4,16512]{2,1,0:T(4,128)(2,1)S(1)}, u32[]{:S(2)}, u32[]{:S(2)}) collective-permute-start(bf16[1,4,16512]{2,1,0:T(4,128)(2,1)S(1)} %bitcast.2), channel_id=1, source_target_pairs={{0,4},{1,5},{2,6},{3,7},{4,12},{5,13},{6,14},{7,15},{8,0},{9,1},{1... | collective-permute-start | bytes 396296 | tf_op jit(solution)/shard_map/ppermute | solution.py:23
  4.5 7.6 %collective-permute-start.2 = (bf16[1,4,16512]{2,1,0:T(4,128)(2,1)S(1)}, bf16[1,4,16512]{2,1,0:T(4,128)(2,1)S(1)}, u32[]{:S(2)}, u32[]{:S(2)}) collective-permute-start(bf16[1,4,16512]{2,1,0:T(4,128)(2,1)S(1)} %bitcast.3), channel_id=1, source_target_pairs={{0,8},{1,9},{2,10},{3,11},{4,0},{5,1},{6,2},{7,3},{8,12},{9,13},{1... | collective-permute-start | bytes 396296 | tf_op jit(solution)/shard_map/ppermute | solution.py:23
  5.6 7.9 %collective-permute-start = (bf16[1,4,16512]{2,1,0:T(4,128)(2,1)S(1)}, bf16[1,4,16512]{2,1,0:T(4,128)(2,1)S(1)}, u32[]{:S(2)}, u32[]{:S(2)}) collective-permute-start(bf16[1,4,16512]{2,1,0:T(4,128)(2,1)S(1)} %bitcast.4), channel_id=1, source_target_pairs={{0,2},{1,3},{2,0},{3,1},{4,6},{5,7},{6,4},{7,5},{8,10},{9,11},{10,... | collective-permute-start | bytes 396296 | tf_op jit(solution)/shard_map/ppermute | solution.py:23
  12.2 8.1 %collective-permute-start.4 = (bf16[2,4,16512]{2,1,0:T(4,128)(2,1)S(1)}, bf16[2,4,16512]{2,1,0:T(4,128)(2,1)S(1)}, u32[]{:S(2)}, u32[]{:S(2)}) collective-permute-start(bf16[2,4,16512]{2,1,0:T(4,128)(2,1)S(1)} %shard_map.75.refs_3_), channel_id=1, source_target_pairs={{0,2},{1,3},{2,0},{3,1},{4,6},{5,7},{6,4},{7,5},{8,10},{9,11},{10,... | collective-permute-start | bytes 792584 | tf_op jit(solution)/shard_map/ppermute | solution.py:23
  13.8 5.2 %collective-permute-start.7 = (bf16[1,4,16512]{2,1,0:T(4,128)(2,1)S(1)}, bf16[1,4,16512]{2,1,0:T(4,128)(2,1)S(1)}, u32[]{:S(2)}, u32[]{:S(2)}) collective-permute-start(bf16[1,4,16512]{2,1,0:T(4,128)(2,1)S(1)} %shard_map.76.refs_2_), channel_id=1, source_target_pairs={{0,8},{1,9},{2,10},{3,11},{4,0},{5,1},{6,2},{7,3},{8,12},{9,13},{1... | collective-permute-start | bytes 396296 | tf_op jit(solution)/shard_map/ppermute | solution.py:23
  15.5 9.1 %collective-permute-start.1 = (bf16[2,4,16512]{2,1,0:T(4,128)(2,1)S(1)}, bf16[2,4,16512]{2,1,0:T(4,128)(2,1)S(1)}, u32[]{:S(2)}, u32[]{:S(2)}) collective-permute-start(bf16[2,4,16512]{2,1,0:T(4,128)(2,1)S(1)} %pad_maximum_fusion.refs_1_), channel_id=1, source_target_pairs={{0,1},{1,0},{2,3},{3,2},{4,5},{5,4},{6,7},{7,6},{8,9},{9,8},{10,11... | collective-permute-start | bytes 792584 | tf_op jit(solution)/shard_map/ppermute | solution.py:23
  19.0 5.6 %collective-permute-start.8 = (bf16[1,4,16512]{2,1,0:T(4,128)(2,1)S(1)}, bf16[1,4,16512]{2,1,0:T(4,128)(2,1)S(1)}, u32[]{:S(2)}, u32[]{:S(2)}) collective-permute-start(bf16[1,4,16512]{2,1,0:T(4,128)(2,1)S(1)} %shard_map.78.refs_2_.refs_7_), channel_id=1, source_target_pairs={{0,2},{1,3},{2,0},{3,1},{4,6},{5,7},{6,4},{7,5},{8,10},{9,11},{10,... | collective-permute-start | bytes 396296 | tf_op jit(solution)/shard_map/ppermute | solution.py:23
  19.6 5.1 %collective-permute-start.5 = (bf16[2,4,16512]{2,1,0:T(4,128)(2,1)S(1)}, bf16[2,4,16512]{2,1,0:T(4,128)(2,1)S(1)}, u32[]{:S(2)}, u32[]{:S(2)}) collective-permute-start(bf16[2,4,16512]{2,1,0:T(4,128)(2,1)S(1)} %shard_map.75.refs_3_), channel_id=1, source_target_pairs={{0,1},{1,0},{2,3},{3,2},{4,5},{5,4},{6,7},{7,6},{8,9},{9,8},{10,11... | collective-permute-start | bytes 792584 | tf_op jit(solution)/shard_map/ppermute | solution.py:23
  20.3 5.7 %collective-permute-start.6 = (bf16[2,4,16512]{2,1,0:T(4,128)(2,1)S(1)}, bf16[2,4,16512]{2,1,0:T(4,128)(2,1)S(1)}, u32[]{:S(2)}, u32[]{:S(2)}) collective-permute-start(bf16[2,4,16512]{2,1,0:T(4,128)(2,1)S(1)} %collective-permute-done.4.refs_4_), channel_id=1, source_target_pairs={{0,1},{1,0},{2,3},{3,2},{4,5},{5,4},{6,7},{7,6},{8,9},{9,8},{10,11... | collective-permute-start | bytes 792584 | tf_op jit(solution)/shard_map/ppermute | solution.py:23
  20.3 4.4 %collective-permute-start.9 = (bf16[1,4,16512]{2,1,0:T(4,128)(2,1)S(1)}, bf16[1,4,16512]{2,1,0:T(4,128)(2,1)S(1)}, u32[]{:S(2)}, u32[]{:S(2)}) collective-permute-start(bf16[1,4,16512]{2,1,0:T(4,128)(2,1)S(1)} %shard_map.78.refs_2_.refs_7_), channel_id=1, source_target_pairs={{0,1},{1,0},{2,3},{3,2},{4,5},{5,4},{6,7},{7,6},{8,9},{9,8},{10,11... | collective-permute-start | bytes 396296 | tf_op jit(solution)/shard_map/ppermute | solution.py:23
  24.6 1.4 %collective-permute-start.10 = (bf16[1,4,16512]{2,1,0:T(4,128)(2,1)S(1)}, bf16[1,4,16512]{2,1,0:T(4,128)(2,1)S(1)}, u32[]{:S(2)}, u32[]{:S(2)}) collective-permute-start(bf16[1,4,16512]{2,1,0:T(4,128)(2,1)S(1)} %shard_map.80.refs_8_), channel_id=1, source_target_pairs={{0,1},{1,0},{2,3},{3,2},{4,5},{5,4},{6,7},{7,6},{8,9},{9,8},{10,11... | collective-permute-start | bytes 396296 | tf_op jit(solution)/shard_map/ppermute | solution.py:23
  29.4 1.5 %collective-permute-start.12 = (f32[8,32,128]{2,1,0:T(8,128)S(1)}, f32[8,32,128]{2,1,0:T(8,128)S(1)}, u32[]{:S(2)}, u32[]{:S(2)}) collective-permute-start(f32[8,32,128]{2,1,0:T(8,128)S(1)} %get-tuple-element.40), channel_id=1, source_target_pairs={{0,1},{1,0},{2,3},{3,2},{4,5},{5,4},{6,7},{7,6},{8,9},{9,8},{10,11... | collective-permute-start | bytes 393224 | tf_op jit(solution)/shard_map/ppermute | solution.py:23
  45.4 6.2 %collective-permute-start.16 = (bf16[1,4,8192]{2,1,0:T(4,128)(2,1)S(1)}, bf16[1,4,8192]{2,1,0:T(4,128)(2,1)S(1)}, u32[]{:S(2)}, u32[]{:S(2)}) collective-permute-start(bf16[1,4,8192]{2,1,0:T(4,128)(2,1)S(1)} %bitcast.8), channel_id=1, source_target_pairs={{0,4},{1,5},{2,6},{3,7},{4,12},{5,13},{6,14},{7,15},{8,0},{9,1},{1... | collective-permute-start | bytes 196616 | tf_op jit(solution)/shard_map/ppermute | solution.py:23
  45.7 6.0 %collective-permute-start.15 = (bf16[1,4,8192]{2,1,0:T(4,128)(2,1)S(1)}, bf16[1,4,8192]{2,1,0:T(4,128)(2,1)S(1)}, u32[]{:S(2)}, u32[]{:S(2)}) collective-permute-start(bf16[1,4,8192]{2,1,0:T(4,128)(2,1)S(1)} %bitcast.9), channel_id=1, source_target_pairs={{0,8},{1,9},{2,10},{3,11},{4,0},{5,1},{6,2},{7,3},{8,12},{9,13},{1... | collective-permute-start | bytes 196616 | tf_op jit(solution)/shard_map/ppermute | solution.py:23
  48.4 6.2 %collective-permute-start.13 = (bf16[1,4,8192]{2,1,0:T(4,128)(2,1)S(1)}, bf16[1,4,8192]{2,1,0:T(4,128)(2,1)S(1)}, u32[]{:S(2)}, u32[]{:S(2)}) collective-permute-start(bf16[1,4,8192]{2,1,0:T(4,128)(2,1)S(1)} %bitcast.10), channel_id=1, source_target_pairs={{0,2},{1,3},{2,0},{3,1},{4,6},{5,7},{6,4},{7,5},{8,10},{9,11},{10,... | collective-permute-start | bytes 196616 | tf_op jit(solution)/shard_map/ppermute | solution.py:23
  51.7 4.7 %collective-permute-start.20 = (bf16[1,4,8192]{2,1,0:T(4,128)(2,1)S(1)}, bf16[1,4,8192]{2,1,0:T(4,128)(2,1)S(1)}, u32[]{:S(2)}, u32[]{:S(2)}) collective-permute-start(bf16[1,4,8192]{2,1,0:T(4,128)(2,1)S(1)} %get-tuple-element.44.refs_1_), channel_id=1, source_target_pairs={{0,8},{1,9},{2,10},{3,11},{4,0},{5,1},{6,2},{7,3},{8,12},{9,13},{1... | collective-permute-start | bytes 196616 | tf_op jit(solution)/shard_map/ppermute | solution.py:23
  53.6 5.0 %collective-permute-start.17 = (bf16[2,4,8192]{2,1,0:T(4,128)(2,1)S(1)}, bf16[2,4,8192]{2,1,0:T(4,128)(2,1)S(1)}, u32[]{:S(2)}, u32[]{:S(2)}) collective-permute-start(bf16[2,4,8192]{2,1,0:T(4,128)(2,1)S(1)} %get-tuple-element.43.refs_3_), channel_id=1, source_target_pairs={{0,2},{1,3},{2,0},{3,1},{4,6},{5,7},{6,4},{7,5},{8,10},{9,11},{10,... | collective-permute-start | bytes 393224 | tf_op jit(solution)/shard_map/ppermute | solution.py:23
  56.3 5.1 %collective-permute-start.14 = (bf16[2,4,8192]{2,1,0:T(4,128)(2,1)S(1)}, bf16[2,4,8192]{2,1,0:T(4,128)(2,1)S(1)}, u32[]{:S(2)}, u32[]{:S(2)}) collective-permute-start(bf16[2,4,8192]{2,1,0:T(4,128)(2,1)S(1)} %pad_maximum_fusion.1), channel_id=1, source_target_pairs={{0,1},{1,0},{2,3},{3,2},{4,5},{5,4},{6,7},{7,6},{8,9},{9,8},{10,11... | collective-permute-start | bytes 393224 | tf_op jit(solution)/shard_map/ppermute | solution.py:23
  56.4 4.9 %collective-permute-start.21 = (bf16[1,4,8192]{2,1,0:T(4,128)(2,1)S(1)}, bf16[1,4,8192]{2,1,0:T(4,128)(2,1)S(1)}, u32[]{:S(2)}, u32[]{:S(2)}) collective-permute-start(bf16[1,4,8192]{2,1,0:T(4,128)(2,1)S(1)} %shard_map.87.refs_1_.refs_7_), channel_id=1, source_target_pairs={{0,2},{1,3},{2,0},{3,1},{4,6},{5,7},{6,4},{7,5},{8,10},{9,11},{10,... | collective-permute-start | bytes 196616 | tf_op jit(solution)/shard_map/ppermute | solution.py:23
  57.5 3.9 %collective-permute-start.18 = (bf16[2,4,8192]{2,1,0:T(4,128)(2,1)S(1)}, bf16[2,4,8192]{2,1,0:T(4,128)(2,1)S(1)}, u32[]{:S(2)}, u32[]{:S(2)}) collective-permute-start(bf16[2,4,8192]{2,1,0:T(4,128)(2,1)S(1)} %get-tuple-element.43.refs_3_), channel_id=1, source_target_pairs={{0,1},{1,0},{2,3},{3,2},{4,5},{5,4},{6,7},{7,6},{8,9},{9,8},{10,11... | collective-permute-start | bytes 393224 | tf_op jit(solution)/shard_map/ppermute | solution.py:23
  58.6 4.1 %collective-permute-start.19 = (bf16[2,4,8192]{2,1,0:T(4,128)(2,1)S(1)}, bf16[2,4,8192]{2,1,0:T(4,128)(2,1)S(1)}, u32[]{:S(2)}, u32[]{:S(2)}) collective-permute-start(bf16[2,4,8192]{2,1,0:T(4,128)(2,1)S(1)} %collective-permute-done.17.refs_4_), channel_id=1, source_target_pairs={{0,1},{1,0},{2,3},{3,2},{4,5},{5,4},{6,7},{7,6},{8,9},{9,8},{10,11... | collective-permute-start | bytes 393224 | tf_op jit(solution)/shard_map/ppermute | solution.py:23
  58.6 2.9 %collective-permute-start.22 = (bf16[1,4,8192]{2,1,0:T(4,128)(2,1)S(1)}, bf16[1,4,8192]{2,1,0:T(4,128)(2,1)S(1)}, u32[]{:S(2)}, u32[]{:S(2)}) collective-permute-start(bf16[1,4,8192]{2,1,0:T(4,128)(2,1)S(1)} %shard_map.87.refs_1_.refs_7_), channel_id=1, source_target_pairs={{0,1},{1,0},{2,3},{3,2},{4,5},{5,4},{6,7},{7,6},{8,9},{9,8},{10,11... | collective-permute-start | bytes 196616 | tf_op jit(solution)/shard_map/ppermute | solution.py:23
  61.4 1.3 %collective-permute-start.23 = (bf16[1,4,8192]{2,1,0:T(4,128)(2,1)S(1)}, bf16[1,4,8192]{2,1,0:T(4,128)(2,1)S(1)}, u32[]{:S(2)}, u32[]{:S(2)}) collective-permute-start(bf16[1,4,8192]{2,1,0:T(4,128)(2,1)S(1)} %shard_map.89.refs_8_), channel_id=1, source_target_pairs={{0,1},{1,0},{2,3},{3,2},{4,5},{5,4},{6,7},{7,6},{8,9},{9,8},{10,11... | collective-permute-start | bytes 196616 | tf_op jit(solution)/shard_map/ppermute | solution.py:23
  66.9 1.3 %collective-permute-start.24 = (bf16[8,4,1024]{2,1,0:T(4,128)(2,1)S(1)}, bf16[8,4,1024]{2,1,0:T(4,128)(2,1)S(1)}, u32[]{:S(2)}, u32[]{:S(2)}) collective-permute-start(bf16[8,4,1024]{2,1,0:T(4,128)(2,1)S(1)} %get-tuple-element.52), channel_id=1, source_target_pairs={{0,1},{1,0},{2,3},{3,2},{4,5},{5,4},{6,7},{7,6},{8,9},{9,8},{10,11... | collective-permute-start | bytes 196616 | tf_op jit(solution)/shard_map/ppermute | solution.py:23
  (1 other events, 1.2 us)

commit v6 on v5

--- a/solution.py
+++ b/solution.py
@@ -105,24 +105,44 @@
     return groups
 
 
-def hold_kernel(count, *refs):
-    stacked, *alone = refs[count + 1 :]
-    for at in range(count):
-        stacked[at] = refs[at][0]
+def gather_direct(block, devices, meanwhile):
+    (size, following, _), inner, core = axes_of(devices)
+    own = Group(block[None], [np.arange(devices)])
+    near = ring(own, inner)
+    groups = [own] + near + [join([own] + near).send(core[1], crossed=True)]
+    arrived, target = [], following
+    for _ in range(size - 1):
+        arrived.append(own.send(target))
+        target = following[target]
+    reached = hold(arrived, 0, meanwhile[0](block), *[group.blocks for group in near])
+    beside = ring(reached[0], inner)
+    if beside:
+        beside[-1:] = hold(beside[-1:], 0, meanwhile[1](reached[0].blocks), groups[-1].blocks)
+    reached += beside
+    return groups + reached + [group.send(core[1], crossed=True) for group in reached]
+
+
+def hold_kernel(count, waits, *refs):
+    stacked, *alone = refs[count + waits :]
+    first = 0
+    for ref in refs[:count]:
+        for at in range(ref.shape[0]):
+            stacked[first + at] = ref[at]
+        first += ref.shape[0]
     for at in range(len(alone)):
         alone[at][...] = refs[at][...]
 
 
-def hold(groups, onward, after):
+def hold(groups, onward, *after):
     blocks = [group.blocks for group in groups]
     stacked, *alone = pl.pallas_call(
-        functools.partial(hold_kernel, len(blocks)),
-        out_shape=[jax.ShapeDtypeStruct((len(blocks), *blocks[0].shape[1:]), blocks[0].dtype)]
+        functools.partial(hold_kernel, len(blocks), len(after)),
+        out_shape=[jax.ShapeDtypeStruct((sum(block.shape[0] for block in blocks), *blocks[0].shape[1:]), blocks[0].dtype)]
         + [jax.ShapeDtypeStruct(block.shape, block.dtype) for block in blocks[:onward]],
-        in_specs=[VMEM] * len(blocks) + [pl.BlockSpec(memory_space=pl.ANY)],
+        in_specs=[VMEM] * len(blocks) + [pl.BlockSpec(memory_space=pl.ANY)] * len(after),
         out_specs=[VMEM] * (onward + 1),
         compiler_params=pltpu.CompilerParams(vmem_limit_bytes=VMEM_LIMIT),
-    )(*blocks, after)
+    )(*blocks, *after)
     sources = [group.sources for group in groups]
     return [Group(stacked, sum(sources, []))] + [Group(block, source) for block, source in zip(alone, sources)]
 
@@ -236,14 +256,14 @@
     return jnp.concatenate([ref[at, :, lanes] for ref, at in slots], 0)
 
 
-def multiply(slots, weights, depth, total, kept, copy=None):
+def multiply(slots, weights, depth, total, kept, copies=()):
     total[...] = jnp.zeros_like(total)
     chunk = 0
     for part in weights:
-        if copy is not None and part is weights[-1]:
-            copy.wait()
         for at in range(0, part.shape[0], depth):
             kept[chunk] = assemble(slots, chunk * depth, depth)
+            if copies and part is weights[-1]:
+                copies[at // depth].wait()
             total[...] += jnp.dot(kept[chunk], part[at : at + depth, :], preferred_element_type=jnp.float32)
             chunk += 1
 
@@ -371,9 +391,12 @@
 def out_kernel(counts, crossed, *refs):
     slots = slots_of(refs, counts)
     *weights, rest, near, far, last, kept, total, arrived = refs[len(counts) :]
-    copy = pltpu.make_async_copy(rest.at[pl.ds(rest.shape[0] - last.shape[0], last.shape[0])], last, arrived)
-    copy.start()
-    multiply(slots, weights + [last], kept.shape[2], total, kept, copy)
+    depth, first, copies = kept.shape[2], rest.shape[0] - last.shape[0], []
+    for at in range(last.shape[0] // depth):
+        source = rest.at[pl.ds(first + at * depth, depth)]
+        copies.append(pltpu.make_async_copy(source, last.at[pl.ds(at * depth, depth)], arrived.at[at]))
+        copies[-1].start()
+    multiply(slots, weights + [last], depth, total, kept, copies)
     own = near.shape[1]
     for slot in range(len(slots)):
         (near, far)[crossed[slot][0]][crossed[slot][1]] = total[slot * own : (slot + 1) * own].astype(near.dtype)
@@ -394,7 +417,7 @@
             pltpu.VMEM((width - sum(part.shape[0] for part in fetched), columns), w_out.dtype),
             pltpu.VMEM((chunks, devices * own, width // chunks), jnp.bfloat16),
             pltpu.VMEM((devices * own, columns), jnp.float32),
-            pltpu.SemaphoreType.DMA(()),
+            pltpu.SemaphoreType.DMA((chunks,)),
         ],
         compiler_params=pltpu.CompilerParams(vmem_limit_bytes=VMEM_LIMIT),
         cost_estimate=pl.CostEstimate(
@@ -532,10 +555,10 @@
 
     mixed = attend(exchange(pieces, devices), near.shape[1], kv_cache, lengths, devices)
     fetched = [w_out_first]
-    waits = [bring((w_out, first * part, count * part)) for first, count in ((1, 2), (3, 1), (4, 2))]
-    groups = gather(mixed, devices, waits)
+    waits = [bring((w_out, first * part, count * part)) for first, count in ((1, 2), (3, 4))]
+    groups = gather_direct(mixed, devices, waits)
     near, far = project_out(groups, fetched, w_out, devices)
-    pieces = pair(place, near, swap_cores(far, devices))
+    pieces = pair(places(groups), near, swap_cores(far, devices))
     return finish(exchange(pieces, devices), steps, devices)
 
 

time: 79.7 us -> 78.9 us (0.990)
  starting transfers between devices: 19.9 us -> 17.8 us
  blocking collectives: 23 us -> 24.7 us
    ppermute x25 -> x22, starting transfers between devices: 19.9 us -> 17.8 us  [permute(): lax.ppermute(block, 'gx', [(int(i), int(t)) for i, t in enumerate(target)])]
    all_to_all x2, blocking collectives: 23 us -> 24.7 us  [exchange(): lax.all_to_all(pieces, 'gx', 0, 0, axis_index_groups=same_core, tiled=True)]
    pallas_call x6 -> x5, Pallas kernels: 16.6 us -> 16.3 us  [fetch(): pl.pallas_call(functools.partial(fetch_kernel, [first for _, first, _ in...]
    ppermute x25 -> x22, waiting for transfers between devices: 7.44 us -> 7.25 us  [permute(): lax.ppermute(block, 'gx', [(int(i), int(t)) for i, t in enumerate(target)])]
  transfers between devices with their start and end apart: 25 -> 22, of which waited for: 8 -> 8; matrix products, arithmetic and copies ran while one was open for 0% -> 0% of each run, Pallas kernels for 21% -> 21%
where the time goes in v6:
time: 78.9 us; the launch traced here: 78.6 us
  Pallas kernels  28.4 us (36%)
  blocking collectives  24.7 us (31%)
  starting transfers between devices  17.8 us (23%)
  waiting for transfers between devices  7.25 us (9%)
    all_to_all x2, blocking collectives, exchange(): lax.all_to_all(pieces, 'gx', 0, 0, axis_index_groups=same_core, tiled=True)  24.7 us
    ppermute x22, starting transfers between devices, permute(): lax.ppermute(block, 'gx', [(int(i), int(t)) for i, t in enumerate(target)])  17.8 us
    pallas_call x5, Pallas kernels, fetch(): pl.pallas_call(functools.partial(fetch_kernel, [first for _, first, _ in...  16.3 us
    ppermute x22, waiting for transfers between devices, permute(): lax.ppermute(block, 'gx', [(int(i), int(t)) for i, t in enumerate(target)])  7.25 us
    pallas_call x1, Pallas kernels, project_out(): pl.pallas_call(functools.partial(out_kernel, counts, crossed), out_shape=...  4.44 us
    pallas_call x1, Pallas kernels, project(): pl.pallas_call(functools.partial(project_kernel, counts, crossed, width),...  3.44 us
    pallas_call x1, Pallas kernels, attend(): pl.pallas_call(functools.partial(attend_kernel, devices, width // HD, til...  1.93 us
  transfers between devices with their start and end apart: 22, of which 8 were waited for; matrix products, arithmetic and copies ran while one was open for 0% of the time, Pallas kernels for 21%

profile of v6, /device:TPU:0, one launch (start us, length us, event | category | flops | bytes accessed | tf_op | source)
XLA Modules:
  0.0 78.6 jit_solution(12748670163619967184)
XLA Ops:
  0.0 1.4 %shard_map.73 = (bf16[4,16512]{1,0:T(4,128)(2,1)S(1)}, s32[2,8,128]{2,1,0:T(8,128)S(1)}) custom-call(s32[2]{0:T(128)} %lengths_far.1, bf16[2,2,16384]{2,1,0:T(2,128)(2,1)} %hidden_far.1, bf16[16384]{0:T(1024)(128)(2,1)} %gain_far.1), custom_call_target="tpu_custom_call" | custom-call | flops 393216 | bytes 262144 | tf_op jit(solution)/shard_map/pallas_call | solution.py:200
  1.5 3.1 %collective-permute-start.3 = (bf16[1,4,16512]{2,1,0:T(4,128)(2,1)S(1)}, bf16[1,4,16512]{2,1,0:T(4,128)(2,1)S(1)}, u32[]{:S(2)}, u32[]{:S(2)}) collective-permute-start(bf16[1,4,16512]{2,1,0:T(4,128)(2,1)S(1)} %bitcast.2), channel_id=1, source_target_pairs={{0,4},{1,5},{2,6},{3,7},{4,12},{5,13},{6,14},{7,15},{8,0},{9,1},{1... | collective-permute-start | bytes 396296 | tf_op jit(solution)/shard_map/ppermute | solution.py:23
  4.5 1.1 %collective-permute-start.2 = (bf16[1,4,16512]{2,1,0:T(4,128)(2,1)S(1)}, bf16[1,4,16512]{2,1,0:T(4,128)(2,1)S(1)}, u32[]{:S(2)}, u32[]{:S(2)}) collective-permute-start(bf16[1,4,16512]{2,1,0:T(4,128)(2,1)S(1)} %bitcast.3), channel_id=1, source_target_pairs={{0,8},{1,9},{2,10},{3,11},{4,0},{5,1},{6,2},{7,3},{8,12},{9,13},{1... | collective-permute-start | bytes 396296 | tf_op jit(solution)/shard_map/ppermute | solution.py:23
  5.6 1.8 %collective-permute-start = (bf16[1,4,16512]{2,1,0:T(4,128)(2,1)S(1)}, bf16[1,4,16512]{2,1,0:T(4,128)(2,1)S(1)}, u32[]{:S(2)}, u32[]{:S(2)}) collective-permute-start(bf16[1,4,16512]{2,1,0:T(4,128)(2,1)S(1)} %bitcast.4), channel_id=1, source_target_pairs={{0,2},{1,3},{2,0},{3,1},{4,6},{5,7},{6,4},{7,5},{8,10},{9,11},{10,... | collective-permute-start | bytes 396296 | tf_op jit(solution)/shard_map/ppermute | solution.py:23
  7.4 4.7 %shard_map.74 = (bf16[12288,512]{1,0:T(8,128)(2,1)S(1)}, f32[8,128]{1,0:T(8,128)S(1)}) custom-call(bf16[16384,512]{1,0:T(8,128)(2,1)} %refs_0_.7, bf16[1,4,16512]{2,1,0:T(4,128)(2,1)S(1)} %bitcast.5), custom_call_target="tpu_custom_call" | custom-call | bytes 12582912 | tf_op jit(solution)/shard_map/pallas_call | solution.py:236
  12.2 1.4 %collective-permute-start.4 = (bf16[2,4,16512]{2,1,0:T(4,128)(2,1)S(1)}, bf16[2,4,16512]{2,1,0:T(4,128)(2,1)S(1)}, u32[]{:S(2)}, u32[]{:S(2)}) collective-permute-start(bf16[2,4,16512]{2,1,0:T(4,128)(2,1)S(1)} %shard_map.75.refs_3_), channel_id=1, source_target_pairs={{0,2},{1,3},{2,0},{3,1},{4,6},{5,7},{6,4},{7,5},{8,10},{9,11},{10,... | collective-permute-start | bytes 792584 | tf_op jit(solution)/shard_map/ppermute | solution.py:23
  13.8 1.7 %collective-permute-start.7 = (bf16[1,4,16512]{2,1,0:T(4,128)(2,1)S(1)}, bf16[1,4,16512]{2,1,0:T(4,128)(2,1)S(1)}, u32[]{:S(2)}, u32[]{:S(2)}) collective-permute-start(bf16[1,4,16512]{2,1,0:T(4,128)(2,1)S(1)} %shard_map.76.refs_2_), channel_id=1, source_target_pairs={{0,8},{1,9},{2,10},{3,11},{4,0},{5,1},{6,2},{7,3},{8,12},{9,13},{1... | collective-permute-start | bytes 396296 | tf_op jit(solution)/shard_map/ppermute | solution.py:23
  15.5 3.0 %shard_map.77 = (bf16[2,1024,512]{2,1,0:T(8,128)(2,1)S(1)}, bf16[2,2,1024,512]{3,2,1,0:T(8,128)(2,1)S(1)}, f32[8,128]{1,0:T(8,128)S(1)}) custom-call(bf16[2,1024,512]{2,1,0:T(8,128)(2,1)} %refs_0_.6, bf16[2,2,1024,512]{3,2,1,0:T(8,128)(2,1)} %refs_1_.2, bf16[1,4,16512]{2,1,0:T(4,128)(2,1)S(1)} %shard_map.76.refs_2_), custom_call_target="tpu_custom_call" | custom-call | bytes 6291456 | tf_op jit(solution)/shard_map/pallas_call | solution.py:236
  20.8 2.9 %shard_map.79 = (bf16[4096,512]{1,0:T(8,128)(2,1)S(1)}, bf16[1024,1024]{1,0:T(8,128)(2,1)S(1)}, f32[8,128]{1,0:T(8,128)S(1)}) custom-call(bf16[16384,512]{1,0:T(8,128)(2,1)} %refs_0_.7, bf16[8192,1024]{1,0:T(8,128)(2,1)} %refs_10_.1, bf16[1,4,16512]{2,1,0:T(4,128)(2,1)S(1)} %shard_map.78.refs_2_.refs_7_), custom_call_target="tpu_custom_call" | custom-call | bytes 6291456 | tf_op jit(solution)/shard_map/pallas_call | solution.py:236
  23.7 0.9 %collective-permute-done.8.refs_0_ = bf16[1,4,16512]{2,1,0:T(4,128)(2,1)S(1)} collective-permute-done((bf16[1,4,16512]{2,1,0:T(4,128)(2,1)S(1)}, bf16[1,4,16512]{2,1,0:T(4,128)(2,1)S(1)}, u32[]{:S(2)}, u32[]{:S(2)}) %collective-permute-start.8) | collective-permute-done | bytes 132128 | tf_op jit(solution)/shard_map/ppermute | solution.py:23
  24.7 1.3 %collective-permute-done.10.refs_10_ = bf16[1,4,16512]{2,1,0:T(4,128)(2,1)S(1)} collective-permute-done((bf16[1,4,16512]{2,1,0:T(4,128)(2,1)S(1)}, bf16[1,4,16512]{2,1,0:T(4,128)(2,1)S(1)}, u32[]{:S(2)}, u32[]{:S(2)}) %collective-permute-start.10) | collective-permute-done | bytes 132128 | tf_op jit(solution)/shard_map/ppermute | solution.py:23
  26.0 3.4 %shard_map.81 = (bf16[8,16,128]{2,1,0:T(8,128)(2,1)S(1)}, bf16[8,16,128]{2,1,0:T(8,128)(2,1)S(1)}, f32[8,32,128]{2,1,0:T(8,128)S(1)}, f32[8,32,128]{2,1,0:T(8,128)S(1)}) custom-call(bf16[1,4,16512]{2,1,0:T(4,128)(2,1)S(1)} %bitcast.7, bf16[1,4,16512]{2,1,0:T(4,128)(2,1)S(1)} %collective-permute-done.refs_1_, ...), custom_call_target="tpu_custom_call" | custom-call | flops 1073741824 | bytes 16777216 | tf_op jit(solution)/shard_map/pallas_call | solution.py:334
  30.0 0.9 %collective-permute-done.11.far = bf16[8,16,128]{2,1,0:T(8,128)(2,1)S(1)} collective-permute-done((bf16[8,16,128]{2,1,0:T(8,128)(2,1)S(1)}, bf16[8,16,128]{2,1,0:T(8,128)(2,1)S(1)}, u32[]{:S(2)}, u32[]{:S(2)}) %collective-permute-start.11) | collective-permute-done | bytes 32800 | tf_op jit(solution)/shard_map/ppermute | solution.py:23
  30.9 12.6 %all_to_all.10.pieces = bf16[8,96,128]{2,1,0:T(8,128)(2,1)S(1)} all-to-all(bf16[8,96,128]{2,1,0:T(8,128)(2,1)S(1)} %shard_map.82), channel_id=1, replica_groups={{0,2,4,6,8,10,12,14},{1,3,5,7,9,11,13,15},{16,18,20,22,24,26,28,30},{17..., dimensions={0} | all-to-all | bytes 393216 | tf_op jit(solution)/shard_map/all_to_all | solution.py:156
  43.5 1.9 %shard_map.83.refs_1_ = bf16[4,8192]{1,0:T(4,128)(2,1)S(1)} custom-call(s32[2,8,128]{2,1,0:T(8,128)S(1)} %get-tuple-element.25.lengths, bf16[8,96,128]{2,1,0:T(8,128)(2,1)S(1)} %all_to_all.10.pieces, bf16[2,2,1024,512]{3,2,1,0:T(8,128)(2,1)S(1)} %get-tuple-element.37.cache), custom_call_target="tpu_custom_call" | custom-call | flops 536870912 | bytes 4194304 | tf_op jit(solution)/shard_map/pallas_call | solution.py:488
  45.7 2.0 %collective-permute-start.16 = (bf16[1,4,8192]{2,1,0:T(4,128)(2,1)S(1)}, bf16[1,4,8192]{2,1,0:T(4,128)(2,1)S(1)}, u32[]{:S(2)}, u32[]{:S(2)}) collective-permute-start(bf16[1,4,8192]{2,1,0:T(4,128)(2,1)S(1)} %bitcast.9), channel_id=1, source_target_pairs={{0,12},{1,13},{2,14},{3,15},{4,8},{5,9},{6,10},{7,11},{8,4},{9,5},... | collective-permute-start | bytes 196616 | tf_op jit(solution)/shard_map/ppermute | solution.py:23
  48.4 1.5 %collective-permute-start.13 = (bf16[1,4,8192]{2,1,0:T(4,128)(2,1)S(1)}, bf16[1,4,8192]{2,1,0:T(4,128)(2,1)S(1)}, u32[]{:S(2)}, u32[]{:S(2)}) collective-permute-start(bf16[1,4,8192]{2,1,0:T(4,128)(2,1)S(1)} %bitcast.11), channel_id=1, source_target_pairs={{0,2},{1,3},{2,0},{3,1},{4,6},{5,7},{6,4},{7,5},{8,10},{9,11},{10,... | collective-permute-start | bytes 196616 | tf_op jit(solution)/shard_map/ppermute | solution.py:23
  49.9 2.2 %shard_map.84 = (bf16[2048,1024]{1,0:T(8,128)(2,1)S(1)}, f32[8,128]{1,0:T(8,128)S(1)}) custom-call(bf16[8192,1024]{1,0:T(8,128)(2,1)} %refs_10_.1, bf16[4,8192]{1,0:T(4,128)(2,1)S(1)} %shard_map.83.refs_1_), custom_call_target="tpu_custom_call" | custom-call | bytes 4194304 | tf_op jit(solution)/shard_map/pallas_call | solution.py:236
  52.7 1.6 %collective-permute-start.18 = (bf16[3,4,8192]{2,1,0:T(4,128)(2,1)S(1)}, bf16[3,4,8192]{2,1,0:T(4,128)(2,1)S(1)}, u32[]{:S(2)}, u32[]{:S(2)}) collective-permute-start(bf16[3,4,8192]{2,1,0:T(4,128)(2,1)S(1)} %shard_map.85.refs_1_.refs_3_), channel_id=1, source_target_pairs={{0,2},{1,3},{2,0},{3,1},{4,6},{5,7},{6,4},{7,5},{8,10},{9,11},{10,... | collective-permute-start | bytes 589832 | tf_op jit(solution)/shard_map/ppermute | solution.py:23
  55.0 3.5 %shard_map.86 = (bf16[4096,1024]{1,0:T(8,128)(2,1)S(1)}, f32[8,128]{1,0:T(8,128)S(1)}) custom-call(bf16[8192,1024]{1,0:T(8,128)(2,1)} %refs_10_.1, bf16[3,4,8192]{2,1,0:T(4,128)(2,1)S(1)} %shard_map.85.refs_1_.refs_3_), custom_call_target="tpu_custom_call" | custom-call | bytes 8388608 | tf_op jit(solution)/shard_map/pallas_call | solution.py:236
  58.6 1.4 %collective-permute-done.20.refs_6_ = bf16[3,4,8192]{2,1,0:T(4,128)(2,1)S(1)} collective-permute-done((bf16[3,4,8192]{2,1,0:T(4,128)(2,1)S(1)}, bf16[3,4,8192]{2,1,0:T(4,128)(2,1)S(1)}, u32[]{:S(2)}, u32[]{:S(2)}) %collective-permute-start.20) | collective-permute-done | bytes 196640 | tf_op jit(solution)/shard_map/ppermute | solution.py:23
  60.0 4.4 %shard_map.88 = (bf16[8,4,1024]{2,1,0:T(4,128)(2,1)S(1)}, bf16[8,4,1024]{2,1,0:T(4,128)(2,1)S(1)}) custom-call(bf16[1,4,8192]{2,1,0:T(4,128)(2,1)S(1)} %bitcast.13, bf16[1,4,8192]{2,1,0:T(4,128)(2,1)S(1)} %collective-permute-done.13.refs_4_.refs_1_, bf16[2,4,8192]{2,1,0:T(4,128)(2,1)S(1)} %collective-permute-done.14.refs_2_, ...), custom_call_target="tpu_custom_call" | custom-call | flops 1073741824 | bytes 16777216 | tf_op jit(solution)/shard_map/pallas_call | solution.py:411
  64.6 1.1 %collective-permute-done.21.far = bf16[8,4,1024]{2,1,0:T(4,128)(2,1)S(1)} collective-permute-done((bf16[8,4,1024]{2,1,0:T(4,128)(2,1)S(1)}, bf16[8,4,1024]{2,1,0:T(4,128)(2,1)S(1)}, u32[]{:S(2)}, u32[]{:S(2)}) %collective-permute-start.21) | collective-permute-done | bytes 65568 | tf_op jit(solution)/shard_map/ppermute | solution.py:23
  65.8 12.1 %all_to_all.11.pieces = bf16[8,2,4,1024]{3,2,1,0:T(4,128)(2,1)S(1)} all-to-all(bf16[8,2,4,1024]{3,2,1,0:T(4,128)(2,1)S(1)} %shard_map.89), channel_id=1, replica_groups={{0,2,4,6,8,10,12,14},{1,3,5,7,9,11,13,15},{16,18,20,22,24,26,28,30},{17..., dimensions={0} | all-to-all | bytes 262144 | tf_op jit(solution)/shard_map/all_to_all | solution.py:156
  (42 shorter events, 6.5 us)
Async XLA Ops:
  1.5 10.7 %collective-permute-start.3 = (bf16[1,4,16512]{2,1,0:T(4,128)(2,1)S(1)}, bf16[1,4,16512]{2,1,0:T(4,128)(2,1)S(1)}, u32[]{:S(2)}, u32[]{:S(2)}) collective-permute-start(bf16[1,4,16512]{2,1,0:T(4,128)(2,1)S(1)} %bitcast.2), channel_id=1, source_target_pairs={{0,4},{1,5},{2,6},{3,7},{4,12},{5,13},{6,14},{7,15},{8,0},{9,1},{1... | collective-permute-start | bytes 396296 | tf_op jit(solution)/shard_map/ppermute | solution.py:23
  4.5 7.6 %collective-permute-start.2 = (bf16[1,4,16512]{2,1,0:T(4,128)(2,1)S(1)}, bf16[1,4,16512]{2,1,0:T(4,128)(2,1)S(1)}, u32[]{:S(2)}, u32[]{:S(2)}) collective-permute-start(bf16[1,4,16512]{2,1,0:T(4,128)(2,1)S(1)} %bitcast.3), channel_id=1, source_target_pairs={{0,8},{1,9},{2,10},{3,11},{4,0},{5,1},{6,2},{7,3},{8,12},{9,13},{1... | collective-permute-start | bytes 396296 | tf_op jit(solution)/shard_map/ppermute | solution.py:23
  5.6 7.9 %collective-permute-start = (bf16[1,4,16512]{2,1,0:T(4,128)(2,1)S(1)}, bf16[1,4,16512]{2,1,0:T(4,128)(2,1)S(1)}, u32[]{:S(2)}, u32[]{:S(2)}) collective-permute-start(bf16[1,4,16512]{2,1,0:T(4,128)(2,1)S(1)} %bitcast.4), channel_id=1, source_target_pairs={{0,2},{1,3},{2,0},{3,1},{4,6},{5,7},{6,4},{7,5},{8,10},{9,11},{10,... | collective-permute-start | bytes 396296 | tf_op jit(solution)/shard_map/ppermute | solution.py:23
  12.2 8.1 %collective-permute-start.4 = (bf16[2,4,16512]{2,1,0:T(4,128)(2,1)S(1)}, bf16[2,4,16512]{2,1,0:T(4,128)(2,1)S(1)}, u32[]{:S(2)}, u32[]{:S(2)}) collective-permute-start(bf16[2,4,16512]{2,1,0:T(4,128)(2,1)S(1)} %shard_map.75.refs_3_), channel_id=1, source_target_pairs={{0,2},{1,3},{2,0},{3,1},{4,6},{5,7},{6,4},{7,5},{8,10},{9,11},{10,... | collective-permute-start | bytes 792584 | tf_op jit(solution)/shard_map/ppermute | solution.py:23
  13.8 5.2 %collective-permute-start.7 = (bf16[1,4,16512]{2,1,0:T(4,128)(2,1)S(1)}, bf16[1,4,16512]{2,1,0:T(4,128)(2,1)S(1)}, u32[]{:S(2)}, u32[]{:S(2)}) collective-permute-start(bf16[1,4,16512]{2,1,0:T(4,128)(2,1)S(1)} %shard_map.76.refs_2_), channel_id=1, source_target_pairs={{0,8},{1,9},{2,10},{3,11},{4,0},{5,1},{6,2},{7,3},{8,12},{9,13},{1... | collective-permute-start | bytes 396296 | tf_op jit(solution)/shard_map/ppermute | solution.py:23
  15.5 9.1 %collective-permute-start.1 = (bf16[2,4,16512]{2,1,0:T(4,128)(2,1)S(1)}, bf16[2,4,16512]{2,1,0:T(4,128)(2,1)S(1)}, u32[]{:S(2)}, u32[]{:S(2)}) collective-permute-start(bf16[2,4,16512]{2,1,0:T(4,128)(2,1)S(1)} %pad_maximum_fusion.refs_1_), channel_id=1, source_target_pairs={{0,1},{1,0},{2,3},{3,2},{4,5},{5,4},{6,7},{7,6},{8,9},{9,8},{10,11... | collective-permute-start | bytes 792584 | tf_op jit(solution)/shard_map/ppermute | solution.py:23
  19.0 5.6 %collective-permute-start.8 = (bf16[1,4,16512]{2,1,0:T(4,128)(2,1)S(1)}, bf16[1,4,16512]{2,1,0:T(4,128)(2,1)S(1)}, u32[]{:S(2)}, u32[]{:S(2)}) collective-permute-start(bf16[1,4,16512]{2,1,0:T(4,128)(2,1)S(1)} %shard_map.78.refs_2_.refs_7_), channel_id=1, source_target_pairs={{0,2},{1,3},{2,0},{3,1},{4,6},{5,7},{6,4},{7,5},{8,10},{9,11},{10,... | collective-permute-start | bytes 396296 | tf_op jit(solution)/shard_map/ppermute | solution.py:23
  19.6 5.1 %collective-permute-start.5 = (bf16[2,4,16512]{2,1,0:T(4,128)(2,1)S(1)}, bf16[2,4,16512]{2,1,0:T(4,128)(2,1)S(1)}, u32[]{:S(2)}, u32[]{:S(2)}) collective-permute-start(bf16[2,4,16512]{2,1,0:T(4,128)(2,1)S(1)} %shard_map.75.refs_3_), channel_id=1, source_target_pairs={{0,1},{1,0},{2,3},{3,2},{4,5},{5,4},{6,7},{7,6},{8,9},{9,8},{10,11... | collective-permute-start | bytes 792584 | tf_op jit(solution)/shard_map/ppermute | solution.py:23
  20.3 5.7 %collective-permute-start.6 = (bf16[2,4,16512]{2,1,0:T(4,128)(2,1)S(1)}, bf16[2,4,16512]{2,1,0:T(4,128)(2,1)S(1)}, u32[]{:S(2)}, u32[]{:S(2)}) collective-permute-start(bf16[2,4,16512]{2,1,0:T(4,128)(2,1)S(1)} %collective-permute-done.4.refs_4_), channel_id=1, source_target_pairs={{0,1},{1,0},{2,3},{3,2},{4,5},{5,4},{6,7},{7,6},{8,9},{9,8},{10,11... | collective-permute-start | bytes 792584 | tf_op jit(solution)/shard_map/ppermute | solution.py:23
  20.3 4.4 %collective-permute-start.9 = (bf16[1,4,16512]{2,1,0:T(4,128)(2,1)S(1)}, bf16[1,4,16512]{2,1,0:T(4,128)(2,1)S(1)}, u32[]{:S(2)}, u32[]{:S(2)}) collective-permute-start(bf16[1,4,16512]{2,1,0:T(4,128)(2,1)S(1)} %shard_map.78.refs_2_.refs_7_), channel_id=1, source_target_pairs={{0,1},{1,0},{2,3},{3,2},{4,5},{5,4},{6,7},{7,6},{8,9},{9,8},{10,11... | collective-permute-start | bytes 396296 | tf_op jit(solution)/shard_map/ppermute | solution.py:23
  24.6 1.4 %collective-permute-start.10 = (bf16[1,4,16512]{2,1,0:T(4,128)(2,1)S(1)}, bf16[1,4,16512]{2,1,0:T(4,128)(2,1)S(1)}, u32[]{:S(2)}, u32[]{:S(2)}) collective-permute-start(bf16[1,4,16512]{2,1,0:T(4,128)(2,1)S(1)} %shard_map.80.refs_8_), channel_id=1, source_target_pairs={{0,1},{1,0},{2,3},{3,2},{4,5},{5,4},{6,7},{7,6},{8,9},{9,8},{10,11... | collective-permute-start | bytes 396296 | tf_op jit(solution)/shard_map/ppermute | solution.py:23
  29.4 1.5 %collective-permute-start.12 = (f32[8,32,128]{2,1,0:T(8,128)S(1)}, f32[8,32,128]{2,1,0:T(8,128)S(1)}, u32[]{:S(2)}, u32[]{:S(2)}) collective-permute-start(f32[8,32,128]{2,1,0:T(8,128)S(1)} %get-tuple-element.36), channel_id=1, source_target_pairs={{0,1},{1,0},{2,3},{3,2},{4,5},{5,4},{6,7},{7,6},{8,9},{9,8},{10,11... | collective-permute-start | bytes 393224 | tf_op jit(solution)/shard_map/ppermute | solution.py:23
  29.6 1.2 %collective-permute-start.11 = (bf16[8,16,128]{2,1,0:T(8,128)(2,1)S(1)}, bf16[8,16,128]{2,1,0:T(8,128)(2,1)S(1)}, u32[]{:S(2)}, u32[]{:S(2)}) collective-permute-start(bf16[8,16,128]{2,1,0:T(8,128)(2,1)S(1)} %get-tuple-element.34), channel_id=1, source_target_pairs={{0,1},{1,0},{2,3},{3,2},{4,5},{5,4},{6,7},{7,6},{8,9},{9,8},{10,11... | collective-permute-start | bytes 98312 | tf_op jit(solution)/shard_map/ppermute | solution.py:23
  45.4 6.7 %collective-permute-start.17 = (bf16[1,4,8192]{2,1,0:T(4,128)(2,1)S(1)}, bf16[1,4,8192]{2,1,0:T(4,128)(2,1)S(1)}, u32[]{:S(2)}, u32[]{:S(2)}) collective-permute-start(bf16[1,4,8192]{2,1,0:T(4,128)(2,1)S(1)} %bitcast.8), channel_id=1, source_target_pairs={{0,4},{1,5},{2,6},{3,7},{4,12},{5,13},{6,14},{7,15},{8,0},{9,1},{1... | collective-permute-start | bytes 196616 | tf_op jit(solution)/shard_map/ppermute | solution.py:23
  45.7 6.5 %collective-permute-start.16 = (bf16[1,4,8192]{2,1,0:T(4,128)(2,1)S(1)}, bf16[1,4,8192]{2,1,0:T(4,128)(2,1)S(1)}, u32[]{:S(2)}, u32[]{:S(2)}) collective-permute-start(bf16[1,4,8192]{2,1,0:T(4,128)(2,1)S(1)} %bitcast.9), channel_id=1, source_target_pairs={{0,12},{1,13},{2,14},{3,15},{4,8},{5,9},{6,10},{7,11},{8,4},{9,5},... | collective-permute-start | bytes 196616 | tf_op jit(solution)/shard_map/ppermute | solution.py:23
  47.7 5.1 %collective-permute-start.15 = (bf16[1,4,8192]{2,1,0:T(4,128)(2,1)S(1)}, bf16[1,4,8192]{2,1,0:T(4,128)(2,1)S(1)}, u32[]{:S(2)}, u32[]{:S(2)}) collective-permute-start(bf16[1,4,8192]{2,1,0:T(4,128)(2,1)S(1)} %bitcast.10), channel_id=1, source_target_pairs={{0,8},{1,9},{2,10},{3,11},{4,0},{5,1},{6,2},{7,3},{8,12},{9,13},{1... | collective-permute-start | bytes 196616 | tf_op jit(solution)/shard_map/ppermute | solution.py:23
  48.4 4.3 %collective-permute-start.13 = (bf16[1,4,8192]{2,1,0:T(4,128)(2,1)S(1)}, bf16[1,4,8192]{2,1,0:T(4,128)(2,1)S(1)}, u32[]{:S(2)}, u32[]{:S(2)}) collective-permute-start(bf16[1,4,8192]{2,1,0:T(4,128)(2,1)S(1)} %bitcast.11), channel_id=1, source_target_pairs={{0,2},{1,3},{2,0},{3,1},{4,6},{5,7},{6,4},{7,5},{8,10},{9,11},{10,... | collective-permute-start | bytes 196616 | tf_op jit(solution)/shard_map/ppermute | solution.py:23
  52.7 5.7 %collective-permute-start.18 = (bf16[3,4,8192]{2,1,0:T(4,128)(2,1)S(1)}, bf16[3,4,8192]{2,1,0:T(4,128)(2,1)S(1)}, u32[]{:S(2)}, u32[]{:S(2)}) collective-permute-start(bf16[3,4,8192]{2,1,0:T(4,128)(2,1)S(1)} %shard_map.85.refs_1_.refs_3_), channel_id=1, source_target_pairs={{0,2},{1,3},{2,0},{3,1},{4,6},{5,7},{6,4},{7,5},{8,10},{9,11},{10,... | collective-permute-start | bytes 589832 | tf_op jit(solution)/shard_map/ppermute | solution.py:23
  54.4 4.1 %collective-permute-start.14 = (bf16[2,4,8192]{2,1,0:T(4,128)(2,1)S(1)}, bf16[2,4,8192]{2,1,0:T(4,128)(2,1)S(1)}, u32[]{:S(2)}, u32[]{:S(2)}) collective-permute-start(bf16[2,4,8192]{2,1,0:T(4,128)(2,1)S(1)} %pad_maximum_fusion.1), channel_id=1, source_target_pairs={{0,1},{1,0},{2,3},{3,2},{4,5},{5,4},{6,7},{7,6},{8,9},{9,8},{10,11... | collective-permute-start | bytes 393224 | tf_op jit(solution)/shard_map/ppermute | solution.py:23
  54.5 4.2 %collective-permute-start.19 = (bf16[3,4,8192]{2,1,0:T(4,128)(2,1)S(1)}, bf16[3,4,8192]{2,1,0:T(4,128)(2,1)S(1)}, u32[]{:S(2)}, u32[]{:S(2)}) collective-permute-start(bf16[3,4,8192]{2,1,0:T(4,128)(2,1)S(1)} %shard_map.85.refs_1_.refs_3_), channel_id=1, source_target_pairs={{0,1},{1,0},{2,3},{3,2},{4,5},{5,4},{6,7},{7,6},{8,9},{9,8},{10,11... | collective-permute-start | bytes 589832 | tf_op jit(solution)/shard_map/ppermute | solution.py:23
  58.5 1.5 %collective-permute-start.20 = (bf16[3,4,8192]{2,1,0:T(4,128)(2,1)S(1)}, bf16[3,4,8192]{2,1,0:T(4,128)(2,1)S(1)}, u32[]{:S(2)}, u32[]{:S(2)}) collective-permute-start(bf16[3,4,8192]{2,1,0:T(4,128)(2,1)S(1)} %shard_map.87.refs_4_), channel_id=1, source_target_pairs={{0,1},{1,0},{2,3},{3,2},{4,5},{5,4},{6,7},{7,6},{8,9},{9,8},{10,11... | collective-permute-start | bytes 589832 | tf_op jit(solution)/shard_map/ppermute | solution.py:23
  64.4 1.3 %collective-permute-start.21 = (bf16[8,4,1024]{2,1,0:T(4,128)(2,1)S(1)}, bf16[8,4,1024]{2,1,0:T(4,128)(2,1)S(1)}, u32[]{:S(2)}, u32[]{:S(2)}) collective-permute-start(bf16[8,4,1024]{2,1,0:T(4,128)(2,1)S(1)} %get-tuple-element.44), channel_id=1, source_target_pairs={{0,1},{1,0},{2,3},{3,2},{4,5},{5,4},{6,7},{7,6},{8,9},{9,8},{10,11... | collective-permute-start | bytes 196616 | tf_op jit(solution)/shard_map/ppermute | solution.py:23

commit v7 on v6

--- a/solution.py
+++ b/solution.py
@@ -13,7 +13,7 @@
 ROPE_BASE = 500000.0
 EPSILON = 1e-05
 TAG = 128
-VMEM_LIMIT = 10 * 1024 * 1024
+VMEM_LIMIT = 8 * 1024 * 1024
 VMEM = pl.BlockSpec(memory_space=pltpu.VMEM)
 SMEM = pl.BlockSpec(memory_space=pltpu.SMEM)
 HBM = pl.BlockSpec(memory_space=pltpu.HBM)
@@ -256,14 +256,12 @@
     return jnp.concatenate([ref[at, :, lanes] for ref, at in slots], 0)
 
 
-def multiply(slots, weights, depth, total, kept, copies=()):
+def multiply(slots, weights, depth, total, kept):
     total[...] = jnp.zeros_like(total)
     chunk = 0
     for part in weights:
         for at in range(0, part.shape[0], depth):
             kept[chunk] = assemble(slots, chunk * depth, depth)
-            if copies and part is weights[-1]:
-                copies[at // depth].wait()
             total[...] += jnp.dot(kept[chunk], part[at : at + depth, :], preferred_element_type=jnp.float32)
             chunk += 1
 
@@ -390,40 +388,33 @@
 
 def out_kernel(counts, crossed, *refs):
     slots = slots_of(refs, counts)
-    *weights, rest, near, far, last, kept, total, arrived = refs[len(counts) :]
-    depth, first, copies = kept.shape[2], rest.shape[0] - last.shape[0], []
-    for at in range(last.shape[0] // depth):
-        source = rest.at[pl.ds(first + at * depth, depth)]
-        copies.append(pltpu.make_async_copy(source, last.at[pl.ds(at * depth, depth)], arrived.at[at]))
-        copies[-1].start()
-    multiply(slots, weights + [last], depth, total, kept, copies)
+    *weights, near, far, kept, total = refs[len(counts) :]
+    multiply(slots, weights, kept.shape[2], total, kept)
     own = near.shape[1]
     for slot in range(len(slots)):
         (near, far)[crossed[slot][0]][crossed[slot][1]] = total[slot * own : (slot + 1) * own].astype(near.dtype)
 
 
-def project_out(groups, fetched, w_out, devices):
+def project_out(groups, w_out, devices):
     counts, crossed = group_shape(groups)
-    columns = w_out.shape[1]
+    columns = w_out[0].shape[1]
     own, width = groups[0].blocks.shape[1:]
     chunks = devices // 2
     piece = jax.ShapeDtypeStruct((devices // 2, own, columns), jnp.bfloat16)
     return pl.pallas_call(
         functools.partial(out_kernel, counts, crossed),
         out_shape=[piece, piece],
-        in_specs=[VMEM] * (len(groups) + len(fetched)) + [HBM],
+        in_specs=[VMEM] * (len(groups) + len(w_out)),
         out_specs=[VMEM, VMEM],
         scratch_shapes=[
-            pltpu.VMEM((width - sum(part.shape[0] for part in fetched), columns), w_out.dtype),
             pltpu.VMEM((chunks, devices * own, width // chunks), jnp.bfloat16),
             pltpu.VMEM((devices * own, columns), jnp.float32),
-            pltpu.SemaphoreType.DMA((chunks,)),
         ],
         compiler_params=pltpu.CompilerParams(vmem_limit_bytes=VMEM_LIMIT),
         cost_estimate=pl.CostEstimate(
             flops=2 * devices * own * columns * width, bytes_accessed=2 * columns * width, transcendentals=0
         ),
-    )(*[group.blocks for group in groups], *fetched, pltpu.with_memory_space_constraint(w_out, pltpu.HBM))
+    )(*[group.blocks for group in groups], *w_out)
 
 
 def attend_kernel(devices, kv_heads, tile, lengths, pieces, cache, out, fresh, queries, mixed):
@@ -545,7 +536,7 @@
     waits = [
         bring((w_query, 0, cut)),
         bring((w_keyval, 0, 2), (kv_cache, 0, 2)),
-        bring((w_query, cut, w_query.shape[0] - cut), (w_out, 0, part)),
+        bring((w_query, cut, w_query.shape[0] - cut), (w_out, 0, 2 * part)),
     ]
     groups = gather(normed, devices, waits, inner_first=True)
     w_first, w_keyval, kv_cache, w_second, w_out_first = fetched
@@ -555,9 +546,9 @@
 
     mixed = attend(exchange(pieces, devices), near.shape[1], kv_cache, lengths, devices)
     fetched = [w_out_first]
-    waits = [bring((w_out, first * part, count * part)) for first, count in ((1, 2), (3, 4))]
+    waits = [bring((w_out, first * part, count * part)) for first, count in ((2, 2), (4, 4))]
     groups = gather_direct(mixed, devices, waits)
-    near, far = project_out(groups, fetched, w_out, devices)
+    near, far = project_out(groups, fetched, devices)
     pieces = pair(places(groups), near, swap_cores(far, devices))
     return finish(exchange(pieces, devices), steps, devices)
 

time: 78.9 us -> 78.1 us (0.990)
    pallas_call x1, Pallas kernels: 4.44 us -> 3.05 us  [project_out(): pl.pallas_call(functools.partial(out_kernel, counts, crossed), out_shape=...]
  transfers between devices with their start and end apart: 22 -> 22, of which waited for: 8 -> 8; matrix products, arithmetic and copies ran while one was open for 0% -> 0% of each run, Pallas kernels for 21% -> 22%
where the time goes in v7:
time: 78.1 us; the launch traced here: 77.9 us
  Pallas kernels  27.7 us (35%)
  blocking collectives  25.3 us (32%)
  starting transfers between devices  17.8 us (23%)
  waiting for transfers between devices  6.61 us (8%)
    all_to_all x2, blocking collectives, exchange(): lax.all_to_all(pieces, 'gx', 0, 0, axis_index_groups=same_core, tiled=True)  25.3 us
    ppermute x22, starting transfers between devices, permute(): lax.ppermute(block, 'gx', [(int(i), int(t)) for i, t in enumerate(target)])  17.8 us
    pallas_call x5, Pallas kernels, fetch(): pl.pallas_call(functools.partial(fetch_kernel, [first for _, first, _ in...  16.9 us
    ppermute x22, waiting for transfers between devices, permute(): lax.ppermute(block, 'gx', [(int(i), int(t)) for i, t in enumerate(target)])  6.61 us
    pallas_call x1, Pallas kernels, project(): pl.pallas_call(functools.partial(project_kernel, counts, crossed, width),...  3.44 us
    pallas_call x1, Pallas kernels, project_out(): pl.pallas_call(functools.partial(out_kernel, counts, crossed), out_shape=...  3.05 us
    pallas_call x1, Pallas kernels, attend(): pl.pallas_call(functools.partial(attend_kernel, devices, width // HD, til...  1.97 us
  transfers between devices with their start and end apart: 22, of which 8 were waited for; matrix products, arithmetic and copies ran while one was open for 0% of the time, Pallas kernels for 22%

profile of v7, /device:TPU:0, one launch (start us, length us, event | category | flops | bytes accessed | tf_op | source)
XLA Modules:
  0.0 77.9 jit_solution(6792520754337642836)
XLA Ops:
  0.0 1.4 %shard_map.73 = (bf16[4,16512]{1,0:T(4,128)(2,1)S(1)}, s32[2,8,128]{2,1,0:T(8,128)S(1)}) custom-call(s32[2]{0:T(128)} %lengths_far.1, bf16[2,2,16384]{2,1,0:T(2,128)(2,1)} %hidden_far.1, bf16[16384]{0:T(1024)(128)(2,1)} %gain_far.1), custom_call_target="tpu_custom_call" | custom-call | flops 393216 | bytes 262144 | tf_op jit(solution)/shard_map/pallas_call | solution.py:200
  1.5 3.1 %collective-permute-start.3 = (bf16[1,4,16512]{2,1,0:T(4,128)(2,1)S(1)}, bf16[1,4,16512]{2,1,0:T(4,128)(2,1)S(1)}, u32[]{:S(2)}, u32[]{:S(2)}) collective-permute-start(bf16[1,4,16512]{2,1,0:T(4,128)(2,1)S(1)} %bitcast.2), channel_id=1, source_target_pairs={{0,4},{1,5},{2,6},{3,7},{4,12},{5,13},{6,14},{7,15},{8,0},{9,1},{1... | collective-permute-start | bytes 396296 | tf_op jit(solution)/shard_map/ppermute | solution.py:23
  4.5 1.1 %collective-permute-start.2 = (bf16[1,4,16512]{2,1,0:T(4,128)(2,1)S(1)}, bf16[1,4,16512]{2,1,0:T(4,128)(2,1)S(1)}, u32[]{:S(2)}, u32[]{:S(2)}) collective-permute-start(bf16[1,4,16512]{2,1,0:T(4,128)(2,1)S(1)} %bitcast.3), channel_id=1, source_target_pairs={{0,8},{1,9},{2,10},{3,11},{4,0},{5,1},{6,2},{7,3},{8,12},{9,13},{1... | collective-permute-start | bytes 396296 | tf_op jit(solution)/shard_map/ppermute | solution.py:23
  5.6 1.8 %collective-permute-start = (bf16[1,4,16512]{2,1,0:T(4,128)(2,1)S(1)}, bf16[1,4,16512]{2,1,0:T(4,128)(2,1)S(1)}, u32[]{:S(2)}, u32[]{:S(2)}) collective-permute-start(bf16[1,4,16512]{2,1,0:T(4,128)(2,1)S(1)} %bitcast.4), channel_id=1, source_target_pairs={{0,2},{1,3},{2,0},{3,1},{4,6},{5,7},{6,4},{7,5},{8,10},{9,11},{10,... | collective-permute-start | bytes 396296 | tf_op jit(solution)/shard_map/ppermute | solution.py:23
  7.4 4.7 %shard_map.74 = (bf16[12288,512]{1,0:T(8,128)(2,1)S(1)}, f32[8,128]{1,0:T(8,128)S(1)}) custom-call(bf16[16384,512]{1,0:T(8,128)(2,1)} %refs_0_.7, bf16[1,4,16512]{2,1,0:T(4,128)(2,1)S(1)} %bitcast.5), custom_call_target="tpu_custom_call" | custom-call | bytes 12582912 | tf_op jit(solution)/shard_map/pallas_call | solution.py:236
  12.2 1.4 %collective-permute-start.4 = (bf16[2,4,16512]{2,1,0:T(4,128)(2,1)S(1)}, bf16[2,4,16512]{2,1,0:T(4,128)(2,1)S(1)}, u32[]{:S(2)}, u32[]{:S(2)}) collective-permute-start(bf16[2,4,16512]{2,1,0:T(4,128)(2,1)S(1)} %shard_map.75.refs_3_), channel_id=1, source_target_pairs={{0,2},{1,3},{2,0},{3,1},{4,6},{5,7},{6,4},{7,5},{8,10},{9,11},{10,... | collective-permute-start | bytes 792584 | tf_op jit(solution)/shard_map/ppermute | solution.py:23
  13.8 1.7 %collective-permute-start.7 = (bf16[1,4,16512]{2,1,0:T(4,128)(2,1)S(1)}, bf16[1,4,16512]{2,1,0:T(4,128)(2,1)S(1)}, u32[]{:S(2)}, u32[]{:S(2)}) collective-permute-start(bf16[1,4,16512]{2,1,0:T(4,128)(2,1)S(1)} %shard_map.76.refs_2_), channel_id=1, source_target_pairs={{0,8},{1,9},{2,10},{3,11},{4,0},{5,1},{6,2},{7,3},{8,12},{9,13},{1... | collective-permute-start | bytes 396296 | tf_op jit(solution)/shard_map/ppermute | solution.py:23
  15.5 3.0 %shard_map.77 = (bf16[2,1024,512]{2,1,0:T(8,128)(2,1)S(1)}, bf16[2,2,1024,512]{3,2,1,0:T(8,128)(2,1)S(1)}, f32[8,128]{1,0:T(8,128)S(1)}) custom-call(bf16[2,1024,512]{2,1,0:T(8,128)(2,1)} %refs_0_.6, bf16[2,2,1024,512]{3,2,1,0:T(8,128)(2,1)} %refs_1_.2, bf16[1,4,16512]{2,1,0:T(4,128)(2,1)S(1)} %shard_map.76.refs_2_), custom_call_target="tpu_custom_call" | custom-call | bytes 6291456 | tf_op jit(solution)/shard_map/pallas_call | solution.py:236
  20.8 3.5 %shard_map.79 = (bf16[4096,512]{1,0:T(8,128)(2,1)S(1)}, bf16[2048,1024]{1,0:T(8,128)(2,1)S(1)}, f32[8,128]{1,0:T(8,128)S(1)}) custom-call(bf16[16384,512]{1,0:T(8,128)(2,1)} %refs_0_.7, bf16[8192,1024]{1,0:T(8,128)(2,1)} %refs_0_.9, bf16[1,4,16512]{2,1,0:T(4,128)(2,1)S(1)} %shard_map.78.refs_2_.refs_7_), custom_call_target="tpu_custom_call" | custom-call | bytes 8388608 | tf_op jit(solution)/shard_map/pallas_call | solution.py:236
  24.7 1.3 %collective-permute-done.10.refs_10_ = bf16[1,4,16512]{2,1,0:T(4,128)(2,1)S(1)} collective-permute-done((bf16[1,4,16512]{2,1,0:T(4,128)(2,1)S(1)}, bf16[1,4,16512]{2,1,0:T(4,128)(2,1)S(1)}, u32[]{:S(2)}, u32[]{:S(2)}) %collective-permute-start.10) | collective-permute-done | bytes 132128 | tf_op jit(solution)/shard_map/ppermute | solution.py:23
  26.0 3.4 %shard_map.81 = (bf16[8,16,128]{2,1,0:T(8,128)(2,1)S(1)}, bf16[8,16,128]{2,1,0:T(8,128)(2,1)S(1)}, f32[8,32,128]{2,1,0:T(8,128)S(1)}, f32[8,32,128]{2,1,0:T(8,128)S(1)}) custom-call(bf16[1,4,16512]{2,1,0:T(4,128)(2,1)S(1)} %bitcast.7, bf16[1,4,16512]{2,1,0:T(4,128)(2,1)S(1)} %collective-permute-done.refs_1_, ...), custom_call_target="tpu_custom_call" | custom-call | flops 1073741824 | bytes 16777216 | tf_op jit(solution)/shard_map/pallas_call | solution.py:332
  30.0 0.9 %collective-permute-done.11.far = bf16[8,16,128]{2,1,0:T(8,128)(2,1)S(1)} collective-permute-done((bf16[8,16,128]{2,1,0:T(8,128)(2,1)S(1)}, bf16[8,16,128]{2,1,0:T(8,128)(2,1)S(1)}, u32[]{:S(2)}, u32[]{:S(2)}) %collective-permute-start.11) | collective-permute-done | bytes 32800 | tf_op jit(solution)/shard_map/ppermute | solution.py:23
  30.9 13.1 %all_to_all.10.pieces = bf16[8,96,128]{2,1,0:T(8,128)(2,1)S(1)} all-to-all(bf16[8,96,128]{2,1,0:T(8,128)(2,1)S(1)} %shard_map.82), channel_id=1, replica_groups={{0,2,4,6,8,10,12,14},{1,3,5,7,9,11,13,15},{16,18,20,22,24,26,28,30},{17..., dimensions={0} | all-to-all | bytes 393216 | tf_op jit(solution)/shard_map/all_to_all | solution.py:156
  44.1 2.0 %shard_map.83.refs_1_ = bf16[4,8192]{1,0:T(4,128)(2,1)S(1)} custom-call(s32[2,8,128]{2,1,0:T(8,128)S(1)} %get-tuple-element.25.lengths, bf16[8,96,128]{2,1,0:T(8,128)(2,1)S(1)} %all_to_all.10.pieces, bf16[2,2,1024,512]{3,2,1,0:T(8,128)(2,1)S(1)} %get-tuple-element.37.cache), custom_call_target="tpu_custom_call" | custom-call | flops 536870912 | bytes 4194304 | tf_op jit(solution)/shard_map/pallas_call | solution.py:479
  46.3 2.0 %collective-permute-start.16 = (bf16[1,4,8192]{2,1,0:T(4,128)(2,1)S(1)}, bf16[1,4,8192]{2,1,0:T(4,128)(2,1)S(1)}, u32[]{:S(2)}, u32[]{:S(2)}) collective-permute-start(bf16[1,4,8192]{2,1,0:T(4,128)(2,1)S(1)} %bitcast.9), channel_id=1, source_target_pairs={{0,12},{1,13},{2,14},{3,15},{4,8},{5,9},{6,10},{7,11},{8,4},{9,5},... | collective-permute-start | bytes 196616 | tf_op jit(solution)/shard_map/ppermute | solution.py:23
  48.3 0.8 collective-permute-start.15
  49.0 1.5 %collective-permute-start.13 = (bf16[1,4,8192]{2,1,0:T(4,128)(2,1)S(1)}, bf16[1,4,8192]{2,1,0:T(4,128)(2,1)S(1)}, u32[]{:S(2)}, u32[]{:S(2)}) collective-permute-start(bf16[1,4,8192]{2,1,0:T(4,128)(2,1)S(1)} %bitcast.11), channel_id=1, source_target_pairs={{0,2},{1,3},{2,0},{3,1},{4,6},{5,7},{6,4},{7,5},{8,10},{9,11},{10,... | collective-permute-start | bytes 196616 | tf_op jit(solution)/shard_map/ppermute | solution.py:23
  50.6 2.2 %shard_map.84 = (bf16[2048,1024]{1,0:T(8,128)(2,1)S(1)}, f32[8,128]{1,0:T(8,128)S(1)}) custom-call(bf16[8192,1024]{1,0:T(8,128)(2,1)} %refs_0_.9, bf16[4,8192]{1,0:T(4,128)(2,1)S(1)} %shard_map.83.refs_1_), custom_call_target="tpu_custom_call" | custom-call | bytes 4194304 | tf_op jit(solution)/shard_map/pallas_call | solution.py:236
  53.4 1.6 %collective-permute-start.18 = (bf16[3,4,8192]{2,1,0:T(4,128)(2,1)S(1)}, bf16[3,4,8192]{2,1,0:T(4,128)(2,1)S(1)}, u32[]{:S(2)}, u32[]{:S(2)}) collective-permute-start(bf16[3,4,8192]{2,1,0:T(4,128)(2,1)S(1)} %shard_map.85.refs_1_.refs_3_), channel_id=1, source_target_pairs={{0,2},{1,3},{2,0},{3,1},{4,6},{5,7},{6,4},{7,5},{8,10},{9,11},{10,... | collective-permute-start | bytes 589832 | tf_op jit(solution)/shard_map/ppermute | solution.py:23
  55.6 3.5 %shard_map.86 = (bf16[4096,1024]{1,0:T(8,128)(2,1)S(1)}, f32[8,128]{1,0:T(8,128)S(1)}) custom-call(bf16[8192,1024]{1,0:T(8,128)(2,1)} %refs_0_.9, bf16[3,4,8192]{2,1,0:T(4,128)(2,1)S(1)} %shard_map.85.refs_1_.refs_3_), custom_call_target="tpu_custom_call" | custom-call | bytes 8388608 | tf_op jit(solution)/shard_map/pallas_call | solution.py:236
  59.3 1.4 %collective-permute-done.20.refs_6_ = bf16[3,4,8192]{2,1,0:T(4,128)(2,1)S(1)} collective-permute-done((bf16[3,4,8192]{2,1,0:T(4,128)(2,1)S(1)}, bf16[3,4,8192]{2,1,0:T(4,128)(2,1)S(1)}, u32[]{:S(2)}, u32[]{:S(2)}) %collective-permute-start.20) | collective-permute-done | bytes 196640 | tf_op jit(solution)/shard_map/ppermute | solution.py:23
  60.6 3.0 %shard_map.88 = (bf16[8,4,1024]{2,1,0:T(4,128)(2,1)S(1)}, bf16[8,4,1024]{2,1,0:T(4,128)(2,1)S(1)}) custom-call(bf16[1,4,8192]{2,1,0:T(4,128)(2,1)S(1)} %bitcast.13, bf16[1,4,8192]{2,1,0:T(4,128)(2,1)S(1)} %collective-permute-done.13.refs_4_.refs_1_, bf16[2,4,8192]{2,1,0:T(4,128)(2,1)S(1)} %collective-permute-done.14.refs_2_, ...), custom_call_target="tpu_custom_call" | custom-call | flops 1073741824 | bytes 16777216 | tf_op jit(solution)/shard_map/pallas_call | solution.py:404
  63.9 1.1 %collective-permute-done.21.far = bf16[8,4,1024]{2,1,0:T(4,128)(2,1)S(1)} collective-permute-done((bf16[8,4,1024]{2,1,0:T(4,128)(2,1)S(1)}, bf16[8,4,1024]{2,1,0:T(4,128)(2,1)S(1)}, u32[]{:S(2)}, u32[]{:S(2)}) %collective-permute-start.21) | collective-permute-done | bytes 65568 | tf_op jit(solution)/shard_map/ppermute | solution.py:23
  65.0 12.1 %all_to_all.11.pieces = bf16[8,2,4,1024]{3,2,1,0:T(4,128)(2,1)S(1)} all-to-all(bf16[8,2,4,1024]{3,2,1,0:T(4,128)(2,1)S(1)} %shard_map.89), channel_id=1, replica_groups={{0,2,4,6,8,10,12,14},{1,3,5,7,9,11,13,15},{16,18,20,22,24,26,28,30},{17..., dimensions={0} | all-to-all | bytes 262144 | tf_op jit(solution)/shard_map/all_to_all | solution.py:156
  (42 shorter events, 6.0 us)
Async XLA Ops:
  1.5 10.7 %collective-permute-start.3 = (bf16[1,4,16512]{2,1,0:T(4,128)(2,1)S(1)}, bf16[1,4,16512]{2,1,0:T(4,128)(2,1)S(1)}, u32[]{:S(2)}, u32[]{:S(2)}) collective-permute-start(bf16[1,4,16512]{2,1,0:T(4,128)(2,1)S(1)} %bitcast.2), channel_id=1, source_target_pairs={{0,4},{1,5},{2,6},{3,7},{4,12},{5,13},{6,14},{7,15},{8,0},{9,1},{1... | collective-permute-start | bytes 396296 | tf_op jit(solution)/shard_map/ppermute | solution.py:23
  4.5 7.6 %collective-permute-start.2 = (bf16[1,4,16512]{2,1,0:T(4,128)(2,1)S(1)}, bf16[1,4,16512]{2,1,0:T(4,128)(2,1)S(1)}, u32[]{:S(2)}, u32[]{:S(2)}) collective-permute-start(bf16[1,4,16512]{2,1,0:T(4,128)(2,1)S(1)} %bitcast.3), channel_id=1, source_target_pairs={{0,8},{1,9},{2,10},{3,11},{4,0},{5,1},{6,2},{7,3},{8,12},{9,13},{1... | collective-permute-start | bytes 396296 | tf_op jit(solution)/shard_map/ppermute | solution.py:23
  5.6 7.9 %collective-permute-start = (bf16[1,4,16512]{2,1,0:T(4,128)(2,1)S(1)}, bf16[1,4,16512]{2,1,0:T(4,128)(2,1)S(1)}, u32[]{:S(2)}, u32[]{:S(2)}) collective-permute-start(bf16[1,4,16512]{2,1,0:T(4,128)(2,1)S(1)} %bitcast.4), channel_id=1, source_target_pairs={{0,2},{1,3},{2,0},{3,1},{4,6},{5,7},{6,4},{7,5},{8,10},{9,11},{10,... | collective-permute-start | bytes 396296 | tf_op jit(solution)/shard_map/ppermute | solution.py:23
  12.2 8.1 %collective-permute-start.4 = (bf16[2,4,16512]{2,1,0:T(4,128)(2,1)S(1)}, bf16[2,4,16512]{2,1,0:T(4,128)(2,1)S(1)}, u32[]{:S(2)}, u32[]{:S(2)}) collective-permute-start(bf16[2,4,16512]{2,1,0:T(4,128)(2,1)S(1)} %shard_map.75.refs_3_), channel_id=1, source_target_pairs={{0,2},{1,3},{2,0},{3,1},{4,6},{5,7},{6,4},{7,5},{8,10},{9,11},{10,... | collective-permute-start | bytes 792584 | tf_op jit(solution)/shard_map/ppermute | solution.py:23
  13.8 5.2 %collective-permute-start.7 = (bf16[1,4,16512]{2,1,0:T(4,128)(2,1)S(1)}, bf16[1,4,16512]{2,1,0:T(4,128)(2,1)S(1)}, u32[]{:S(2)}, u32[]{:S(2)}) collective-permute-start(bf16[1,4,16512]{2,1,0:T(4,128)(2,1)S(1)} %shard_map.76.refs_2_), channel_id=1, source_target_pairs={{0,8},{1,9},{2,10},{3,11},{4,0},{5,1},{6,2},{7,3},{8,12},{9,13},{1... | collective-permute-start | bytes 396296 | tf_op jit(solution)/shard_map/ppermute | solution.py:23
  15.5 9.1 %collective-permute-start.1 = (bf16[2,4,16512]{2,1,0:T(4,128)(2,1)S(1)}, bf16[2,4,16512]{2,1,0:T(4,128)(2,1)S(1)}, u32[]{:S(2)}, u32[]{:S(2)}) collective-permute-start(bf16[2,4,16512]{2,1,0:T(4,128)(2,1)S(1)} %pad_maximum_fusion.refs_1_), channel_id=1, source_target_pairs={{0,1},{1,0},{2,3},{3,2},{4,5},{5,4},{6,7},{7,6},{8,9},{9,8},{10,11... | collective-permute-start | bytes 792584 | tf_op jit(solution)/shard_map/ppermute | solution.py:23
  19.0 5.6 %collective-permute-start.8 = (bf16[1,4,16512]{2,1,0:T(4,128)(2,1)S(1)}, bf16[1,4,16512]{2,1,0:T(4,128)(2,1)S(1)}, u32[]{:S(2)}, u32[]{:S(2)}) collective-permute-start(bf16[1,4,16512]{2,1,0:T(4,128)(2,1)S(1)} %shard_map.78.refs_2_.refs_7_), channel_id=1, source_target_pairs={{0,2},{1,3},{2,0},{3,1},{4,6},{5,7},{6,4},{7,5},{8,10},{9,11},{10,... | collective-permute-start | bytes 396296 | tf_op jit(solution)/shard_map/ppermute | solution.py:23
  19.6 5.1 %collective-permute-start.5 = (bf16[2,4,16512]{2,1,0:T(4,128)(2,1)S(1)}, bf16[2,4,16512]{2,1,0:T(4,128)(2,1)S(1)}, u32[]{:S(2)}, u32[]{:S(2)}) collective-permute-start(bf16[2,4,16512]{2,1,0:T(4,128)(2,1)S(1)} %shard_map.75.refs_3_), channel_id=1, source_target_pairs={{0,1},{1,0},{2,3},{3,2},{4,5},{5,4},{6,7},{7,6},{8,9},{9,8},{10,11... | collective-permute-start | bytes 792584 | tf_op jit(solution)/shard_map/ppermute | solution.py:23
  20.3 5.7 %collective-permute-start.6 = (bf16[2,4,16512]{2,1,0:T(4,128)(2,1)S(1)}, bf16[2,4,16512]{2,1,0:T(4,128)(2,1)S(1)}, u32[]{:S(2)}, u32[]{:S(2)}) collective-permute-start(bf16[2,4,16512]{2,1,0:T(4,128)(2,1)S(1)} %collective-permute-done.4.refs_4_), channel_id=1, source_target_pairs={{0,1},{1,0},{2,3},{3,2},{4,5},{5,4},{6,7},{7,6},{8,9},{9,8},{10,11... | collective-permute-start | bytes 792584 | tf_op jit(solution)/shard_map/ppermute | solution.py:23
  20.3 4.4 %collective-permute-start.9 = (bf16[1,4,16512]{2,1,0:T(4,128)(2,1)S(1)}, bf16[1,4,16512]{2,1,0:T(4,128)(2,1)S(1)}, u32[]{:S(2)}, u32[]{:S(2)}) collective-permute-start(bf16[1,4,16512]{2,1,0:T(4,128)(2,1)S(1)} %shard_map.78.refs_2_.refs_7_), channel_id=1, source_target_pairs={{0,1},{1,0},{2,3},{3,2},{4,5},{5,4},{6,7},{7,6},{8,9},{9,8},{10,11... | collective-permute-start | bytes 396296 | tf_op jit(solution)/shard_map/ppermute | solution.py:23
  24.6 1.4 %collective-permute-start.10 = (bf16[1,4,16512]{2,1,0:T(4,128)(2,1)S(1)}, bf16[1,4,16512]{2,1,0:T(4,128)(2,1)S(1)}, u32[]{:S(2)}, u32[]{:S(2)}) collective-permute-start(bf16[1,4,16512]{2,1,0:T(4,128)(2,1)S(1)} %shard_map.80.refs_8_), channel_id=1, source_target_pairs={{0,1},{1,0},{2,3},{3,2},{4,5},{5,4},{6,7},{7,6},{8,9},{9,8},{10,11... | collective-permute-start | bytes 396296 | tf_op jit(solution)/shard_map/ppermute | solution.py:23
  29.4 1.5 %collective-permute-start.12 = (f32[8,32,128]{2,1,0:T(8,128)S(1)}, f32[8,32,128]{2,1,0:T(8,128)S(1)}, u32[]{:S(2)}, u32[]{:S(2)}) collective-permute-start(f32[8,32,128]{2,1,0:T(8,128)S(1)} %get-tuple-element.36), channel_id=1, source_target_pairs={{0,1},{1,0},{2,3},{3,2},{4,5},{5,4},{6,7},{7,6},{8,9},{9,8},{10,11... | collective-permute-start | bytes 393224 | tf_op jit(solution)/shard_map/ppermute | solution.py:23
  29.6 1.2 %collective-permute-start.11 = (bf16[8,16,128]{2,1,0:T(8,128)(2,1)S(1)}, bf16[8,16,128]{2,1,0:T(8,128)(2,1)S(1)}, u32[]{:S(2)}, u32[]{:S(2)}) collective-permute-start(bf16[8,16,128]{2,1,0:T(8,128)(2,1)S(1)} %get-tuple-element.34), channel_id=1, source_target_pairs={{0,1},{1,0},{2,3},{3,2},{4,5},{5,4},{6,7},{7,6},{8,9},{9,8},{10,11... | collective-permute-start | bytes 98312 | tf_op jit(solution)/shard_map/ppermute | solution.py:23
  46.1 6.7 %collective-permute-start.17 = (bf16[1,4,8192]{2,1,0:T(4,128)(2,1)S(1)}, bf16[1,4,8192]{2,1,0:T(4,128)(2,1)S(1)}, u32[]{:S(2)}, u32[]{:S(2)}) collective-permute-start(bf16[1,4,8192]{2,1,0:T(4,128)(2,1)S(1)} %bitcast.8), channel_id=1, source_target_pairs={{0,4},{1,5},{2,6},{3,7},{4,12},{5,13},{6,14},{7,15},{8,0},{9,1},{1... | collective-permute-start | bytes 196616 | tf_op jit(solution)/shard_map/ppermute | solution.py:23
  46.3 6.5 %collective-permute-start.16 = (bf16[1,4,8192]{2,1,0:T(4,128)(2,1)S(1)}, bf16[1,4,8192]{2,1,0:T(4,128)(2,1)S(1)}, u32[]{:S(2)}, u32[]{:S(2)}) collective-permute-start(bf16[1,4,8192]{2,1,0:T(4,128)(2,1)S(1)} %bitcast.9), channel_id=1, source_target_pairs={{0,12},{1,13},{2,14},{3,15},{4,8},{5,9},{6,10},{7,11},{8,4},{9,5},... | collective-permute-start | bytes 196616 | tf_op jit(solution)/shard_map/ppermute | solution.py:23
  48.3 5.0 %collective-permute-start.15 = (bf16[1,4,8192]{2,1,0:T(4,128)(2,1)S(1)}, bf16[1,4,8192]{2,1,0:T(4,128)(2,1)S(1)}, u32[]{:S(2)}, u32[]{:S(2)}) collective-permute-start(bf16[1,4,8192]{2,1,0:T(4,128)(2,1)S(1)} %bitcast.10), channel_id=1, source_target_pairs={{0,8},{1,9},{2,10},{3,11},{4,0},{5,1},{6,2},{7,3},{8,12},{9,13},{1... | collective-permute-start | bytes 196616 | tf_op jit(solution)/shard_map/ppermute | solution.py:23
  49.0 4.3 %collective-permute-start.13 = (bf16[1,4,8192]{2,1,0:T(4,128)(2,1)S(1)}, bf16[1,4,8192]{2,1,0:T(4,128)(2,1)S(1)}, u32[]{:S(2)}, u32[]{:S(2)}) collective-permute-start(bf16[1,4,8192]{2,1,0:T(4,128)(2,1)S(1)} %bitcast.11), channel_id=1, source_target_pairs={{0,2},{1,3},{2,0},{3,1},{4,6},{5,7},{6,4},{7,5},{8,10},{9,11},{10,... | collective-permute-start | bytes 196616 | tf_op jit(solution)/shard_map/ppermute | solution.py:23
  53.4 5.7 %collective-permute-start.18 = (bf16[3,4,8192]{2,1,0:T(4,128)(2,1)S(1)}, bf16[3,4,8192]{2,1,0:T(4,128)(2,1)S(1)}, u32[]{:S(2)}, u32[]{:S(2)}) collective-permute-start(bf16[3,4,8192]{2,1,0:T(4,128)(2,1)S(1)} %shard_map.85.refs_1_.refs_3_), channel_id=1, source_target_pairs={{0,2},{1,3},{2,0},{3,1},{4,6},{5,7},{6,4},{7,5},{8,10},{9,11},{10,... | collective-permute-start | bytes 589832 | tf_op jit(solution)/shard_map/ppermute | solution.py:23
  55.0 4.1 %collective-permute-start.14 = (bf16[2,4,8192]{2,1,0:T(4,128)(2,1)S(1)}, bf16[2,4,8192]{2,1,0:T(4,128)(2,1)S(1)}, u32[]{:S(2)}, u32[]{:S(2)}) collective-permute-start(bf16[2,4,8192]{2,1,0:T(4,128)(2,1)S(1)} %pad_maximum_fusion.1), channel_id=1, source_target_pairs={{0,1},{1,0},{2,3},{3,2},{4,5},{5,4},{6,7},{7,6},{8,9},{9,8},{10,11... | collective-permute-start | bytes 393224 | tf_op jit(solution)/shard_map/ppermute | solution.py:23
  55.1 4.2 %collective-permute-start.19 = (bf16[3,4,8192]{2,1,0:T(4,128)(2,1)S(1)}, bf16[3,4,8192]{2,1,0:T(4,128)(2,1)S(1)}, u32[]{:S(2)}, u32[]{:S(2)}) collective-permute-start(bf16[3,4,8192]{2,1,0:T(4,128)(2,1)S(1)} %shard_map.85.refs_1_.refs_3_), channel_id=1, source_target_pairs={{0,1},{1,0},{2,3},{3,2},{4,5},{5,4},{6,7},{7,6},{8,9},{9,8},{10,11... | collective-permute-start | bytes 589832 | tf_op jit(solution)/shard_map/ppermute | solution.py:23
  59.1 1.5 %collective-permute-start.20 = (bf16[3,4,8192]{2,1,0:T(4,128)(2,1)S(1)}, bf16[3,4,8192]{2,1,0:T(4,128)(2,1)S(1)}, u32[]{:S(2)}, u32[]{:S(2)}) collective-permute-start(bf16[3,4,8192]{2,1,0:T(4,128)(2,1)S(1)} %shard_map.87.refs_4_), channel_id=1, source_target_pairs={{0,1},{1,0},{2,3},{3,2},{4,5},{5,4},{6,7},{7,6},{8,9},{9,8},{10,11... | collective-permute-start | bytes 589832 | tf_op jit(solution)/shard_map/ppermute | solution.py:23
  63.7 1.3 %collective-permute-start.21 = (bf16[8,4,1024]{2,1,0:T(4,128)(2,1)S(1)}, bf16[8,4,1024]{2,1,0:T(4,128)(2,1)S(1)}, u32[]{:S(2)}, u32[]{:S(2)}) collective-permute-start(bf16[8,4,1024]{2,1,0:T(4,128)(2,1)S(1)} %get-tuple-element.44), channel_id=1, source_target_pairs={{0,1},{1,0},{2,3},{3,2},{4,5},{5,4},{6,7},{7,6},{8,9},{9,8},{10,11... | collective-permute-start | bytes 196616 | tf_op jit(solution)/shard_map/ppermute | solution.py:23

commit v8 on v7

--- a/solution.py
+++ b/solution.py
@@ -369,17 +369,18 @@
     )(near, far, near_sum, far_sum)
 
 
-def pair_kernel(place, near, far, out):
+def sort_kernel(place, near, far, out):
+    core = lax.axis_index("gx") % 2
     for slot in range(near.shape[0]):
         chip = look_up(place[slot])
-        out[chip, 0] = near[slot]
-        out[chip, 1] = far[slot]
-
-
-def pair(place, near, far):
-    return pl.pallas_call(
-        functools.partial(pair_kernel, place),
-        out_shape=jax.ShapeDtypeStruct((near.shape[0], 2, *near.shape[1:]), near.dtype),
+        out[2 * chip + core] = near[slot]
+        out[2 * chip + 1 - core] = far[slot]
+
+
+def sort(place, near, far):
+    return pl.pallas_call(
+        functools.partial(sort_kernel, place),
+        out_shape=jax.ShapeDtypeStruct((2 * near.shape[0], *near.shape[1:]), near.dtype),
         in_specs=[VMEM] * 2,
         out_specs=VMEM,
         compiler_params=pltpu.CompilerParams(vmem_limit_bytes=VMEM_LIMIT),
@@ -493,22 +494,19 @@
     )(lengths, pieces, cache)
 
 
-def finish_kernel(devices, pieces, out):
-    columns = pieces.shape[3]
+def finish_kernel(pieces, out):
+    columns = pieces.shape[2]
     steps, rows = out.shape[:2]
-    for chip in range(devices // 2):
-        for other in range(2):
-            source = 2 * chip + (lax.axis_index("gx") % 2 + other) % 2
-            lanes = pl.ds(pl.multiple_of(source * columns, columns), columns)
-            piece = pieces[chip, other].astype(jnp.float32)
-            for step in range(steps):
-                out[step, :, lanes] = piece[step * rows : (step + 1) * rows].astype(out.dtype)
-
-
-def finish(pieces, steps, devices):
-    own, columns = pieces.shape[2:]
-    return pl.pallas_call(
-        functools.partial(finish_kernel, devices),
+    for source in range(pieces.shape[0]):
+        piece = pieces[source].astype(jnp.float32)
+        for step in range(steps):
+            out[step, :, source * columns : (source + 1) * columns] = piece[step * rows : (step + 1) * rows].astype(out.dtype)
+
+
+def finish(pieces, steps):
+    devices, own, columns = pieces.shape
+    return pl.pallas_call(
+        finish_kernel,
         out_shape=jax.ShapeDtypeStruct((steps, own // steps, devices * columns), jnp.bfloat16),
         in_specs=[VMEM],
         out_specs=VMEM,
@@ -549,8 +547,8 @@
     waits = [bring((w_out, first * part, count * part)) for first, count in ((2, 2), (4, 4))]
     groups = gather_direct(mixed, devices, waits)
     near, far = project_out(groups, fetched, devices)
-    pieces = pair(places(groups), near, swap_cores(far, devices))
-    return finish(exchange(pieces, devices), steps, devices)
+    pieces = sort(places(groups), near, far)
+    return finish(lax.all_to_all(pieces, "gx", 0, 0, tiled=True), steps)
 
 
 def rotate(values, positions):

time: 78.1 us -> 77.5 us (level)
  waiting for transfers between devices: 6.61 us -> 5.49 us
    all_to_all x0 -> x1, blocking collectives: none -> 12.8 us  [body(): return finish(lax.all_to_all(pieces, 'gx', 0, 0, tiled=True), steps)]
    all_to_all x2 -> x1, blocking collectives: 25.3 us -> 13.1 us  [exchange(): lax.all_to_all(pieces, 'gx', 0, 0, axis_index_groups=same_core, tiled=True)]
    ppermute x22 -> x21, waiting for transfers between devices: 6.61 us -> 5.49 us  [permute(): lax.ppermute(block, 'gx', [(int(i), int(t)) for i, t in enumerate(target)])]
    ppermute x22 -> x21, starting transfers between devices: 17.8 us -> 17.6 us  [permute(): lax.ppermute(block, 'gx', [(int(i), int(t)) for i, t in enumerate(target)])]
  transfers between devices with their start and end apart: 22 -> 21, of which waited for: 8 -> 7; matrix products, arithmetic and copies ran while one was open for 0% -> 0% of each run, Pallas kernels for 22% -> 22%
where the time goes in v8:
time: 77.5 us; the launch traced here: 77.3 us
  Pallas kernels  27.7 us (36%)
  blocking collectives  26 us (34%)
  starting transfers between devices  17.6 us (23%)
  waiting for transfers between devices  5.49 us (7%)
    ppermute x21, starting transfers between devices, permute(): lax.ppermute(block, 'gx', [(int(i), int(t)) for i, t in enumerate(target)])  17.6 us
    pallas_call x5, Pallas kernels, fetch(): pl.pallas_call(functools.partial(fetch_kernel, [first for _, first, _ in...  16.9 us
    all_to_all x1, blocking collectives, exchange(): lax.all_to_all(pieces, 'gx', 0, 0, axis_index_groups=same_core, tiled=True)  13.1 us
    all_to_all x1, blocking collectives, body(): return finish(lax.all_to_all(pieces, 'gx', 0, 0, tiled=True), steps)  12.8 us
    ppermute x21, waiting for transfers between devices, permute(): lax.ppermute(block, 'gx', [(int(i), int(t)) for i, t in enumerate(target)])  5.49 us
    pallas_call x1, Pallas kernels, project(): pl.pallas_call(functools.partial(project_kernel, counts, crossed, width),...  3.44 us
    pallas_call x1, Pallas kernels, project_out(): pl.pallas_call(functools.partial(out_kernel, counts, crossed), out_shape=...  3.05 us
    pallas_call x1, Pallas kernels, attend(): pl.pallas_call(functools.partial(attend_kernel, devices, width // HD, til...  1.97 us
  transfers between devices with their start and end apart: 21, of which 7 were waited for; matrix products, arithmetic and copies ran while one was open for 0% of the time, Pallas kernels for 22%

profile of v8, /device:TPU:0, one launch (start us, length us, event | category | flops | bytes accessed | tf_op | source)
XLA Modules:
  0.0 77.3 jit_solution(9691483370043325218)
XLA Ops:
  0.0 1.4 %shard_map.73 = (bf16[4,16512]{1,0:T(4,128)(2,1)S(1)}, s32[2,8,128]{2,1,0:T(8,128)S(1)}) custom-call(s32[2]{0:T(128)} %lengths_far.1, bf16[2,2,16384]{2,1,0:T(2,128)(2,1)} %hidden_far.1, bf16[16384]{0:T(1024)(128)(2,1)} %gain_far.1), custom_call_target="tpu_custom_call" | custom-call | flops 393216 | bytes 262144 | tf_op jit(solution)/shard_map/pallas_call | solution.py:200
  1.5 3.1 %collective-permute-start.3 = (bf16[1,4,16512]{2,1,0:T(4,128)(2,1)S(1)}, bf16[1,4,16512]{2,1,0:T(4,128)(2,1)S(1)}, u32[]{:S(2)}, u32[]{:S(2)}) collective-permute-start(bf16[1,4,16512]{2,1,0:T(4,128)(2,1)S(1)} %bitcast.2), channel_id=1, source_target_pairs={{0,4},{1,5},{2,6},{3,7},{4,12},{5,13},{6,14},{7,15},{8,0},{9,1},{1... | collective-permute-start | bytes 396296 | tf_op jit(solution)/shard_map/ppermute | solution.py:23
  4.5 1.1 %collective-permute-start.2 = (bf16[1,4,16512]{2,1,0:T(4,128)(2,1)S(1)}, bf16[1,4,16512]{2,1,0:T(4,128)(2,1)S(1)}, u32[]{:S(2)}, u32[]{:S(2)}) collective-permute-start(bf16[1,4,16512]{2,1,0:T(4,128)(2,1)S(1)} %bitcast.3), channel_id=1, source_target_pairs={{0,8},{1,9},{2,10},{3,11},{4,0},{5,1},{6,2},{7,3},{8,12},{9,13},{1... | collective-permute-start | bytes 396296 | tf_op jit(solution)/shard_map/ppermute | solution.py:23
  5.6 1.8 %collective-permute-start = (bf16[1,4,16512]{2,1,0:T(4,128)(2,1)S(1)}, bf16[1,4,16512]{2,1,0:T(4,128)(2,1)S(1)}, u32[]{:S(2)}, u32[]{:S(2)}) collective-permute-start(bf16[1,4,16512]{2,1,0:T(4,128)(2,1)S(1)} %bitcast.4), channel_id=1, source_target_pairs={{0,2},{1,3},{2,0},{3,1},{4,6},{5,7},{6,4},{7,5},{8,10},{9,11},{10,... | collective-permute-start | bytes 396296 | tf_op jit(solution)/shard_map/ppermute | solution.py:23
  7.4 4.7 %shard_map.74 = (bf16[12288,512]{1,0:T(8,128)(2,1)S(1)}, f32[8,128]{1,0:T(8,128)S(1)}) custom-call(bf16[16384,512]{1,0:T(8,128)(2,1)} %refs_0_.7, bf16[1,4,16512]{2,1,0:T(4,128)(2,1)S(1)} %bitcast.5), custom_call_target="tpu_custom_call" | custom-call | bytes 12582912 | tf_op jit(solution)/shard_map/pallas_call | solution.py:236
  12.2 1.4 %collective-permute-start.4 = (bf16[2,4,16512]{2,1,0:T(4,128)(2,1)S(1)}, bf16[2,4,16512]{2,1,0:T(4,128)(2,1)S(1)}, u32[]{:S(2)}, u32[]{:S(2)}) collective-permute-start(bf16[2,4,16512]{2,1,0:T(4,128)(2,1)S(1)} %shard_map.75.refs_3_), channel_id=1, source_target_pairs={{0,2},{1,3},{2,0},{3,1},{4,6},{5,7},{6,4},{7,5},{8,10},{9,11},{10,... | collective-permute-start | bytes 792584 | tf_op jit(solution)/shard_map/ppermute | solution.py:23
  13.8 1.7 %collective-permute-start.7 = (bf16[1,4,16512]{2,1,0:T(4,128)(2,1)S(1)}, bf16[1,4,16512]{2,1,0:T(4,128)(2,1)S(1)}, u32[]{:S(2)}, u32[]{:S(2)}) collective-permute-start(bf16[1,4,16512]{2,1,0:T(4,128)(2,1)S(1)} %shard_map.76.refs_2_), channel_id=1, source_target_pairs={{0,8},{1,9},{2,10},{3,11},{4,0},{5,1},{6,2},{7,3},{8,12},{9,13},{1... | collective-permute-start | bytes 396296 | tf_op jit(solution)/shard_map/ppermute | solution.py:23
  15.5 3.0 %shard_map.77 = (bf16[2,1024,512]{2,1,0:T(8,128)(2,1)S(1)}, bf16[2,2,1024,512]{3,2,1,0:T(8,128)(2,1)S(1)}, f32[8,128]{1,0:T(8,128)S(1)}) custom-call(bf16[2,1024,512]{2,1,0:T(8,128)(2,1)} %refs_0_.6, bf16[2,2,1024,512]{3,2,1,0:T(8,128)(2,1)} %refs_1_.2, bf16[1,4,16512]{2,1,0:T(4,128)(2,1)S(1)} %shard_map.76.refs_2_), custom_call_target="tpu_custom_call" | custom-call | bytes 6291456 | tf_op jit(solution)/shard_map/pallas_call | solution.py:236
  20.8 3.5 %shard_map.79 = (bf16[4096,512]{1,0:T(8,128)(2,1)S(1)}, bf16[2048,1024]{1,0:T(8,128)(2,1)S(1)}, f32[8,128]{1,0:T(8,128)S(1)}) custom-call(bf16[16384,512]{1,0:T(8,128)(2,1)} %refs_0_.7, bf16[8192,1024]{1,0:T(8,128)(2,1)} %refs_0_.9, bf16[1,4,16512]{2,1,0:T(4,128)(2,1)S(1)} %shard_map.78.refs_2_.refs_7_), custom_call_target="tpu_custom_call" | custom-call | bytes 8388608 | tf_op jit(solution)/shard_map/pallas_call | solution.py:236
  24.7 1.3 %collective-permute-done.10.refs_10_ = bf16[1,4,16512]{2,1,0:T(4,128)(2,1)S(1)} collective-permute-done((bf16[1,4,16512]{2,1,0:T(4,128)(2,1)S(1)}, bf16[1,4,16512]{2,1,0:T(4,128)(2,1)S(1)}, u32[]{:S(2)}, u32[]{:S(2)}) %collective-permute-start.10) | collective-permute-done | bytes 132128 | tf_op jit(solution)/shard_map/ppermute | solution.py:23
  26.0 3.4 %shard_map.81 = (bf16[8,16,128]{2,1,0:T(8,128)(2,1)S(1)}, bf16[8,16,128]{2,1,0:T(8,128)(2,1)S(1)}, f32[8,32,128]{2,1,0:T(8,128)S(1)}, f32[8,32,128]{2,1,0:T(8,128)S(1)}) custom-call(bf16[1,4,16512]{2,1,0:T(4,128)(2,1)S(1)} %bitcast.7, bf16[1,4,16512]{2,1,0:T(4,128)(2,1)S(1)} %collective-permute-done.refs_1_, ...), custom_call_target="tpu_custom_call" | custom-call | flops 1073741824 | bytes 16777216 | tf_op jit(solution)/shard_map/pallas_call | solution.py:332
  30.0 0.9 %collective-permute-done.11.far = bf16[8,16,128]{2,1,0:T(8,128)(2,1)S(1)} collective-permute-done((bf16[8,16,128]{2,1,0:T(8,128)(2,1)S(1)}, bf16[8,16,128]{2,1,0:T(8,128)(2,1)S(1)}, u32[]{:S(2)}, u32[]{:S(2)}) %collective-permute-start.11) | collective-permute-done | bytes 32800 | tf_op jit(solution)/shard_map/ppermute | solution.py:23
  30.9 13.1 %all_to_all.10.pieces = bf16[8,96,128]{2,1,0:T(8,128)(2,1)S(1)} all-to-all(bf16[8,96,128]{2,1,0:T(8,128)(2,1)S(1)} %shard_map.82), channel_id=1, replica_groups={{0,2,4,6,8,10,12,14},{1,3,5,7,9,11,13,15},{16,18,20,22,24,26,28,30},{17..., dimensions={0} | all-to-all | bytes 393216 | tf_op jit(solution)/shard_map/all_to_all | solution.py:156
  44.1 2.0 %shard_map.83.refs_1_ = bf16[4,8192]{1,0:T(4,128)(2,1)S(1)} custom-call(s32[2,8,128]{2,1,0:T(8,128)S(1)} %get-tuple-element.25.lengths, bf16[8,96,128]{2,1,0:T(8,128)(2,1)S(1)} %all_to_all.10.pieces, bf16[2,2,1024,512]{3,2,1,0:T(8,128)(2,1)S(1)} %get-tuple-element.37.cache), custom_call_target="tpu_custom_call" | custom-call | flops 536870912 | bytes 4194304 | tf_op jit(solution)/shard_map/pallas_call | solution.py:480
  46.3 2.0 %collective-permute-start.16 = (bf16[1,4,8192]{2,1,0:T(4,128)(2,1)S(1)}, bf16[1,4,8192]{2,1,0:T(4,128)(2,1)S(1)}, u32[]{:S(2)}, u32[]{:S(2)}) collective-permute-start(bf16[1,4,8192]{2,1,0:T(4,128)(2,1)S(1)} %bitcast.9), channel_id=1, source_target_pairs={{0,12},{1,13},{2,14},{3,15},{4,8},{5,9},{6,10},{7,11},{8,4},{9,5},... | collective-permute-start | bytes 196616 | tf_op jit(solution)/shard_map/ppermute | solution.py:23
  48.3 0.8 collective-permute-start.15
  49.0 1.5 %collective-permute-start.13 = (bf16[1,4,8192]{2,1,0:T(4,128)(2,1)S(1)}, bf16[1,4,8192]{2,1,0:T(4,128)(2,1)S(1)}, u32[]{:S(2)}, u32[]{:S(2)}) collective-permute-start(bf16[1,4,8192]{2,1,0:T(4,128)(2,1)S(1)} %bitcast.11), channel_id=1, source_target_pairs={{0,2},{1,3},{2,0},{3,1},{4,6},{5,7},{6,4},{7,5},{8,10},{9,11},{10,... | collective-permute-start | bytes 196616 | tf_op jit(solution)/shard_map/ppermute | solution.py:23
  50.6 2.2 %shard_map.84 = (bf16[2048,1024]{1,0:T(8,128)(2,1)S(1)}, f32[8,128]{1,0:T(8,128)S(1)}) custom-call(bf16[8192,1024]{1,0:T(8,128)(2,1)} %refs_0_.9, bf16[4,8192]{1,0:T(4,128)(2,1)S(1)} %shard_map.83.refs_1_), custom_call_target="tpu_custom_call" | custom-call | bytes 4194304 | tf_op jit(solution)/shard_map/pallas_call | solution.py:236
  53.4 1.6 %collective-permute-start.18 = (bf16[3,4,8192]{2,1,0:T(4,128)(2,1)S(1)}, bf16[3,4,8192]{2,1,0:T(4,128)(2,1)S(1)}, u32[]{:S(2)}, u32[]{:S(2)}) collective-permute-start(bf16[3,4,8192]{2,1,0:T(4,128)(2,1)S(1)} %shard_map.85.refs_1_.refs_3_), channel_id=1, source_target_pairs={{0,2},{1,3},{2,0},{3,1},{4,6},{5,7},{6,4},{7,5},{8,10},{9,11},{10,... | collective-permute-start | bytes 589832 | tf_op jit(solution)/shard_map/ppermute | solution.py:23
  55.6 3.5 %shard_map.86 = (bf16[4096,1024]{1,0:T(8,128)(2,1)S(1)}, f32[8,128]{1,0:T(8,128)S(1)}) custom-call(bf16[8192,1024]{1,0:T(8,128)(2,1)} %refs_0_.9, bf16[3,4,8192]{2,1,0:T(4,128)(2,1)S(1)} %shard_map.85.refs_1_.refs_3_), custom_call_target="tpu_custom_call" | custom-call | bytes 8388608 | tf_op jit(solution)/shard_map/pallas_call | solution.py:236
  59.3 1.4 %collective-permute-done.20.refs_6_ = bf16[3,4,8192]{2,1,0:T(4,128)(2,1)S(1)} collective-permute-done((bf16[3,4,8192]{2,1,0:T(4,128)(2,1)S(1)}, bf16[3,4,8192]{2,1,0:T(4,128)(2,1)S(1)}, u32[]{:S(2)}, u32[]{:S(2)}) %collective-permute-start.20) | collective-permute-done | bytes 196640 | tf_op jit(solution)/shard_map/ppermute | solution.py:23
  60.6 3.0 %shard_map.88 = (bf16[8,4,1024]{2,1,0:T(4,128)(2,1)S(1)}, bf16[8,4,1024]{2,1,0:T(4,128)(2,1)S(1)}) custom-call(bf16[1,4,8192]{2,1,0:T(4,128)(2,1)S(1)} %bitcast.13, bf16[1,4,8192]{2,1,0:T(4,128)(2,1)S(1)} %collective-permute-done.13.refs_4_.refs_1_, bf16[2,4,8192]{2,1,0:T(4,128)(2,1)S(1)} %collective-permute-done.14.refs_2_, ...), custom_call_target="tpu_custom_call" | custom-call | flops 1073741824 | bytes 16777216 | tf_op jit(solution)/shard_map/pallas_call | solution.py:405
  63.8 12.8 %all_to_all.11.pieces = bf16[16,4,1024]{2,1,0:T(4,128)(2,1)S(1)} all-to-all(bf16[16,4,1024]{2,1,0:T(4,128)(2,1)S(1)} %shard_map.89), channel_id=1, replica_groups=mesh['group'=2,'gx'=16] {'gx'}, dimensions={0} | all-to-all | bytes 262144 | tf_op jit(solution)/shard_map/all_to_all | solution.py:551
  76.6 0.7 shard_map.90
  (40 shorter events, 5.1 us)
Async XLA Ops:
  1.5 10.7 %collective-permute-start.3 = (bf16[1,4,16512]{2,1,0:T(4,128)(2,1)S(1)}, bf16[1,4,16512]{2,1,0:T(4,128)(2,1)S(1)}, u32[]{:S(2)}, u32[]{:S(2)}) collective-permute-start(bf16[1,4,16512]{2,1,0:T(4,128)(2,1)S(1)} %bitcast.2), channel_id=1, source_target_pairs={{0,4},{1,5},{2,6},{3,7},{4,12},{5,13},{6,14},{7,15},{8,0},{9,1},{1... | collective-permute-start | bytes 396296 | tf_op jit(solution)/shard_map/ppermute | solution.py:23
  4.5 7.6 %collective-permute-start.2 = (bf16[1,4,16512]{2,1,0:T(4,128)(2,1)S(1)}, bf16[1,4,16512]{2,1,0:T(4,128)(2,1)S(1)}, u32[]{:S(2)}, u32[]{:S(2)}) collective-permute-start(bf16[1,4,16512]{2,1,0:T(4,128)(2,1)S(1)} %bitcast.3), channel_id=1, source_target_pairs={{0,8},{1,9},{2,10},{3,11},{4,0},{5,1},{6,2},{7,3},{8,12},{9,13},{1... | collective-permute-start | bytes 396296 | tf_op jit(solution)/shard_map/ppermute | solution.py:23
  5.6 7.9 %collective-permute-start = (bf16[1,4,16512]{2,1,0:T(4,128)(2,1)S(1)}, bf16[1,4,16512]{2,1,0:T(4,128)(2,1)S(1)}, u32[]{:S(2)}, u32[]{:S(2)}) collective-permute-start(bf16[1,4,16512]{2,1,0:T(4,128)(2,1)S(1)} %bitcast.4), channel_id=1, source_target_pairs={{0,2},{1,3},{2,0},{3,1},{4,6},{5,7},{6,4},{7,5},{8,10},{9,11},{10,... | collective-permute-start | bytes 396296 | tf_op jit(solution)/shard_map/ppermute | solution.py:23
  12.2 8.1 %collective-permute-start.4 = (bf16[2,4,16512]{2,1,0:T(4,128)(2,1)S(1)}, bf16[2,4,16512]{2,1,0:T(4,128)(2,1)S(1)}, u32[]{:S(2)}, u32[]{:S(2)}) collective-permute-start(bf16[2,4,16512]{2,1,0:T(4,128)(2,1)S(1)} %shard_map.75.refs_3_), channel_id=1, source_target_pairs={{0,2},{1,3},{2,0},{3,1},{4,6},{5,7},{6,4},{7,5},{8,10},{9,11},{10,... | collective-permute-start | bytes 792584 | tf_op jit(solution)/shard_map/ppermute | solution.py:23
  13.8 5.2 %collective-permute-start.7 = (bf16[1,4,16512]{2,1,0:T(4,128)(2,1)S(1)}, bf16[1,4,16512]{2,1,0:T(4,128)(2,1)S(1)}, u32[]{:S(2)}, u32[]{:S(2)}) collective-permute-start(bf16[1,4,16512]{2,1,0:T(4,128)(2,1)S(1)} %shard_map.76.refs_2_), channel_id=1, source_target_pairs={{0,8},{1,9},{2,10},{3,11},{4,0},{5,1},{6,2},{7,3},{8,12},{9,13},{1... | collective-permute-start | bytes 396296 | tf_op jit(solution)/shard_map/ppermute | solution.py:23
  15.5 9.1 %collective-permute-start.1 = (bf16[2,4,16512]{2,1,0:T(4,128)(2,1)S(1)}, bf16[2,4,16512]{2,1,0:T(4,128)(2,1)S(1)}, u32[]{:S(2)}, u32[]{:S(2)}) collective-permute-start(bf16[2,4,16512]{2,1,0:T(4,128)(2,1)S(1)} %pad_maximum_fusion.refs_1_), channel_id=1, source_target_pairs={{0,1},{1,0},{2,3},{3,2},{4,5},{5,4},{6,7},{7,6},{8,9},{9,8},{10,11... | collective-permute-start | bytes 792584 | tf_op jit(solution)/shard_map/ppermute | solution.py:23
  19.0 5.6 %collective-permute-start.8 = (bf16[1,4,16512]{2,1,0:T(4,128)(2,1)S(1)}, bf16[1,4,16512]{2,1,0:T(4,128)(2,1)S(1)}, u32[]{:S(2)}, u32[]{:S(2)}) collective-permute-start(bf16[1,4,16512]{2,1,0:T(4,128)(2,1)S(1)} %shard_map.78.refs_2_.refs_7_), channel_id=1, source_target_pairs={{0,2},{1,3},{2,0},{3,1},{4,6},{5,7},{6,4},{7,5},{8,10},{9,11},{10,... | collective-permute-start | bytes 396296 | tf_op jit(solution)/shard_map/ppermute | solution.py:23
  19.6 5.1 %collective-permute-start.5 = (bf16[2,4,16512]{2,1,0:T(4,128)(2,1)S(1)}, bf16[2,4,16512]{2,1,0:T(4,128)(2,1)S(1)}, u32[]{:S(2)}, u32[]{:S(2)}) collective-permute-start(bf16[2,4,16512]{2,1,0:T(4,128)(2,1)S(1)} %shard_map.75.refs_3_), channel_id=1, source_target_pairs={{0,1},{1,0},{2,3},{3,2},{4,5},{5,4},{6,7},{7,6},{8,9},{9,8},{10,11... | collective-permute-start | bytes 792584 | tf_op jit(solution)/shard_map/ppermute | solution.py:23
  20.3 5.7 %collective-permute-start.6 = (bf16[2,4,16512]{2,1,0:T(4,128)(2,1)S(1)}, bf16[2,4,16512]{2,1,0:T(4,128)(2,1)S(1)}, u32[]{:S(2)}, u32[]{:S(2)}) collective-permute-start(bf16[2,4,16512]{2,1,0:T(4,128)(2,1)S(1)} %collective-permute-done.4.refs_4_), channel_id=1, source_target_pairs={{0,1},{1,0},{2,3},{3,2},{4,5},{5,4},{6,7},{7,6},{8,9},{9,8},{10,11... | collective-permute-start | bytes 792584 | tf_op jit(solution)/shard_map/ppermute | solution.py:23
  20.3 4.4 %collective-permute-start.9 = (bf16[1,4,16512]{2,1,0:T(4,128)(2,1)S(1)}, bf16[1,4,16512]{2,1,0:T(4,128)(2,1)S(1)}, u32[]{:S(2)}, u32[]{:S(2)}) collective-permute-start(bf16[1,4,16512]{2,1,0:T(4,128)(2,1)S(1)} %shard_map.78.refs_2_.refs_7_), channel_id=1, source_target_pairs={{0,1},{1,0},{2,3},{3,2},{4,5},{5,4},{6,7},{7,6},{8,9},{9,8},{10,11... | collective-permute-start | bytes 396296 | tf_op jit(solution)/shard_map/ppermute | solution.py:23
  24.6 1.4 %collective-permute-start.10 = (bf16[1,4,16512]{2,1,0:T(4,128)(2,1)S(1)}, bf16[1,4,16512]{2,1,0:T(4,128)(2,1)S(1)}, u32[]{:S(2)}, u32[]{:S(2)}) collective-permute-start(bf16[1,4,16512]{2,1,0:T(4,128)(2,1)S(1)} %shard_map.80.refs_8_), channel_id=1, source_target_pairs={{0,1},{1,0},{2,3},{3,2},{4,5},{5,4},{6,7},{7,6},{8,9},{9,8},{10,11... | collective-permute-start | bytes 396296 | tf_op jit(solution)/shard_map/ppermute | solution.py:23
  29.4 1.5 %collective-permute-start.12 = (f32[8,32,128]{2,1,0:T(8,128)S(1)}, f32[8,32,128]{2,1,0:T(8,128)S(1)}, u32[]{:S(2)}, u32[]{:S(2)}) collective-permute-start(f32[8,32,128]{2,1,0:T(8,128)S(1)} %get-tuple-element.36), channel_id=1, source_target_pairs={{0,1},{1,0},{2,3},{3,2},{4,5},{5,4},{6,7},{7,6},{8,9},{9,8},{10,11... | collective-permute-start | bytes 393224 | tf_op jit(solution)/shard_map/ppermute | solution.py:23
  29.6 1.2 %collective-permute-start.11 = (bf16[8,16,128]{2,1,0:T(8,128)(2,1)S(1)}, bf16[8,16,128]{2,1,0:T(8,128)(2,1)S(1)}, u32[]{:S(2)}, u32[]{:S(2)}) collective-permute-start(bf16[8,16,128]{2,1,0:T(8,128)(2,1)S(1)} %get-tuple-element.34), channel_id=1, source_target_pairs={{0,1},{1,0},{2,3},{3,2},{4,5},{5,4},{6,7},{7,6},{8,9},{9,8},{10,11... | collective-permute-start | bytes 98312 | tf_op jit(solution)/shard_map/ppermute | solution.py:23
  46.1 6.7 %collective-permute-start.17 = (bf16[1,4,8192]{2,1,0:T(4,128)(2,1)S(1)}, bf16[1,4,8192]{2,1,0:T(4,128)(2,1)S(1)}, u32[]{:S(2)}, u32[]{:S(2)}) collective-permute-start(bf16[1,4,8192]{2,1,0:T(4,128)(2,1)S(1)} %bitcast.8), channel_id=1, source_target_pairs={{0,4},{1,5},{2,6},{3,7},{4,12},{5,13},{6,14},{7,15},{8,0},{9,1},{1... | collective-permute-start | bytes 196616 | tf_op jit(solution)/shard_map/ppermute | solution.py:23
  46.3 6.5 %collective-permute-start.16 = (bf16[1,4,8192]{2,1,0:T(4,128)(2,1)S(1)}, bf16[1,4,8192]{2,1,0:T(4,128)(2,1)S(1)}, u32[]{:S(2)}, u32[]{:S(2)}) collective-permute-start(bf16[1,4,8192]{2,1,0:T(4,128)(2,1)S(1)} %bitcast.9), channel_id=1, source_target_pairs={{0,12},{1,13},{2,14},{3,15},{4,8},{5,9},{6,10},{7,11},{8,4},{9,5},... | collective-permute-start | bytes 196616 | tf_op jit(solution)/shard_map/ppermute | solution.py:23
  48.3 5.0 %collective-permute-start.15 = (bf16[1,4,8192]{2,1,0:T(4,128)(2,1)S(1)}, bf16[1,4,8192]{2,1,0:T(4,128)(2,1)S(1)}, u32[]{:S(2)}, u32[]{:S(2)}) collective-permute-start(bf16[1,4,8192]{2,1,0:T(4,128)(2,1)S(1)} %bitcast.10), channel_id=1, source_target_pairs={{0,8},{1,9},{2,10},{3,11},{4,0},{5,1},{6,2},{7,3},{8,12},{9,13},{1... | collective-permute-start | bytes 196616 | tf_op jit(solution)/shard_map/ppermute | solution.py:23
  49.0 4.3 %collective-permute-start.13 = (bf16[1,4,8192]{2,1,0:T(4,128)(2,1)S(1)}, bf16[1,4,8192]{2,1,0:T(4,128)(2,1)S(1)}, u32[]{:S(2)}, u32[]{:S(2)}) collective-permute-start(bf16[1,4,8192]{2,1,0:T(4,128)(2,1)S(1)} %bitcast.11), channel_id=1, source_target_pairs={{0,2},{1,3},{2,0},{3,1},{4,6},{5,7},{6,4},{7,5},{8,10},{9,11},{10,... | collective-permute-start | bytes 196616 | tf_op jit(solution)/shard_map/ppermute | solution.py:23
  53.4 5.7 %collective-permute-start.18 = (bf16[3,4,8192]{2,1,0:T(4,128)(2,1)S(1)}, bf16[3,4,8192]{2,1,0:T(4,128)(2,1)S(1)}, u32[]{:S(2)}, u32[]{:S(2)}) collective-permute-start(bf16[3,4,8192]{2,1,0:T(4,128)(2,1)S(1)} %shard_map.85.refs_1_.refs_3_), channel_id=1, source_target_pairs={{0,2},{1,3},{2,0},{3,1},{4,6},{5,7},{6,4},{7,5},{8,10},{9,11},{10,... | collective-permute-start | bytes 589832 | tf_op jit(solution)/shard_map/ppermute | solution.py:23
  55.0 4.1 %collective-permute-start.14 = (bf16[2,4,8192]{2,1,0:T(4,128)(2,1)S(1)}, bf16[2,4,8192]{2,1,0:T(4,128)(2,1)S(1)}, u32[]{:S(2)}, u32[]{:S(2)}) collective-permute-start(bf16[2,4,8192]{2,1,0:T(4,128)(2,1)S(1)} %pad_maximum_fusion.1), channel_id=1, source_target_pairs={{0,1},{1,0},{2,3},{3,2},{4,5},{5,4},{6,7},{7,6},{8,9},{9,8},{10,11... | collective-permute-start | bytes 393224 | tf_op jit(solution)/shard_map/ppermute | solution.py:23
  55.1 4.2 %collective-permute-start.19 = (bf16[3,4,8192]{2,1,0:T(4,128)(2,1)S(1)}, bf16[3,4,8192]{2,1,0:T(4,128)(2,1)S(1)}, u32[]{:S(2)}, u32[]{:S(2)}) collective-permute-start(bf16[3,4,8192]{2,1,0:T(4,128)(2,1)S(1)} %shard_map.85.refs_1_.refs_3_), channel_id=1, source_target_pairs={{0,1},{1,0},{2,3},{3,2},{4,5},{5,4},{6,7},{7,6},{8,9},{9,8},{10,11... | collective-permute-start | bytes 589832 | tf_op jit(solution)/shard_map/ppermute | solution.py:23
  59.1 1.5 %collective-permute-start.20 = (bf16[3,4,8192]{2,1,0:T(4,128)(2,1)S(1)}, bf16[3,4,8192]{2,1,0:T(4,128)(2,1)S(1)}, u32[]{:S(2)}, u32[]{:S(2)}) collective-permute-start(bf16[3,4,8192]{2,1,0:T(4,128)(2,1)S(1)} %shard_map.87.refs_4_), channel_id=1, source_target_pairs={{0,1},{1,0},{2,3},{3,2},{4,5},{5,4},{6,7},{7,6},{8,9},{9,8},{10,11... | collective-permute-start | bytes 589832 | tf_op jit(solution)/shard_map/ppermute | solution.py:23

commit v9 on v8

--- a/solution.py
+++ b/solution.py
@@ -544,7 +544,7 @@
 
     mixed = attend(exchange(pieces, devices), near.shape[1], kv_cache, lengths, devices)
     fetched = [w_out_first]
-    waits = [bring((w_out, first * part, count * part)) for first, count in ((2, 2), (4, 4))]
+    waits = [bring((w_out, first * part, count * part)) for first, count in ((2, 3), (5, 3))]
     groups = gather_direct(mixed, devices, waits)
     near, far = project_out(groups, fetched, devices)
     pieces = sort(places(groups), near, far)

time: 77.5 us -> 77.3 us (level)
  no operation moved by 1% of the time
where the time goes in v9:
time: 77.3 us; the launch traced here: 77.1 us
  Pallas kernels  27.7 us (36%)
  blocking collectives  25.7 us (33%)
  starting transfers between devices  17.4 us (23%)
  waiting for transfers between devices  5.81 us (8%)
    ppermute x21, starting transfers between devices, permute(): lax.ppermute(block, 'gx', [(int(i), int(t)) for i, t in enumerate(target)])  17.4 us
    pallas_call x5, Pallas kernels, fetch(): pl.pallas_call(functools.partial(fetch_kernel, [first for _, first, _ in...  16.9 us
    all_to_all x1, blocking collectives, exchange(): lax.all_to_all(pieces, 'gx', 0, 0, axis_index_groups=same_core, tiled=True)  13.1 us
    all_to_all x1, blocking collectives, body(): return finish(lax.all_to_all(pieces, 'gx', 0, 0, tiled=True), steps)  12.5 us
    ppermute x21, waiting for transfers between devices, permute(): lax.ppermute(block, 'gx', [(int(i), int(t)) for i, t in enumerate(target)])  5.81 us
    pallas_call x1, Pallas kernels, project(): pl.pallas_call(functools.partial(project_kernel, counts, crossed, width),...  3.44 us
    pallas_call x1, Pallas kernels, project_out(): pl.pallas_call(functools.partial(out_kernel, counts, crossed), out_shape=...  3.05 us
    pallas_call x1, Pallas kernels, attend(): pl.pallas_call(functools.partial(attend_kernel, devices, width // HD, til...  1.97 us
  transfers between devices with their start and end apart: 21, of which 7 were waited for; matrix products, arithmetic and copies ran while one was open for 0% of the time, Pallas kernels for 22%

profile of v9, /device:TPU:0, one launch (start us, length us, event | category | flops | bytes accessed | tf_op | source)
XLA Modules:
  0.0 77.1 jit_solution(39689897486224524)
XLA Ops:
  0.0 1.4 %shard_map.73 = (bf16[4,16512]{1,0:T(4,128)(2,1)S(1)}, s32[2,8,128]{2,1,0:T(8,128)S(1)}) custom-call(s32[2]{0:T(128)} %lengths_far.1, bf16[2,2,16384]{2,1,0:T(2,128)(2,1)} %hidden_far.1, bf16[16384]{0:T(1024)(128)(2,1)} %gain_far.1), custom_call_target="tpu_custom_call" | custom-call | flops 393216 | bytes 262144 | tf_op jit(solution)/shard_map/pallas_call | solution.py:200
  1.5 3.1 %collective-permute-start.3 = (bf16[1,4,16512]{2,1,0:T(4,128)(2,1)S(1)}, bf16[1,4,16512]{2,1,0:T(4,128)(2,1)S(1)}, u32[]{:S(2)}, u32[]{:S(2)}) collective-permute-start(bf16[1,4,16512]{2,1,0:T(4,128)(2,1)S(1)} %bitcast.2), channel_id=1, source_target_pairs={{0,4},{1,5},{2,6},{3,7},{4,12},{5,13},{6,14},{7,15},{8,0},{9,1},{1... | collective-permute-start | bytes 396296 | tf_op jit(solution)/shard_map/ppermute | solution.py:23
  4.5 1.1 %collective-permute-start.2 = (bf16[1,4,16512]{2,1,0:T(4,128)(2,1)S(1)}, bf16[1,4,16512]{2,1,0:T(4,128)(2,1)S(1)}, u32[]{:S(2)}, u32[]{:S(2)}) collective-permute-start(bf16[1,4,16512]{2,1,0:T(4,128)(2,1)S(1)} %bitcast.3), channel_id=1, source_target_pairs={{0,8},{1,9},{2,10},{3,11},{4,0},{5,1},{6,2},{7,3},{8,12},{9,13},{1... | collective-permute-start | bytes 396296 | tf_op jit(solution)/shard_map/ppermute | solution.py:23
  5.6 1.8 %collective-permute-start = (bf16[1,4,16512]{2,1,0:T(4,128)(2,1)S(1)}, bf16[1,4,16512]{2,1,0:T(4,128)(2,1)S(1)}, u32[]{:S(2)}, u32[]{:S(2)}) collective-permute-start(bf16[1,4,16512]{2,1,0:T(4,128)(2,1)S(1)} %bitcast.4), channel_id=1, source_target_pairs={{0,2},{1,3},{2,0},{3,1},{4,6},{5,7},{6,4},{7,5},{8,10},{9,11},{10,... | collective-permute-start | bytes 396296 | tf_op jit(solution)/shard_map/ppermute | solution.py:23
  7.4 4.7 %shard_map.74 = (bf16[12288,512]{1,0:T(8,128)(2,1)S(1)}, f32[8,128]{1,0:T(8,128)S(1)}) custom-call(bf16[16384,512]{1,0:T(8,128)(2,1)} %refs_0_.7, bf16[1,4,16512]{2,1,0:T(4,128)(2,1)S(1)} %bitcast.5), custom_call_target="tpu_custom_call" | custom-call | bytes 12582912 | tf_op jit(solution)/shard_map/pallas_call | solution.py:236
  12.2 1.4 %collective-permute-start.4 = (bf16[2,4,16512]{2,1,0:T(4,128)(2,1)S(1)}, bf16[2,4,16512]{2,1,0:T(4,128)(2,1)S(1)}, u32[]{:S(2)}, u32[]{:S(2)}) collective-permute-start(bf16[2,4,16512]{2,1,0:T(4,128)(2,1)S(1)} %shard_map.75.refs_3_), channel_id=1, source_target_pairs={{0,2},{1,3},{2,0},{3,1},{4,6},{5,7},{6,4},{7,5},{8,10},{9,11},{10,... | collective-permute-start | bytes 792584 | tf_op jit(solution)/shard_map/ppermute | solution.py:23
  13.8 1.7 %collective-permute-start.7 = (bf16[1,4,16512]{2,1,0:T(4,128)(2,1)S(1)}, bf16[1,4,16512]{2,1,0:T(4,128)(2,1)S(1)}, u32[]{:S(2)}, u32[]{:S(2)}) collective-permute-start(bf16[1,4,16512]{2,1,0:T(4,128)(2,1)S(1)} %shard_map.76.refs_2_), channel_id=1, source_target_pairs={{0,8},{1,9},{2,10},{3,11},{4,0},{5,1},{6,2},{7,3},{8,12},{9,13},{1... | collective-permute-start | bytes 396296 | tf_op jit(solution)/shard_map/ppermute | solution.py:23
  15.5 3.0 %shard_map.77 = (bf16[2,1024,512]{2,1,0:T(8,128)(2,1)S(1)}, bf16[2,2,1024,512]{3,2,1,0:T(8,128)(2,1)S(1)}, f32[8,128]{1,0:T(8,128)S(1)}) custom-call(bf16[2,1024,512]{2,1,0:T(8,128)(2,1)} %refs_0_.6, bf16[2,2,1024,512]{3,2,1,0:T(8,128)(2,1)} %refs_1_.2, bf16[1,4,16512]{2,1,0:T(4,128)(2,1)S(1)} %shard_map.76.refs_2_), custom_call_target="tpu_custom_call" | custom-call | bytes 6291456 | tf_op jit(solution)/shard_map/pallas_call | solution.py:236
  20.8 3.5 %shard_map.79 = (bf16[4096,512]{1,0:T(8,128)(2,1)S(1)}, bf16[2048,1024]{1,0:T(8,128)(2,1)S(1)}, f32[8,128]{1,0:T(8,128)S(1)}) custom-call(bf16[16384,512]{1,0:T(8,128)(2,1)} %refs_0_.7, bf16[8192,1024]{1,0:T(8,128)(2,1)} %refs_0_.9, bf16[1,4,16512]{2,1,0:T(4,128)(2,1)S(1)} %shard_map.78.refs_2_.refs_7_), custom_call_target="tpu_custom_call" | custom-call | bytes 8388608 | tf_op jit(solution)/shard_map/pallas_call | solution.py:236
  24.7 1.3 %collective-permute-done.10.refs_10_ = bf16[1,4,16512]{2,1,0:T(4,128)(2,1)S(1)} collective-permute-done((bf16[1,4,16512]{2,1,0:T(4,128)(2,1)S(1)}, bf16[1,4,16512]{2,1,0:T(4,128)(2,1)S(1)}, u32[]{:S(2)}, u32[]{:S(2)}) %collective-permute-start.10) | collective-permute-done | bytes 132128 | tf_op jit(solution)/shard_map/ppermute | solution.py:23
  26.0 3.4 %shard_map.81 = (bf16[8,16,128]{2,1,0:T(8,128)(2,1)S(1)}, bf16[8,16,128]{2,1,0:T(8,128)(2,1)S(1)}, f32[8,32,128]{2,1,0:T(8,128)S(1)}, f32[8,32,128]{2,1,0:T(8,128)S(1)}) custom-call(bf16[1,4,16512]{2,1,0:T(4,128)(2,1)S(1)} %bitcast.7, bf16[1,4,16512]{2,1,0:T(4,128)(2,1)S(1)} %collective-permute-done.refs_1_, ...), custom_call_target="tpu_custom_call" | custom-call | flops 1073741824 | bytes 16777216 | tf_op jit(solution)/shard_map/pallas_call | solution.py:332
  30.0 0.9 %collective-permute-done.11.far = bf16[8,16,128]{2,1,0:T(8,128)(2,1)S(1)} collective-permute-done((bf16[8,16,128]{2,1,0:T(8,128)(2,1)S(1)}, bf16[8,16,128]{2,1,0:T(8,128)(2,1)S(1)}, u32[]{:S(2)}, u32[]{:S(2)}) %collective-permute-start.11) | collective-permute-done | bytes 32800 | tf_op jit(solution)/shard_map/ppermute | solution.py:23
  30.9 13.1 %all_to_all.10.pieces = bf16[8,96,128]{2,1,0:T(8,128)(2,1)S(1)} all-to-all(bf16[8,96,128]{2,1,0:T(8,128)(2,1)S(1)} %shard_map.82), channel_id=1, replica_groups={{0,2,4,6,8,10,12,14},{1,3,5,7,9,11,13,15},{16,18,20,22,24,26,28,30},{17..., dimensions={0} | all-to-all | bytes 393216 | tf_op jit(solution)/shard_map/all_to_all | solution.py:156
  44.1 2.0 %shard_map.83.refs_1_ = bf16[4,8192]{1,0:T(4,128)(2,1)S(1)} custom-call(s32[2,8,128]{2,1,0:T(8,128)S(1)} %get-tuple-element.25.lengths, bf16[8,96,128]{2,1,0:T(8,128)(2,1)S(1)} %all_to_all.10.pieces, bf16[2,2,1024,512]{3,2,1,0:T(8,128)(2,1)S(1)} %get-tuple-element.37.cache), custom_call_target="tpu_custom_call" | custom-call | flops 536870912 | bytes 4194304 | tf_op jit(solution)/shard_map/pallas_call | solution.py:480
  46.3 2.0 %collective-permute-start.16 = (bf16[1,4,8192]{2,1,0:T(4,128)(2,1)S(1)}, bf16[1,4,8192]{2,1,0:T(4,128)(2,1)S(1)}, u32[]{:S(2)}, u32[]{:S(2)}) collective-permute-start(bf16[1,4,8192]{2,1,0:T(4,128)(2,1)S(1)} %bitcast.9), channel_id=1, source_target_pairs={{0,12},{1,13},{2,14},{3,15},{4,8},{5,9},{6,10},{7,11},{8,4},{9,5},... | collective-permute-start | bytes 196616 | tf_op jit(solution)/shard_map/ppermute | solution.py:23
  48.3 0.8 collective-permute-start.15
  49.0 1.5 %collective-permute-start.13 = (bf16[1,4,8192]{2,1,0:T(4,128)(2,1)S(1)}, bf16[1,4,8192]{2,1,0:T(4,128)(2,1)S(1)}, u32[]{:S(2)}, u32[]{:S(2)}) collective-permute-start(bf16[1,4,8192]{2,1,0:T(4,128)(2,1)S(1)} %bitcast.11), channel_id=1, source_target_pairs={{0,2},{1,3},{2,0},{3,1},{4,6},{5,7},{6,4},{7,5},{8,10},{9,11},{10,... | collective-permute-start | bytes 196616 | tf_op jit(solution)/shard_map/ppermute | solution.py:23
  50.6 2.9 %shard_map.84 = (bf16[3072,1024]{1,0:T(8,128)(2,1)S(1)}, f32[8,128]{1,0:T(8,128)S(1)}) custom-call(bf16[8192,1024]{1,0:T(8,128)(2,1)} %refs_0_.9, bf16[4,8192]{1,0:T(4,128)(2,1)S(1)} %shard_map.83.refs_1_), custom_call_target="tpu_custom_call" | custom-call | bytes 6291456 | tf_op jit(solution)/shard_map/pallas_call | solution.py:236
  53.5 1.4 %collective-permute-start.18 = (bf16[3,4,8192]{2,1,0:T(4,128)(2,1)S(1)}, bf16[3,4,8192]{2,1,0:T(4,128)(2,1)S(1)}, u32[]{:S(2)}, u32[]{:S(2)}) collective-permute-start(bf16[3,4,8192]{2,1,0:T(4,128)(2,1)S(1)} %shard_map.85.refs_1_.refs_3_), channel_id=1, source_target_pairs={{0,2},{1,3},{2,0},{3,1},{4,6},{5,7},{6,4},{7,5},{8,10},{9,11},{10,... | collective-permute-start | bytes 589832 | tf_op jit(solution)/shard_map/ppermute | solution.py:23
  55.6 2.9 %shard_map.86 = (bf16[3072,1024]{1,0:T(8,128)(2,1)S(1)}, f32[8,128]{1,0:T(8,128)S(1)}) custom-call(bf16[8192,1024]{1,0:T(8,128)(2,1)} %refs_0_.9, bf16[3,4,8192]{2,1,0:T(4,128)(2,1)S(1)} %shard_map.85.refs_1_.refs_3_), custom_call_target="tpu_custom_call" | custom-call | bytes 6291456 | tf_op jit(solution)/shard_map/pallas_call | solution.py:236
  58.5 0.8 collective-permute-done.18.refs_0_
  59.4 1.4 %collective-permute-done.20.refs_6_ = bf16[3,4,8192]{2,1,0:T(4,128)(2,1)S(1)} collective-permute-done((bf16[3,4,8192]{2,1,0:T(4,128)(2,1)S(1)}, bf16[3,4,8192]{2,1,0:T(4,128)(2,1)S(1)}, u32[]{:S(2)}, u32[]{:S(2)}) %collective-permute-start.20) | collective-permute-done | bytes 196640 | tf_op jit(solution)/shard_map/ppermute | solution.py:23
  60.8 3.0 %shard_map.88 = (bf16[8,4,1024]{2,1,0:T(4,128)(2,1)S(1)}, bf16[8,4,1024]{2,1,0:T(4,128)(2,1)S(1)}) custom-call(bf16[1,4,8192]{2,1,0:T(4,128)(2,1)S(1)} %bitcast.13, bf16[1,4,8192]{2,1,0:T(4,128)(2,1)S(1)} %collective-permute-done.13.refs_4_.refs_1_, bf16[2,4,8192]{2,1,0:T(4,128)(2,1)S(1)} %collective-permute-done.14.refs_2_, ...), custom_call_target="tpu_custom_call" | custom-call | flops 1073741824 | bytes 16777216 | tf_op jit(solution)/shard_map/pallas_call | solution.py:405
  63.9 12.5 %all_to_all.11.pieces = bf16[16,4,1024]{2,1,0:T(4,128)(2,1)S(1)} all-to-all(bf16[16,4,1024]{2,1,0:T(4,128)(2,1)S(1)} %shard_map.89), channel_id=1, replica_groups=mesh['group'=2,'gx'=16] {'gx'}, dimensions={0} | all-to-all | bytes 262144 | tf_op jit(solution)/shard_map/all_to_all | solution.py:551
  (40 shorter events, 5.2 us)
Async XLA Ops:
  1.5 10.7 %collective-permute-start.3 = (bf16[1,4,16512]{2,1,0:T(4,128)(2,1)S(1)}, bf16[1,4,16512]{2,1,0:T(4,128)(2,1)S(1)}, u32[]{:S(2)}, u32[]{:S(2)}) collective-permute-start(bf16[1,4,16512]{2,1,0:T(4,128)(2,1)S(1)} %bitcast.2), channel_id=1, source_target_pairs={{0,4},{1,5},{2,6},{3,7},{4,12},{5,13},{6,14},{7,15},{8,0},{9,1},{1... | collective-permute-start | bytes 396296 | tf_op jit(solution)/shard_map/ppermute | solution.py:23
  4.5 7.6 %collective-permute-start.2 = (bf16[1,4,16512]{2,1,0:T(4,128)(2,1)S(1)}, bf16[1,4,16512]{2,1,0:T(4,128)(2,1)S(1)}, u32[]{:S(2)}, u32[]{:S(2)}) collective-permute-start(bf16[1,4,16512]{2,1,0:T(4,128)(2,1)S(1)} %bitcast.3), channel_id=1, source_target_pairs={{0,8},{1,9},{2,10},{3,11},{4,0},{5,1},{6,2},{7,3},{8,12},{9,13},{1... | collective-permute-start | bytes 396296 | tf_op jit(solution)/shard_map/ppermute | solution.py:23
  5.6 7.9 %collective-permute-start = (bf16[1,4,16512]{2,1,0:T(4,128)(2,1)S(1)}, bf16[1,4,16512]{2,1,0:T(4,128)(2,1)S(1)}, u32[]{:S(2)}, u32[]{:S(2)}) collective-permute-start(bf16[1,4,16512]{2,1,0:T(4,128)(2,1)S(1)} %bitcast.4), channel_id=1, source_target_pairs={{0,2},{1,3},{2,0},{3,1},{4,6},{5,7},{6,4},{7,5},{8,10},{9,11},{10,... | collective-permute-start | bytes 396296 | tf_op jit(solution)/shard_map/ppermute | solution.py:23
  12.2 8.1 %collective-permute-start.4 = (bf16[2,4,16512]{2,1,0:T(4,128)(2,1)S(1)}, bf16[2,4,16512]{2,1,0:T(4,128)(2,1)S(1)}, u32[]{:S(2)}, u32[]{:S(2)}) collective-permute-start(bf16[2,4,16512]{2,1,0:T(4,128)(2,1)S(1)} %shard_map.75.refs_3_), channel_id=1, source_target_pairs={{0,2},{1,3},{2,0},{3,1},{4,6},{5,7},{6,4},{7,5},{8,10},{9,11},{10,... | collective-permute-start | bytes 792584 | tf_op jit(solution)/shard_map/ppermute | solution.py:23
  13.8 5.2 %collective-permute-start.7 = (bf16[1,4,16512]{2,1,0:T(4,128)(2,1)S(1)}, bf16[1,4,16512]{2,1,0:T(4,128)(2,1)S(1)}, u32[]{:S(2)}, u32[]{:S(2)}) collective-permute-start(bf16[1,4,16512]{2,1,0:T(4,128)(2,1)S(1)} %shard_map.76.refs_2_), channel_id=1, source_target_pairs={{0,8},{1,9},{2,10},{3,11},{4,0},{5,1},{6,2},{7,3},{8,12},{9,13},{1... | collective-permute-start | bytes 396296 | tf_op jit(solution)/shard_map/ppermute | solution.py:23
  15.5 9.1 %collective-permute-start.1 = (bf16[2,4,16512]{2,1,0:T(4,128)(2,1)S(1)}, bf16[2,4,16512]{2,1,0:T(4,128)(2,1)S(1)}, u32[]{:S(2)}, u32[]{:S(2)}) collective-permute-start(bf16[2,4,16512]{2,1,0:T(4,128)(2,1)S(1)} %pad_maximum_fusion.refs_1_), channel_id=1, source_target_pairs={{0,1},{1,0},{2,3},{3,2},{4,5},{5,4},{6,7},{7,6},{8,9},{9,8},{10,11... | collective-permute-start | bytes 792584 | tf_op jit(solution)/shard_map/ppermute | solution.py:23
  19.0 5.6 %collective-permute-start.8 = (bf16[1,4,16512]{2,1,0:T(4,128)(2,1)S(1)}, bf16[1,4,16512]{2,1,0:T(4,128)(2,1)S(1)}, u32[]{:S(2)}, u32[]{:S(2)}) collective-permute-start(bf16[1,4,16512]{2,1,0:T(4,128)(2,1)S(1)} %shard_map.78.refs_2_.refs_7_), channel_id=1, source_target_pairs={{0,2},{1,3},{2,0},{3,1},{4,6},{5,7},{6,4},{7,5},{8,10},{9,11},{10,... | collective-permute-start | bytes 396296 | tf_op jit(solution)/shard_map/ppermute | solution.py:23
  19.6 5.1 %collective-permute-start.5 = (bf16[2,4,16512]{2,1,0:T(4,128)(2,1)S(1)}, bf16[2,4,16512]{2,1,0:T(4,128)(2,1)S(1)}, u32[]{:S(2)}, u32[]{:S(2)}) collective-permute-start(bf16[2,4,16512]{2,1,0:T(4,128)(2,1)S(1)} %shard_map.75.refs_3_), channel_id=1, source_target_pairs={{0,1},{1,0},{2,3},{3,2},{4,5},{5,4},{6,7},{7,6},{8,9},{9,8},{10,11... | collective-permute-start | bytes 792584 | tf_op jit(solution)/shard_map/ppermute | solution.py:23
  20.3 5.7 %collective-permute-start.6 = (bf16[2,4,16512]{2,1,0:T(4,128)(2,1)S(1)}, bf16[2,4,16512]{2,1,0:T(4,128)(2,1)S(1)}, u32[]{:S(2)}, u32[]{:S(2)}) collective-permute-start(bf16[2,4,16512]{2,1,0:T(4,128)(2,1)S(1)} %collective-permute-done.4.refs_4_), channel_id=1, source_target_pairs={{0,1},{1,0},{2,3},{3,2},{4,5},{5,4},{6,7},{7,6},{8,9},{9,8},{10,11... | collective-permute-start | bytes 792584 | tf_op jit(solution)/shard_map/ppermute | solution.py:23
  20.3 4.4 %collective-permute-start.9 = (bf16[1,4,16512]{2,1,0:T(4,128)(2,1)S(1)}, bf16[1,4,16512]{2,1,0:T(4,128)(2,1)S(1)}, u32[]{:S(2)}, u32[]{:S(2)}) collective-permute-start(bf16[1,4,16512]{2,1,0:T(4,128)(2,1)S(1)} %shard_map.78.refs_2_.refs_7_), channel_id=1, source_target_pairs={{0,1},{1,0},{2,3},{3,2},{4,5},{5,4},{6,7},{7,6},{8,9},{9,8},{10,11... | collective-permute-start | bytes 396296 | tf_op jit(solution)/shard_map/ppermute | solution.py:23
  24.6 1.4 %collective-permute-start.10 = (bf16[1,4,16512]{2,1,0:T(4,128)(2,1)S(1)}, bf16[1,4,16512]{2,1,0:T(4,128)(2,1)S(1)}, u32[]{:S(2)}, u32[]{:S(2)}) collective-permute-start(bf16[1,4,16512]{2,1,0:T(4,128)(2,1)S(1)} %shard_map.80.refs_8_), channel_id=1, source_target_pairs={{0,1},{1,0},{2,3},{3,2},{4,5},{5,4},{6,7},{7,6},{8,9},{9,8},{10,11... | collective-permute-start | bytes 396296 | tf_op jit(solution)/shard_map/ppermute | solution.py:23
  29.4 1.5 %collective-permute-start.12 = (f32[8,32,128]{2,1,0:T(8,128)S(1)}, f32[8,32,128]{2,1,0:T(8,128)S(1)}, u32[]{:S(2)}, u32[]{:S(2)}) collective-permute-start(f32[8,32,128]{2,1,0:T(8,128)S(1)} %get-tuple-element.36), channel_id=1, source_target_pairs={{0,1},{1,0},{2,3},{3,2},{4,5},{5,4},{6,7},{7,6},{8,9},{9,8},{10,11... | collective-permute-start | bytes 393224 | tf_op jit(solution)/shard_map/ppermute | solution.py:23
  29.6 1.2 %collective-permute-start.11 = (bf16[8,16,128]{2,1,0:T(8,128)(2,1)S(1)}, bf16[8,16,128]{2,1,0:T(8,128)(2,1)S(1)}, u32[]{:S(2)}, u32[]{:S(2)}) collective-permute-start(bf16[8,16,128]{2,1,0:T(8,128)(2,1)S(1)} %get-tuple-element.34), channel_id=1, source_target_pairs={{0,1},{1,0},{2,3},{3,2},{4,5},{5,4},{6,7},{7,6},{8,9},{9,8},{10,11... | collective-permute-start | bytes 98312 | tf_op jit(solution)/shard_map/ppermute | solution.py:23
  46.1 7.4 %collective-permute-start.17 = (bf16[1,4,8192]{2,1,0:T(4,128)(2,1)S(1)}, bf16[1,4,8192]{2,1,0:T(4,128)(2,1)S(1)}, u32[]{:S(2)}, u32[]{:S(2)}) collective-permute-start(bf16[1,4,8192]{2,1,0:T(4,128)(2,1)S(1)} %bitcast.8), channel_id=1, source_target_pairs={{0,4},{1,5},{2,6},{3,7},{4,12},{5,13},{6,14},{7,15},{8,0},{9,1},{1... | collective-permute-start | bytes 196616 | tf_op jit(solution)/shard_map/ppermute | solution.py:23
  46.3 7.2 %collective-permute-start.16 = (bf16[1,4,8192]{2,1,0:T(4,128)(2,1)S(1)}, bf16[1,4,8192]{2,1,0:T(4,128)(2,1)S(1)}, u32[]{:S(2)}, u32[]{:S(2)}) collective-permute-start(bf16[1,4,8192]{2,1,0:T(4,128)(2,1)S(1)} %bitcast.9), channel_id=1, source_target_pairs={{0,12},{1,13},{2,14},{3,15},{4,8},{5,9},{6,10},{7,11},{8,4},{9,5},... | collective-permute-start | bytes 196616 | tf_op jit(solution)/shard_map/ppermute | solution.py:23
  48.3 5.2 %collective-permute-start.15 = (bf16[1,4,8192]{2,1,0:T(4,128)(2,1)S(1)}, bf16[1,4,8192]{2,1,0:T(4,128)(2,1)S(1)}, u32[]{:S(2)}, u32[]{:S(2)}) collective-permute-start(bf16[1,4,8192]{2,1,0:T(4,128)(2,1)S(1)} %bitcast.10), channel_id=1, source_target_pairs={{0,8},{1,9},{2,10},{3,11},{4,0},{5,1},{6,2},{7,3},{8,12},{9,13},{1... | collective-permute-start | bytes 196616 | tf_op jit(solution)/shard_map/ppermute | solution.py:23
  49.0 4.4 %collective-permute-start.13 = (bf16[1,4,8192]{2,1,0:T(4,128)(2,1)S(1)}, bf16[1,4,8192]{2,1,0:T(4,128)(2,1)S(1)}, u32[]{:S(2)}, u32[]{:S(2)}) collective-permute-start(bf16[1,4,8192]{2,1,0:T(4,128)(2,1)S(1)} %bitcast.11), channel_id=1, source_target_pairs={{0,2},{1,3},{2,0},{3,1},{4,6},{5,7},{6,4},{7,5},{8,10},{9,11},{10,... | collective-permute-start | bytes 196616 | tf_op jit(solution)/shard_map/ppermute | solution.py:23
  53.5 5.7 %collective-permute-start.18 = (bf16[3,4,8192]{2,1,0:T(4,128)(2,1)S(1)}, bf16[3,4,8192]{2,1,0:T(4,128)(2,1)S(1)}, u32[]{:S(2)}, u32[]{:S(2)}) collective-permute-start(bf16[3,4,8192]{2,1,0:T(4,128)(2,1)S(1)} %shard_map.85.refs_1_.refs_3_), channel_id=1, source_target_pairs={{0,2},{1,3},{2,0},{3,1},{4,6},{5,7},{6,4},{7,5},{8,10},{9,11},{10,... | collective-permute-start | bytes 589832 | tf_op jit(solution)/shard_map/ppermute | solution.py:23
  55.0 3.4 %collective-permute-start.14 = (bf16[2,4,8192]{2,1,0:T(4,128)(2,1)S(1)}, bf16[2,4,8192]{2,1,0:T(4,128)(2,1)S(1)}, u32[]{:S(2)}, u32[]{:S(2)}) collective-permute-start(bf16[2,4,8192]{2,1,0:T(4,128)(2,1)S(1)} %pad_maximum_fusion.1), channel_id=1, source_target_pairs={{0,1},{1,0},{2,3},{3,2},{4,5},{5,4},{6,7},{7,6},{8,9},{9,8},{10,11... | collective-permute-start | bytes 393224 | tf_op jit(solution)/shard_map/ppermute | solution.py:23
  55.1 4.2 %collective-permute-start.19 = (bf16[3,4,8192]{2,1,0:T(4,128)(2,1)S(1)}, bf16[3,4,8192]{2,1,0:T(4,128)(2,1)S(1)}, u32[]{:S(2)}, u32[]{:S(2)}) collective-permute-start(bf16[3,4,8192]{2,1,0:T(4,128)(2,1)S(1)} %shard_map.85.refs_1_.refs_3_), channel_id=1, source_target_pairs={{0,1},{1,0},{2,3},{3,2},{4,5},{5,4},{6,7},{7,6},{8,9},{9,8},{10,11... | collective-permute-start | bytes 589832 | tf_op jit(solution)/shard_map/ppermute | solution.py:23
  59.3 1.5 %collective-permute-start.20 = (bf16[3,4,8192]{2,1,0:T(4,128)(2,1)S(1)}, bf16[3,4,8192]{2,1,0:T(4,128)(2,1)S(1)}, u32[]{:S(2)}, u32[]{:S(2)}) collective-permute-start(bf16[3,4,8192]{2,1,0:T(4,128)(2,1)S(1)} %shard_map.87.refs_4_), channel_id=1, source_target_pairs={{0,1},{1,0},{2,3},{3,2},{4,5},{5,4},{6,7},{7,6},{8,9},{9,8},{10,11... | collective-permute-start | bytes 589832 | tf_op jit(solution)/shard_map/ppermute | solution.py:23

commit v10 on v9

--- a/solution.py
+++ b/solution.py
@@ -519,7 +519,7 @@
     devices = lax.axis_size("gx")
 
     normed, lengths = norm(hidden, norm_gain, lengths)
-    cut = w_query.shape[0] * 3 // 4
+    cut = w_query.shape[0] * 11 // 16
     fetched = []
 
     def bring(*ranges):

time: 77.3 us -> 77.7 us (level)
  no operation moved by 1% of the time
where the time goes in v10:
time: 77.7 us; the launch traced here: 77.5 us
  Pallas kernels  27.7 us (36%)
  blocking collectives  25.9 us (33%)
  starting transfers between devices  17.6 us (23%)
  waiting for transfers between devices  5.69 us (7%)
    ppermute x21, starting transfers between devices, permute(): lax.ppermute(block, 'gx', [(int(i), int(t)) for i, t in enumerate(target)])  17.6 us
    pallas_call x5, Pallas kernels, fetch(): pl.pallas_call(functools.partial(fetch_kernel, [first for _, first, _ in...  16.9 us
    all_to_all x1, blocking collectives, exchange(): lax.all_to_all(pieces, 'gx', 0, 0, axis_index_groups=same_core, tiled=True)  13.4 us
    all_to_all x1, blocking collectives, body(): return finish(lax.all_to_all(pieces, 'gx', 0, 0, tiled=True), steps)  12.5 us
    ppermute x21, waiting for transfers between devices, permute(): lax.ppermute(block, 'gx', [(int(i), int(t)) for i, t in enumerate(target)])  5.69 us
    pallas_call x1, Pallas kernels, project(): pl.pallas_call(functools.partial(project_kernel, counts, crossed, width),...  3.44 us
    pallas_call x1, Pallas kernels, project_out(): pl.pallas_call(functools.partial(out_kernel, counts, crossed), out_shape=...  3.05 us
    pallas_call x1, Pallas kernels, attend(): pl.pallas_call(functools.partial(attend_kernel, devices, width // HD, til...  1.97 us
  transfers between devices with their start and end apart: 21, of which 7 were waited for; matrix products, arithmetic and copies ran while one was open for 0% of the time, Pallas kernels for 22%

profile of v10, /device:TPU:0, one launch (start us, length us, event | category | flops | bytes accessed | tf_op | source)
XLA Modules:
  0.0 77.5 jit_solution(17143301592636521457)
XLA Ops:
  0.0 1.4 %shard_map.73 = (bf16[4,16512]{1,0:T(4,128)(2,1)S(1)}, s32[2,8,128]{2,1,0:T(8,128)S(1)}) custom-call(s32[2]{0:T(128)} %lengths_far.1, bf16[2,2,16384]{2,1,0:T(2,128)(2,1)} %hidden_far.1, bf16[16384]{0:T(1024)(128)(2,1)} %gain_far.1), custom_call_target="tpu_custom_call" | custom-call | flops 393216 | bytes 262144 | tf_op jit(solution)/shard_map/pallas_call | solution.py:200
  1.5 3.1 %collective-permute-start.3 = (bf16[1,4,16512]{2,1,0:T(4,128)(2,1)S(1)}, bf16[1,4,16512]{2,1,0:T(4,128)(2,1)S(1)}, u32[]{:S(2)}, u32[]{:S(2)}) collective-permute-start(bf16[1,4,16512]{2,1,0:T(4,128)(2,1)S(1)} %bitcast.2), channel_id=1, source_target_pairs={{0,4},{1,5},{2,6},{3,7},{4,12},{5,13},{6,14},{7,15},{8,0},{9,1},{1... | collective-permute-start | bytes 396296 | tf_op jit(solution)/shard_map/ppermute | solution.py:23
  4.5 1.1 %collective-permute-start.2 = (bf16[1,4,16512]{2,1,0:T(4,128)(2,1)S(1)}, bf16[1,4,16512]{2,1,0:T(4,128)(2,1)S(1)}, u32[]{:S(2)}, u32[]{:S(2)}) collective-permute-start(bf16[1,4,16512]{2,1,0:T(4,128)(2,1)S(1)} %bitcast.3), channel_id=1, source_target_pairs={{0,8},{1,9},{2,10},{3,11},{4,0},{5,1},{6,2},{7,3},{8,12},{9,13},{1... | collective-permute-start | bytes 396296 | tf_op jit(solution)/shard_map/ppermute | solution.py:23
  5.6 1.8 %collective-permute-start = (bf16[1,4,16512]{2,1,0:T(4,128)(2,1)S(1)}, bf16[1,4,16512]{2,1,0:T(4,128)(2,1)S(1)}, u32[]{:S(2)}, u32[]{:S(2)}) collective-permute-start(bf16[1,4,16512]{2,1,0:T(4,128)(2,1)S(1)} %bitcast.4), channel_id=1, source_target_pairs={{0,2},{1,3},{2,0},{3,1},{4,6},{5,7},{6,4},{7,5},{8,10},{9,11},{10,... | collective-permute-start | bytes 396296 | tf_op jit(solution)/shard_map/ppermute | solution.py:23
  7.4 4.4 %shard_map.74 = (bf16[11264,512]{1,0:T(8,128)(2,1)S(1)}, f32[8,128]{1,0:T(8,128)S(1)}) custom-call(bf16[16384,512]{1,0:T(8,128)(2,1)} %refs_0_.7, bf16[1,4,16512]{2,1,0:T(4,128)(2,1)S(1)} %bitcast.5), custom_call_target="tpu_custom_call" | custom-call | bytes 11534336 | tf_op jit(solution)/shard_map/pallas_call | solution.py:236
  11.9 1.6 %collective-permute-start.4 = (bf16[2,4,16512]{2,1,0:T(4,128)(2,1)S(1)}, bf16[2,4,16512]{2,1,0:T(4,128)(2,1)S(1)}, u32[]{:S(2)}, u32[]{:S(2)}) collective-permute-start(bf16[2,4,16512]{2,1,0:T(4,128)(2,1)S(1)} %shard_map.75.refs_3_), channel_id=1, source_target_pairs={{0,2},{1,3},{2,0},{3,1},{4,6},{5,7},{6,4},{7,5},{8,10},{9,11},{10,... | collective-permute-start | bytes 792584 | tf_op jit(solution)/shard_map/ppermute | solution.py:23
  13.8 1.7 %collective-permute-start.7 = (bf16[1,4,16512]{2,1,0:T(4,128)(2,1)S(1)}, bf16[1,4,16512]{2,1,0:T(4,128)(2,1)S(1)}, u32[]{:S(2)}, u32[]{:S(2)}) collective-permute-start(bf16[1,4,16512]{2,1,0:T(4,128)(2,1)S(1)} %shard_map.76.refs_2_), channel_id=1, source_target_pairs={{0,8},{1,9},{2,10},{3,11},{4,0},{5,1},{6,2},{7,3},{8,12},{9,13},{1... | collective-permute-start | bytes 396296 | tf_op jit(solution)/shard_map/ppermute | solution.py:23
  15.5 3.0 %shard_map.77 = (bf16[2,1024,512]{2,1,0:T(8,128)(2,1)S(1)}, bf16[2,2,1024,512]{3,2,1,0:T(8,128)(2,1)S(1)}, f32[8,128]{1,0:T(8,128)S(1)}) custom-call(bf16[2,1024,512]{2,1,0:T(8,128)(2,1)} %refs_0_.6, bf16[2,2,1024,512]{3,2,1,0:T(8,128)(2,1)} %refs_1_.2, bf16[1,4,16512]{2,1,0:T(4,128)(2,1)S(1)} %shard_map.76.refs_2_), custom_call_target="tpu_custom_call" | custom-call | bytes 6291456 | tf_op jit(solution)/shard_map/pallas_call | solution.py:236
  20.8 3.8 %shard_map.79 = (bf16[5120,512]{1,0:T(8,128)(2,1)S(1)}, bf16[2048,1024]{1,0:T(8,128)(2,1)S(1)}, f32[8,128]{1,0:T(8,128)S(1)}) custom-call(bf16[16384,512]{1,0:T(8,128)(2,1)} %refs_0_.7, bf16[8192,1024]{1,0:T(8,128)(2,1)} %refs_0_.9, bf16[1,4,16512]{2,1,0:T(4,128)(2,1)S(1)} %shard_map.78.refs_2_.refs_7_), custom_call_target="tpu_custom_call" | custom-call | bytes 9437184 | tf_op jit(solution)/shard_map/pallas_call | solution.py:236
  24.7 1.3 %collective-permute-done.10.refs_10_ = bf16[1,4,16512]{2,1,0:T(4,128)(2,1)S(1)} collective-permute-done((bf16[1,4,16512]{2,1,0:T(4,128)(2,1)S(1)}, bf16[1,4,16512]{2,1,0:T(4,128)(2,1)S(1)}, u32[]{:S(2)}, u32[]{:S(2)}) %collective-permute-start.10) | collective-permute-done | bytes 132128 | tf_op jit(solution)/shard_map/ppermute | solution.py:23
  26.0 3.4 %shard_map.81 = (bf16[8,16,128]{2,1,0:T(8,128)(2,1)S(1)}, bf16[8,16,128]{2,1,0:T(8,128)(2,1)S(1)}, f32[8,32,128]{2,1,0:T(8,128)S(1)}, f32[8,32,128]{2,1,0:T(8,128)S(1)}) custom-call(bf16[1,4,16512]{2,1,0:T(4,128)(2,1)S(1)} %bitcast.7, bf16[1,4,16512]{2,1,0:T(4,128)(2,1)S(1)} %collective-permute-done.refs_1_, ...), custom_call_target="tpu_custom_call" | custom-call | flops 1073741824 | bytes 16777216 | tf_op jit(solution)/shard_map/pallas_call | solution.py:332
  30.0 0.9 %collective-permute-done.11.far = bf16[8,16,128]{2,1,0:T(8,128)(2,1)S(1)} collective-permute-done((bf16[8,16,128]{2,1,0:T(8,128)(2,1)S(1)}, bf16[8,16,128]{2,1,0:T(8,128)(2,1)S(1)}, u32[]{:S(2)}, u32[]{:S(2)}) %collective-permute-start.11) | collective-permute-done | bytes 32800 | tf_op jit(solution)/shard_map/ppermute | solution.py:23
  31.0 13.4 %all_to_all.10.pieces = bf16[8,96,128]{2,1,0:T(8,128)(2,1)S(1)} all-to-all(bf16[8,96,128]{2,1,0:T(8,128)(2,1)S(1)} %shard_map.82), channel_id=1, replica_groups={{0,2,4,6,8,10,12,14},{1,3,5,7,9,11,13,15},{16,18,20,22,24,26,28,30},{17..., dimensions={0} | all-to-all | bytes 393216 | tf_op jit(solution)/shard_map/all_to_all | solution.py:156
  44.4 2.0 %shard_map.83.refs_1_ = bf16[4,8192]{1,0:T(4,128)(2,1)S(1)} custom-call(s32[2,8,128]{2,1,0:T(8,128)S(1)} %get-tuple-element.25.lengths, bf16[8,96,128]{2,1,0:T(8,128)(2,1)S(1)} %all_to_all.10.pieces, bf16[2,2,1024,512]{3,2,1,0:T(8,128)(2,1)S(1)} %get-tuple-element.37.cache), custom_call_target="tpu_custom_call" | custom-call | flops 536870912 | bytes 4194304 | tf_op jit(solution)/shard_map/pallas_call | solution.py:480
  46.6 2.0 %collective-permute-start.16 = (bf16[1,4,8192]{2,1,0:T(4,128)(2,1)S(1)}, bf16[1,4,8192]{2,1,0:T(4,128)(2,1)S(1)}, u32[]{:S(2)}, u32[]{:S(2)}) collective-permute-start(bf16[1,4,8192]{2,1,0:T(4,128)(2,1)S(1)} %bitcast.9), channel_id=1, source_target_pairs={{0,12},{1,13},{2,14},{3,15},{4,8},{5,9},{6,10},{7,11},{8,4},{9,5},... | collective-permute-start | bytes 196616 | tf_op jit(solution)/shard_map/ppermute | solution.py:23
  48.6 0.8 collective-permute-start.15
  49.3 1.5 %collective-permute-start.13 = (bf16[1,4,8192]{2,1,0:T(4,128)(2,1)S(1)}, bf16[1,4,8192]{2,1,0:T(4,128)(2,1)S(1)}, u32[]{:S(2)}, u32[]{:S(2)}) collective-permute-start(bf16[1,4,8192]{2,1,0:T(4,128)(2,1)S(1)} %bitcast.11), channel_id=1, source_target_pairs={{0,2},{1,3},{2,0},{3,1},{4,6},{5,7},{6,4},{7,5},{8,10},{9,11},{10,... | collective-permute-start | bytes 196616 | tf_op jit(solution)/shard_map/ppermute | solution.py:23
  50.9 2.9 %shard_map.84 = (bf16[3072,1024]{1,0:T(8,128)(2,1)S(1)}, f32[8,128]{1,0:T(8,128)S(1)}) custom-call(bf16[8192,1024]{1,0:T(8,128)(2,1)} %refs_0_.9, bf16[4,8192]{1,0:T(4,128)(2,1)S(1)} %shard_map.83.refs_1_), custom_call_target="tpu_custom_call" | custom-call | bytes 6291456 | tf_op jit(solution)/shard_map/pallas_call | solution.py:236
  53.8 1.4 %collective-permute-start.18 = (bf16[3,4,8192]{2,1,0:T(4,128)(2,1)S(1)}, bf16[3,4,8192]{2,1,0:T(4,128)(2,1)S(1)}, u32[]{:S(2)}, u32[]{:S(2)}) collective-permute-start(bf16[3,4,8192]{2,1,0:T(4,128)(2,1)S(1)} %shard_map.85.refs_1_.refs_3_), channel_id=1, source_target_pairs={{0,2},{1,3},{2,0},{3,1},{4,6},{5,7},{6,4},{7,5},{8,10},{9,11},{10,... | collective-permute-start | bytes 589832 | tf_op jit(solution)/shard_map/ppermute | solution.py:23
  55.9 2.9 %shard_map.86 = (bf16[3072,1024]{1,0:T(8,128)(2,1)S(1)}, f32[8,128]{1,0:T(8,128)S(1)}) custom-call(bf16[8192,1024]{1,0:T(8,128)(2,1)} %refs_0_.9, bf16[3,4,8192]{2,1,0:T(4,128)(2,1)S(1)} %shard_map.85.refs_1_.refs_3_), custom_call_target="tpu_custom_call" | custom-call | bytes 6291456 | tf_op jit(solution)/shard_map/pallas_call | solution.py:236
  58.8 0.8 collective-permute-done.18.refs_0_
  59.6 1.4 %collective-permute-done.20.refs_6_ = bf16[3,4,8192]{2,1,0:T(4,128)(2,1)S(1)} collective-permute-done((bf16[3,4,8192]{2,1,0:T(4,128)(2,1)S(1)}, bf16[3,4,8192]{2,1,0:T(4,128)(2,1)S(1)}, u32[]{:S(2)}, u32[]{:S(2)}) %collective-permute-start.20) | collective-permute-done | bytes 196640 | tf_op jit(solution)/shard_map/ppermute | solution.py:23
  61.1 3.0 %shard_map.88 = (bf16[8,4,1024]{2,1,0:T(4,128)(2,1)S(1)}, bf16[8,4,1024]{2,1,0:T(4,128)(2,1)S(1)}) custom-call(bf16[1,4,8192]{2,1,0:T(4,128)(2,1)S(1)} %bitcast.13, bf16[1,4,8192]{2,1,0:T(4,128)(2,1)S(1)} %collective-permute-done.13.refs_4_.refs_1_, bf16[2,4,8192]{2,1,0:T(4,128)(2,1)S(1)} %collective-permute-done.14.refs_2_, ...), custom_call_target="tpu_custom_call" | custom-call | flops 1073741824 | bytes 16777216 | tf_op jit(solution)/shard_map/pallas_call | solution.py:405
  64.2 12.5 %all_to_all.11.pieces = bf16[16,4,1024]{2,1,0:T(4,128)(2,1)S(1)} all-to-all(bf16[16,4,1024]{2,1,0:T(4,128)(2,1)S(1)} %shard_map.89), channel_id=1, replica_groups=mesh['group'=2,'gx'=16] {'gx'}, dimensions={0} | all-to-all | bytes 262144 | tf_op jit(solution)/shard_map/all_to_all | solution.py:551
  (40 shorter events, 5.1 us)
Async XLA Ops:
  1.5 10.3 %collective-permute-start.3 = (bf16[1,4,16512]{2,1,0:T(4,128)(2,1)S(1)}, bf16[1,4,16512]{2,1,0:T(4,128)(2,1)S(1)}, u32[]{:S(2)}, u32[]{:S(2)}) collective-permute-start(bf16[1,4,16512]{2,1,0:T(4,128)(2,1)S(1)} %bitcast.2), channel_id=1, source_target_pairs={{0,4},{1,5},{2,6},{3,7},{4,12},{5,13},{6,14},{7,15},{8,0},{9,1},{1... | collective-permute-start | bytes 396296 | tf_op jit(solution)/shard_map/ppermute | solution.py:23
  4.5 7.4 %collective-permute-start.2 = (bf16[1,4,16512]{2,1,0:T(4,128)(2,1)S(1)}, bf16[1,4,16512]{2,1,0:T(4,128)(2,1)S(1)}, u32[]{:S(2)}, u32[]{:S(2)}) collective-permute-start(bf16[1,4,16512]{2,1,0:T(4,128)(2,1)S(1)} %bitcast.3), channel_id=1, source_target_pairs={{0,8},{1,9},{2,10},{3,11},{4,0},{5,1},{6,2},{7,3},{8,12},{9,13},{1... | collective-permute-start | bytes 396296 | tf_op jit(solution)/shard_map/ppermute | solution.py:23
  5.6 7.9 %collective-permute-start = (bf16[1,4,16512]{2,1,0:T(4,128)(2,1)S(1)}, bf16[1,4,16512]{2,1,0:T(4,128)(2,1)S(1)}, u32[]{:S(2)}, u32[]{:S(2)}) collective-permute-start(bf16[1,4,16512]{2,1,0:T(4,128)(2,1)S(1)} %bitcast.4), channel_id=1, source_target_pairs={{0,2},{1,3},{2,0},{3,1},{4,6},{5,7},{6,4},{7,5},{8,10},{9,11},{10,... | collective-permute-start | bytes 396296 | tf_op jit(solution)/shard_map/ppermute | solution.py:23
  11.9 8.3 %collective-permute-start.4 = (bf16[2,4,16512]{2,1,0:T(4,128)(2,1)S(1)}, bf16[2,4,16512]{2,1,0:T(4,128)(2,1)S(1)}, u32[]{:S(2)}, u32[]{:S(2)}) collective-permute-start(bf16[2,4,16512]{2,1,0:T(4,128)(2,1)S(1)} %shard_map.75.refs_3_), channel_id=1, source_target_pairs={{0,2},{1,3},{2,0},{3,1},{4,6},{5,7},{6,4},{7,5},{8,10},{9,11},{10,... | collective-permute-start | bytes 792584 | tf_op jit(solution)/shard_map/ppermute | solution.py:23
  13.8 5.2 %collective-permute-start.7 = (bf16[1,4,16512]{2,1,0:T(4,128)(2,1)S(1)}, bf16[1,4,16512]{2,1,0:T(4,128)(2,1)S(1)}, u32[]{:S(2)}, u32[]{:S(2)}) collective-permute-start(bf16[1,4,16512]{2,1,0:T(4,128)(2,1)S(1)} %shard_map.76.refs_2_), channel_id=1, source_target_pairs={{0,8},{1,9},{2,10},{3,11},{4,0},{5,1},{6,2},{7,3},{8,12},{9,13},{1... | collective-permute-start | bytes 396296 | tf_op jit(solution)/shard_map/ppermute | solution.py:23
  15.5 9.2 %collective-permute-start.1 = (bf16[2,4,16512]{2,1,0:T(4,128)(2,1)S(1)}, bf16[2,4,16512]{2,1,0:T(4,128)(2,1)S(1)}, u32[]{:S(2)}, u32[]{:S(2)}) collective-permute-start(bf16[2,4,16512]{2,1,0:T(4,128)(2,1)S(1)} %pad_maximum_fusion.refs_1_), channel_id=1, source_target_pairs={{0,1},{1,0},{2,3},{3,2},{4,5},{5,4},{6,7},{7,6},{8,9},{9,8},{10,11... | collective-permute-start | bytes 792584 | tf_op jit(solution)/shard_map/ppermute | solution.py:23
  19.0 5.6 %collective-permute-start.8 = (bf16[1,4,16512]{2,1,0:T(4,128)(2,1)S(1)}, bf16[1,4,16512]{2,1,0:T(4,128)(2,1)S(1)}, u32[]{:S(2)}, u32[]{:S(2)}) collective-permute-start(bf16[1,4,16512]{2,1,0:T(4,128)(2,1)S(1)} %shard_map.78.refs_2_.refs_7_), channel_id=1, source_target_pairs={{0,2},{1,3},{2,0},{3,1},{4,6},{5,7},{6,4},{7,5},{8,10},{9,11},{10,... | collective-permute-start | bytes 396296 | tf_op jit(solution)/shard_map/ppermute | solution.py:23
  19.5 5.2 %collective-permute-start.5 = (bf16[2,4,16512]{2,1,0:T(4,128)(2,1)S(1)}, bf16[2,4,16512]{2,1,0:T(4,128)(2,1)S(1)}, u32[]{:S(2)}, u32[]{:S(2)}) collective-permute-start(bf16[2,4,16512]{2,1,0:T(4,128)(2,1)S(1)} %shard_map.75.refs_3_), channel_id=1, source_target_pairs={{0,1},{1,0},{2,3},{3,2},{4,5},{5,4},{6,7},{7,6},{8,9},{9,8},{10,11... | collective-permute-start | bytes 792584 | tf_op jit(solution)/shard_map/ppermute | solution.py:23
  20.3 5.8 %collective-permute-start.6 = (bf16[2,4,16512]{2,1,0:T(4,128)(2,1)S(1)}, bf16[2,4,16512]{2,1,0:T(4,128)(2,1)S(1)}, u32[]{:S(2)}, u32[]{:S(2)}) collective-permute-start(bf16[2,4,16512]{2,1,0:T(4,128)(2,1)S(1)} %collective-permute-done.4.refs_4_), channel_id=1, source_target_pairs={{0,1},{1,0},{2,3},{3,2},{4,5},{5,4},{6,7},{7,6},{8,9},{9,8},{10,11... | collective-permute-start | bytes 792584 | tf_op jit(solution)/shard_map/ppermute | solution.py:23
  20.3 4.4 %collective-permute-start.9 = (bf16[1,4,16512]{2,1,0:T(4,128)(2,1)S(1)}, bf16[1,4,16512]{2,1,0:T(4,128)(2,1)S(1)}, u32[]{:S(2)}, u32[]{:S(2)}) collective-permute-start(bf16[1,4,16512]{2,1,0:T(4,128)(2,1)S(1)} %shard_map.78.refs_2_.refs_7_), channel_id=1, source_target_pairs={{0,1},{1,0},{2,3},{3,2},{4,5},{5,4},{6,7},{7,6},{8,9},{9,8},{10,11... | collective-permute-start | bytes 396296 | tf_op jit(solution)/shard_map/ppermute | solution.py:23
  24.6 1.4 %collective-permute-start.10 = (bf16[1,4,16512]{2,1,0:T(4,128)(2,1)S(1)}, bf16[1,4,16512]{2,1,0:T(4,128)(2,1)S(1)}, u32[]{:S(2)}, u32[]{:S(2)}) collective-permute-start(bf16[1,4,16512]{2,1,0:T(4,128)(2,1)S(1)} %shard_map.80.refs_8_), channel_id=1, source_target_pairs={{0,1},{1,0},{2,3},{3,2},{4,5},{5,4},{6,7},{7,6},{8,9},{9,8},{10,11... | collective-permute-start | bytes 396296 | tf_op jit(solution)/shard_map/ppermute | solution.py:23
  29.5 1.5 %collective-permute-start.12 = (f32[8,32,128]{2,1,0:T(8,128)S(1)}, f32[8,32,128]{2,1,0:T(8,128)S(1)}, u32[]{:S(2)}, u32[]{:S(2)}) collective-permute-start(f32[8,32,128]{2,1,0:T(8,128)S(1)} %get-tuple-element.36), channel_id=1, source_target_pairs={{0,1},{1,0},{2,3},{3,2},{4,5},{5,4},{6,7},{7,6},{8,9},{9,8},{10,11... | collective-permute-start | bytes 393224 | tf_op jit(solution)/shard_map/ppermute | solution.py:23
  29.7 1.2 %collective-permute-start.11 = (bf16[8,16,128]{2,1,0:T(8,128)(2,1)S(1)}, bf16[8,16,128]{2,1,0:T(8,128)(2,1)S(1)}, u32[]{:S(2)}, u32[]{:S(2)}) collective-permute-start(bf16[8,16,128]{2,1,0:T(8,128)(2,1)S(1)} %get-tuple-element.34), channel_id=1, source_target_pairs={{0,1},{1,0},{2,3},{3,2},{4,5},{5,4},{6,7},{7,6},{8,9},{9,8},{10,11... | collective-permute-start | bytes 98312 | tf_op jit(solution)/shard_map/ppermute | solution.py:23
  46.4 7.4 %collective-permute-start.17 = (bf16[1,4,8192]{2,1,0:T(4,128)(2,1)S(1)}, bf16[1,4,8192]{2,1,0:T(4,128)(2,1)S(1)}, u32[]{:S(2)}, u32[]{:S(2)}) collective-permute-start(bf16[1,4,8192]{2,1,0:T(4,128)(2,1)S(1)} %bitcast.8), channel_id=1, source_target_pairs={{0,4},{1,5},{2,6},{3,7},{4,12},{5,13},{6,14},{7,15},{8,0},{9,1},{1... | collective-permute-start | bytes 196616 | tf_op jit(solution)/shard_map/ppermute | solution.py:23
  46.6 7.2 %collective-permute-start.16 = (bf16[1,4,8192]{2,1,0:T(4,128)(2,1)S(1)}, bf16[1,4,8192]{2,1,0:T(4,128)(2,1)S(1)}, u32[]{:S(2)}, u32[]{:S(2)}) collective-permute-start(bf16[1,4,8192]{2,1,0:T(4,128)(2,1)S(1)} %bitcast.9), channel_id=1, source_target_pairs={{0,12},{1,13},{2,14},{3,15},{4,8},{5,9},{6,10},{7,11},{8,4},{9,5},... | collective-permute-start | bytes 196616 | tf_op jit(solution)/shard_map/ppermute | solution.py:23
  48.6 5.2 %collective-permute-start.15 = (bf16[1,4,8192]{2,1,0:T(4,128)(2,1)S(1)}, bf16[1,4,8192]{2,1,0:T(4,128)(2,1)S(1)}, u32[]{:S(2)}, u32[]{:S(2)}) collective-permute-start(bf16[1,4,8192]{2,1,0:T(4,128)(2,1)S(1)} %bitcast.10), channel_id=1, source_target_pairs={{0,8},{1,9},{2,10},{3,11},{4,0},{5,1},{6,2},{7,3},{8,12},{9,13},{1... | collective-permute-start | bytes 196616 | tf_op jit(solution)/shard_map/ppermute | solution.py:23
  49.3 4.4 %collective-permute-start.13 = (bf16[1,4,8192]{2,1,0:T(4,128)(2,1)S(1)}, bf16[1,4,8192]{2,1,0:T(4,128)(2,1)S(1)}, u32[]{:S(2)}, u32[]{:S(2)}) collective-permute-start(bf16[1,4,8192]{2,1,0:T(4,128)(2,1)S(1)} %bitcast.11), channel_id=1, source_target_pairs={{0,2},{1,3},{2,0},{3,1},{4,6},{5,7},{6,4},{7,5},{8,10},{9,11},{10,... | collective-permute-start | bytes 196616 | tf_op jit(solution)/shard_map/ppermute | solution.py:23
  53.8 5.7 %collective-permute-start.18 = (bf16[3,4,8192]{2,1,0:T(4,128)(2,1)S(1)}, bf16[3,4,8192]{2,1,0:T(4,128)(2,1)S(1)}, u32[]{:S(2)}, u32[]{:S(2)}) collective-permute-start(bf16[3,4,8192]{2,1,0:T(4,128)(2,1)S(1)} %shard_map.85.refs_1_.refs_3_), channel_id=1, source_target_pairs={{0,2},{1,3},{2,0},{3,1},{4,6},{5,7},{6,4},{7,5},{8,10},{9,11},{10,... | collective-permute-start | bytes 589832 | tf_op jit(solution)/shard_map/ppermute | solution.py:23
  55.3 3.4 %collective-permute-start.14 = (bf16[2,4,8192]{2,1,0:T(4,128)(2,1)S(1)}, bf16[2,4,8192]{2,1,0:T(4,128)(2,1)S(1)}, u32[]{:S(2)}, u32[]{:S(2)}) collective-permute-start(bf16[2,4,8192]{2,1,0:T(4,128)(2,1)S(1)} %pad_maximum_fusion.1), channel_id=1, source_target_pairs={{0,1},{1,0},{2,3},{3,2},{4,5},{5,4},{6,7},{7,6},{8,9},{9,8},{10,11... | collective-permute-start | bytes 393224 | tf_op jit(solution)/shard_map/ppermute | solution.py:23
  55.4 4.2 %collective-permute-start.19 = (bf16[3,4,8192]{2,1,0:T(4,128)(2,1)S(1)}, bf16[3,4,8192]{2,1,0:T(4,128)(2,1)S(1)}, u32[]{:S(2)}, u32[]{:S(2)}) collective-permute-start(bf16[3,4,8192]{2,1,0:T(4,128)(2,1)S(1)} %shard_map.85.refs_1_.refs_3_), channel_id=1, source_target_pairs={{0,1},{1,0},{2,3},{3,2},{4,5},{5,4},{6,7},{7,6},{8,9},{9,8},{10,11... | collective-permute-start | bytes 589832 | tf_op jit(solution)/shard_map/ppermute | solution.py:23
  59.6 1.5 %collective-permute-start.20 = (bf16[3,4,8192]{2,1,0:T(4,128)(2,1)S(1)}, bf16[3,4,8192]{2,1,0:T(4,128)(2,1)S(1)}, u32[]{:S(2)}, u32[]{:S(2)}) collective-permute-start(bf16[3,4,8192]{2,1,0:T(4,128)(2,1)S(1)} %shard_map.87.refs_4_), channel_id=1, source_target_pairs={{0,1},{1,0},{2,3},{3,2},{4,5},{5,4},{6,7},{7,6},{8,9},{9,8},{10,11... | collective-permute-start | bytes 589832 | tf_op jit(solution)/shard_map/ppermute | solution.py:23
